TPU v7x, 128 devices: a whole 4x4x4 slice. The times are simulated.
128 devices in a mesh: scen: 32 (over x, z, core), col: 4 (over y).
Axes of the slice: x: 4, y: 4, z: 4, core: 2. Of those that a mesh axis runs over, the one named last changes fastest.
Arguments:
- tile_values: float32 [32, 4, 64, 256, 256], P('scen', 'col'), may hold values from -1100 to 1100
- tile_rows: int32 [32, 4, 64], P('scen', 'col'), may hold values from 0 to 127, as said below
- tile_cols: int32 [32, 4, 64], P('scen', 'col'), may hold values from 0 to 263, as said below
- cost_local: float32 [32, 4, 8, 256], P('scen', 'col'), may hold values from -12 to 12
- cost_link: float32 [4, 256, 256], P('col'), may hold values from -5 to 5
- bound_local: float32 [32, 4, 8, 256], P('scen', 'col'), may hold values from 0.5 to 4
- bound_link: float32 [4, 256, 256], P('col'), may hold values from 0.5 to 4
- rhs: float32 [32, 128, 256], P('scen', 'col'), may hold values from -12 to 12
- start_local: float32 [32, 4, 8, 256], P('scen', 'col'), may hold values from 0 to 1
- start_link: float32 [4, 256, 256], P('col'), may hold values from 0 to 1
- start_dual: float32 [32, 128, 256], P('scen', 'col'), may hold values from -5 to 5
Outputs:
- solution_local: float32 [32, 4, 8, 256], P('scen', 'col')
- solution_link: float32 [4, 256, 256], P('col')
- multipliers: float32 [32, 128, 256], P('scen', 'col')
Inputs may be any that keep to these rules, and one draw needn't show every extreme that they name: Within one block the tiles stand at distinct positions, listed in increasing order of tile_rows * 264 + tile_cols. Every tile row of a scenario has a tile in some block of that scenario, every one of a block's first 8 tile columns has a tile in that block, and every linking tile column has a tile in some block of that index of col. `tile_cols`: tile columns below 8 are the block's scenario columns, the others linking tile columns.
All inputs are finite; a program needn't handle non-finite values.
Results may differ from a plain program's by a relative error of at most 0.0003.
Values sent between devices are 32-bit elements; how exact they have to be, the bound alone decides.
No kernel may reach another device: no remote copies, remote signals or barrier semaphores. Data moves between devices by JAX's collectives and lax.ppermute only.
A program may use at most 64 MiB of HBM per device.

v0:
```python
import jax
import jax.numpy as jnp
from jax import lax
from jax.sharding import PartitionSpec as P

TILE = 256
RT = 128
CT = 8
LT = 256
ITERS = 3


EPS = 1e-06
STEP = 0.9
HIGH = lax.Precision.HIGHEST


def indicator_tables(row_ids, col_ids):
    row_table = (jnp.arange(RT, dtype=jnp.int32)[:, None] == row_ids[None, :]).astype(jnp.float32)
    col_table = (jnp.arange(CT + LT, dtype=jnp.int32)[:, None] == col_ids[None, :]).astype(
        jnp.float32
    )
    return (row_table, col_table)


def block_stats(blocks, row_table, col_table, row_factor, col_factor, use_max):
    magnitude = jnp.abs(blocks) * row_factor[:, :, None] * col_factor[:, None, :]
    if use_max:
        row_part = jnp.max(magnitude, axis=2)
        col_part = jnp.max(magnitude, axis=1)
        row_stat = jnp.max(jnp.where(row_table[:, :, None] > 0, row_part[None], 0.0), axis=1)
        col_stat = jnp.max(jnp.where(col_table[:, :, None] > 0, col_part[None], 0.0), axis=1)
    else:
        row_stat = jnp.dot(row_table, jnp.sum(magnitude, axis=2), precision=HIGH)
        col_stat = jnp.dot(col_table, jnp.sum(magnitude, axis=1), precision=HIGH)
    return (row_stat, col_stat)


def apply_forward(blocks, row_table, col_ids, col_factor, values):
    picked = jnp.take(col_factor * values, col_ids, axis=0)
    product = jnp.einsum("nab,nb->na", blocks, picked, precision=HIGH)
    return jnp.dot(row_table, product, precision=HIGH)


def apply_backward(blocks, col_table, row_ids, row_factor, values):
    picked = jnp.take(row_factor * values, row_ids, axis=0)
    product = jnp.einsum("nab,na->nb", blocks, picked, precision=HIGH)
    return jnp.dot(col_table, product, precision=HIGH)


def owned_slice(values, start, count):
    return lax.dynamic_slice_in_dim(values, start, count, 0)


def body(
    tile_values,
    tile_rows,
    tile_cols,
    cost_local,
    cost_link,
    bound_local,
    bound_link,
    rhs,
    start_local,
    start_link,
    start_dual,
):
    blocks = tile_values[0, 0]
    row_ids = tile_rows[0, 0]
    col_ids = tile_cols[0, 0]
    row_table, col_table = indicator_tables(row_ids, col_ids)
    share_rows = rhs.shape[1]
    row_start = lax.axis_index("col") * share_rows
    row_scale = jnp.ones((RT, TILE), jnp.float32)
    local_scale = jnp.ones((CT, TILE), jnp.float32)
    link_scale = jnp.ones((LT, TILE), jnp.float32)
    for sweep_index in range(3):
        use_max = sweep_index < 2
        col_scale = jnp.concatenate([local_scale, link_scale], axis=0)
        row_stat, col_stat = block_stats(
            blocks,
            row_table,
            col_table,
            jnp.take(row_scale, row_ids, axis=0),
            jnp.take(col_scale, col_ids, axis=0),
            use_max,
        )
        if use_max:
            row_stat = lax.pmax(row_stat, "col")
            link_stat = lax.pmax(col_stat[CT:], "scen")
        else:
            row_stat = lax.psum(row_stat, "col")
            link_stat = lax.psum(col_stat[CT:], "scen")
        row_scale = row_scale / jnp.sqrt(row_stat + EPS)
        local_scale = local_scale / jnp.sqrt(col_stat[:CT] + EPS)
        link_scale = link_scale / jnp.sqrt(link_stat + EPS)
    col_scale = jnp.concatenate([local_scale, link_scale], axis=0)
    cost_loc = local_scale * cost_local[0, 0]
    cost_lnk = link_scale * cost_link[0]
    upper_loc = bound_local[0, 0] / local_scale
    upper_lnk = bound_link[0] / link_scale
    primal_loc = start_local[0, 0] / local_scale
    primal_lnk = start_link[0] / link_scale
    scale_share = owned_slice(row_scale, row_start, share_rows)
    rhs_share = scale_share * rhs[0]
    link_term = jnp.where(lax.axis_index("scen") == 0, jnp.sum(cost_lnk * cost_lnk), 0.0)
    cost_square, rhs_square = lax.psum(
        (jnp.sum(cost_loc * cost_loc) + link_term, jnp.sum(rhs_share * rhs_share)), ("scen", "col")
    )
    weight_ratio = jnp.sqrt((cost_square + EPS) / (rhs_square + EPS))
    primal_step = STEP / weight_ratio
    dual_step = STEP * weight_ratio
    gathered = (
        lax.all_gather(rhs[0], "col", axis=0, tiled=True),
        lax.all_gather(start_dual[0], "col", axis=0, tiled=True),
    )
    rhs_scaled = row_scale * gathered[0]
    dual_scaled = gathered[1] / row_scale
    for step_index in range(ITERS):
        dual_full = dual_scaled
        backward_sums = apply_backward(blocks, col_table, row_ids, row_scale, dual_full)
        grad_loc = local_scale * backward_sums[:CT]
        fresh_loc = jnp.clip(primal_loc - primal_step * (cost_loc - grad_loc), 0.0, upper_loc)
        grad_lnk = link_scale * lax.psum(backward_sums[CT:], "scen")
        fresh_lnk = jnp.clip(primal_lnk - primal_step * (cost_lnk - grad_lnk), 0.0, upper_lnk)
        bar_loc = 2.0 * fresh_loc - primal_loc
        bar_lnk = 2.0 * fresh_lnk - primal_lnk
        forward_sums = apply_forward(
            blocks, row_table, col_ids, col_scale, jnp.concatenate([bar_loc, bar_lnk], axis=0)
        )
        row_total = lax.psum(forward_sums, "col")
        dual_scaled = dual_scaled + dual_step * (rhs_scaled - row_scale * row_total)
        primal_loc = fresh_loc
        primal_lnk = fresh_lnk
    multipliers = owned_slice(row_scale * dual_scaled, row_start, share_rows)
    return (
        (local_scale * primal_loc)[None, None],
        (link_scale * primal_lnk)[None],
        multipliers[None],
    )


def solution(mesh):
    placed = (
        P("scen", "col", None, None, None),
        P("scen", "col", None),
        P("scen", "col", None),
        P("scen", "col", None, None),
        P("col", None, None),
        P("scen", "col", None, None),
        P("col", None, None),
        P("scen", "col", None),
        P("scen", "col", None, None),
        P("col", None, None),
        P("scen", "col", None),
    )
    return jax.shard_map(
        body,
        mesh=mesh,
        in_specs=placed,
        out_specs=(P("scen", "col", None, None), P("col", None, None), P("scen", "col", None)),
        check_vma=False,
    )
```

profile of v0, /device:TPU:0, one launch (start us, length us, event | category | flops | bytes accessed | tf_op | source)
XLA Modules:
  0.0 997.9 jit_solution(2040115541582286903)
XLA Ops:
  11.5 9.5 fusion.12
  31.5 12.6 %all-gather = f32[1,128,256]{2,1,0:T(8,128)S(1)} all-gather(f32[1,32,256]{2,1,0:T(8,128)S(1)} %copy-done.11), channel_id=2, replica_groups=mesh['scen'=32,'col'=4] {'col'}, dimensions={1}, use_global_device_ids=true | all-gather | bytes 163840 | tf_op jit(solution)/shard_map/all_gather | solution.py:115
  44.1 24.0 %all-reduce.15.cloned.1.call-done = f32[128,256]{1,0:T(8,128)} async-done(((f32[128,256]{1,0:T(8,128)}), f32[128,256]{1,0:T(8,128)}) %all-reduce.15.cloned.1.call-update) | async-done | bytes 131088 | tf_op jit(solution)/shard_map/pmax | solution.py:89
  69.9 104.5 %all-reduce.17.cloned.1.call-done = f32[256,256]{1,0:T(8,128)} async-done(((f32[256,256]{1,0:T(8,128)}), f32[256,256]{1,0:T(8,128)}) %all-reduce.17.cloned.1.call-update) | async-done | bytes 262160 | tf_op jit(solution)/shard_map/pmax | solution.py:90
  176.2 9.6 fusion.14
  189.1 6.2 select_reduce_fusion
  196.1 33.8 %all-reduce.19.cloned.1.call-done = f32[128,256]{1,0:T(8,128)} async-done(((f32[128,256]{1,0:T(8,128)}), f32[128,256]{1,0:T(8,128)}) %all-reduce.19.cloned.1.call-update) | async-done | bytes 131088 | tf_op jit(solution)/shard_map/pmax | solution.py:89
  231.6 104.0 %all-reduce.21.cloned.1.call-done = f32[256,256]{1,0:T(8,128)} async-done(((f32[256,256]{1,0:T(8,128)}), f32[256,256]{1,0:T(8,128)}) %all-reduce.21.cloned.1.call-update) | async-done | bytes 262160 | tf_op jit(solution)/shard_map/pmax | solution.py:90
  337.5 9.4 fusion.16
  349.3 39.3 %all-reduce.23.cloned.1.call-done = f32[128,256]{1,0:T(8,128)} async-done(((f32[128,256]{1,0:T(8,128)}), f32[128,256]{1,0:T(8,128)}) %all-reduce.23.cloned.1.call-update) | async-done | bytes 131088 | tf_op jit(solution)/shard_map/psum | solution.py:92
  390.2 11.5 %fusion.10 = f32[64,1,256]{2,1,0:T(1,128)S(1)} fusion(f32[1,1,64,256,256]{4,3,2,1,0:T(8,128)} %param.15, f32[64,256,1]{1,0,2:T(8,128)S(1)} %select_bitcast_fusion.5), kind=kOutput, calls=%fused_computation.24 | convolution fusion | flops 50331648 | bytes 16908288 | tf_op jit(solution)/shard_map/nab,na->nb/dot_general | solution.py:47
  404.1 103.1 %all-reduce.35.cloned.1.call-done = (f32[256,256]{1,0:T(8,128)}, f32[256,256]{1,0:T(8,128)}) async-done(((f32[256,256]{1,0:T(8,128)}, f32[256,256]{1,0:T(8,128)}), (f32[256,256]{1,0:T(8,128)}, f32[256,256]{1,0:T(8,128)})) %all-reduce.35.cloned.1.call-update) | async-done | bytes 524304 | tf_op jit(solution)/shard_map/psum | solution.py:93
  510.2 65.7 %all-reduce.1 = (f32[]{:T(128)}, f32[]{:T(128)}) all-reduce(f32[]{:T(128)S(6)} %add.91, f32[]{:T(128)} %fusion.54), channel_id=1, replica_groups=mesh['scen'=32,'col'=4] {'scen','col'}, use_global_device_ids=true, to_apply=%region_16.19 | all-reduce | flops 2 | bytes 16 | tf_op jit(solution)/shard_map/psum | solution.py:107
  579.2 17.2 %fusion.8 = f32[64,1,256]{2,1,0:T(1,128)S(1)} fusion(f32[1,1,64,256,256]{4,3,2,1,0:T(8,128)} %param.15, f32[64,256,1]{1,0,2:T(8,128)S(1)} %select_bitcast_fusion.4), kind=kOutput, calls=%fused_computation.22 | convolution fusion | flops 50331648 | bytes 16908288 | tf_op jit(solution)/shard_map/nab,nb->na/dot_general | solution.py:41
  597.4 12.0 %all-gather.1 = f32[1,128,256]{2,1,0:T(8,128)S(1)} all-gather(f32[1,32,256]{2,1,0:T(8,128)S(1)} %copy-done.8), channel_id=3, replica_groups=mesh['scen'=32,'col'=4] {'col'}, dimensions={1}, use_global_device_ids=true | all-gather | bytes 163840 | tf_op jit(solution)/shard_map/all_gather | solution.py:114
  609.4 25.5 %all-reduce.25.cloned.1.call-done = f32[128,256]{1,0:T(8,128)} async-done(((f32[128,256]{1,0:T(8,128)}), f32[128,256]{1,0:T(8,128)}) %all-reduce.25.cloned.1.call-update) | async-done | bytes 131088 | tf_op jit(solution)/shard_map/psum | solution.py:131
  636.5 11.6 %fusion.6 = f32[64,1,256]{2,1,0:T(1,128)S(1)} fusion(f32[1,1,64,256,256]{4,3,2,1,0:T(8,128)} %param.15, f32[64,256,1]{1,0,2:T(8,128)S(1)} %select_bitcast_fusion.3), kind=kOutput, calls=%fused_computation.20 | convolution fusion | flops 50331648 | bytes 16908288 | tf_op jit(solution)/shard_map/nab,na->nb/dot_general | solution.py:47
  649.3 101.8 %all-reduce.27.cloned.1.call-done = f32[256,256]{1,0:T(8,128)} async-done(((f32[256,256]{1,0:T(8,128)}), f32[256,256]{1,0:T(8,128)}) %all-reduce.27.cloned.1.call-update) | async-done | bytes 262160 | tf_op jit(solution)/shard_map/psum | solution.py:124
  753.1 17.2 %fusion.4 = f32[64,1,256]{2,1,0:T(1,128)S(1)} fusion(f32[1,1,64,256,256]{4,3,2,1,0:T(8,128)} %param.15, f32[64,256,1]{1,0,2:T(8,128)S(1)} %select_bitcast_fusion.2), kind=kOutput, calls=%fused_computation.18 | convolution fusion | flops 50331648 | bytes 16908288 | tf_op jit(solution)/shard_map/nab,nb->na/dot_general | solution.py:41
  771.2 40.7 %all-reduce.29.cloned.1.call-done = f32[128,256]{1,0:T(8,128)} async-done(((f32[128,256]{1,0:T(8,128)}), f32[128,256]{1,0:T(8,128)}) %all-reduce.29.cloned.1.call-update) | async-done | bytes 131088 | tf_op jit(solution)/shard_map/psum | solution.py:131
  813.7 11.5 %fusion.2 = f32[64,1,256]{2,1,0:T(1,128)S(1)} fusion(f32[1,1,64,256,256]{4,3,2,1,0:T(8,128)} %param.15, f32[64,256,1]{1,0,2:T(8,128)S(1)} %select_bitcast_fusion.1), kind=kOutput, calls=%fused_computation.16 | convolution fusion | flops 50331648 | bytes 16908288 | tf_op jit(solution)/shard_map/nab,na->nb/dot_general | solution.py:47
  826.5 101.8 %all-reduce.31.cloned.1.call-done = f32[256,256]{1,0:T(8,128)} async-done(((f32[256,256]{1,0:T(8,128)}), f32[256,256]{1,0:T(8,128)}) %all-reduce.31.cloned.1.call-update) | async-done | bytes 262160 | tf_op jit(solution)/shard_map/psum | solution.py:124
  931.0 17.1 %fusion = f32[64,1,256]{2,1,0:T(1,128)S(1)} fusion(f32[1,1,64,256,256]{4,3,2,1,0:T(8,128)} %param.15, f32[64,256,1]{1,0,2:T(8,128)S(1)} %select_bitcast_fusion), kind=kOutput, calls=%fused_computation.14 | convolution fusion | flops 50331648 | bytes 16908288 | tf_op jit(solution)/shard_map/nab,nb->na/dot_general | solution.py:41
  949.6 40.2 %all-reduce.33.cloned.1.call-done = f32[128,256]{1,0:T(8,128)} async-done(((f32[128,256]{1,0:T(8,128)}), f32[128,256]{1,0:T(8,128)}) %all-reduce.33.cloned.1.call-update) | async-done | bytes 131088 | tf_op jit(solution)/shard_map/psum | solution.py:131
  (129 shorter events, 50.9 us)
Async XLA Ops:
  7.2 61.0 %all-reduce.15.cloned.1.call-start = ((), (), s32[]{:S(2)}) async-start(), calls=%async_computation | async-start | bytes 262144 | tf_op jit(solution)/shard_map/pmax | solution.py:89
  24.4 150.0 %all-reduce.17.cloned.1.call-start = ((), (), s32[]{:S(2)}) async-start(), calls=%async_computation.1 | async-start | bytes 524288 | tf_op jit(solution)/shard_map/pmax | solution.py:90
  31.4 198.5 %all-reduce.19.cloned.1.call-start = ((), (), s32[]{:S(2)}) async-start(), calls=%async_computation.2 | async-start | bytes 262144 | tf_op jit(solution)/shard_map/pmax | solution.py:89
  68.2 161.8 %copy-start.6 = (f32[128,256]{1,0:T(8,128)S(1)}, f32[128,256]{1,0:T(8,128)}, u32[]{:S(2)}) copy-start(f32[128,256]{1,0:T(8,128)} %all-reduce.15.cloned.1.call-done) | copy-start | bytes 393220
  174.4 161.3 %copy-start.4 = (f32[256,256]{1,0:T(8,128)S(1)}, f32[256,256]{1,0:T(8,128)}, u32[]{:S(2)}) copy-start(f32[256,256]{1,0:T(8,128)} %all-reduce.17.cloned.1.call-done) | copy-start | bytes 786436
  176.2 170.7 %copy-start.13 = (s32[1,1,64]{2,1,0:T(1,128)S(1)}, s32[1,1,64]{2,1,0:T(1,128)}, u32[]{:S(2)}) copy-start(s32[1,1,64]{2,1,0:T(1,128)} %param.16) | copy-start | bytes 772
  189.1 146.5 %all-reduce.21.cloned.1.call-start = ((), (), s32[]{:S(2)}) async-start(), calls=%async_computation.3 | async-start | bytes 524288 | tf_op jit(solution)/shard_map/pmax | solution.py:90
  196.1 192.5 %all-reduce.23.cloned.1.call-start = ((), (), s32[]{:S(2)}) async-start(), calls=%async_computation.4 | async-start | bytes 262144 | tf_op jit(solution)/shard_map/psum | solution.py:92
  337.4 65.4 %copy-start.9 = (f32[1,1,8,256]{3,2,1,0:T(8,128)S(1)}, f32[1,1,8,256]{3,2,1,0:T(8,128)}, u32[]{:S(2)}) copy-start(f32[1,1,8,256]{3,2,1,0:T(8,128)} %param.18) | copy-start | bytes 24580
  337.4 66.0 %copy-start.8 = (f32[1,32,256]{2,1,0:T(8,128)S(1)}, f32[1,32,256]{2,1,0:T(8,128)}, u32[]{:S(2)}) copy-start(f32[1,32,256]{2,1,0:T(8,128)} %param.22) | copy-start | bytes 98308
  337.4 169.8 %copy-start = (f32[1,256,256]{2,1,0:T(8,128)S(1)}, f32[1,256,256]{2,1,0:T(8,128)}, u32[]{:S(2)}) copy-start(f32[1,256,256]{2,1,0:T(8,128)} %param.19) | copy-start | bytes 786436
  337.4 239.9 %copy-start.10 = (f32[1,1,8,256]{3,2,1,0:T(8,128)S(1)}, f32[1,1,8,256]{3,2,1,0:T(8,128)}, u32[]{:S(2)}) copy-start(f32[1,1,8,256]{3,2,1,0:T(8,128)} %param.20) | copy-start | bytes 24580
  337.5 239.9 %copy-start.14 = (f32[1,1,8,256]{3,2,1,0:T(8,128)S(1)}, f32[1,1,8,256]{3,2,1,0:T(8,128)}, u32[]{:S(2)}) copy-start(f32[1,1,8,256]{3,2,1,0:T(8,128)} %param.23) | copy-start | bytes 24580
  337.5 239.9 %copy-start.1 = (f32[1,256,256]{2,1,0:T(8,128)S(1)}, f32[1,256,256]{2,1,0:T(8,128)}, u32[]{:S(2)}) copy-start(f32[1,256,256]{2,1,0:T(8,128)} %param.24) | copy-start | bytes 786436
  337.5 239.9 %copy-start.2 = (f32[1,256,256]{2,1,0:T(8,128)S(1)}, f32[1,256,256]{2,1,0:T(8,128)}, u32[]{:S(2)}) copy-start(f32[1,256,256]{2,1,0:T(8,128)} %param.21) | copy-start | bytes 786436
  347.8 159.4 %all-reduce.35.cloned.1.call-start = ((), (), s32[]{:S(2)}) async-start(), calls=%async_computation.10 | async-start | bytes 1048576 | tf_op jit(solution)/shard_map/psum | solution.py:93
  402.8 232.0 %all-reduce.25.cloned.1.call-start = ((), (), s32[]{:S(2)}) async-start(), calls=%async_computation.5 | async-start | bytes 262144 | tf_op jit(solution)/shard_map/psum | solution.py:131
  579.2 171.9 %copy-start.3 = (f32[256,256]{1,0:T(8,128)S(1)}, f32[256,256]{1,0:T(8,128)}, u32[]{:S(2)}) copy-start(f32[256,256]{1,0:T(8,128)} %get-tuple-element.14) | copy-start | bytes 786436
  597.3 153.8 %all-reduce.27.cloned.1.call-start = ((), (), s32[]{:S(2)}) async-start(), calls=%async_computation.6 | async-start | bytes 524288 | tf_op jit(solution)/shard_map/psum | solution.py:124
  636.5 175.5 %copy-start.7 = (f32[128,256]{1,0:T(8,128)S(1)}, f32[128,256]{1,0:T(8,128)}, u32[]{:S(2)}) copy-start(f32[128,256]{1,0:T(8,128)} %all-reduce.25.cloned.1.call-done) | copy-start | bytes 393220
  649.1 162.9 %all-reduce.29.cloned.1.call-start = ((), (), s32[]{:S(2)}) async-start(), calls=%async_computation.7 | async-start | bytes 262144 | tf_op jit(solution)/shard_map/psum | solution.py:131
  753.1 175.2 %copy-start.5 = (f32[256,256]{1,0:T(8,128)S(1)}, f32[256,256]{1,0:T(8,128)}, u32[]{:S(2)}) copy-start(f32[256,256]{1,0:T(8,128)} %all-reduce.27.cloned.1.call-done) | copy-start | bytes 786436
  771.2 157.1 %all-reduce.31.cloned.1.call-start = ((), (), s32[]{:S(2)}) async-start(), calls=%async_computation.8 | async-start | bytes 524288 | tf_op jit(solution)/shard_map/psum | solution.py:124
  826.2 163.6 %all-reduce.33.cloned.1.call-start = ((), (), s32[]{:S(2)}) async-start(), calls=%async_computation.9 | async-start | bytes 262144 | tf_op jit(solution)/shard_map/psum | solution.py:131
  (2 other events, 41.6 us)
Sparse Core Ops, SparseCore 0:
  24.5 43.6 all-reduce.14
  72.3 102.0 all-reduce.16
  189.2 40.6 all-reduce.18
  233.6 102.0 all-reduce.20
  347.9 40.6 all-reduce.22
  402.9 104.2 all-reduce.34
  597.4 37.3 all-reduce.24
  649.2 101.9 all-reduce.26
  771.3 40.6 all-reduce.28
  826.3 101.9 all-reduce.30
  949.1 40.6 all-reduce.32
where the time goes:
time: 1010 us; the launch traced here: 998 us
  waiting for transfers between devices  719 us (71%)
  matrix products  90.6 us (9%)
  blocking collectives  90.4 us (9%)
  other arithmetic  67.2 us (7%)
  between operations  17.2 us (2%)
  local copies, waits for them, and re-layouts  12.4 us (1%)
    pmax x2, waiting for transfers between devices, body(): link_stat = lax.pmax(col_stat[CT:], 'scen')  208 us
    psum x2, waiting for transfers between devices, body(): grad_lnk = link_scale * lax.psum(backward_sums[CT:], 'scen')  204 us
    psum x3, waiting for transfers between devices, body(): row_total = lax.psum(forward_sums, 'col')  106 us
    psum x1, waiting for transfers between devices, body(): link_stat = lax.psum(col_stat[CT:], 'scen')  103 us
    psum x1, blocking collectives, body(): lax.psum((jnp.sum(cost_loc * cost_loc) + link_term, jnp.sum(rhs_share * r...  65.7 us
    pmax x2, waiting for transfers between devices, body(): row_stat = lax.pmax(row_stat, 'col')  57.8 us
    dot_general x3, matrix products, apply_forward(): product = jnp.einsum('nab,nb->na', blocks, picked, precision=HIGH)  51.5 us
    psum x1, waiting for transfers between devices, body(): row_stat = lax.psum(row_stat, 'col')  39.3 us
  transfers between devices with their start and end apart: 11, of which 11 were waited for; matrix products, arithmetic and copies ran while one was open for 2% of the time, Pallas kernels for 0%

commit v1 on v0

v1 whole, which is shorter than its diff:
```python
import functools

import jax
import jax.numpy as jnp
from jax import lax
from jax.experimental import pallas as pl
from jax.experimental.pallas import tpu as pltpu
from jax.sharding import PartitionSpec as P

TILE = 256
RT = 128
CT = 8
LT = 256
ITERS = 3
NT = 64
HALF = LT // 2
CW = CT + LT
GROUP = 8
STEPS = NT // GROUP

EPS = 1e-06
STEP = 0.9
F32 = jnp.float32
LANES = 128


def swap_core(x):
    return lax.ppermute(x, "scen", [(i, i ^ 1) for i in range(32)])


def swap_z(x, k):
    return lax.ppermute(x, "scen", [(i, i ^ (k << 1)) for i in range(32)])


def swap_x(x, k):
    return lax.ppermute(x, "scen", [(i, i ^ (k << 3)) for i in range(32)])


def swap_y(x, k):
    return lax.ppermute(x, "col", [(i, i ^ k) for i in range(4)])


def tree(op, own, got):
    return op(op(own, got[0]), op(got[1], got[2]))


def row_pass(tiles_ref, t, col, row, colf_ref, rowout_ref, op, magnitude):
    for h in range(2):
        a = tiles_ref[t, h * LANES : (h + 1) * LANES, 0:LANES]
        b = tiles_ref[t, h * LANES : (h + 1) * LANES, LANES:TILE]
        if magnitude:
            a, b = jnp.abs(a), jnp.abs(b)
        if colf_ref is not None:
            a = a * colf_ref[0, pl.ds(col, 1), :]
            b = b * colf_ref[1, pl.ds(col, 1), :]
        m = op(a, b).T
        s = jnp.max(m, axis=0, keepdims=True) if op is jnp.maximum else jnp.sum(m, axis=0, keepdims=True)
        at = (h, pl.ds(row, 1), slice(None))
        rowout_ref[at] = op(rowout_ref[at], s)


def col_pass(tiles_ref, t, col, row, rowf_ref, colout_ref, op, magnitude):
    parts = [None, None]
    for h in range(2):
        if rowf_ref is not None:
            f = jnp.broadcast_to(rowf_ref[h, pl.ds(row, 1), :], (LANES, LANES)).T
        for w in range(2):
            a = tiles_ref[t, h * LANES : (h + 1) * LANES, w * LANES : (w + 1) * LANES]
            if magnitude:
                a = jnp.abs(a)
            if rowf_ref is not None:
                a = a * f
            a = a.reshape(16, 8, LANES)
            s = jnp.max(a, axis=0) if op is jnp.maximum else jnp.sum(a, axis=0)
            parts[w] = s if parts[w] is None else op(parts[w], s)
    for w in range(2):
        s = parts[w]
        s = jnp.max(s, axis=0, keepdims=True) if op is jnp.maximum else jnp.sum(s, axis=0, keepdims=True)
        at = (w, pl.ds(col, 1), slice(None))
        colout_ref[at] = op(colout_ref[at], s)


def split_to(ref, value, lo=0):
    for w in range(2):
        ref[w, lo : lo + value.shape[0], :] = value[:, w * LANES : (w + 1) * LANES]


def join_from(ref, out):
    for w in range(2):
        out[:, w * LANES : (w + 1) * LANES] = ref[w]


ROWS = pltpu.VMEM((2, RT, LANES), F32)
COLS = pltpu.VMEM((2, CW, LANES), F32)


def tile_call(kernel, ids, tiles, operands, outs, scratch=()):
    def spec(x):
        if x.shape[0] == 1:
            return pl.BlockSpec(memory_space=pltpu.SMEM)
        return pl.BlockSpec(x.shape, lambda i, *_: (0,) * len(x.shape))

    return pl.pallas_call(
        kernel,
        out_shape=tuple(jax.ShapeDtypeStruct(s, F32) for s in outs),
        grid_spec=pltpu.PrefetchScalarGridSpec(
            num_scalar_prefetch=2,
            grid=(STEPS,),
            in_specs=[pl.BlockSpec((GROUP, TILE, TILE), lambda i, *_: (i, 0, 0))]
            + [spec(x) for x in operands],
            out_specs=tuple(pl.BlockSpec(s, lambda i, *_: (0, 0)) for s in outs),
            scratch_shapes=list(scratch),
        ),
        compiler_params=pltpu.CompilerParams(vmem_limit_bytes=40 * 1024 * 1024),
    )(*ids, tiles, *operands)


def each_tile(rows_ref, cols_ref, visit):
    base = pl.program_id(0) * GROUP
    for t in range(GROUP):
        visit(t, cols_ref[base + t], rows_ref[base + t])


def at_first(fn):
    pl.when(pl.program_id(0) == 0)(fn)


def at_last(fn):
    pl.when(pl.program_id(0) == STEPS - 1)(fn)


def first_stats_kernel(rows_ref, cols_ref, tiles_ref, rowout, colout, racc, cacc):
    @at_first
    def _():
        racc[...] = jnp.zeros_like(racc)
        cacc[...] = jnp.zeros_like(cacc)

    def visit(t, col, row):
        row_pass(tiles_ref, t, col, row, None, racc, jnp.maximum, True)
        col_pass(tiles_ref, t, col, row, None, cacc, jnp.maximum, True)

    each_tile(rows_ref, cols_ref, visit)

    @at_last
    def _():
        join_from(racc, rowout)
        join_from(cacc, colout)


def next_stats_kernel(
    op, first, rows_ref, cols_ref, tiles_ref, r0, r1, r2, r3, loc, mine, other, *rest
):
    if first:
        rowout, colout, rownew, colnew, racc, cacc, rowf, colf = rest
    else:
        rowold, colold, rowout, colout, rownew, colnew, racc, cacc, rowf, colf = rest

    @at_first
    def _():
        row = tree(jnp.maximum, r0[...], (r1[...], r2[...], r3[...]))
        if first:
            new = 1.0 / jnp.sqrt(row + EPS)
        else:
            old = rowold[...]
            new = old / jnp.sqrt(old * row + EPS)
        rownew[...] = new
        split_to(rowf, new)
        for lo, hi, src in ((0, CT, loc), (CT, CT + HALF, mine), (CT + HALF, CW, other)):
            stat = src[0 : hi - lo]
            if first:
                new = 1.0 / jnp.sqrt(stat + EPS)
            else:
                old = colold[lo:hi]
                new = old / jnp.sqrt(old * stat + EPS)
            colnew[lo:hi] = new
            split_to(colf, new, lo)
        racc[...] = jnp.zeros_like(racc)
        cacc[...] = jnp.zeros_like(cacc)

    def visit(t, col, row):
        row_pass(tiles_ref, t, col, row, colf, racc, op, True)
        col_pass(tiles_ref, t, col, row, rowf, cacc, op, True)

    each_tile(rows_ref, cols_ref, visit)

    @at_last
    def _():
        join_from(racc, rowout)
        join_from(cacc, colout)


def first_backward_kernel(rows_ref, cols_ref, tiles_ref, dual, colout, cacc, work):
    @at_first
    def _():
        split_to(work, dual[...])
        cacc[...] = jnp.zeros_like(cacc)

    def visit(t, col, row):
        col_pass(tiles_ref, t, col, row, work, cacc, jnp.add, False)

    each_tile(rows_ref, cols_ref, visit)

    @at_last
    def _():
        join_from(cacc, colout)


def backward_kernel(
    rows_ref, cols_ref, tiles_ref, scalars, r0, r1, r2, r3, dual, rhs, rowf, colout, dualnew, cacc, work
):
    @at_first
    def _():
        total = tree(jnp.add, r0[...], (r1[...], r2[...], r3[...]))
        new = dual[...] + scalars[0, 1] * (rhs[...] - rowf[...] * total)
        dualnew[...] = new
        split_to(work, rowf[...] * new)
        cacc[...] = jnp.zeros_like(cacc)

    def visit(t, col, row):
        col_pass(tiles_ref, t, col, row, work, cacc, jnp.add, False)

    each_tile(rows_ref, cols_ref, visit)

    @at_last
    def _():
        join_from(cacc, colout)


def forward_kernel(
    rows_ref, cols_ref, tiles_ref, scalars, loc, mine, other, primal, cost, upper, colf, rowout, fresh, racc, work
):
    @at_first
    def _():
        for lo, hi, src in ((0, CT, loc), (CT, CT + HALF, mine), (CT + HALF, CW, other)):
            at = slice(lo, hi)
            x, scale = primal[at], colf[at]
            grad = scale * src[0 : hi - lo]
            new = jnp.clip(x - scalars[0, 0] * (cost[at] - grad), 0.0, upper[at])
            fresh[at] = new
            split_to(work, scale * (2.0 * new - x), lo)
        racc[...] = jnp.zeros_like(racc)

    def visit(t, col, row):
        row_pass(tiles_ref, t, col, row, work, racc, jnp.add, False)

    each_tile(rows_ref, cols_ref, visit)

    @at_last
    def _():
        join_from(racc, rowout)


def body(
    tile_values,
    tile_rows,
    tile_cols,
    cost_local,
    cost_link,
    bound_local,
    bound_link,
    rhs,
    start_local,
    start_link,
    start_dual,
):
    tiles = tile_values[0, 0]
    scen = lax.axis_index("scen")
    y_at = lax.axis_index("col")
    x_at = scen // 8
    core = scen % 2
    share = RT // 4
    chunk = HALF // 4

    raw_cols = tile_cols[0, 0]
    turned = CT + ((raw_cols - CT) ^ (core * HALF))
    ids = (tile_rows[0, 0], jnp.where(raw_cols < CT, raw_cols, turned))

    def turn(x):
        return jnp.where(core == 0, x, jnp.concatenate([x[HALF:], x[:HALF]], axis=0))

    def whole_columns(local, link):
        return jnp.concatenate([local[0, 0], turn(link[0])], axis=0)

    def halves(x):
        return x[CT : CT + HALF], x[CT + HALF :]

    pair = jnp.concatenate([rhs[0], start_dual[0]], axis=0)
    parts = jnp.stack([pair] + [swap_y(pair, k) for k in (1, 2, 3)])
    parts = jnp.take(parts, y_at ^ jnp.arange(4), axis=0)
    rhs_rows = parts[:, :share].reshape(RT, TILE)
    dual_rows = parts[:, share:].reshape(RT, TILE)

    row_part, col_part = tile_call(
        first_stats_kernel, ids, tiles, (), ((RT, TILE), (CW, TILE)), (ROWS, COLS)
    )
    mine, other = halves(col_part)
    rows_got = [swap_y(row_part, k) for k in (1, 2, 3)]
    link = jnp.maximum(mine, swap_core(other))
    link = tree(jnp.maximum, link, [swap_x(link, k) for k in (1, 2, 3)])
    link = tree(jnp.maximum, link, [swap_z(link, k) for k in (1, 2, 3)])
    (grad0,) = tile_call(first_backward_kernel, ids, tiles, (dual_rows,), ((CW, TILE),), (COLS, ROWS))
    grad_mine, grad_other = halves(grad0)
    grad_half = grad_mine + swap_core(grad_other)

    def scales(row_total, loc, mine, other, row_old, col_old):
        row = row_old / jnp.sqrt(row_old * row_total + EPS)
        stat = jnp.concatenate([loc, mine, other], axis=0)
        return row, col_old / jnp.sqrt(col_old * stat + EPS)

    operands = (row_part, *rows_got, col_part, link, swap_core(link))
    row_part, col_part, row_scale, col_scale = tile_call(
        functools.partial(next_stats_kernel, jnp.maximum, True),
        ids,
        tiles,
        operands,
        ((RT, TILE), (CW, TILE), (RT, TILE), (CW, TILE)),
        (ROWS, COLS, ROWS, COLS),
    )
    mine, other = halves(col_part)
    rows_got = [swap_y(row_part, k) for k in (1, 2, 3)]
    link = jnp.maximum(mine, swap_core(other))
    got = [
        swap_x(
            jnp.concatenate(
                [link, lax.dynamic_slice_in_dim(grad_half, (x_at ^ k) * chunk, chunk, 0)], axis=0
            ),
            k,
        )
        for k in (1, 2, 3)
    ]
    link = tree(jnp.maximum, link, [g[:HALF] for g in got])
    grad_chunk = tree(
        jnp.add,
        lax.dynamic_slice_in_dim(grad_half, x_at * chunk, chunk, 0),
        [g[HALF:] for g in got],
    )
    both = jnp.concatenate([link, grad_chunk], axis=0)
    got = [swap_z(both, k) for k in (1, 2, 3)]
    link = tree(jnp.maximum, link, [g[:HALF] for g in got])
    grad_chunk = tree(jnp.add, grad_chunk, [g[HALF:] for g in got])

    operands = (row_part, *rows_got, col_part, link, swap_core(link), row_scale, col_scale)
    row_part, col_part, row_scale, col_scale = tile_call(
        functools.partial(next_stats_kernel, jnp.add, False),
        ids,
        tiles,
        operands,
        ((RT, TILE), (CW, TILE), (RT, TILE), (CW, TILE)),
        (ROWS, COLS, ROWS, COLS),
    )
    mine, other = halves(col_part)
    rows_got = [swap_y(row_part, k) for k in (1, 2, 3)]
    link = mine + swap_core(other)
    both = jnp.concatenate([link, grad_chunk], axis=0)
    got = [swap_x(both, k) for k in (1, 2, 3)]
    link = tree(jnp.add, link, [g[:HALF] for g in got])
    parts = jnp.stack([grad_chunk] + [g[HALF:] for g in got])
    grad_half = jnp.take(parts, x_at ^ jnp.arange(4), axis=0).reshape(HALF, TILE)
    row_total = tree(jnp.add, row_part, rows_got)
    row_scale = row_scale / jnp.sqrt(row_scale * row_total + EPS)
    rhs_scaled = row_scale * rhs_rows
    dual_scaled = dual_rows / row_scale
    rhs_square = jnp.sum((rhs_scaled * rhs_scaled).reshape(16, 8, TILE), axis=0)
    local_old = col_scale[:CT]
    cost_loc = local_old / jnp.sqrt(local_old * col_part[:CT] + EPS) * cost_local[0, 0]
    squares = jnp.concatenate([rhs_square, cost_loc * cost_loc], axis=0)
    both = jnp.concatenate([link, squares], axis=0)
    got = [swap_z(both, k) for k in (1, 2, 3)]
    both = tree(jnp.add, both, got)
    back = swap_core(jnp.concatenate([both, grad_half], axis=0))
    squares = both[HALF:] + back[HALF : HALF + 2 * CT]
    stat = jnp.concatenate([col_part[:CT], both[:HALF], back[:HALF]], axis=0)
    col_scale = col_scale / jnp.sqrt(col_scale * stat + EPS)
    grads = (grad0, grad_half, back[HALF + 2 * CT :])
    cost = col_scale * whole_columns(cost_local, cost_link)
    upper = whole_columns(bound_local, bound_link) / col_scale
    primal = whole_columns(start_local, start_link) / col_scale

    link_square = jnp.sum((cost[CT:] * cost[CT:]).reshape(LT // 8, 8, TILE), axis=0)
    by_x = tree(jnp.add, squares, [swap_x(squares, k) for k in (1, 2, 3)])
    cost_part = by_x[CT:] + link_square
    cost_total = tree(jnp.add, cost_part, [swap_y(cost_part, k) for k in (1, 2, 3)])
    weight_ratio = jnp.sqrt((jnp.sum(cost_total) + EPS) / (jnp.sum(by_x[:CT]) + EPS))
    steps = jnp.stack([STEP / weight_ratio, STEP * weight_ratio])[None]

    for index in range(ITERS):
        row_part, primal = tile_call(
            forward_kernel,
            ids,
            tiles,
            (steps, *grads, primal, cost, upper, col_scale),
            ((RT, TILE), (CW, TILE)),
            (ROWS, COLS),
        )
        if index == ITERS - 1:
            break
        rows_got = [swap_y(row_part, k) for k in (1, 2, 3)]
        col_part, dual_scaled = tile_call(
            backward_kernel,
            ids,
            tiles,
            (steps, row_part, *rows_got, dual_scaled, rhs_scaled, row_scale),
            ((CW, TILE), (RT, TILE)),
            (COLS, ROWS),
        )
        mine, other = halves(col_part)
        link = mine + swap_core(other)
        link = tree(jnp.add, link, [swap_x(link, k) for k in (1, 2, 3)])
        link = tree(jnp.add, link, [swap_z(link, k) for k in (1, 2, 3)])
        grads = (col_part, link, swap_core(link))

    def piece(x, k):
        return lax.dynamic_slice_in_dim(x, (y_at ^ k) * share, share, 0)

    total = tree(jnp.add, piece(row_part, 0), [swap_y(piece(row_part, k), k) for k in (1, 2, 3)])
    scale = piece(row_scale, 0)
    dual = piece(dual_scaled, 0) + steps[0, 1] * (piece(rhs_scaled, 0) - scale * total)
    solved = col_scale * primal
    return (
        solved[:CT][None, None],
        turn(solved[CT:])[None],
        (scale * dual)[None],
    )


def solution(mesh):
    placed = (
        P("scen", "col", None, None, None),
        P("scen", "col", None),
        P("scen", "col", None),
        P("scen", "col", None, None),
        P("col", None, None),
        P("scen", "col", None, None),
        P("col", None, None),
        P("scen", "col", None),
        P("scen", "col", None, None),
        P("col", None, None),
        P("scen", "col", None),
    )
    return jax.shard_map(
        body,
        mesh=mesh,
        in_specs=placed,
        out_specs=(P("scen", "col", None, None), P("col", None, None), P("scen", "col", None)),
        check_vma=False,
    )
```

time: 1010 us -> 291 us (0.29); the launches traced: 998 us -> 290 us
  waiting for transfers between devices: 719 us -> 95.3 us
  starting transfers between devices: 1.31 us -> 92.9 us
  matrix products: 90.6 us -> 0 us
  blocking collectives: 90.4 us -> 0 us
  Pallas kernels: 0 us -> 88.5 us
  other arithmetic: 67.2 us -> 7.02 us
  between operations: 17.2 us -> 2.9 us
    psum x7 -> x0, waiting for transfers between devices: 452 us -> none  [the longest x2 204 us: body(): grad_lnk = link_scale * lax.psum(backward_sums[CT:], 'scen')]
    pmax x4 -> x0, waiting for transfers between devices: 266 us -> none  [the longest x2 208 us: body(): link_stat = lax.pmax(col_stat[CT:], 'scen')]
    ppermute x0 -> x68, waiting for transfers between devices: none -> 95.3 us  [the longest x18 41.4 us: swap_x(): return lax.ppermute(x, 'scen', [(i, i ^ k << 3) for i in range(32)])]
    ppermute x0 -> x68, starting transfers between devices: none -> 92.9 us  [the longest x24 38.1 us: swap_y(): return lax.ppermute(x, 'col', [(i, i ^ k) for i in range(4)])]
    dot_general x14 -> x0, matrix products: 90.6 us -> none  [the longest x3 51.5 us: apply_forward(): product = jnp.einsum('nab,nb->na', blocks, picked, precision=HIGH)]
    pallas_call x0 -> x9, Pallas kernels: none -> 88.5 us  [tile_call(): pl.pallas_call(kernel, out_shape=tuple((jax.ShapeDtypeStruct(s, F32) for...]
    psum x1 -> x0, blocking collectives: 65.7 us -> none  [body(): lax.psum((jnp.sum(cost_loc * cost_loc) + link_term, jnp.sum(rhs_share * r...]
    reduce_max x6 -> x0, other arithmetic: 38 us -> none  [the longest x2 19 us: block_stats(): row_part = jnp.max(magnitude, axis=2)]
  transfers between devices with their start and end apart: 11 -> 68, of which waited for: 11 -> 47; matrix products, arithmetic and copies ran while one was open for 2% -> 2% of each run, Pallas kernels for 0% -> 10%
where the time goes in v1:
time: 291 us; the launch traced here: 290 us
  waiting for transfers between devices  95.3 us (33%)
  starting transfers between devices  92.9 us (32%)
  Pallas kernels  88.5 us (30%)
  other arithmetic  7.02 us (2%)
  local copies, waits for them, and re-layouts  3.45 us (1%)
    pallas_call x9, Pallas kernels, tile_call(): pl.pallas_call(kernel, out_shape=tuple((jax.ShapeDtypeStruct(s, F32) for...  88.5 us
    ppermute x18, waiting for transfers between devices, swap_x(): return lax.ppermute(x, 'scen', [(i, i ^ k << 3) for i in range(32)])  41.4 us
    ppermute x24, starting transfers between devices, swap_y(): return lax.ppermute(x, 'col', [(i, i ^ k) for i in range(4)])  38.1 us
    ppermute x18, starting transfers between devices, swap_x(): return lax.ppermute(x, 'scen', [(i, i ^ k << 3) for i in range(32)])  28.7 us
    ppermute x15, starting transfers between devices, swap_z(): return lax.ppermute(x, 'scen', [(i, i ^ k << 1) for i in range(32)])  24.7 us
    ppermute x15, waiting for transfers between devices, swap_z(): return lax.ppermute(x, 'scen', [(i, i ^ k << 1) for i in range(32)])  23.6 us
    ppermute x24, waiting for transfers between devices, swap_y(): return lax.ppermute(x, 'col', [(i, i ^ k) for i in range(4)])  20.3 us
    ppermute x11, waiting for transfers between devices, swap_core(): return lax.ppermute(x, 'scen', [(i, i ^ 1) for i in range(32)])  9.96 us
  transfers between devices with their start and end apart: 68, of which 47 were waited for; matrix products, arithmetic and copies ran while one was open for 2% of the time, Pallas kernels for 10%

profile of v1, /device:TPU:0, one launch (start us, length us, event | category | flops | bytes accessed | tf_op | source)
XLA Modules:
  0.0 290.1 jit_solution(5819013724800895850)
XLA Ops:
  7.5 9.5 %shard_map.130 = (f32[128,256]{1,0:T(8,128)S(1)}, f32[264,256]{1,0:T(8,128)S(1)}) custom-call(s32[64]{0:T(128)S(1)} %bitcast.76, s32[64]{0:T(128)S(1)} %compare_select_fusion.4.cols_ref, f32[64,256,256]{2,1,0:T(8,128)} %bitcast.85), custom_call_target="tpu_custom_call" | custom-call | tf_op jit(solution)/shard_map/pallas_call | solution.py:103
  17.8 4.2 %collective-permute-start.1 = (f32[128,256]{1,0:T(8,128)S(1)}, f32[128,256]{1,0:T(8,128)S(1)}, u32[]{:S(2)}, u32[]{:S(2)}) collective-permute-start(f32[128,256]{1,0:T(8,128)S(1)} %get-tuple-element.23.r0), channel_id=1, source_target_pairs={{0,2},{1,3},{2,0},{3,1},{4,6},{5,7},{6,4},{7,5},{8,10},{9,11},{10,... | collective-permute-start | bytes 393224 | tf_op jit(solution)/shard_map/ppermute | solution.py:40
  28.7 4.4 %collective-permute-done.5 = f32[128,256]{1,0:T(8,128)S(1)} collective-permute-done((f32[128,256]{1,0:T(8,128)S(1)}, f32[128,256]{1,0:T(8,128)S(1)}, u32[]{:S(2)}, u32[]{:S(2)}) %collective-permute-start.5) | collective-permute-done | bytes 131104 | tf_op jit(solution)/shard_map/ppermute | solution.py:36
  37.3 3.6 %collective-permute-start.8 = (f32[128,256]{1,0:T(8,128)S(1)}, f32[128,256]{1,0:T(8,128)S(1)}, u32[]{:S(2)}, u32[]{:S(2)}) collective-permute-start(f32[128,256]{1,0:T(8,128)S(1)} %maximum_maximum_fusion.1), channel_id=1, source_target_pairs={{0,16},{4,20},{8,24},{12,28},{16,0},{20,4},{24,8},{28,12},{32,48},... | collective-permute-start | bytes 393224 | tf_op jit(solution)/shard_map/ppermute | solution.py:32
  40.9 9.5 %shard_map.132.loc = f32[264,256]{1,0:T(8,128)S(1)} custom-call(s32[64]{0:T(128)S(1)} %bitcast.77, s32[64]{0:T(128)S(1)} %compare_select_fusion.4.cols_ref, f32[64,256,256]{2,1,0:T(8,128)} %bitcast.86, f32[128,256]{1,0:T(8,128)S(1)} %bitcast.75), custom_call_target="tpu_custom_call" | custom-call | tf_op jit(solution)/shard_map/pallas_call | solution.py:103
  51.4 5.2 %collective-permute-done.2.r3 = f32[128,256]{1,0:T(8,128)S(1)} collective-permute-done((f32[128,256]{1,0:T(8,128)S(1)}, f32[128,256]{1,0:T(8,128)S(1)}, u32[]{:S(2)}, u32[]{:S(2)}) %collective-permute-start.2) | collective-permute-done | bytes 131104 | tf_op jit(solution)/shard_map/ppermute | solution.py:40
  56.7 10.8 %shard_map.131 = (f32[128,256]{1,0:T(8,128)S(1)}, f32[264,256]{1,0:T(8,128)S(1)}, f32[128,256]{1,0:T(8,128)S(1)}, f32[264,256]{1,0:T(8,128)S(1)}) custom-call(s32[64]{0:T(128)S(1)} %bitcast.78, s32[64]{0:T(128)S(1)} %compare_select_fusion.4.cols_ref, f32[64,256,256]{2,1,0:T(8,128)} %bitcast.87, f32[128,256]{1,0:T(8,128)S(1)} %get-tuple-element.23.r0, ...), custom_call_target="tpu_custom_call" | custom-call | tf_op jit(solution)/shard_map/pallas_call | solution.py:103
  76.1 3.0 %collective-permute-done.20 = f32[160,256]{1,0:T(8,128)S(1)} collective-permute-done((f32[160,256]{1,0:T(8,128)S(1)}, f32[160,256]{1,0:T(8,128)S(1)}, u32[]{:S(2)}, u32[]{:S(2)}) %collective-permute-start.20) | collective-permute-done | bytes 163872 | tf_op jit(solution)/shard_map/ppermute | solution.py:36
  81.8 4.7 %collective-permute-start.23 = (f32[160,256]{1,0:T(8,128)S(1)}, f32[160,256]{1,0:T(8,128)S(1)}, u32[]{:S(2)}, u32[]{:S(2)}) collective-permute-start(f32[160,256]{1,0:T(8,128)S(1)} %pad_maximum_fusion.5), channel_id=1, source_target_pairs={{0,16},{4,20},{8,24},{12,28},{16,0},{20,4},{24,8},{28,12},{32,48},... | collective-permute-start | bytes 491528 | tf_op jit(solution)/shard_map/ppermute | solution.py:32
  97.2 10.8 %shard_map.133 = (f32[128,256]{1,0:T(8,128)S(1)}, f32[264,256]{1,0:T(8,128)S(1)}, f32[128,256]{1,0:T(8,128)S(1)}, f32[264,256]{1,0:T(8,128)S(1)}) custom-call(s32[64]{0:T(128)S(1)} %bitcast.79, s32[64]{0:T(128)S(1)} %compare_select_fusion.4.cols_ref, f32[64,256,256]{2,1,0:T(8,128)} %bitcast.88, f32[128,256]{1,0:T(8,128)S(1)} %get-tuple-element.25.r0, ...), custom_call_target="tpu_custom_call" | custom-call | tf_op jit(solution)/shard_map/pallas_call | solution.py:103
  114.5 4.0 %collective-permute-start.28 = (f32[160,256]{1,0:T(8,128)S(1)}, f32[160,256]{1,0:T(8,128)S(1)}, u32[]{:S(2)}, u32[]{:S(2)}) collective-permute-start(f32[160,256]{1,0:T(8,128)S(1)} %pad_maximum_fusion.6), channel_id=1, source_target_pairs={{0,64},{4,68},{8,72},{12,76},{16,80},{20,84},{24,88},{28,92},{32,9... | collective-permute-start | bytes 491528 | tf_op jit(solution)/shard_map/ppermute | solution.py:36
  121.6 4.8 %collective-permute-done.28 = f32[160,256]{1,0:T(8,128)S(1)} collective-permute-done((f32[160,256]{1,0:T(8,128)S(1)}, f32[160,256]{1,0:T(8,128)S(1)}, u32[]{:S(2)}, u32[]{:S(2)}) %collective-permute-start.28) | collective-permute-done | bytes 163872 | tf_op jit(solution)/shard_map/ppermute | solution.py:36
  150.6 3.9 %collective-permute-start.41 = (f32[8,256]{1,0:T(8,128)S(1)}, f32[8,256]{1,0:T(8,128)S(1)}, u32[]{:S(2)}, u32[]{:S(2)}) collective-permute-start(f32[8,256]{1,0:T(8,128)S(1)} %get-tuple-element.77), channel_id=1, source_target_pairs={{0,2},{1,3},{2,0},{3,1},{4,6},{5,7},{6,4},{7,5},{8,10},{9,11},{10,... | collective-permute-start | bytes 24584 | tf_op jit(solution)/shard_map/ppermute | solution.py:40
  156.2 3.1 %collective-permute-done.42 = f32[8,256]{1,0:T(8,128)S(1)} collective-permute-done((f32[8,256]{1,0:T(8,128)S(1)}, f32[8,256]{1,0:T(8,128)S(1)}, u32[]{:S(2)}, u32[]{:S(2)}) %collective-permute-start.42) | collective-permute-done | bytes 8224 | tf_op jit(solution)/shard_map/ppermute | solution.py:40
  160.8 9.6 %shard_map.134 = (f32[128,256]{1,0:T(8,128)S(1)}, f32[264,256]{1,0:T(8,128)S(1)}) custom-call(s32[64]{0:T(128)S(1)} %bitcast.80, s32[64]{0:T(128)S(1)} %compare_select_fusion.4.cols_ref, f32[64,256,256]{2,1,0:T(8,128)} %bitcast.89, f32[1,2]{1,0:T(1,128)S(1)} %maximum_bitcast_fusion.scalars, f32[264,256]{1,0:T(8,128)S(1)} %shard_map.132.loc, ...), custom_call_target="tpu_custom_call" | custom-call | tf_op jit(solution)/shard_map/pallas_call | solution.py:103
  179.0 9.6 %shard_map.135 = (f32[264,256]{1,0:T(8,128)S(1)}, f32[128,256]{1,0:T(8,128)S(1)}) custom-call(s32[64]{0:T(128)S(1)} %bitcast.81, s32[64]{0:T(128)S(1)} %compare_select_fusion.4.cols_ref, f32[64,256,256]{2,1,0:T(8,128)} %bitcast.90, f32[1,2]{1,0:T(1,128)S(1)} %maximum_bitcast_fusion.scalars, f32[128,256]{1,0:T(8,128)S(1)} %get-tuple-element.33.r0, ...), custom_call_target="tpu_custom_call" | custom-call | tf_op jit(solution)/shard_map/pallas_call | solution.py:103
  190.3 3.8 %collective-permute-start.48 = (f32[128,256]{1,0:T(8,128)S(1)}, f32[128,256]{1,0:T(8,128)S(1)}, u32[]{:S(2)}, u32[]{:S(2)}) collective-permute-start(f32[128,256]{1,0:T(8,128)S(1)} %slice_add_fusion.4), channel_id=1, source_target_pairs={{0,64},{4,68},{8,72},{12,76},{16,80},{20,84},{24,88},{28,92},{32,9... | collective-permute-start | bytes 393224 | tf_op jit(solution)/shard_map/ppermute | solution.py:36
  196.5 4.1 %collective-permute-done.48 = f32[128,256]{1,0:T(8,128)S(1)} collective-permute-done((f32[128,256]{1,0:T(8,128)S(1)}, f32[128,256]{1,0:T(8,128)S(1)}, u32[]{:S(2)}, u32[]{:S(2)}) %collective-permute-start.48) | collective-permute-done | bytes 131104 | tf_op jit(solution)/shard_map/ppermute | solution.py:36
  202.9 3.4 %collective-permute-start.51 = (f32[128,256]{1,0:T(8,128)S(1)}, f32[128,256]{1,0:T(8,128)S(1)}, u32[]{:S(2)}, u32[]{:S(2)}) collective-permute-start(f32[128,256]{1,0:T(8,128)S(1)} %add_add_fusion.4), channel_id=1, source_target_pairs={{0,16},{4,20},{8,24},{12,28},{16,0},{20,4},{24,8},{28,12},{32,48},... | collective-permute-start | bytes 393224 | tf_op jit(solution)/shard_map/ppermute | solution.py:32
  215.4 9.6 %shard_map.136 = (f32[128,256]{1,0:T(8,128)S(1)}, f32[264,256]{1,0:T(8,128)S(1)}) custom-call(s32[64]{0:T(128)S(1)} %bitcast.82, s32[64]{0:T(128)S(1)} %compare_select_fusion.4.cols_ref, f32[64,256,256]{2,1,0:T(8,128)} %bitcast.91, f32[1,2]{1,0:T(1,128)S(1)} %maximum_bitcast_fusion.scalars, f32[264,256]{1,0:T(8,128)S(1)} %get-tuple-element.34.loc, ...), custom_call_target="tpu_custom_call" | custom-call | tf_op jit(solution)/shard_map/pallas_call | solution.py:103
  236.5 9.6 %shard_map.137 = (f32[264,256]{1,0:T(8,128)S(1)}, f32[128,256]{1,0:T(8,128)S(1)}) custom-call(s32[64]{0:T(128)S(1)} %bitcast.83, s32[64]{0:T(128)S(1)} %compare_select_fusion.4.cols_ref, f32[64,256,256]{2,1,0:T(8,128)} %bitcast.92, f32[1,2]{1,0:T(1,128)S(1)} %maximum_bitcast_fusion.scalars, f32[128,256]{1,0:T(8,128)S(1)} %get-tuple-element.36.r0, ...), custom_call_target="tpu_custom_call" | custom-call | tf_op jit(solution)/shard_map/pallas_call | solution.py:103
  258.6 4.0 %collective-permute-start.62 = (f32[128,256]{1,0:T(8,128)S(1)}, f32[128,256]{1,0:T(8,128)S(1)}, u32[]{:S(2)}, u32[]{:S(2)}) collective-permute-start(f32[128,256]{1,0:T(8,128)S(1)} %add_add_fusion.2), channel_id=1, source_target_pairs={{0,16},{4,20},{8,24},{12,28},{16,0},{20,4},{24,8},{28,12},{32,48},... | collective-permute-start | bytes 393224 | tf_op jit(solution)/shard_map/ppermute | solution.py:32
  264.9 3.4 %collective-permute-done.62 = f32[128,256]{1,0:T(8,128)S(1)} collective-permute-done((f32[128,256]{1,0:T(8,128)S(1)}, f32[128,256]{1,0:T(8,128)S(1)}, u32[]{:S(2)}, u32[]{:S(2)}) %collective-permute-start.62) | collective-permute-done | bytes 131104 | tf_op jit(solution)/shard_map/ppermute | solution.py:32
  271.7 9.6 %shard_map.138 = (f32[128,256]{1,0:T(8,128)S(1)}, f32[264,256]{1,0:T(8,128)S(1)}) custom-call(s32[64]{0:T(128)S(1)} %bitcast.84, s32[64]{0:T(128)S(1)} %compare_select_fusion.4.cols_ref, f32[64,256,256]{2,1,0:T(8,128)} %bitcast.93, f32[1,2]{1,0:T(1,128)S(1)} %maximum_bitcast_fusion.scalars, f32[264,256]{1,0:T(8,128)S(1)} %get-tuple-element.38.loc, ...), custom_call_target="tpu_custom_call" | custom-call | tf_op jit(solution)/shard_map/pallas_call | solution.py:103
  (211 shorter events, 139.1 us)
Async XLA Ops:
  1.4 16.4 %collective-permute-start.15 = (f32[64,256]{1,0:T(8,128)S(1)}, f32[64,256]{1,0:T(8,128)S(1)}, u32[]{:S(2)}, u32[]{:S(2)}) collective-permute-start(f32[64,256]{1,0:T(8,128)S(1)} %get-tuple-element.75), channel_id=1, source_target_pairs={{0,1},{1,0},{2,3},{3,2},{4,5},{5,4},{6,7},{7,6},{8,9},{9,8},{10,11... | collective-permute-start | bytes 196616 | tf_op jit(solution)/shard_map/ppermute | solution.py:40
  3.2 18.9 %collective-permute-start.16 = (f32[64,256]{1,0:T(8,128)S(1)}, f32[64,256]{1,0:T(8,128)S(1)}, u32[]{:S(2)}, u32[]{:S(2)}) collective-permute-start(f32[64,256]{1,0:T(8,128)S(1)} %get-tuple-element.75), channel_id=1, source_target_pairs={{0,2},{1,3},{2,0},{3,1},{4,6},{5,7},{6,4},{7,5},{8,10},{9,11},{10,... | collective-permute-start | bytes 196616 | tf_op jit(solution)/shard_map/ppermute | solution.py:40
  6.1 16.0 %collective-permute-start.17 = (f32[64,256]{1,0:T(8,128)S(1)}, f32[64,256]{1,0:T(8,128)S(1)}, u32[]{:S(2)}, u32[]{:S(2)}) collective-permute-start(f32[64,256]{1,0:T(8,128)S(1)} %get-tuple-element.75), channel_id=1, source_target_pairs={{0,3},{1,2},{2,1},{3,0},{4,7},{5,6},{6,5},{7,4},{8,11},{9,10},{10,... | collective-permute-start | bytes 196616 | tf_op jit(solution)/shard_map/ppermute | solution.py:40
  17.2 34.2 %collective-permute-start = (f32[128,256]{1,0:T(8,128)S(1)}, f32[128,256]{1,0:T(8,128)S(1)}, u32[]{:S(2)}, u32[]{:S(2)}) collective-permute-start(f32[128,256]{1,0:T(8,128)S(1)} %get-tuple-element.23.r0), channel_id=1, source_target_pairs={{0,1},{1,0},{2,3},{3,2},{4,5},{5,4},{6,7},{7,6},{8,9},{9,8},{10,11... | collective-permute-start | bytes 393224 | tf_op jit(solution)/shard_map/ppermute | solution.py:40
  17.8 33.6 %collective-permute-start.1 = (f32[128,256]{1,0:T(8,128)S(1)}, f32[128,256]{1,0:T(8,128)S(1)}, u32[]{:S(2)}, u32[]{:S(2)}) collective-permute-start(f32[128,256]{1,0:T(8,128)S(1)} %get-tuple-element.23.r0), channel_id=1, source_target_pairs={{0,2},{1,3},{2,0},{3,1},{4,6},{5,7},{6,4},{7,5},{8,10},{9,11},{10,... | collective-permute-start | bytes 393224 | tf_op jit(solution)/shard_map/ppermute | solution.py:40
  35.3 15.1 %collective-permute-start.7 = (f32[128,256]{1,0:T(8,128)S(1)}, f32[128,256]{1,0:T(8,128)S(1)}, u32[]{:S(2)}, u32[]{:S(2)}) collective-permute-start(f32[128,256]{1,0:T(8,128)S(1)} %maximum_maximum_fusion.1), channel_id=1, source_target_pairs={{0,8},{4,12},{8,0},{12,4},{16,24},{20,28},{24,16},{28,20},{32,40},... | collective-permute-start | bytes 393224 | tf_op jit(solution)/shard_map/ppermute | solution.py:32
  37.3 13.4 %collective-permute-start.8 = (f32[128,256]{1,0:T(8,128)S(1)}, f32[128,256]{1,0:T(8,128)S(1)}, u32[]{:S(2)}, u32[]{:S(2)}) collective-permute-start(f32[128,256]{1,0:T(8,128)S(1)} %maximum_maximum_fusion.1), channel_id=1, source_target_pairs={{0,16},{4,20},{8,24},{12,28},{16,0},{20,4},{24,8},{28,12},{32,48},... | collective-permute-start | bytes 393224 | tf_op jit(solution)/shard_map/ppermute | solution.py:32
  40.8 9.9 %collective-permute-start.9 = (f32[128,256]{1,0:T(8,128)S(1)}, f32[128,256]{1,0:T(8,128)S(1)}, u32[]{:S(2)}, u32[]{:S(2)}) collective-permute-start(f32[128,256]{1,0:T(8,128)S(1)} %maximum_maximum_fusion.1), channel_id=1, source_target_pairs={{0,24},{4,28},{8,16},{12,20},{16,8},{20,12},{24,0},{28,4},{32,56},... | collective-permute-start | bytes 393224 | tf_op jit(solution)/shard_map/ppermute | solution.py:32
  50.7 16.9 %collective-permute-start.18 = (f32[128,256]{1,0:T(8,128)S(1)}, f32[128,256]{1,0:T(8,128)S(1)}, u32[]{:S(2)}, u32[]{:S(2)}) collective-permute-start(f32[128,256]{1,0:T(8,128)S(1)} %slice.246), channel_id=1, source_target_pairs={{0,4},{4,0},{8,12},{12,8},{16,20},{20,16},{24,28},{28,24},{32,36},... | collective-permute-start | bytes 393224 | tf_op jit(solution)/shard_map/ppermute | solution.py:28
  69.1 10.0 %collective-permute-start.20 = (f32[160,256]{1,0:T(8,128)S(1)}, f32[160,256]{1,0:T(8,128)S(1)}, u32[]{:S(2)}, u32[]{:S(2)}) collective-permute-start(f32[160,256]{1,0:T(8,128)S(1)} %get-tuple-element.69), channel_id=1, source_target_pairs={{0,64},{4,68},{8,72},{12,76},{16,80},{20,84},{24,88},{28,92},{32,9... | collective-permute-start | bytes 491528 | tf_op jit(solution)/shard_map/ppermute | solution.py:36
  71.2 10.4 %collective-permute-start.21 = (f32[160,256]{1,0:T(8,128)S(1)}, f32[160,256]{1,0:T(8,128)S(1)}, u32[]{:S(2)}, u32[]{:S(2)}) collective-permute-start(f32[160,256]{1,0:T(8,128)S(1)} %get-tuple-element.70), channel_id=1, source_target_pairs={{0,96},{4,100},{8,104},{12,108},{16,112},{20,116},{24,120},{28,124... | collective-permute-start | bytes 491528 | tf_op jit(solution)/shard_map/ppermute | solution.py:36
  81.8 11.7 %collective-permute-start.23 = (f32[160,256]{1,0:T(8,128)S(1)}, f32[160,256]{1,0:T(8,128)S(1)}, u32[]{:S(2)}, u32[]{:S(2)}) collective-permute-start(f32[160,256]{1,0:T(8,128)S(1)} %pad_maximum_fusion.5), channel_id=1, source_target_pairs={{0,16},{4,20},{8,24},{12,28},{16,0},{20,4},{24,8},{28,12},{32,48},... | collective-permute-start | bytes 491528 | tf_op jit(solution)/shard_map/ppermute | solution.py:32
  86.5 9.2 %collective-permute-start.24 = (f32[160,256]{1,0:T(8,128)S(1)}, f32[160,256]{1,0:T(8,128)S(1)}, u32[]{:S(2)}, u32[]{:S(2)}) collective-permute-start(f32[160,256]{1,0:T(8,128)S(1)} %pad_maximum_fusion.5), channel_id=1, source_target_pairs={{0,24},{4,28},{8,16},{12,20},{16,8},{20,12},{24,0},{28,4},{32,56},... | collective-permute-start | bytes 491528 | tf_op jit(solution)/shard_map/ppermute | solution.py:32
  86.7 9.2 %collective-permute-start.11 = (f32[128,256]{1,0:T(8,128)S(1)}, f32[128,256]{1,0:T(8,128)S(1)}, u32[]{:S(2)}, u32[]{:S(2)}) collective-permute-start(f32[128,256]{1,0:T(8,128)S(1)} %get-tuple-element.25.r0), channel_id=1, source_target_pairs={{0,1},{1,0},{2,3},{3,2},{4,5},{5,4},{6,7},{7,6},{8,9},{9,8},{10,11... | collective-permute-start | bytes 393224 | tf_op jit(solution)/shard_map/ppermute | solution.py:40
  86.8 9.1 %collective-permute-start.12 = (f32[128,256]{1,0:T(8,128)S(1)}, f32[128,256]{1,0:T(8,128)S(1)}, u32[]{:S(2)}, u32[]{:S(2)}) collective-permute-start(f32[128,256]{1,0:T(8,128)S(1)} %get-tuple-element.25.r0), channel_id=1, source_target_pairs={{0,2},{1,3},{2,0},{3,1},{4,6},{5,7},{6,4},{7,5},{8,10},{9,11},{10,... | collective-permute-start | bytes 393224 | tf_op jit(solution)/shard_map/ppermute | solution.py:40
  108.0 10.5 %collective-permute-start.30 = (f32[128,256]{1,0:T(8,128)S(1)}, f32[128,256]{1,0:T(8,128)S(1)}, u32[]{:S(2)}, u32[]{:S(2)}) collective-permute-start(f32[128,256]{1,0:T(8,128)S(1)} %get-tuple-element.32), channel_id=1, source_target_pairs={{0,1},{1,0},{2,3},{3,2},{4,5},{5,4},{6,7},{7,6},{8,9},{9,8},{10,11... | collective-permute-start | bytes 393224 | tf_op jit(solution)/shard_map/ppermute | solution.py:40
  108.1 11.1 %collective-permute-start.31 = (f32[128,256]{1,0:T(8,128)S(1)}, f32[128,256]{1,0:T(8,128)S(1)}, u32[]{:S(2)}, u32[]{:S(2)}) collective-permute-start(f32[128,256]{1,0:T(8,128)S(1)} %get-tuple-element.32), channel_id=1, source_target_pairs={{0,2},{1,3},{2,0},{3,1},{4,6},{5,7},{6,4},{7,5},{8,10},{9,11},{10,... | collective-permute-start | bytes 393224 | tf_op jit(solution)/shard_map/ppermute | solution.py:40
  114.5 11.8 %collective-permute-start.28 = (f32[160,256]{1,0:T(8,128)S(1)}, f32[160,256]{1,0:T(8,128)S(1)}, u32[]{:S(2)}, u32[]{:S(2)}) collective-permute-start(f32[160,256]{1,0:T(8,128)S(1)} %pad_maximum_fusion.6), channel_id=1, source_target_pairs={{0,64},{4,68},{8,72},{12,76},{16,80},{20,84},{24,88},{28,92},{32,9... | collective-permute-start | bytes 491528 | tf_op jit(solution)/shard_map/ppermute | solution.py:36
  118.5 10.4 %collective-permute-start.29 = (f32[160,256]{1,0:T(8,128)S(1)}, f32[160,256]{1,0:T(8,128)S(1)}, u32[]{:S(2)}, u32[]{:S(2)}) collective-permute-start(f32[160,256]{1,0:T(8,128)S(1)} %pad_maximum_fusion.6), channel_id=1, source_target_pairs={{0,96},{4,100},{8,104},{12,108},{16,112},{20,116},{24,120},{28,124... | collective-permute-start | bytes 491528 | tf_op jit(solution)/shard_map/ppermute | solution.py:36
  129.1 9.1 %collective-permute-start.34 = (f32[144,256]{1,0:T(8,128)S(1)}, f32[144,256]{1,0:T(8,128)S(1)}, u32[]{:S(2)}, u32[]{:S(2)}) collective-permute-start(f32[144,256]{1,0:T(8,128)S(1)} %pad_maximum_fusion.7), channel_id=1, source_target_pairs={{0,16},{4,20},{8,24},{12,28},{16,0},{20,4},{24,8},{28,12},{32,48},... | collective-permute-start | bytes 442376 | tf_op jit(solution)/shard_map/ppermute | solution.py:32
  190.3 10.3 %collective-permute-start.48 = (f32[128,256]{1,0:T(8,128)S(1)}, f32[128,256]{1,0:T(8,128)S(1)}, u32[]{:S(2)}, u32[]{:S(2)}) collective-permute-start(f32[128,256]{1,0:T(8,128)S(1)} %slice_add_fusion.4), channel_id=1, source_target_pairs={{0,64},{4,68},{8,72},{12,76},{16,80},{20,84},{24,88},{28,92},{32,9... | collective-permute-start | bytes 393224 | tf_op jit(solution)/shard_map/ppermute | solution.py:36
  202.9 9.2 %collective-permute-start.51 = (f32[128,256]{1,0:T(8,128)S(1)}, f32[128,256]{1,0:T(8,128)S(1)}, u32[]{:S(2)}, u32[]{:S(2)}) collective-permute-start(f32[128,256]{1,0:T(8,128)S(1)} %add_add_fusion.4), channel_id=1, source_target_pairs={{0,16},{4,20},{8,24},{12,28},{16,0},{20,4},{24,8},{28,12},{32,48},... | collective-permute-start | bytes 393224 | tf_op jit(solution)/shard_map/ppermute | solution.py:32
  225.1 9.1 %collective-permute-start.55 = (f32[128,256]{1,0:T(8,128)S(1)}, f32[128,256]{1,0:T(8,128)S(1)}, u32[]{:S(2)}, u32[]{:S(2)}) collective-permute-start(f32[128,256]{1,0:T(8,128)S(1)} %get-tuple-element.36.r0), channel_id=1, source_target_pairs={{0,2},{1,3},{2,0},{3,1},{4,6},{5,7},{6,4},{7,5},{8,10},{9,11},{10,... | collective-permute-start | bytes 393224 | tf_op jit(solution)/shard_map/ppermute | solution.py:40
  258.6 9.8 %collective-permute-start.62 = (f32[128,256]{1,0:T(8,128)S(1)}, f32[128,256]{1,0:T(8,128)S(1)}, u32[]{:S(2)}, u32[]{:S(2)}) collective-permute-start(f32[128,256]{1,0:T(8,128)S(1)} %add_add_fusion.2), channel_id=1, source_target_pairs={{0,16},{4,20},{8,24},{12,28},{16,0},{20,4},{24,8},{28,12},{32,48},... | collective-permute-start | bytes 393224 | tf_op jit(solution)/shard_map/ppermute | solution.py:32
  (52 other events, 633.3 us)

commit v2 on v1

--- a/solution.py
+++ b/solution.py
@@ -14,6 +14,7 @@
 ITERS = 3
 NT = 64
 HALF = LT // 2
+SHARE = RT // 4
 CW = CT + LT
 GROUP = 8
 STEPS = NT // GROUP
@@ -22,6 +23,7 @@
 STEP = 0.9
 F32 = jnp.float32
 LANES = 128
+VMEM_LIMIT = 24 * 1024 * 1024
 
 
 def swap_core(x):
@@ -87,64 +89,71 @@
 
 def join_from(ref, out):
     for w in range(2):
-        out[:, w * LANES : (w + 1) * LANES] = ref[w]
+        out[0 : ref.shape[1], w * LANES : (w + 1) * LANES] = ref[w]
 
 
 ROWS = pltpu.VMEM((2, RT, LANES), F32)
 COLS = pltpu.VMEM((2, CW, LANES), F32)
 
 
-def tile_call(kernel, ids, tiles, operands, outs, scratch=()):
+def tile_call(kernel, ids, tiles, operands, outs, scratch=(), load=False):
     def spec(x):
-        if x.shape[0] == 1:
-            return pl.BlockSpec(memory_space=pltpu.SMEM)
-        return pl.BlockSpec(x.shape, lambda i, *_: (0,) * len(x.shape))
-
+        return pl.BlockSpec(memory_space=pltpu.SMEM if x.shape[0] == 1 else pltpu.VMEM)
+
+    shapes = [jax.ShapeDtypeStruct(s, F32) for s in outs]
+    where = pl.BlockSpec(memory_space=pltpu.VMEM)
+    scratch = list(scratch)
+    if load:
+        where = pl.BlockSpec(memory_space=pl.ANY)
+        shapes.append(pltpu.VMEM((NT, TILE, TILE), F32))
+        scratch.append(pltpu.SemaphoreType.DMA((STEPS,)))
+    else:
+        tiles = pltpu.with_memory_space_constraint(tiles, pltpu.VMEM)
+    ids_spec = pl.BlockSpec(memory_space=pltpu.SMEM)
     return pl.pallas_call(
         kernel,
-        out_shape=tuple(jax.ShapeDtypeStruct(s, F32) for s in outs),
-        grid_spec=pltpu.PrefetchScalarGridSpec(
-            num_scalar_prefetch=2,
-            grid=(STEPS,),
-            in_specs=[pl.BlockSpec((GROUP, TILE, TILE), lambda i, *_: (i, 0, 0))]
-            + [spec(x) for x in operands],
-            out_specs=tuple(pl.BlockSpec(s, lambda i, *_: (0, 0)) for s in outs),
-            scratch_shapes=list(scratch),
-        ),
-        compiler_params=pltpu.CompilerParams(vmem_limit_bytes=40 * 1024 * 1024),
+        out_shape=tuple(shapes),
+        in_specs=[ids_spec, ids_spec, where] + [spec(x) for x in operands],
+        out_specs=tuple(pl.BlockSpec(memory_space=pltpu.VMEM) for _ in shapes),
+        scratch_shapes=scratch,
+        compiler_params=pltpu.CompilerParams(vmem_limit_bytes=VMEM_LIMIT),
     )(*ids, tiles, *operands)
 
 
-def each_tile(rows_ref, cols_ref, visit):
-    base = pl.program_id(0) * GROUP
-    for t in range(GROUP):
-        visit(t, cols_ref[base + t], rows_ref[base + t])
-
-
-def at_first(fn):
-    pl.when(pl.program_id(0) == 0)(fn)
-
-
-def at_last(fn):
-    pl.when(pl.program_id(0) == STEPS - 1)(fn)
-
-
-def first_stats_kernel(rows_ref, cols_ref, tiles_ref, rowout, colout, racc, cacc):
-    @at_first
-    def _():
-        racc[...] = jnp.zeros_like(racc)
-        cacc[...] = jnp.zeros_like(cacc)
+def each_tile(rows_ref, cols_ref, visit, ready=None):
+    def group(step, carry):
+        if ready is not None:
+            ready(step)
+        for i in range(GROUP):
+            t = step * GROUP + i
+            visit(t, cols_ref[t], rows_ref[t])
+        return carry
+
+    lax.fori_loop(0, STEPS, group, 0)
+
+
+def first_stats_kernel(
+    rows_ref, cols_ref, source, rhs, dual, rowout, colout, tiles_ref, racc, cacc, sems
+):
+    def load(step):
+        part = pl.ds(step * GROUP, GROUP)
+        return pltpu.make_async_copy(source.at[part], tiles_ref.at[part], sems.at[step])
+
+    for step in range(STEPS):
+        load(step).start()
+    racc[...] = jnp.zeros_like(racc)
+    cacc[...] = jnp.zeros_like(cacc)
 
     def visit(t, col, row):
         row_pass(tiles_ref, t, col, row, None, racc, jnp.maximum, True)
         col_pass(tiles_ref, t, col, row, None, cacc, jnp.maximum, True)
 
-    each_tile(rows_ref, cols_ref, visit)
-
-    @at_last
-    def _():
-        join_from(racc, rowout)
-        join_from(cacc, colout)
+    each_tile(rows_ref, cols_ref, visit, lambda step: load(step).wait())
+
+    join_from(racc, rowout)
+    rowout[RT : RT + SHARE] = rhs[...]
+    rowout[RT + SHARE :] = dual[...]
+    join_from(cacc, colout)
 
 
 def next_stats_kernel(
@@ -155,27 +164,25 @@
     else:
         rowold, colold, rowout, colout, rownew, colnew, racc, cacc, rowf, colf = rest
 
-    @at_first
-    def _():
-        row = tree(jnp.maximum, r0[...], (r1[...], r2[...], r3[...]))
+    row = tree(jnp.maximum, r0[0:RT], (r1[0:RT], r2[0:RT], r3[0:RT]))
+    if first:
+        new = 1.0 / jnp.sqrt(row + EPS)
+    else:
+        old = rowold[...]
+        new = old / jnp.sqrt(old * row + EPS)
+    rownew[...] = new
+    split_to(rowf, new)
+    for lo, hi, src in ((0, CT, loc), (CT, CT + HALF, mine), (CT + HALF, CW, other)):
+        stat = src[0 : hi - lo]
         if first:
-            new = 1.0 / jnp.sqrt(row + EPS)
+            new = 1.0 / jnp.sqrt(stat + EPS)
         else:
-            old = rowold[...]
-            new = old / jnp.sqrt(old * row + EPS)
-        rownew[...] = new
-        split_to(rowf, new)
-        for lo, hi, src in ((0, CT, loc), (CT, CT + HALF, mine), (CT + HALF, CW, other)):
-            stat = src[0 : hi - lo]
-            if first:
-                new = 1.0 / jnp.sqrt(stat + EPS)
-            else:
-                old = colold[lo:hi]
-                new = old / jnp.sqrt(old * stat + EPS)
-            colnew[lo:hi] = new
-            split_to(colf, new, lo)
-        racc[...] = jnp.zeros_like(racc)
-        cacc[...] = jnp.zeros_like(cacc)
+            old = colold[lo:hi]
+            new = old / jnp.sqrt(old * stat + EPS)
+        colnew[lo:hi] = new
+        split_to(colf, new, lo)
+    racc[...] = jnp.zeros_like(racc)
+    cacc[...] = jnp.zeros_like(cacc)
 
     def visit(t, col, row):
         row_pass(tiles_ref, t, col, row, colf, racc, op, True)
@@ -183,71 +190,63 @@
 
     each_tile(rows_ref, cols_ref, visit)
 
-    @at_last
-    def _():
-        join_from(racc, rowout)
-        join_from(cacc, colout)
-
-
-def first_backward_kernel(rows_ref, cols_ref, tiles_ref, dual, colout, cacc, work):
-    @at_first
-    def _():
-        split_to(work, dual[...])
-        cacc[...] = jnp.zeros_like(cacc)
+    join_from(racc, rowout)
+    join_from(cacc, colout)
+
+
+def first_backward_kernel(
+    rows_ref, cols_ref, tiles_ref, y_at, r0, r1, r2, r3, colout, rhsout, dualout, cacc, work
+):
+    for k, ref in enumerate((r0, r1, r2, r3)):
+        at = pl.ds(pl.multiple_of((y_at[0, 0] ^ k) * SHARE, SHARE), SHARE)
+        rhsout[at, :] = ref[RT : RT + SHARE]
+        dualout[at, :] = ref[RT + SHARE :]
+    split_to(work, dualout[...])
+    cacc[...] = jnp.zeros_like(cacc)
 
     def visit(t, col, row):
         col_pass(tiles_ref, t, col, row, work, cacc, jnp.add, False)
 
     each_tile(rows_ref, cols_ref, visit)
 
-    @at_last
-    def _():
-        join_from(cacc, colout)
+    join_from(cacc, colout)
 
 
 def backward_kernel(
     rows_ref, cols_ref, tiles_ref, scalars, r0, r1, r2, r3, dual, rhs, rowf, colout, dualnew, cacc, work
 ):
-    @at_first
-    def _():
-        total = tree(jnp.add, r0[...], (r1[...], r2[...], r3[...]))
-        new = dual[...] + scalars[0, 1] * (rhs[...] - rowf[...] * total)
-        dualnew[...] = new
-        split_to(work, rowf[...] * new)
-        cacc[...] = jnp.zeros_like(cacc)
+    total = tree(jnp.add, r0[...], (r1[...], r2[...], r3[...]))
+    new = dual[...] + scalars[0, 1] * (rhs[...] - rowf[...] * total)
+    dualnew[...] = new
+    split_to(work, rowf[...] * new)
+    cacc[...] = jnp.zeros_like(cacc)
 
     def visit(t, col, row):
         col_pass(tiles_ref, t, col, row, work, cacc, jnp.add, False)
 
     each_tile(rows_ref, cols_ref, visit)
 
-    @at_last
-    def _():
-        join_from(cacc, colout)
+    join_from(cacc, colout)
 
 
 def forward_kernel(
     rows_ref, cols_ref, tiles_ref, scalars, loc, mine, other, primal, cost, upper, colf, rowout, fresh, racc, work
 ):
-    @at_first
-    def _():
-        for lo, hi, src in ((0, CT, loc), (CT, CT + HALF, mine), (CT + HALF, CW, other)):
-            at = slice(lo, hi)
-            x, scale = primal[at], colf[at]
-            grad = scale * src[0 : hi - lo]
-            new = jnp.clip(x - scalars[0, 0] * (cost[at] - grad), 0.0, upper[at])
-            fresh[at] = new
-            split_to(work, scale * (2.0 * new - x), lo)
-        racc[...] = jnp.zeros_like(racc)
+    for lo, hi, src in ((0, CT, loc), (CT, CT + HALF, mine), (CT + HALF, CW, other)):
+        at = slice(lo, hi)
+        x, scale = primal[at], colf[at]
+        grad = scale * src[0 : hi - lo]
+        new = jnp.clip(x - scalars[0, 0] * (cost[at] - grad), 0.0, upper[at])
+        fresh[at] = new
+        split_to(work, scale * (2.0 * new - x), lo)
+    racc[...] = jnp.zeros_like(racc)
 
     def visit(t, col, row):
         row_pass(tiles_ref, t, col, row, work, racc, jnp.add, False)
 
     each_tile(rows_ref, cols_ref, visit)
 
-    @at_last
-    def _():
-        join_from(racc, rowout)
+    join_from(racc, rowout)
 
 
 def body(
@@ -268,7 +267,6 @@
     y_at = lax.axis_index("col")
     x_at = scen // 8
     core = scen % 2
-    share = RT // 4
     chunk = HALF // 4
 
     raw_cols = tile_cols[0, 0]
@@ -284,28 +282,30 @@
     def halves(x):
         return x[CT : CT + HALF], x[CT + HALF :]
 
-    pair = jnp.concatenate([rhs[0], start_dual[0]], axis=0)
-    parts = jnp.stack([pair] + [swap_y(pair, k) for k in (1, 2, 3)])
-    parts = jnp.take(parts, y_at ^ jnp.arange(4), axis=0)
-    rhs_rows = parts[:, :share].reshape(RT, TILE)
-    dual_rows = parts[:, share:].reshape(RT, TILE)
-
-    row_part, col_part = tile_call(
-        first_stats_kernel, ids, tiles, (), ((RT, TILE), (CW, TILE)), (ROWS, COLS)
+    row_part, col_part, tiles = tile_call(
+        first_stats_kernel,
+        ids,
+        tiles,
+        (rhs[0], start_dual[0]),
+        ((RT + 2 * SHARE, TILE), (CW, TILE)),
+        (ROWS, COLS),
+        load=True,
     )
     mine, other = halves(col_part)
     rows_got = [swap_y(row_part, k) for k in (1, 2, 3)]
     link = jnp.maximum(mine, swap_core(other))
     link = tree(jnp.maximum, link, [swap_x(link, k) for k in (1, 2, 3)])
     link = tree(jnp.maximum, link, [swap_z(link, k) for k in (1, 2, 3)])
-    (grad0,) = tile_call(first_backward_kernel, ids, tiles, (dual_rows,), ((CW, TILE),), (COLS, ROWS))
+    grad0, rhs_rows, dual_rows = tile_call(
+        first_backward_kernel,
+        ids,
+        tiles,
+        (y_at.reshape(1, 1), row_part, *rows_got),
+        ((CW, TILE), (RT, TILE), (RT, TILE)),
+        (COLS, ROWS),
+    )
     grad_mine, grad_other = halves(grad0)
     grad_half = grad_mine + swap_core(grad_other)
-
-    def scales(row_total, loc, mine, other, row_old, col_old):
-        row = row_old / jnp.sqrt(row_old * row_total + EPS)
-        stat = jnp.concatenate([loc, mine, other], axis=0)
-        return row, col_old / jnp.sqrt(col_old * stat + EPS)
 
     operands = (row_part, *rows_got, col_part, link, swap_core(link))
     row_part, col_part, row_scale, col_scale = tile_call(
@@ -351,22 +351,19 @@
     mine, other = halves(col_part)
     rows_got = [swap_y(row_part, k) for k in (1, 2, 3)]
     link = mine + swap_core(other)
-    both = jnp.concatenate([link, grad_chunk], axis=0)
-    got = [swap_x(both, k) for k in (1, 2, 3)]
-    link = tree(jnp.add, link, [g[:HALF] for g in got])
-    parts = jnp.stack([grad_chunk] + [g[HALF:] for g in got])
-    grad_half = jnp.take(parts, x_at ^ jnp.arange(4), axis=0).reshape(HALF, TILE)
     row_total = tree(jnp.add, row_part, rows_got)
     row_scale = row_scale / jnp.sqrt(row_scale * row_total + EPS)
     rhs_scaled = row_scale * rhs_rows
     dual_scaled = dual_rows / row_scale
-    rhs_square = jnp.sum((rhs_scaled * rhs_scaled).reshape(16, 8, TILE), axis=0)
+    rhs_square = jnp.sum((rhs_scaled * rhs_scaled).reshape(RT // 8, 8, TILE), axis=0)
     local_old = col_scale[:CT]
     cost_loc = local_old / jnp.sqrt(local_old * col_part[:CT] + EPS) * cost_local[0, 0]
-    squares = jnp.concatenate([rhs_square, cost_loc * cost_loc], axis=0)
-    both = jnp.concatenate([link, squares], axis=0)
-    got = [swap_z(both, k) for k in (1, 2, 3)]
-    both = tree(jnp.add, both, got)
+    both = jnp.concatenate([link, rhs_square, cost_loc * cost_loc], axis=0)
+    got = [swap_x(jnp.concatenate([both, grad_chunk], axis=0), k) for k in (1, 2, 3)]
+    parts = jnp.stack([grad_chunk] + [g[HALF + 2 * CT :] for g in got])
+    grad_half = jnp.take(parts, x_at ^ jnp.arange(4), axis=0).reshape(HALF, TILE)
+    both = tree(jnp.add, both, [g[: HALF + 2 * CT] for g in got])
+    both = tree(jnp.add, both, [swap_z(both, k) for k in (1, 2, 3)])
     back = swap_core(jnp.concatenate([both, grad_half], axis=0))
     squares = both[HALF:] + back[HALF : HALF + 2 * CT]
     stat = jnp.concatenate([col_part[:CT], both[:HALF], back[:HALF]], axis=0)
@@ -376,11 +373,10 @@
     upper = whole_columns(bound_local, bound_link) / col_scale
     primal = whole_columns(start_local, start_link) / col_scale
 
-    link_square = jnp.sum((cost[CT:] * cost[CT:]).reshape(LT // 8, 8, TILE), axis=0)
-    by_x = tree(jnp.add, squares, [swap_x(squares, k) for k in (1, 2, 3)])
-    cost_part = by_x[CT:] + link_square
+    half_squares = [jnp.sum((c * c).reshape(HALF // 8, 8, TILE), axis=0) for c in halves(cost)]
+    cost_part = squares[CT:] + (half_squares[0] + half_squares[1])
     cost_total = tree(jnp.add, cost_part, [swap_y(cost_part, k) for k in (1, 2, 3)])
-    weight_ratio = jnp.sqrt((jnp.sum(cost_total) + EPS) / (jnp.sum(by_x[:CT]) + EPS))
+    weight_ratio = jnp.sqrt((jnp.sum(cost_total) + EPS) / (jnp.sum(squares[:CT]) + EPS))
     steps = jnp.stack([STEP / weight_ratio, STEP * weight_ratio])[None]
 
     for index in range(ITERS):
@@ -410,7 +406,7 @@
         grads = (col_part, link, swap_core(link))
 
     def piece(x, k):
-        return lax.dynamic_slice_in_dim(x, (y_at ^ k) * share, share, 0)
+        return lax.dynamic_slice_in_dim(x, (y_at ^ k) * SHARE, SHARE, 0)
 
     total = tree(jnp.add, piece(row_part, 0), [swap_y(piece(row_part, k), k) for k in (1, 2, 3)])
     scale = piece(row_scale, 0)

time: 291 us -> 258 us (0.89)
  Pallas kernels: 88.5 us -> 39.3 us
  local copies, waits for them, and re-layouts: 3.45 us -> 33.9 us
  starting transfers between devices: 92.9 us -> 84.2 us
  waiting for transfers between devices: 95.3 us -> 90.2 us
    pallas_call x9, Pallas kernels: 88.5 us -> 39.3 us  [tile_call(): pl.pallas_call(kernel, out_shape=tuple(shapes), in_specs=[ids_spec, ids_s...]
    unnamed x16 -> x34, local copies, waits for them, and re-layouts: 0.7 us -> 31.7 us
    ppermute x18 -> x15, waiting for transfers between devices: 41.4 us -> 34.6 us  [swap_x(): return lax.ppermute(x, 'scen', [(i, i ^ k << 3) for i in range(32)])]
    ppermute x18 -> x15, starting transfers between devices: 28.7 us -> 23.8 us  [swap_x(): return lax.ppermute(x, 'scen', [(i, i ^ k << 3) for i in range(32)])]
    ppermute x24 -> x21, starting transfers between devices: 38.1 us -> 33.3 us  [swap_y(): return lax.ppermute(x, 'col', [(i, i ^ k) for i in range(4)])]
    ppermute x24 -> x21, waiting for transfers between devices: 20.3 us -> 24.1 us  [swap_y(): return lax.ppermute(x, 'col', [(i, i ^ k) for i in range(4)])]
    ppermute x15, waiting for transfers between devices: 23.6 us -> 20.5 us  [swap_z(): return lax.ppermute(x, 'scen', [(i, i ^ k << 1) for i in range(32)])]
  transfers between devices with their start and end apart: 68 -> 62, of which waited for: 47 -> 47; matrix products, arithmetic and copies ran while one was open for 2% -> 2% of each run, Pallas kernels for 10% -> 4%
where the time goes in v2:
time: 258 us
  waiting for transfers between devices  90.2 us (35%)
  starting transfers between devices  84.2 us (33%)
  Pallas kernels  39.3 us (15%)
  local copies, waits for them, and re-layouts  33.9 us (13%)
  other arithmetic  7.4 us (3%)
  between operations  2.81 us (1%)
    pallas_call x9, Pallas kernels, tile_call(): pl.pallas_call(kernel, out_shape=tuple(shapes), in_specs=[ids_spec, ids_s...  39.3 us
    ppermute x15, waiting for transfers between devices, swap_x(): return lax.ppermute(x, 'scen', [(i, i ^ k << 3) for i in range(32)])  34.6 us
    ppermute x21, starting transfers between devices, swap_y(): return lax.ppermute(x, 'col', [(i, i ^ k) for i in range(4)])  33.3 us
    unnamed x34, local copies, waits for them, and re-layouts  31.7 us
    ppermute x15, starting transfers between devices, swap_z(): return lax.ppermute(x, 'scen', [(i, i ^ k << 1) for i in range(32)])  25.6 us
    ppermute x21, waiting for transfers between devices, swap_y(): return lax.ppermute(x, 'col', [(i, i ^ k) for i in range(4)])  24.1 us
    ppermute x15, starting transfers between devices, swap_x(): return lax.ppermute(x, 'scen', [(i, i ^ k << 3) for i in range(32)])  23.8 us
    ppermute x15, waiting for transfers between devices, swap_z(): return lax.ppermute(x, 'scen', [(i, i ^ k << 1) for i in range(32)])  20.5 us
  transfers between devices with their start and end apart: 62, of which 47 were waited for; matrix products, arithmetic and copies ran while one was open for 2% of the time, Pallas kernels for 4%

profile of v2, /device:TPU:0, one launch (start us, length us, event | category | flops | bytes accessed | tf_op | source)
XLA Modules:
  0.0 257.8 jit_solution(1786662794383027018)
XLA Ops:
  3.5 6.9 %shard_map.130 = (f32[192,256]{1,0:T(8,128)S(1)}, f32[264,256]{1,0:T(8,128)S(1)}, f32[64,256,256]{2,1,0:T(8,128)S(1)}) custom-call(s32[64]{0:T(128)S(1)} %bitcast.68, s32[64]{0:T(128)S(1)} %compare_select_fusion.2.cols_ref, f32[64,256,256]{2,1,0:T(8,128)} %bitcast.79, f32[32,256]{1,0:T(8,128)S(1)} %bitcast.77, f32[32,256]{1,0:T(8,128)S(1)} %bitcast.78), custom_call_target="tpu_custom_call" | custom-call | tf_op jit(solution)/shard_map/pallas_call | solution.py:113
  10.4 5.8 %copy-done = f32[64,256,256]{2,1,0:T(8,128)} copy-done((f32[64,256,256]{2,1,0:T(8,128)}, f32[64,256,256]{2,1,0:T(8,128)S(1)}, u32[]{:S(2)}) %copy-start) | copy-done | bytes 16777240
  32.8 3.6 %collective-permute-start.8 = (f32[128,256]{1,0:T(8,128)S(1)}, f32[128,256]{1,0:T(8,128)S(1)}, u32[]{:S(2)}, u32[]{:S(2)}) collective-permute-start(f32[128,256]{1,0:T(8,128)S(1)} %maximum_maximum_fusion.1), channel_id=1, source_target_pairs={{0,16},{4,20},{8,24},{12,28},{16,0},{20,4},{24,8},{28,12},{32,48},... | collective-permute-start | bytes 393224 | tf_op jit(solution)/shard_map/ppermute | solution.py:34
  37.9 5.8 %copy-done.1 = f32[64,256,256]{2,1,0:T(8,128)S(1)} copy-done((f32[64,256,256]{2,1,0:T(8,128)S(1)}, f32[64,256,256]{2,1,0:T(8,128)}, u32[]{:S(2)}) %copy-start.1) | copy-done | bytes 16777240
  49.4 5.7 %shard_map.131 = (f32[128,256]{1,0:T(8,128)S(1)}, f32[264,256]{1,0:T(8,128)S(1)}, f32[128,256]{1,0:T(8,128)S(1)}, f32[264,256]{1,0:T(8,128)S(1)}) custom-call(s32[64]{0:T(128)S(1)} %bitcast.70, s32[64]{0:T(128)S(1)} %compare_select_fusion.2.cols_ref, f32[64,256,256]{2,1,0:T(8,128)S(1)} %copy-done.2, f32[192,256]{1,0:T(8,128)S(1)} %get-tuple-element.28.r0, ...), custom_call_target="tpu_custom_call" | custom-call | tf_op jit(solution)/shard_map/pallas_call | solution.py:113
  57.7 3.9 %collective-permute-start.17 = (f32[160,256]{1,0:T(8,128)S(1)}, f32[160,256]{1,0:T(8,128)S(1)}, u32[]{:S(2)}, u32[]{:S(2)}) collective-permute-start(f32[160,256]{1,0:T(8,128)S(1)} %get-tuple-element.77), channel_id=1, source_target_pairs={{0,64},{4,68},{8,72},{12,76},{16,80},{20,84},{24,88},{28,92},{32,9... | collective-permute-start | bytes 491528 | tf_op jit(solution)/shard_map/ppermute | solution.py:38
  64.6 5.0 %collective-permute-done.17 = f32[160,256]{1,0:T(8,128)S(1)} collective-permute-done((f32[160,256]{1,0:T(8,128)S(1)}, f32[160,256]{1,0:T(8,128)S(1)}, u32[]{:S(2)}, u32[]{:S(2)}) %collective-permute-start.17) | collective-permute-done | bytes 163872 | tf_op jit(solution)/shard_map/ppermute | solution.py:38
  74.1 3.6 %collective-permute-start.20 = (f32[160,256]{1,0:T(8,128)S(1)}, f32[160,256]{1,0:T(8,128)S(1)}, u32[]{:S(2)}, u32[]{:S(2)}) collective-permute-start(f32[160,256]{1,0:T(8,128)S(1)} %pad_maximum_fusion.5), channel_id=1, source_target_pairs={{0,16},{4,20},{8,24},{12,28},{16,0},{20,4},{24,8},{28,12},{32,48},... | collective-permute-start | bytes 491528 | tf_op jit(solution)/shard_map/ppermute | solution.py:34
  88.2 5.8 %copy-done.3 = f32[64,256,256]{2,1,0:T(8,128)S(1)} copy-done((f32[64,256,256]{2,1,0:T(8,128)S(1)}, f32[64,256,256]{2,1,0:T(8,128)}, u32[]{:S(2)}) %copy-start.3) | copy-done | bytes 16777240
  94.0 5.8 %shard_map.133 = (f32[128,256]{1,0:T(8,128)S(1)}, f32[264,256]{1,0:T(8,128)S(1)}, f32[128,256]{1,0:T(8,128)S(1)}, f32[264,256]{1,0:T(8,128)S(1)}) custom-call(s32[64]{0:T(128)S(1)} %bitcast.71, s32[64]{0:T(128)S(1)} %compare_select_fusion.2.cols_ref, f32[64,256,256]{2,1,0:T(8,128)S(1)} %copy-done.3, f32[128,256]{1,0:T(8,128)S(1)} %get-tuple-element.30.r0, ...), custom_call_target="tpu_custom_call" | custom-call | tf_op jit(solution)/shard_map/pallas_call | solution.py:113
  123.3 4.6 %collective-permute-start.32 = (f32[144,256]{1,0:T(8,128)S(1)}, f32[144,256]{1,0:T(8,128)}, u32[]{:S(2)}, u32[]{:S(2)}) collective-permute-start(f32[144,256]{1,0:T(8,128)S(1)} %fusion.4), channel_id=1, source_target_pairs={{0,24},{4,28},{8,16},{12,20},{16,8},{20,12},{24,0},{28,4},{32,56},... | collective-permute-start | bytes 442376 | tf_op jit(solution)/shard_map/ppermute | solution.py:34
  136.3 4.8 %collective-permute-start.35 = (f32[8,256]{1,0:T(8,128)S(1)}, f32[8,256]{1,0:T(8,128)S(1)}, u32[]{:S(2)}, u32[]{:S(2)}) collective-permute-start(f32[8,256]{1,0:T(8,128)S(1)} %get-tuple-element.83), channel_id=1, source_target_pairs={{0,2},{1,3},{2,0},{3,1},{4,6},{5,7},{6,4},{7,5},{8,10},{9,11},{10,... | collective-permute-start | bytes 24584 | tf_op jit(solution)/shard_map/ppermute | solution.py:42
  147.4 5.8 %copy-done.4 = f32[64,256,256]{2,1,0:T(8,128)S(1)} copy-done((f32[64,256,256]{2,1,0:T(8,128)S(1)}, f32[64,256,256]{2,1,0:T(8,128)}, u32[]{:S(2)}) %copy-start.4) | copy-done | bytes 16777240
  153.2 3.5 %shard_map.134 = (f32[128,256]{1,0:T(8,128)S(1)}, f32[264,256]{1,0:T(8,128)S(1)}) custom-call(s32[64]{0:T(128)S(1)} %bitcast.72, s32[64]{0:T(128)S(1)} %compare_select_fusion.2.cols_ref, f32[64,256,256]{2,1,0:T(8,128)S(1)} %copy-done.4, f32[1,2]{1,0:T(1,128)S(1)} %maximum_bitcast_fusion.scalars, f32[264,256]{1,0:T(8,128)S(1)} %get-tuple-element.32.loc, ...), custom_call_target="tpu_custom_call" | custom-call | tf_op jit(solution)/shard_map/pallas_call | solution.py:113
  170.4 4.2 %collective-permute-start.42 = (f32[128,256]{1,0:T(8,128)S(1)}, f32[128,256]{1,0:T(8,128)S(1)}, u32[]{:S(2)}, u32[]{:S(2)}) collective-permute-start(f32[128,256]{1,0:T(8,128)S(1)} %slice_add_fusion.3), channel_id=1, source_target_pairs={{0,64},{4,68},{8,72},{12,76},{16,80},{20,84},{24,88},{28,92},{32,9... | collective-permute-start | bytes 393224 | tf_op jit(solution)/shard_map/ppermute | solution.py:38
  176.7 4.3 %collective-permute-done.42 = f32[128,256]{1,0:T(8,128)S(1)} collective-permute-done((f32[128,256]{1,0:T(8,128)S(1)}, f32[128,256]{1,0:T(8,128)S(1)}, u32[]{:S(2)}, u32[]{:S(2)}) %collective-permute-start.42) | collective-permute-done | bytes 131104 | tf_op jit(solution)/shard_map/ppermute | solution.py:38
  183.4 4.0 %collective-permute-start.45 = (f32[128,256]{1,0:T(8,128)S(1)}, f32[128,256]{1,0:T(8,128)S(1)}, u32[]{:S(2)}, u32[]{:S(2)}) collective-permute-start(f32[128,256]{1,0:T(8,128)S(1)} %add_add_fusion.4), channel_id=1, source_target_pairs={{0,16},{4,20},{8,24},{12,28},{16,0},{20,4},{24,8},{28,12},{32,48},... | collective-permute-start | bytes 393224 | tf_op jit(solution)/shard_map/ppermute | solution.py:34
  189.7 3.5 %collective-permute-done.45 = f32[128,256]{1,0:T(8,128)S(1)} collective-permute-done((f32[128,256]{1,0:T(8,128)S(1)}, f32[128,256]{1,0:T(8,128)S(1)}, u32[]{:S(2)}, u32[]{:S(2)}) %collective-permute-start.45) | collective-permute-done | bytes 131104 | tf_op jit(solution)/shard_map/ppermute | solution.py:34
  196.6 3.5 %shard_map.136 = (f32[128,256]{1,0:T(8,128)S(1)}, f32[264,256]{1,0:T(8,128)S(1)}) custom-call(s32[64]{0:T(128)S(1)} %bitcast.74, s32[64]{0:T(128)S(1)} %compare_select_fusion.2.cols_ref, f32[64,256,256]{2,1,0:T(8,128)S(1)} %copy-done.4, f32[1,2]{1,0:T(1,128)S(1)} %maximum_bitcast_fusion.scalars, f32[264,256]{1,0:T(8,128)S(1)} %get-tuple-element.42.loc, ...), custom_call_target="tpu_custom_call" | custom-call | tf_op jit(solution)/shard_map/pallas_call | solution.py:113
  200.5 3.5 %collective-permute-start.49 = (f32[128,256]{1,0:T(8,128)S(1)}, f32[128,256]{1,0:T(8,128)S(1)}, u32[]{:S(2)}, u32[]{:S(2)}) collective-permute-start(f32[128,256]{1,0:T(8,128)S(1)} %get-tuple-element.44.r0), channel_id=1, source_target_pairs={{0,2},{1,3},{2,0},{3,1},{4,6},{5,7},{6,4},{7,5},{8,10},{9,11},{10,... | collective-permute-start | bytes 393224 | tf_op jit(solution)/shard_map/ppermute | solution.py:42
  206.5 3.8 %collective-permute-done.49.r2 = f32[128,256]{1,0:T(8,128)S(1)} collective-permute-done((f32[128,256]{1,0:T(8,128)S(1)}, f32[128,256]{1,0:T(8,128)S(1)}, u32[]{:S(2)}, u32[]{:S(2)}) %collective-permute-start.49) | collective-permute-done | bytes 131104 | tf_op jit(solution)/shard_map/ppermute | solution.py:42
  212.6 3.4 %shard_map.137 = (f32[264,256]{1,0:T(8,128)S(1)}, f32[128,256]{1,0:T(8,128)S(1)}) custom-call(s32[64]{0:T(128)S(1)} %bitcast.75, s32[64]{0:T(128)S(1)} %compare_select_fusion.2.cols_ref, f32[64,256,256]{2,1,0:T(8,128)S(1)} %copy-done.4, f32[1,2]{1,0:T(1,128)S(1)} %maximum_bitcast_fusion.scalars, f32[128,256]{1,0:T(8,128)S(1)} %get-tuple-element.44.r0, ...), custom_call_target="tpu_custom_call" | custom-call | tf_op jit(solution)/shard_map/pallas_call | solution.py:113
  239.7 5.8 %copy-done.5 = f32[64,256,256]{2,1,0:T(8,128)S(1)} copy-done((f32[64,256,256]{2,1,0:T(8,128)S(1)}, f32[64,256,256]{2,1,0:T(8,128)}, u32[]{:S(2)}) %copy-start.5) | copy-done | bytes 16777240
  245.5 3.5 %shard_map.138 = (f32[128,256]{1,0:T(8,128)S(1)}, f32[264,256]{1,0:T(8,128)S(1)}) custom-call(s32[64]{0:T(128)S(1)} %bitcast.76, s32[64]{0:T(128)S(1)} %compare_select_fusion.2.cols_ref, f32[64,256,256]{2,1,0:T(8,128)S(1)} %copy-done.5, f32[1,2]{1,0:T(1,128)S(1)} %maximum_bitcast_fusion.scalars, f32[264,256]{1,0:T(8,128)S(1)} %get-tuple-element.46.loc, ...), custom_call_target="tpu_custom_call" | custom-call | tf_op jit(solution)/shard_map/pallas_call | solution.py:113
  (208 shorter events, 144.7 us)
Async XLA Ops:
  17.7 9.3 %collective-permute-start.4 = (f32[128,256]{1,0:T(8,128)S(1)}, f32[128,256]{1,0:T(8,128)S(1)}, u32[]{:S(2)}, u32[]{:S(2)}) collective-permute-start(f32[128,256]{1,0:T(8,128)S(1)} %slice_maximum_fusion.5), channel_id=1, source_target_pairs={{0,32},{4,36},{8,40},{12,44},{16,48},{20,52},{24,56},{28,60},{32,0... | collective-permute-start | bytes 393224 | tf_op jit(solution)/shard_map/ppermute | solution.py:38
  19.3 9.2 %collective-permute-start.5 = (f32[128,256]{1,0:T(8,128)S(1)}, f32[128,256]{1,0:T(8,128)S(1)}, u32[]{:S(2)}, u32[]{:S(2)}) collective-permute-start(f32[128,256]{1,0:T(8,128)S(1)} %slice_maximum_fusion.5), channel_id=1, source_target_pairs={{0,64},{4,68},{8,72},{12,76},{16,80},{20,84},{24,88},{28,92},{32,9... | collective-permute-start | bytes 393224 | tf_op jit(solution)/shard_map/ppermute | solution.py:38
  22.0 8.7 %collective-permute-start.6 = (f32[128,256]{1,0:T(8,128)S(1)}, f32[128,256]{1,0:T(8,128)S(1)}, u32[]{:S(2)}, u32[]{:S(2)}) collective-permute-start(f32[128,256]{1,0:T(8,128)S(1)} %slice_maximum_fusion.5), channel_id=1, source_target_pairs={{0,96},{4,100},{8,104},{12,108},{16,112},{20,116},{24,120},{28,124... | collective-permute-start | bytes 393224 | tf_op jit(solution)/shard_map/ppermute | solution.py:38
  22.4 13.9 %collective-permute-start = (f32[192,256]{1,0:T(8,128)S(1)}, f32[192,256]{1,0:T(8,128)S(1)}, u32[]{:S(2)}, u32[]{:S(2)}) collective-permute-start(f32[192,256]{1,0:T(8,128)S(1)} %get-tuple-element.28.r0), channel_id=1, source_target_pairs={{0,1},{1,0},{2,3},{3,2},{4,5},{5,4},{6,7},{7,6},{8,9},{9,8},{10,11... | collective-permute-start | bytes 589832 | tf_op jit(solution)/shard_map/ppermute | solution.py:42
  24.1 12.3 %collective-permute-start.1 = (f32[192,256]{1,0:T(8,128)S(1)}, f32[192,256]{1,0:T(8,128)S(1)}, u32[]{:S(2)}, u32[]{:S(2)}) collective-permute-start(f32[192,256]{1,0:T(8,128)S(1)} %get-tuple-element.28.r0), channel_id=1, source_target_pairs={{0,2},{1,3},{2,0},{3,1},{4,6},{5,7},{6,4},{7,5},{8,10},{9,11},{10,... | collective-permute-start | bytes 589832 | tf_op jit(solution)/shard_map/ppermute | solution.py:42
  27.0 10.9 %collective-permute-start.2 = (f32[192,256]{1,0:T(8,128)S(1)}, f32[192,256]{1,0:T(8,128)S(1)}, u32[]{:S(2)}, u32[]{:S(2)}) collective-permute-start(f32[192,256]{1,0:T(8,128)S(1)} %get-tuple-element.28.r0), channel_id=1, source_target_pairs={{0,3},{1,2},{2,1},{3,0},{4,7},{5,6},{6,5},{7,4},{8,11},{9,10},{10,... | collective-permute-start | bytes 589832 | tf_op jit(solution)/shard_map/ppermute | solution.py:42
  30.8 16.4 %collective-permute-start.7 = (f32[128,256]{1,0:T(8,128)S(1)}, f32[128,256]{1,0:T(8,128)S(1)}, u32[]{:S(2)}, u32[]{:S(2)}) collective-permute-start(f32[128,256]{1,0:T(8,128)S(1)} %maximum_maximum_fusion.1), channel_id=1, source_target_pairs={{0,8},{4,12},{8,0},{12,4},{16,24},{20,28},{24,16},{28,20},{32,40},... | collective-permute-start | bytes 393224 | tf_op jit(solution)/shard_map/ppermute | solution.py:34
  32.8 14.4 %collective-permute-start.8 = (f32[128,256]{1,0:T(8,128)S(1)}, f32[128,256]{1,0:T(8,128)S(1)}, u32[]{:S(2)}, u32[]{:S(2)}) collective-permute-start(f32[128,256]{1,0:T(8,128)S(1)} %maximum_maximum_fusion.1), channel_id=1, source_target_pairs={{0,16},{4,20},{8,24},{12,28},{16,0},{20,4},{24,8},{28,12},{32,48},... | collective-permute-start | bytes 393224 | tf_op jit(solution)/shard_map/ppermute | solution.py:34
  36.3 10.8 %collective-permute-start.9 = (f32[128,256]{1,0:T(8,128)S(1)}, f32[128,256]{1,0:T(8,128)S(1)}, u32[]{:S(2)}, u32[]{:S(2)}) collective-permute-start(f32[128,256]{1,0:T(8,128)S(1)} %maximum_maximum_fusion.1), channel_id=1, source_target_pairs={{0,24},{4,28},{8,16},{12,20},{16,8},{20,12},{24,0},{28,4},{32,56},... | collective-permute-start | bytes 393224 | tf_op jit(solution)/shard_map/ppermute | solution.py:34
  57.7 12.0 %collective-permute-start.17 = (f32[160,256]{1,0:T(8,128)S(1)}, f32[160,256]{1,0:T(8,128)S(1)}, u32[]{:S(2)}, u32[]{:S(2)}) collective-permute-start(f32[160,256]{1,0:T(8,128)S(1)} %get-tuple-element.77), channel_id=1, source_target_pairs={{0,64},{4,68},{8,72},{12,76},{16,80},{20,84},{24,88},{28,92},{32,9... | collective-permute-start | bytes 491528 | tf_op jit(solution)/shard_map/ppermute | solution.py:38
  61.6 10.4 %collective-permute-start.18 = (f32[160,256]{1,0:T(8,128)S(1)}, f32[160,256]{1,0:T(8,128)S(1)}, u32[]{:S(2)}, u32[]{:S(2)}) collective-permute-start(f32[160,256]{1,0:T(8,128)S(1)} %get-tuple-element.78), channel_id=1, source_target_pairs={{0,96},{4,100},{8,104},{12,108},{16,112},{20,116},{24,120},{28,124... | collective-permute-start | bytes 491528 | tf_op jit(solution)/shard_map/ppermute | solution.py:38
  74.1 10.5 %collective-permute-start.20 = (f32[160,256]{1,0:T(8,128)S(1)}, f32[160,256]{1,0:T(8,128)S(1)}, u32[]{:S(2)}, u32[]{:S(2)}) collective-permute-start(f32[160,256]{1,0:T(8,128)S(1)} %pad_maximum_fusion.5), channel_id=1, source_target_pairs={{0,16},{4,20},{8,24},{12,28},{16,0},{20,4},{24,8},{28,12},{32,48},... | collective-permute-start | bytes 491528 | tf_op jit(solution)/shard_map/ppermute | solution.py:34
  77.7 9.0 %collective-permute-start.21 = (f32[160,256]{1,0:T(8,128)S(1)}, f32[160,256]{1,0:T(8,128)S(1)}, u32[]{:S(2)}, u32[]{:S(2)}) collective-permute-start(f32[160,256]{1,0:T(8,128)S(1)} %pad_maximum_fusion.5), channel_id=1, source_target_pairs={{0,24},{4,28},{8,16},{12,20},{16,8},{20,12},{24,0},{28,4},{32,56},... | collective-permute-start | bytes 491528 | tf_op jit(solution)/shard_map/ppermute | solution.py:34
  77.9 9.0 %collective-permute-start.11 = (f32[128,256]{1,0:T(8,128)S(1)}, f32[128,256]{1,0:T(8,128)S(1)}, u32[]{:S(2)}, u32[]{:S(2)}) collective-permute-start(f32[128,256]{1,0:T(8,128)S(1)} %get-tuple-element.30.r0), channel_id=1, source_target_pairs={{0,1},{1,0},{2,3},{3,2},{4,5},{5,4},{6,7},{7,6},{8,9},{9,8},{10,11... | collective-permute-start | bytes 393224 | tf_op jit(solution)/shard_map/ppermute | solution.py:42
  78.0 8.9 %collective-permute-start.12 = (f32[128,256]{1,0:T(8,128)S(1)}, f32[128,256]{1,0:T(8,128)S(1)}, u32[]{:S(2)}, u32[]{:S(2)}) collective-permute-start(f32[128,256]{1,0:T(8,128)S(1)} %get-tuple-element.30.r0), channel_id=1, source_target_pairs={{0,2},{1,3},{2,0},{3,1},{4,6},{5,7},{6,4},{7,5},{8,10},{9,11},{10,... | collective-permute-start | bytes 393224 | tf_op jit(solution)/shard_map/ppermute | solution.py:42
  110.5 10.1 %collective-permute-start.28 = (f32[176,256]{1,0:T(8,128)S(1)}, f32[176,256]{1,0:T(8,128)S(1)}, u32[]{:S(2)}, u32[]{:S(2)}) collective-permute-start(f32[176,256]{1,0:T(8,128)S(1)} %pad_maximum_fusion.1), channel_id=1, source_target_pairs={{0,64},{4,68},{8,72},{12,76},{16,80},{20,84},{24,88},{28,92},{32,9... | collective-permute-start | bytes 540680 | tf_op jit(solution)/shard_map/ppermute | solution.py:38
  112.8 10.1 %collective-permute-start.29 = (f32[176,256]{1,0:T(8,128)S(1)}, f32[176,256]{1,0:T(8,128)S(1)}, u32[]{:S(2)}, u32[]{:S(2)}) collective-permute-start(f32[176,256]{1,0:T(8,128)S(1)} %pad_maximum_fusion.1), channel_id=1, source_target_pairs={{0,96},{4,100},{8,104},{12,108},{16,112},{20,116},{24,120},{28,124... | collective-permute-start | bytes 540680 | tf_op jit(solution)/shard_map/ppermute | solution.py:38
  123.3 9.5 %collective-permute-start.32 = (f32[144,256]{1,0:T(8,128)S(1)}, f32[144,256]{1,0:T(8,128)}, u32[]{:S(2)}, u32[]{:S(2)}) collective-permute-start(f32[144,256]{1,0:T(8,128)S(1)} %fusion.4), channel_id=1, source_target_pairs={{0,24},{4,28},{8,16},{12,20},{16,8},{20,12},{24,0},{28,4},{32,56},... | collective-permute-start | bytes 442376 | tf_op jit(solution)/shard_map/ppermute | solution.py:34
  170.4 10.7 %collective-permute-start.42 = (f32[128,256]{1,0:T(8,128)S(1)}, f32[128,256]{1,0:T(8,128)S(1)}, u32[]{:S(2)}, u32[]{:S(2)}) collective-permute-start(f32[128,256]{1,0:T(8,128)S(1)} %slice_add_fusion.3), channel_id=1, source_target_pairs={{0,64},{4,68},{8,72},{12,76},{16,80},{20,84},{24,88},{28,92},{32,9... | collective-permute-start | bytes 393224 | tf_op jit(solution)/shard_map/ppermute | solution.py:38
  174.6 8.7 %collective-permute-start.43 = (f32[128,256]{1,0:T(8,128)S(1)}, f32[128,256]{1,0:T(8,128)S(1)}, u32[]{:S(2)}, u32[]{:S(2)}) collective-permute-start(f32[128,256]{1,0:T(8,128)S(1)} %slice_add_fusion.3), channel_id=1, source_target_pairs={{0,96},{4,100},{8,104},{12,108},{16,112},{20,116},{24,120},{28,124... | collective-permute-start | bytes 393224 | tf_op jit(solution)/shard_map/ppermute | solution.py:38
  183.4 9.8 %collective-permute-start.45 = (f32[128,256]{1,0:T(8,128)S(1)}, f32[128,256]{1,0:T(8,128)S(1)}, u32[]{:S(2)}, u32[]{:S(2)}) collective-permute-start(f32[128,256]{1,0:T(8,128)S(1)} %add_add_fusion.4), channel_id=1, source_target_pairs={{0,16},{4,20},{8,24},{12,28},{16,0},{20,4},{24,8},{28,12},{32,48},... | collective-permute-start | bytes 393224 | tf_op jit(solution)/shard_map/ppermute | solution.py:34
  200.5 9.9 %collective-permute-start.49 = (f32[128,256]{1,0:T(8,128)S(1)}, f32[128,256]{1,0:T(8,128)S(1)}, u32[]{:S(2)}, u32[]{:S(2)}) collective-permute-start(f32[128,256]{1,0:T(8,128)S(1)} %get-tuple-element.44.r0), channel_id=1, source_target_pairs={{0,2},{1,3},{2,0},{3,1},{4,6},{5,7},{6,4},{7,5},{8,10},{9,11},{10,... | collective-permute-start | bytes 393224 | tf_op jit(solution)/shard_map/ppermute | solution.py:42
  203.9 8.7 %collective-permute-start.50 = (f32[128,256]{1,0:T(8,128)S(1)}, f32[128,256]{1,0:T(8,128)S(1)}, u32[]{:S(2)}, u32[]{:S(2)}) collective-permute-start(f32[128,256]{1,0:T(8,128)S(1)} %get-tuple-element.44.r0), channel_id=1, source_target_pairs={{0,3},{1,2},{2,1},{3,0},{4,7},{5,6},{6,5},{7,4},{8,11},{9,10},{10,... | collective-permute-start | bytes 393224 | tf_op jit(solution)/shard_map/ppermute | solution.py:42
  219.5 8.7 %collective-permute-start.54 = (f32[128,256]{1,0:T(8,128)S(1)}, f32[128,256]{1,0:T(8,128)S(1)}, u32[]{:S(2)}, u32[]{:S(2)}) collective-permute-start(f32[128,256]{1,0:T(8,128)S(1)} %slice_add_fusion.2), channel_id=1, source_target_pairs={{0,96},{4,100},{8,104},{12,108},{16,112},{20,116},{24,120},{28,124... | collective-permute-start | bytes 393224 | tf_op jit(solution)/shard_map/ppermute | solution.py:38
  (55 other events, 757.2 us)

commit v3 on v2

v3 whole, which is shorter than its diff:
```python
import functools

import jax
import jax.numpy as jnp
from jax import lax
from jax.experimental import pallas as pl
from jax.experimental.pallas import tpu as pltpu
from jax.sharding import PartitionSpec as P

TILE = 256
RT = 128
CT = 8
LT = 256
ITERS = 3
NT = 64
HALF = LT // 2
SHARE = RT // 4
CW = CT + LT
GROUP = 8
STEPS = NT // GROUP

EPS = 1e-06
STEP = 0.9
F32 = jnp.float32
LANES = 128
VMEM_LIMIT = 24 * 1024 * 1024


def swap_core(x):
    return lax.ppermute(x, "scen", [(i, i ^ 1) for i in range(32)])


def swap_z(x, k):
    return lax.ppermute(x, "scen", [(i, i ^ (k << 1)) for i in range(32)])


def swap_x(x, k):
    return lax.ppermute(x, "scen", [(i, i ^ (k << 3)) for i in range(32)])


def swap_y(x, k):
    return lax.ppermute(x, "col", [(i, i ^ k) for i in range(4)])


def tree(op, own, got):
    return op(op(own, got[0]), op(got[1], got[2]))


def row_pass(tiles_ref, t, col, row, colf_ref, rowout_ref, op, magnitude):
    for h in range(2):
        a = tiles_ref[t, h * LANES : (h + 1) * LANES, 0:LANES]
        b = tiles_ref[t, h * LANES : (h + 1) * LANES, LANES:TILE]
        if magnitude:
            a, b = jnp.abs(a), jnp.abs(b)
        if colf_ref is not None:
            a = a * colf_ref[0, pl.ds(col, 1), :]
            b = b * colf_ref[1, pl.ds(col, 1), :]
        m = op(a, b).T
        s = jnp.max(m, axis=0, keepdims=True) if op is jnp.maximum else jnp.sum(m, axis=0, keepdims=True)
        at = (h, pl.ds(row, 1), slice(None))
        rowout_ref[at] = op(rowout_ref[at], s)


def col_pass(tiles_ref, t, col, row, rowf_ref, colout_ref, op, magnitude):
    parts = [None, None]
    for h in range(2):
        if rowf_ref is not None:
            f = jnp.broadcast_to(rowf_ref[h, pl.ds(row, 1), :], (LANES, LANES)).T
        for w in range(2):
            a = tiles_ref[t, h * LANES : (h + 1) * LANES, w * LANES : (w + 1) * LANES]
            if magnitude:
                a = jnp.abs(a)
            if rowf_ref is not None:
                a = a * f
            a = a.reshape(16, 8, LANES)
            s = jnp.max(a, axis=0) if op is jnp.maximum else jnp.sum(a, axis=0)
            parts[w] = s if parts[w] is None else op(parts[w], s)
    for w in range(2):
        s = parts[w]
        s = jnp.max(s, axis=0, keepdims=True) if op is jnp.maximum else jnp.sum(s, axis=0, keepdims=True)
        at = (w, pl.ds(col, 1), slice(None))
        colout_ref[at] = op(colout_ref[at], s)


def split_to(ref, value, lo=0):
    for w in range(2):
        ref[w, lo : lo + value.shape[0], :] = value[:, w * LANES : (w + 1) * LANES]


def join_from(ref, out, lo, hi):
    for w in range(2):
        out[0 : hi - lo, w * LANES : (w + 1) * LANES] = ref[w, lo:hi, :]


ROWS = pltpu.VMEM((2, RT, LANES), F32)
COLS = pltpu.VMEM((2, CW, LANES), F32)
OWN = CT + HALF
EIGHT = 2 * CT
CHUNK = HALF // 4


def call(kernel, smem, tiles, operands, outs, scratch=()):
    operands = [pltpu.with_memory_space_constraint(tiles, pltpu.VMEM)] + list(operands)
    vmem = pl.BlockSpec(memory_space=pltpu.VMEM)
    return pl.pallas_call(
        kernel,
        out_shape=tuple(jax.ShapeDtypeStruct((n, TILE), F32) for n in outs),
        in_specs=[pl.BlockSpec(memory_space=pltpu.SMEM) for _ in smem] + [vmem for _ in operands],
        out_specs=tuple(vmem for _ in outs),
        scratch_shapes=list(scratch),
        compiler_params=pltpu.CompilerParams(vmem_limit_bytes=VMEM_LIMIT),
    )(*smem, *operands)


def each_tile(rows_ref, cols_ref, place_ref, visit, ready=None):
    turn = place_ref[0] * HALF

    def group(step, carry):
        if ready is not None:
            ready(step)
        for i in range(GROUP):
            t = step * GROUP + i
            col = cols_ref[t]
            col = jnp.where(col < CT, col, CT + ((col - CT) ^ turn))
            visit(t, col, rows_ref[t])
        return carry

    lax.fori_loop(0, STEPS, group, 0)


def put_columns(cacc, colown, colother):
    join_from(cacc, colown, 0, OWN)
    join_from(cacc, colother, OWN, CW)


def first_stats_kernel(
    rows_ref, cols_ref, place, source, rhs, dual, rowout, colown, colother, tiles_ref, racc, cacc, sems
):
    def load(step):
        part = pl.ds(step * GROUP, GROUP)
        return pltpu.make_async_copy(source.at[part], tiles_ref.at[part], sems.at[step])

    for step in range(STEPS):
        load(step).start()
    extra = [
        pltpu.make_async_copy(src, rowout.at[pl.ds(RT + i * SHARE, SHARE)], sems.at[STEPS + i])
        for i, src in enumerate((rhs, dual))
    ]
    for copy in extra:
        copy.start()
    racc[...] = jnp.zeros_like(racc)
    cacc[...] = jnp.zeros_like(cacc)

    def visit(t, col, row):
        row_pass(tiles_ref, t, col, row, None, racc, jnp.maximum, True)
        col_pass(tiles_ref, t, col, row, None, cacc, jnp.maximum, True)

    each_tile(rows_ref, cols_ref, place, visit, lambda step: load(step).wait())
    join_from(racc, rowout, 0, RT)
    put_columns(cacc, colown, colother)
    for copy in extra:
        copy.wait()


def first_stats(ids, source, rhs, dual):
    vmem = pl.BlockSpec(memory_space=pltpu.VMEM)
    shapes = [jax.ShapeDtypeStruct((n, TILE), F32) for n in (RT + 2 * SHARE, OWN, HALF)]
    return pl.pallas_call(
        first_stats_kernel,
        out_shape=(*shapes, pltpu.VMEM((NT, TILE, TILE), F32)),
        in_specs=[pl.BlockSpec(memory_space=pltpu.SMEM)] * 3 + [pl.BlockSpec(memory_space=pl.ANY)] * 3,
        out_specs=(vmem,) * 4,
        scratch_shapes=[ROWS, COLS, pltpu.SemaphoreType.DMA((STEPS + 2,))],
        compiler_params=pltpu.CompilerParams(vmem_limit_bytes=VMEM_LIMIT),
    )(*ids, source, rhs, dual)


def next_stats_kernel(
    op, first, rows_ref, cols_ref, place, tiles_ref, r0, r1, r2, r3, loc, mine, other, *rest
):
    if first:
        rowout, colown, colother, rownew, colnew, racc, cacc, rowf, colf = rest
    else:
        rowold, colold, rowout, colown, colother, rownew, colnew, racc, cacc, rowf, colf = rest
    row = tree(jnp.maximum, r0[0:RT], (r1[0:RT], r2[0:RT], r3[0:RT]))
    if first:
        new = 1.0 / jnp.sqrt(row + EPS)
    else:
        old = rowold[...]
        new = old / jnp.sqrt(old * row + EPS)
    rownew[...] = new
    split_to(rowf, new)
    for lo, hi, src in ((0, CT, loc), (CT, OWN, mine), (OWN, CW, other)):
        stat = src[0 : hi - lo]
        if first:
            new = 1.0 / jnp.sqrt(stat + EPS)
        else:
            old = colold[lo:hi]
            new = old / jnp.sqrt(old * stat + EPS)
        colnew[lo:hi] = new
        split_to(colf, new, lo)
    racc[...] = jnp.zeros_like(racc)
    cacc[...] = jnp.zeros_like(cacc)

    def visit(t, col, row):
        row_pass(tiles_ref, t, col, row, colf, racc, op, True)
        col_pass(tiles_ref, t, col, row, rowf, cacc, op, True)

    each_tile(rows_ref, cols_ref, place, visit)
    join_from(racc, rowout, 0, RT)
    put_columns(cacc, colown, colother)


def first_backward_kernel(
    rows_ref, cols_ref, place, tiles_ref, r0, r1, r2, r3, colown, colother, rhsout, dualout, cacc, work
):
    for k, ref in enumerate((r0, r1, r2, r3)):
        at = pl.ds(pl.multiple_of((place[2] ^ k) * SHARE, SHARE), SHARE)
        rhsout[at, :] = ref[RT : RT + SHARE]
        dualout[at, :] = ref[RT + SHARE :]
    split_to(work, dualout[...])
    cacc[...] = jnp.zeros_like(cacc)

    def visit(t, col, row):
        col_pass(tiles_ref, t, col, row, work, cacc, jnp.add, False)

    each_tile(rows_ref, cols_ref, place, visit)
    put_columns(cacc, colown, colother)


def backward_kernel(
    rows_ref, cols_ref, place, tiles_ref, steps, r0, r1, r2, r3, dual, rhs, rowf, colown, colother, dualnew,
    cacc, work,
):
    total = tree(jnp.add, r0[...], (r1[...], r2[...], r3[...]))
    new = dual[...] + steps[1:2] * (rhs[...] - rowf[...] * total)
    dualnew[...] = new
    split_to(work, rowf[...] * new)
    cacc[...] = jnp.zeros_like(cacc)

    def visit(t, col, row):
        col_pass(tiles_ref, t, col, row, work, cacc, jnp.add, False)

    each_tile(rows_ref, cols_ref, place, visit)
    put_columns(cacc, colown, colother)


def forward_kernel(index, grad_at, rows_ref, cols_ref, place, tiles_ref, *rest):
    if index == 0:
        c0, c1, c2, c3, rhs_square, *rest = rest
    else:
        steps, *rest = rest
    loc, mine, other, primal, cost, upper, colf, *rest = rest
    if index == 0:
        steps, *rest = rest
        total = tree(jnp.add, c0[...], (c1[...], c2[...], c3[...]))
        cost_sum = jnp.sum(total, axis=(0, 1), keepdims=True)
        rhs_sum = jnp.sum(rhs_square[...], axis=(0, 1), keepdims=True)
        ratio = jnp.sqrt((cost_sum + EPS) / (rhs_sum + EPS))
        steps[...] = jnp.zeros_like(steps)
        steps[0:1] = jnp.broadcast_to(STEP / ratio, (1, TILE))
        steps[1:2] = jnp.broadcast_to(STEP * ratio, (1, TILE))
    if index < ITERS - 1:
        rowout, fresh, racc, work = rest
    else:
        local, link, p0, p1, p2, p3, racc, work = rest
    for lo, hi, src, first in ((0, CT, loc, 0), (CT, OWN, mine, grad_at), (OWN, CW, other, grad_at)):
        at = slice(lo, hi)
        x, scale = primal[at], colf[at]
        grad = scale * src[first : first + hi - lo]
        new = jnp.clip(x - steps[0:1] * (cost[at] - grad), 0.0, upper[at])
        if index < ITERS - 1:
            fresh[at] = new
        elif lo == 0:
            local[...] = scale * new
        else:
            half = place[0] if lo == CT else 1 - place[0]
            link[pl.ds(pl.multiple_of(half * HALF, HALF), HALF), :] = scale * new
        split_to(work, scale * (2.0 * new - x), lo)
    racc[...] = jnp.zeros_like(racc)

    def visit(t, col, row):
        row_pass(tiles_ref, t, col, row, work, racc, jnp.add, False)

    each_tile(rows_ref, cols_ref, place, visit)
    if index < ITERS - 1:
        join_from(racc, rowout, 0, RT)
    else:
        for k, out in enumerate((p0, p1, p2, p3)):
            at = pl.ds(pl.multiple_of((place[2] ^ k) * SHARE, SHARE), SHARE)
            for w in range(2):
                out[:, w * LANES : (w + 1) * LANES] = racc[w, at, :]


def core_kernel(op, tiles_ref, colown, got, out):
    out[...] = op(colown[CT:OWN], got[...])


def merge_kernel(op, tiles_ref, own, r1, r2, r3, out):
    out[...] = tree(op, own[...], (r1[...], r2[...], r3[...]))


def core_grad_kernel(place, tiles_ref, colown, got, gradown, gradgot, m0, m1, m2, m3, half):
    link = jnp.maximum(colown[CT:OWN], got[...])
    half[...] = gradown[CT:OWN] + gradgot[...]
    for k, out in enumerate((m0, m1, m2, m3)):
        out[0:HALF] = link
        out[HALF:] = half[pl.ds(pl.multiple_of((place[1] ^ k) * CHUNK, CHUNK), CHUNK), :]


def merge_grad_kernel(parts, tiles_ref, own, r1, r2, r3, *outs):
    link = tree(jnp.maximum, own[0:HALF], (r1[0:HALF], r2[0:HALF], r3[0:HALF]))
    grad = tree(jnp.add, own[HALF:], (r1[HALF:], r2[HALF:], r3[HALF:]))
    if parts == 1:
        outs[0][0:HALF] = link
        outs[0][HALF:] = grad
    else:
        outs[0][...] = link
        outs[1][...] = grad


def rows_kernel(
    tiles_ref, r0, r1, r2, r3, rowold, rhs, dual, colown, got, colold, cost, chunk, rownew, rhs_scaled,
    dual_scaled, out,
):
    total = tree(jnp.add, r0[...], (r1[...], r2[...], r3[...]))
    old = rowold[...]
    new = old / jnp.sqrt(old * total + EPS)
    rownew[...] = new
    scaled = new * rhs[...]
    rhs_scaled[...] = scaled
    dual_scaled[...] = dual[...] / new
    out[0:HALF] = colown[CT:OWN] + got[...]
    out[HALF:OWN] = jnp.sum((scaled * scaled).reshape(RT // 8, 8, TILE), axis=0)
    old = colold[0:CT]
    part = old / jnp.sqrt(old * colown[0:CT] + EPS) * cost[...]
    out[OWN : OWN + CT] = part * part
    out[OWN + CT :] = chunk[...]


def merge_norm_kernel(place, tiles_ref, own, r1, r2, r3, both, half):
    for k, ref in enumerate((own, r1, r2, r3)):
        half[pl.ds(pl.multiple_of((place[1] ^ k) * CHUNK, CHUNK), CHUNK), :] = ref[HALF + EIGHT :]
    at = slice(0, HALF + EIGHT)
    both[...] = tree(jnp.add, own[at], (r1[at], r2[at], r3[at]))


def merge_all_kernel(tiles_ref, own, r1, r2, r3, half, out):
    out[0 : HALF + EIGHT] = tree(jnp.add, own[...], (r1[...], r2[...], r3[...]))
    out[HALF + EIGHT :] = half[...]


def setup_kernel(
    place, tiles_ref, own, back, colown, colold, cost_loc, cost_lnk, bound_loc, bound_lnk, start_loc, start_lnk,
    colnew, cost, upper, primal, rhs_square, cost_square,
):
    squares = own[HALF : HALF + EIGHT] + back[HALF : HALF + EIGHT]
    rhs_square[...] = squares[0:CT]
    sums = []
    for lo, hi, stat, half in (
        (0, CT, colown, None),
        (CT, OWN, own, place[0]),
        (OWN, CW, back, 1 - place[0]),
    ):
        at = slice(lo, hi)
        if half is None:
            c, b, x = cost_loc[...], bound_loc[...], start_loc[...]
        else:
            rows = pl.ds(pl.multiple_of(half * HALF, HALF), HALF)
            c, b, x = cost_lnk[rows, :], bound_lnk[rows, :], start_lnk[rows, :]
        old = colold[at]
        new = old / jnp.sqrt(old * stat[0 : hi - lo] + EPS)
        colnew[at] = new
        c = new * c
        cost[at] = c
        upper[at] = b / new
        primal[at] = x / new
        if half is not None:
            sums.append(jnp.sum((c * c).reshape(HALF // 8, 8, TILE), axis=0))
    cost_square[...] = squares[CT:] + (sums[0] + sums[1])


def end_kernel(place, steps, p0, p1, p2, p3, dual, rhs, rowf, out):
    at = pl.ds(pl.multiple_of(place[2] * SHARE, SHARE), SHARE)
    total = tree(jnp.add, p0[...], (p1[...], p2[...], p3[...]))
    scale = rowf[at, :]
    out[...] = scale * (dual[at, :] + steps[1:2] * (rhs[at, :] - scale * total))


def body(
    tile_values,
    tile_rows,
    tile_cols,
    cost_local,
    cost_link,
    bound_local,
    bound_link,
    rhs,
    start_local,
    start_link,
    start_dual,
):
    scen = lax.axis_index("scen")
    place = jnp.stack([scen % 2, scen // 8, lax.axis_index("col")])
    ids = (tile_rows[0, 0], tile_cols[0, 0], place)

    def over(swap, x):
        got = {k: swap(x, k) for k in (2, 1, 3)}
        return x, got[1], got[2], got[3]

    row_part, colown, colother, tiles = first_stats(ids, tile_values[0, 0], rhs[0], start_dual[0])

    def run(kernel, smem, operands, outs, scratch=()):
        return call(kernel, smem, tiles, operands, outs, scratch)

    rows = over(swap_y, row_part)
    (link,) = run(functools.partial(core_kernel, jnp.maximum), (), (colown, swap_core(colother)), (HALF,))
    gradown, gradother, rhs_rows, dual_rows = run(
        first_backward_kernel, ids, rows, (OWN, HALF, RT, RT), (COLS, ROWS)
    )
    gradgot = swap_core(gradother)
    (link,) = run(functools.partial(merge_kernel, jnp.maximum), (), over(swap_x, link), (HALF,))
    (link,) = run(functools.partial(merge_kernel, jnp.maximum), (), over(swap_z, link), (HALF,))

    row_part, colown, colother, row_scale, col_scale = run(
        functools.partial(next_stats_kernel, jnp.maximum, True),
        ids,
        (*rows, colown, link, swap_core(link)),
        (RT, OWN, HALF, RT, CW),
        (ROWS, COLS, ROWS, COLS),
    )
    rows = over(swap_y, row_part)
    sent = run(
        core_grad_kernel,
        (place,),
        (colown, swap_core(colother), gradown, gradgot),
        (HALF + CHUNK,) * 4,
        (pltpu.VMEM((HALF, TILE), F32),),
    )
    got = {k: swap_x(sent[k], k) for k in (2, 1, 3)}
    (both,) = run(
        functools.partial(merge_grad_kernel, 1), (), (sent[0], got[1], got[2], got[3]), (HALF + CHUNK,)
    )
    link, chunk = run(functools.partial(merge_grad_kernel, 2), (), over(swap_z, both), (HALF, CHUNK))

    row_part, colown, colother, row_scale, col_scale = run(
        functools.partial(next_stats_kernel, jnp.add, False),
        ids,
        (*rows, colown, link, swap_core(link), row_scale, col_scale),
        (RT, OWN, HALF, RT, CW),
        (ROWS, COLS, ROWS, COLS),
    )
    rows = over(swap_y, row_part)
    row_scale, rhs_scaled, dual_scaled, both = run(
        rows_kernel,
        (),
        (*rows, row_scale, rhs_rows, dual_rows, colown, swap_core(colother), col_scale, cost_local[0, 0], chunk),
        (RT, RT, RT, HALF + EIGHT + CHUNK),
    )
    both, half = run(merge_norm_kernel, (place,), over(swap_x, both), (HALF + EIGHT, HALF))
    (mine,) = run(merge_all_kernel, (), (*over(swap_z, both), half), (LT + EIGHT,))
    other = swap_core(mine)
    col_scale, cost, upper, primal, rhs_square, cost_square = run(
        setup_kernel,
        (place,),
        (
            mine,
            other,
            colown,
            col_scale,
            cost_local[0, 0],
            cost_link[0],
            bound_local[0, 0],
            bound_link[0],
            start_local[0, 0],
            start_link[0],
        ),
        (CW, CW, CW, CW, CT, CT),
    )
    norms = (*over(swap_y, cost_square), rhs_square)

    grads, grad_at = (gradown, mine, other), HALF + EIGHT
    for index in range(ITERS):
        given = norms if index == 0 else (steps,)
        outs = (RT, CW) if index < ITERS - 1 else (CT, LT) + (SHARE,) * 4
        result = run(
            functools.partial(forward_kernel, index, grad_at),
            ids,
            (*given, *grads, primal, cost, upper, col_scale),
            ((CT,) if index == 0 else ()) + outs,
            (ROWS, COLS),
        )
        if index == 0:
            steps, *result = result
        if index == ITERS - 1:
            break
        row_part, primal = result
        colown, colother, dual_scaled = run(
            backward_kernel,
            ids,
            (steps, *over(swap_y, row_part), dual_scaled, rhs_scaled, row_scale),
            (OWN, HALF, RT),
            (COLS, ROWS),
        )
        (link,) = run(functools.partial(core_kernel, jnp.add), (), (colown, swap_core(colother)), (HALF,))
        (link,) = run(functools.partial(merge_kernel, jnp.add), (), over(swap_x, link), (HALF,))
        (link,) = run(functools.partial(merge_kernel, jnp.add), (), over(swap_z, link), (HALF,))
        grads, grad_at = (colown, link, swap_core(link)), 0

    local, link, *pieces = result
    got = {k: swap_y(pieces[k], k) for k in (2, 1, 3)}
    vmem = pl.BlockSpec(memory_space=pltpu.VMEM)
    multipliers = pl.pallas_call(
        end_kernel,
        out_shape=jax.ShapeDtypeStruct((SHARE, TILE), F32),
        in_specs=[pl.BlockSpec(memory_space=pltpu.SMEM)] + [vmem] * 8,
        out_specs=vmem,
    )(place, steps, pieces[0], got[1], got[2], got[3], dual_scaled, rhs_scaled, row_scale)
    return local[None, None], link[None], multipliers[None]


def solution(mesh):
    placed = (
        P("scen", "col", None, None, None),
        P("scen", "col", None),
        P("scen", "col", None),
        P("scen", "col", None, None),
        P("col", None, None),
        P("scen", "col", None, None),
        P("col", None, None),
        P("scen", "col", None),
        P("scen", "col", None, None),
        P("col", None, None),
        P("scen", "col", None),
    )
    return jax.shard_map(
        body,
        mesh=mesh,
        in_specs=placed,
        out_specs=(P("scen", "col", None, None), P("col", None, None), P("scen", "col", None)),
        check_vma=False,
    )
```

time: 258 us -> 225 us (0.87)
  local copies, waits for them, and re-layouts: 33.9 us -> 4.1 us
  waiting for transfers between devices: 90.2 us -> 97.6 us
  other arithmetic: 7.4 us -> 0.08 us
  starting transfers between devices: 84.2 us -> 77.2 us
  Pallas kernels: 39.3 us -> 44.6 us
    unnamed x34 -> x40, local copies, waits for them, and re-layouts: 31.7 us -> 4.1 us
    ppermute x21, waiting for transfers between devices: 24.1 us -> 32.8 us  [swap_y(): return lax.ppermute(x, 'col', [(i, i ^ k) for i in range(4)])]
    pallas_call x9 -> x26, Pallas kernels: 39.3 us -> 44.6 us  [the longest x24 35.9 us: call(): pl.pallas_call(kernel, out_shape=tuple((jax.ShapeDtypeStruct((n, TILE), F...]
    ppermute x15, starting transfers between devices: 25.6 us -> 22.7 us  [swap_z(): return lax.ppermute(x, 'scen', [(i, i ^ k << 1) for i in range(32)])]
  transfers between devices with their start and end apart: 62 -> 62, of which waited for: 47 -> 42; matrix products, arithmetic and copies ran while one was open for 2% -> 0% of each run, Pallas kernels for 4% -> 4%
where the time goes in v3:
time: 225 us
  waiting for transfers between devices  97.6 us (43%)
  starting transfers between devices  77.2 us (34%)
  Pallas kernels  44.6 us (20%)
  local copies, waits for them, and re-layouts  4.1 us (2%)
    ppermute x15, waiting for transfers between devices, swap_x(): return lax.ppermute(x, 'scen', [(i, i ^ k << 3) for i in range(32)])  36 us
    pallas_call x24, Pallas kernels, call(): pl.pallas_call(kernel, out_shape=tuple((jax.ShapeDtypeStruct((n, TILE), F...  35.9 us
    ppermute x21, waiting for transfers between devices, swap_y(): return lax.ppermute(x, 'col', [(i, i ^ k) for i in range(4)])  32.8 us
    ppermute x21, starting transfers between devices, swap_y(): return lax.ppermute(x, 'col', [(i, i ^ k) for i in range(4)])  31.6 us
    ppermute x15, starting transfers between devices, swap_z(): return lax.ppermute(x, 'scen', [(i, i ^ k << 1) for i in range(32)])  22.7 us
    ppermute x15, starting transfers between devices, swap_x(): return lax.ppermute(x, 'scen', [(i, i ^ k << 3) for i in range(32)])  21.6 us
    ppermute x15, waiting for transfers between devices, swap_z(): return lax.ppermute(x, 'scen', [(i, i ^ k << 1) for i in range(32)])  19.6 us
    ppermute x11, waiting for transfers between devices, swap_core(): return lax.ppermute(x, 'scen', [(i, i ^ 1) for i in range(32)])  9.21 us
  transfers between devices with their start and end apart: 62, of which 42 were waited for; matrix products, arithmetic and copies ran while one was open for 0% of the time, Pallas kernels for 4%

profile of v3, /device:TPU:0, one launch (start us, length us, event | category | flops | bytes accessed | tf_op | source)
XLA Modules:
  0.0 224.6 jit_solution(10260970677806174781)
XLA Ops:
  3.6 6.9 %shard_map.130 = (f32[192,256]{1,0:T(8,128)S(1)}, f32[136,256]{1,0:T(8,128)S(1)}, f32[128,256]{1,0:T(8,128)S(1)}, f32[64,256,256]{2,1,0:T(8,128)S(1)}) custom-call(s32[64]{0:T(128)S(1)} %bitcast.20, s32[64]{0:T(128)S(1)} %bitcast.29, s32[3]{0:T(128)S(1)} %pad_add_fusion.place, f32[64,256,256]{2,1,0:T(8,128)} %bitcast.44, f32[32,256]{1,0:T(8,128)S(1)} %bitcast.40, ...), custom_call_target="tpu_custom_call" | custom-call | tf_op jit(solution)/shard_map/pallas_call | solution.py:168
  16.1 4.6 %collective-permute-done.6.r3 = f32[128,256]{1,0:T(8,128)S(1)} collective-permute-done((f32[128,256]{1,0:T(8,128)S(1)}, f32[128,256]{1,0:T(8,128)S(1)}, u32[]{:S(2)}, u32[]{:S(2)}) %collective-permute-start.6) | collective-permute-done | bytes 131104 | tf_op jit(solution)/shard_map/ppermute | solution.py:38
  22.8 4.1 %collective-permute-start.9 = (f32[128,256]{1,0:T(8,128)S(1)}, f32[128,256]{1,0:T(8,128)S(1)}, u32[]{:S(2)}, u32[]{:S(2)}) collective-permute-start(f32[128,256]{1,0:T(8,128)S(1)} %shard_map.132.own), channel_id=1, source_target_pairs={{0,24},{4,28},{8,16},{12,20},{16,8},{20,12},{24,0},{28,4},{32,56},... | collective-permute-start | bytes 393224 | tf_op jit(solution)/shard_map/ppermute | solution.py:34
  33.7 4.0 %collective-permute-done.2.r3 = f32[192,256]{1,0:T(8,128)S(1)} collective-permute-done((f32[192,256]{1,0:T(8,128)S(1)}, f32[192,256]{1,0:T(8,128)S(1)}, u32[]{:S(2)}, u32[]{:S(2)}) %collective-permute-start.2) | collective-permute-done | bytes 196640 | tf_op jit(solution)/shard_map/ppermute | solution.py:42
  39.1 3.4 %shard_map.135 = (f32[136,256]{1,0:T(8,128)S(1)}, f32[128,256]{1,0:T(8,128)S(1)}, f32[128,256]{1,0:T(8,128)S(1)}, f32[128,256]{1,0:T(8,128)S(1)}) custom-call(s32[64]{0:T(128)S(1)} %bitcast.21, s32[64]{0:T(128)S(1)} %bitcast.30, s32[3]{0:T(128)S(1)} %pad_add_fusion.place, f32[64,256,256]{2,1,0:T(8,128)S(1)} %get-tuple-element.56.tiles_ref, ...), custom_call_target="tpu_custom_call" | custom-call | tf_op jit(solution)/shard_map/pallas_call | solution.py:105
  42.6 5.8 %shard_map.134 = (f32[128,256]{1,0:T(8,128)S(1)}, f32[136,256]{1,0:T(8,128)S(1)}, f32[128,256]{1,0:T(8,128)S(1)}, f32[128,256]{1,0:T(8,128)S(1)}, f32[264,256]{1,0:T(8,128)S(1)}) custom-call(s32[64]{0:T(128)S(1)} %bitcast.22, s32[64]{0:T(128)S(1)} %bitcast.31, s32[3]{0:T(128)S(1)} %pad_add_fusion.place, f32[64,256,256]{2,1,0:T(8,128)S(1)} %get-tuple-element.56.tiles_ref, ...), custom_call_target="tpu_custom_call" | custom-call | tf_op jit(solution)/shard_map/pallas_call | solution.py:105
  57.7 5.3 %collective-permute-done.17.r2 = f32[160,256]{1,0:T(8,128)S(1)} collective-permute-done((f32[160,256]{1,0:T(8,128)S(1)}, f32[160,256]{1,0:T(8,128)S(1)}, u32[]{:S(2)}, u32[]{:S(2)}) %collective-permute-start.17) | collective-permute-done | bytes 163872 | tf_op jit(solution)/shard_map/ppermute | solution.py:38
  65.6 3.4 %collective-permute-start.21 = (f32[160,256]{1,0:T(8,128)S(1)}, f32[160,256]{1,0:T(8,128)S(1)}, u32[]{:S(2)}, u32[]{:S(2)}) collective-permute-start(f32[160,256]{1,0:T(8,128)S(1)} %shard_map.137.own), channel_id=1, source_target_pairs={{0,24},{4,28},{8,16},{12,20},{16,8},{20,12},{24,0},{28,4},{32,56},... | collective-permute-start | bytes 491528 | tf_op jit(solution)/shard_map/ppermute | solution.py:34
  80.5 5.9 %shard_map.139 = (f32[128,256]{1,0:T(8,128)S(1)}, f32[136,256]{1,0:T(8,128)S(1)}, f32[128,256]{1,0:T(8,128)S(1)}, f32[128,256]{1,0:T(8,128)S(1)}, f32[264,256]{1,0:T(8,128)S(1)}) custom-call(s32[64]{0:T(128)S(1)} %bitcast.23, s32[64]{0:T(128)S(1)} %bitcast.32, s32[3]{0:T(128)S(1)} %pad_add_fusion.place, f32[64,256,256]{2,1,0:T(8,128)S(1)} %get-tuple-element.56.tiles_ref, ...), custom_call_target="tpu_custom_call" | custom-call | tf_op jit(solution)/shard_map/pallas_call | solution.py:105
  90.6 5.1 %collective-permute-done.25.r3 = f32[128,256]{1,0:T(8,128)S(1)} collective-permute-done((f32[128,256]{1,0:T(8,128)S(1)}, f32[128,256]{1,0:T(8,128)S(1)}, u32[]{:S(2)}, u32[]{:S(2)}) %collective-permute-start.25) | collective-permute-done | bytes 131104 | tf_op jit(solution)/shard_map/ppermute | solution.py:42
  98.4 3.4 %collective-permute-start.27 = (f32[176,256]{1,0:T(8,128)S(1)}, f32[176,256]{1,0:T(8,128)S(1)}, u32[]{:S(2)}, u32[]{:S(2)}) collective-permute-start(f32[176,256]{1,0:T(8,128)S(1)} %get-tuple-element.80.own), channel_id=1, source_target_pairs={{0,32},{4,36},{8,40},{12,44},{16,48},{20,52},{24,56},{28,60},{32,0... | collective-permute-start | bytes 540680 | tf_op jit(solution)/shard_map/ppermute | solution.py:38
  101.8 6.5 %collective-permute-done.29.r3 = f32[176,256]{1,0:T(8,128)S(1)} collective-permute-done((f32[176,256]{1,0:T(8,128)S(1)}, f32[176,256]{1,0:T(8,128)S(1)}, u32[]{:S(2)}, u32[]{:S(2)}) %collective-permute-start.29) | collective-permute-done | bytes 180256 | tf_op jit(solution)/shard_map/ppermute | solution.py:38
  109.5 3.8 %collective-permute-start.32 = (f32[144,256]{1,0:T(8,128)S(1)}, f32[144,256]{1,0:T(8,128)S(1)}, u32[]{:S(2)}, u32[]{:S(2)}) collective-permute-start(f32[144,256]{1,0:T(8,128)S(1)} %get-tuple-element.81.own), channel_id=1, source_target_pairs={{0,24},{4,28},{8,16},{12,20},{16,8},{20,12},{24,0},{28,4},{32,56},... | collective-permute-start | bytes 442376 | tf_op jit(solution)/shard_map/ppermute | solution.py:34
  114.4 4.2 %collective-permute-done.32.r3 = f32[144,256]{1,0:T(8,128)S(1)} collective-permute-done((f32[144,256]{1,0:T(8,128)S(1)}, f32[144,256]{1,0:T(8,128)S(1)}, u32[]{:S(2)}, u32[]{:S(2)}) %collective-permute-start.32) | collective-permute-done | bytes 147488 | tf_op jit(solution)/shard_map/ppermute | solution.py:34
  131.3 3.7 %shard_map.144 = (f32[8,256]{1,0:T(8,128)S(1)}, f32[128,256]{1,0:T(8,128)S(1)}, f32[264,256]{1,0:T(8,128)S(1)}) custom-call(s32[64]{0:T(128)S(1)} %bitcast.24, s32[64]{0:T(128)S(1)} %bitcast.33, s32[3]{0:T(128)S(1)} %pad_add_fusion.place, f32[64,256,256]{2,1,0:T(8,128)S(1)} %get-tuple-element.56.tiles_ref, f32[8,256]{1,0:T(8,128)S(1)} %get-tuple-element.83.rest_0_, ...), custom_call_target="tpu_custom_call" | custom-call | tf_op jit(solution)/shard_map/pallas_call | solution.py:105
  143.7 3.4 %shard_map.145 = (f32[136,256]{1,0:T(8,128)S(1)}, f32[128,256]{1,0:T(8,128)S(1)}, f32[128,256]{1,0:T(8,128)S(1)}) custom-call(s32[64]{0:T(128)S(1)} %bitcast.25, s32[64]{0:T(128)S(1)} %bitcast.34, s32[3]{0:T(128)S(1)} %pad_add_fusion.place, f32[64,256,256]{2,1,0:T(8,128)S(1)} %get-tuple-element.56.tiles_ref, f32[8,256]{1,0:T(8,128)S(1)} %get-tuple-element.89.steps.rest_0_, ...), custom_call_target="tpu_custom_call" | custom-call | tf_op jit(solution)/shard_map/pallas_call | solution.py:105
  152.8 5.5 %collective-permute-done.43.r3 = f32[128,256]{1,0:T(8,128)S(1)} collective-permute-done((f32[128,256]{1,0:T(8,128)S(1)}, f32[128,256]{1,0:T(8,128)S(1)}, u32[]{:S(2)}, u32[]{:S(2)}) %collective-permute-start.43) | collective-permute-done | bytes 131104 | tf_op jit(solution)/shard_map/ppermute | solution.py:38
  163.1 3.8 %collective-permute-done.46.r3 = f32[128,256]{1,0:T(8,128)S(1)} collective-permute-done((f32[128,256]{1,0:T(8,128)S(1)}, f32[128,256]{1,0:T(8,128)S(1)}, u32[]{:S(2)}, u32[]{:S(2)}) %collective-permute-start.46) | collective-permute-done | bytes 131104 | tf_op jit(solution)/shard_map/ppermute | solution.py:34
  169.8 3.5 %shard_map.149 = (f32[128,256]{1,0:T(8,128)S(1)}, f32[264,256]{1,0:T(8,128)S(1)}) custom-call(s32[64]{0:T(128)S(1)} %bitcast.26, s32[64]{0:T(128)S(1)} %bitcast.35, s32[3]{0:T(128)S(1)} %pad_add_fusion.place, f32[64,256,256]{2,1,0:T(8,128)S(1)} %get-tuple-element.56.tiles_ref, f32[8,256]{1,0:T(8,128)S(1)} %get-tuple-element.89.steps.rest_0_, ...), custom_call_target="tpu_custom_call" | custom-call | tf_op jit(solution)/shard_map/pallas_call | solution.py:105
  177.5 5.5 %collective-permute-done.50.r3 = f32[128,256]{1,0:T(8,128)S(1)} collective-permute-done((f32[128,256]{1,0:T(8,128)S(1)}, f32[128,256]{1,0:T(8,128)S(1)}, u32[]{:S(2)}, u32[]{:S(2)}) %collective-permute-start.50) | collective-permute-done | bytes 131104 | tf_op jit(solution)/shard_map/ppermute | solution.py:42
  183.6 3.4 %shard_map.150 = (f32[136,256]{1,0:T(8,128)S(1)}, f32[128,256]{1,0:T(8,128)S(1)}, f32[128,256]{1,0:T(8,128)S(1)}) custom-call(s32[64]{0:T(128)S(1)} %bitcast.27, s32[64]{0:T(128)S(1)} %bitcast.36, s32[3]{0:T(128)S(1)} %pad_add_fusion.place, f32[64,256,256]{2,1,0:T(8,128)S(1)} %get-tuple-element.56.tiles_ref, f32[8,256]{1,0:T(8,128)S(1)} %get-tuple-element.89.steps.rest_0_, ...), custom_call_target="tpu_custom_call" | custom-call | tf_op jit(solution)/shard_map/pallas_call | solution.py:105
  192.7 5.5 %collective-permute-done.54.r3 = f32[128,256]{1,0:T(8,128)S(1)} collective-permute-done((f32[128,256]{1,0:T(8,128)S(1)}, f32[128,256]{1,0:T(8,128)S(1)}, u32[]{:S(2)}, u32[]{:S(2)}) %collective-permute-start.54) | collective-permute-done | bytes 131104 | tf_op jit(solution)/shard_map/ppermute | solution.py:38
  203.0 4.0 %collective-permute-done.57.r3 = f32[128,256]{1,0:T(8,128)S(1)} collective-permute-done((f32[128,256]{1,0:T(8,128)S(1)}, f32[128,256]{1,0:T(8,128)S(1)}, u32[]{:S(2)}, u32[]{:S(2)}) %collective-permute-start.57) | collective-permute-done | bytes 131104 | tf_op jit(solution)/shard_map/ppermute | solution.py:34
  209.4 4.3 %shard_map.154 = (f32[8,256]{1,0:T(8,128)}, f32[256,256]{1,0:T(8,128)}, f32[32,256]{1,0:T(8,128)S(1)}, f32[32,256]{1,0:T(8,128)S(1)}, f32[32,256]{1,0:T(8,128)S(1)}, /*index=5*/f32[32,256]{1,0:T(8,128)S(1)}) custom-call(s32[64]{0:T(128)S(1)} %bitcast.28, s32[64]{0:T(128)S(1)} %bitcast.37, s32[3]{0:T(128)S(1)} %pad_add_fusion.place, ...), custom_call_target="tpu_custom_call" | custom-call | tf_op jit(solution)/shard_map/pallas_call | solution.py:105
  (167 shorter events, 114.7 us)
Async XLA Ops:
  11.9 8.8 %collective-permute-start.6 = (f32[128,256]{1,0:T(8,128)S(1)}, f32[128,256]{1,0:T(8,128)S(1)}, u32[]{:S(2)}, u32[]{:S(2)}) collective-permute-start(f32[128,256]{1,0:T(8,128)S(1)} %shard_map.131.own), channel_id=1, source_target_pairs={{0,96},{4,100},{8,104},{12,108},{16,112},{20,116},{24,120},{28,124... | collective-permute-start | bytes 393224 | tf_op jit(solution)/shard_map/ppermute | solution.py:38
  22.8 8.7 %collective-permute-start.9 = (f32[128,256]{1,0:T(8,128)S(1)}, f32[128,256]{1,0:T(8,128)S(1)}, u32[]{:S(2)}, u32[]{:S(2)}) collective-permute-start(f32[128,256]{1,0:T(8,128)S(1)} %shard_map.132.own), channel_id=1, source_target_pairs={{0,24},{4,28},{8,16},{12,20},{16,8},{20,12},{24,0},{28,4},{32,56},... | collective-permute-start | bytes 393224 | tf_op jit(solution)/shard_map/ppermute | solution.py:34
  27.8 9.8 %collective-permute-start.2 = (f32[192,256]{1,0:T(8,128)S(1)}, f32[192,256]{1,0:T(8,128)S(1)}, u32[]{:S(2)}, u32[]{:S(2)}) collective-permute-start(f32[192,256]{1,0:T(8,128)S(1)} %get-tuple-element.57.r0), channel_id=1, source_target_pairs={{0,3},{1,2},{2,1},{3,0},{4,7},{5,6},{6,5},{7,4},{8,11},{9,10},{10,... | collective-permute-start | bytes 589832 | tf_op jit(solution)/shard_map/ppermute | solution.py:42
  30.9 8.2 %collective-permute-start.1 = (f32[192,256]{1,0:T(8,128)S(1)}, f32[192,256]{1,0:T(8,128)S(1)}, u32[]{:S(2)}, u32[]{:S(2)}) collective-permute-start(f32[192,256]{1,0:T(8,128)S(1)} %get-tuple-element.57.r0), channel_id=1, source_target_pairs={{0,2},{1,3},{2,0},{3,1},{4,6},{5,7},{6,4},{7,5},{8,10},{9,11},{10,... | collective-permute-start | bytes 589832 | tf_op jit(solution)/shard_map/ppermute | solution.py:42
  33.6 9.0 %collective-permute-start.10 = (f32[128,256]{1,0:T(8,128)S(1)}, f32[128,256]{1,0:T(8,128)S(1)}, u32[]{:S(2)}, u32[]{:S(2)}) collective-permute-start(f32[128,256]{1,0:T(8,128)S(1)} %shard_map.133.mine), channel_id=1, source_target_pairs={{0,4},{4,0},{8,12},{12,8},{16,20},{20,16},{24,28},{28,24},{32,36},... | collective-permute-start | bytes 393224 | tf_op jit(solution)/shard_map/ppermute | solution.py:30
  52.7 10.3 %collective-permute-start.17 = (f32[160,256]{1,0:T(8,128)S(1)}, f32[160,256]{1,0:T(8,128)S(1)}, u32[]{:S(2)}, u32[]{:S(2)}) collective-permute-start(f32[160,256]{1,0:T(8,128)S(1)} %get-tuple-element.67), channel_id=1, source_target_pairs={{0,64},{4,68},{8,72},{12,76},{16,80},{20,84},{24,88},{28,92},{32,9... | collective-permute-start | bytes 491528 | tf_op jit(solution)/shard_map/ppermute | solution.py:38
  54.9 10.6 %collective-permute-start.18 = (f32[160,256]{1,0:T(8,128)S(1)}, f32[160,256]{1,0:T(8,128)S(1)}, u32[]{:S(2)}, u32[]{:S(2)}) collective-permute-start(f32[160,256]{1,0:T(8,128)S(1)} %get-tuple-element.68), channel_id=1, source_target_pairs={{0,96},{4,100},{8,104},{12,108},{16,112},{20,116},{24,120},{28,124... | collective-permute-start | bytes 491528 | tf_op jit(solution)/shard_map/ppermute | solution.py:38
  65.6 9.9 %collective-permute-start.21 = (f32[160,256]{1,0:T(8,128)S(1)}, f32[160,256]{1,0:T(8,128)S(1)}, u32[]{:S(2)}, u32[]{:S(2)}) collective-permute-start(f32[160,256]{1,0:T(8,128)S(1)} %shard_map.137.own), channel_id=1, source_target_pairs={{0,24},{4,28},{8,16},{12,20},{16,8},{20,12},{24,0},{28,4},{32,56},... | collective-permute-start | bytes 491528 | tf_op jit(solution)/shard_map/ppermute | solution.py:34
  69.0 8.5 %collective-permute-start.20 = (f32[160,256]{1,0:T(8,128)S(1)}, f32[160,256]{1,0:T(8,128)S(1)}, u32[]{:S(2)}, u32[]{:S(2)}) collective-permute-start(f32[160,256]{1,0:T(8,128)S(1)} %shard_map.137.own), channel_id=1, source_target_pairs={{0,16},{4,20},{8,24},{12,28},{16,0},{20,4},{24,8},{28,12},{32,48},... | collective-permute-start | bytes 491528 | tf_op jit(solution)/shard_map/ppermute | solution.py:34
  69.0 8.5 %collective-permute-start.19 = (f32[160,256]{1,0:T(8,128)S(1)}, f32[160,256]{1,0:T(8,128)S(1)}, u32[]{:S(2)}, u32[]{:S(2)}) collective-permute-start(f32[160,256]{1,0:T(8,128)S(1)} %shard_map.137.own), channel_id=1, source_target_pairs={{0,8},{4,12},{8,0},{12,4},{16,24},{20,28},{24,16},{28,20},{32,40},... | collective-permute-start | bytes 491528 | tf_op jit(solution)/shard_map/ppermute | solution.py:34
  86.5 9.3 %collective-permute-start.25 = (f32[128,256]{1,0:T(8,128)S(1)}, f32[128,256]{1,0:T(8,128)S(1)}, u32[]{:S(2)}, u32[]{:S(2)}) collective-permute-start(f32[128,256]{1,0:T(8,128)S(1)} %get-tuple-element.72.r0), channel_id=1, source_target_pairs={{0,3},{1,2},{2,1},{3,0},{4,7},{5,6},{6,5},{7,4},{8,11},{9,10},{10,... | collective-permute-start | bytes 393224 | tf_op jit(solution)/shard_map/ppermute | solution.py:42
  97.6 10.6 %collective-permute-start.29 = (f32[176,256]{1,0:T(8,128)S(1)}, f32[176,256]{1,0:T(8,128)S(1)}, u32[]{:S(2)}, u32[]{:S(2)}) collective-permute-start(f32[176,256]{1,0:T(8,128)S(1)} %get-tuple-element.80.own), channel_id=1, source_target_pairs={{0,96},{4,100},{8,104},{12,108},{16,112},{20,116},{24,120},{28,124... | collective-permute-start | bytes 540680 | tf_op jit(solution)/shard_map/ppermute | solution.py:38
  98.2 10.1 %collective-permute-start.28 = (f32[176,256]{1,0:T(8,128)S(1)}, f32[176,256]{1,0:T(8,128)S(1)}, u32[]{:S(2)}, u32[]{:S(2)}) collective-permute-start(f32[176,256]{1,0:T(8,128)S(1)} %get-tuple-element.80.own), channel_id=1, source_target_pairs={{0,64},{4,68},{8,72},{12,76},{16,80},{20,84},{24,88},{28,92},{32,9... | collective-permute-start | bytes 540680 | tf_op jit(solution)/shard_map/ppermute | solution.py:38
  98.4 10.5 %collective-permute-start.27 = (f32[176,256]{1,0:T(8,128)S(1)}, f32[176,256]{1,0:T(8,128)S(1)}, u32[]{:S(2)}, u32[]{:S(2)}) collective-permute-start(f32[176,256]{1,0:T(8,128)S(1)} %get-tuple-element.80.own), channel_id=1, source_target_pairs={{0,32},{4,36},{8,40},{12,44},{16,48},{20,52},{24,56},{28,60},{32,0... | collective-permute-start | bytes 540680 | tf_op jit(solution)/shard_map/ppermute | solution.py:38
  109.5 9.1 %collective-permute-start.32 = (f32[144,256]{1,0:T(8,128)S(1)}, f32[144,256]{1,0:T(8,128)S(1)}, u32[]{:S(2)}, u32[]{:S(2)}) collective-permute-start(f32[144,256]{1,0:T(8,128)S(1)} %get-tuple-element.81.own), channel_id=1, source_target_pairs={{0,24},{4,28},{8,16},{12,20},{16,8},{20,12},{24,0},{28,4},{32,56},... | collective-permute-start | bytes 442376 | tf_op jit(solution)/shard_map/ppermute | solution.py:34
  148.7 9.6 %collective-permute-start.43 = (f32[128,256]{1,0:T(8,128)S(1)}, f32[128,256]{1,0:T(8,128)S(1)}, u32[]{:S(2)}, u32[]{:S(2)}) collective-permute-start(f32[128,256]{1,0:T(8,128)S(1)} %shard_map.146.own), channel_id=1, source_target_pairs={{0,96},{4,100},{8,104},{12,108},{16,112},{20,116},{24,120},{28,124... | collective-permute-start | bytes 393224 | tf_op jit(solution)/shard_map/ppermute | solution.py:38
  148.7 9.6 %collective-permute-start.42 = (f32[128,256]{1,0:T(8,128)S(1)}, f32[128,256]{1,0:T(8,128)S(1)}, u32[]{:S(2)}, u32[]{:S(2)}) collective-permute-start(f32[128,256]{1,0:T(8,128)S(1)} %shard_map.146.own), channel_id=1, source_target_pairs={{0,64},{4,68},{8,72},{12,76},{16,80},{20,84},{24,88},{28,92},{32,9... | collective-permute-start | bytes 393224 | tf_op jit(solution)/shard_map/ppermute | solution.py:38
  149.6 9.2 %collective-permute-start.41 = (f32[128,256]{1,0:T(8,128)S(1)}, f32[128,256]{1,0:T(8,128)S(1)}, u32[]{:S(2)}, u32[]{:S(2)}) collective-permute-start(f32[128,256]{1,0:T(8,128)S(1)} %shard_map.146.own), channel_id=1, source_target_pairs={{0,32},{4,36},{8,40},{12,44},{16,48},{20,52},{24,56},{28,60},{32,0... | collective-permute-start | bytes 393224 | tf_op jit(solution)/shard_map/ppermute | solution.py:38
  173.3 9.7 %collective-permute-start.50 = (f32[128,256]{1,0:T(8,128)S(1)}, f32[128,256]{1,0:T(8,128)S(1)}, u32[]{:S(2)}, u32[]{:S(2)}) collective-permute-start(f32[128,256]{1,0:T(8,128)S(1)} %get-tuple-element.97.r0), channel_id=1, source_target_pairs={{0,3},{1,2},{2,1},{3,0},{4,7},{5,6},{6,5},{7,4},{8,11},{9,10},{10,... | collective-permute-start | bytes 393224 | tf_op jit(solution)/shard_map/ppermute | solution.py:42
  174.7 8.2 %collective-permute-start.49 = (f32[128,256]{1,0:T(8,128)S(1)}, f32[128,256]{1,0:T(8,128)S(1)}, u32[]{:S(2)}, u32[]{:S(2)}) collective-permute-start(f32[128,256]{1,0:T(8,128)S(1)} %get-tuple-element.97.r0), channel_id=1, source_target_pairs={{0,2},{1,3},{2,0},{3,1},{4,6},{5,7},{6,4},{7,5},{8,10},{9,11},{10,... | collective-permute-start | bytes 393224 | tf_op jit(solution)/shard_map/ppermute | solution.py:42
  188.5 9.6 %collective-permute-start.54 = (f32[128,256]{1,0:T(8,128)S(1)}, f32[128,256]{1,0:T(8,128)S(1)}, u32[]{:S(2)}, u32[]{:S(2)}) collective-permute-start(f32[128,256]{1,0:T(8,128)S(1)} %shard_map.151.own), channel_id=1, source_target_pairs={{0,96},{4,100},{8,104},{12,108},{16,112},{20,116},{24,120},{28,124... | collective-permute-start | bytes 393224 | tf_op jit(solution)/shard_map/ppermute | solution.py:38
  189.2 9.0 %collective-permute-start.53 = (f32[128,256]{1,0:T(8,128)S(1)}, f32[128,256]{1,0:T(8,128)S(1)}, u32[]{:S(2)}, u32[]{:S(2)}) collective-permute-start(f32[128,256]{1,0:T(8,128)S(1)} %shard_map.151.own), channel_id=1, source_target_pairs={{0,64},{4,68},{8,72},{12,76},{16,80},{20,84},{24,88},{28,92},{32,9... | collective-permute-start | bytes 393224 | tf_op jit(solution)/shard_map/ppermute | solution.py:38
  190.1 8.7 %collective-permute-start.52 = (f32[128,256]{1,0:T(8,128)S(1)}, f32[128,256]{1,0:T(8,128)S(1)}, u32[]{:S(2)}, u32[]{:S(2)}) collective-permute-start(f32[128,256]{1,0:T(8,128)S(1)} %shard_map.151.own), channel_id=1, source_target_pairs={{0,32},{4,36},{8,40},{12,44},{16,48},{20,52},{24,56},{28,60},{32,0... | collective-permute-start | bytes 393224 | tf_op jit(solution)/shard_map/ppermute | solution.py:38
  198.8 8.2 %collective-permute-start.57 = (f32[128,256]{1,0:T(8,128)S(1)}, f32[128,256]{1,0:T(8,128)S(1)}, u32[]{:S(2)}, u32[]{:S(2)}) collective-permute-start(f32[128,256]{1,0:T(8,128)S(1)} %shard_map.152.own), channel_id=1, source_target_pairs={{0,24},{4,28},{8,16},{12,20},{16,8},{20,12},{24,0},{28,4},{32,56},... | collective-permute-start | bytes 393224 | tf_op jit(solution)/shard_map/ppermute | solution.py:34
  (58 other events, 853.1 us)

commit v4 on v3

--- a/solution.py
+++ b/solution.py
@@ -30,12 +30,12 @@
     return lax.ppermute(x, "scen", [(i, i ^ 1) for i in range(32)])
 
 
-def swap_z(x, k):
-    return lax.ppermute(x, "scen", [(i, i ^ (k << 1)) for i in range(32)])
-
-
-def swap_x(x, k):
-    return lax.ppermute(x, "scen", [(i, i ^ (k << 3)) for i in range(32)])
+def swap_first(x, k):
+    return lax.ppermute(x, "scen", [(i, i ^ (k << (1 if i % 2 else 3))) for i in range(32)])
+
+
+def swap_second(x, k):
+    return lax.ppermute(x, "scen", [(i, i ^ (k << (3 if i % 2 else 1))) for i in range(32)])
 
 
 def swap_y(x, k):
@@ -134,8 +134,16 @@
 
 
 def first_stats_kernel(
-    rows_ref, cols_ref, place, source, rhs, dual, rowout, colown, colother, tiles_ref, racc, cacc, sems
-):
+    place, rows_hbm, cols_hbm, source, rhs, dual, rowout, colown, colother, tiles_ref, racc, cacc,
+    rows_ref, cols_ref, sems,
+):
+    indices = [
+        pltpu.make_async_copy(src, dst, sems.at[STEPS + 2 + i])
+        for i, (src, dst) in enumerate(((rows_hbm, rows_ref), (cols_hbm, cols_ref)))
+    ]
+    for copy in indices:
+        copy.start()
+
     def load(step):
         part = pl.ds(step * GROUP, GROUP)
         return pltpu.make_async_copy(source.at[part], tiles_ref.at[part], sems.at[step])
@@ -151,6 +159,9 @@
     racc[...] = jnp.zeros_like(racc)
     cacc[...] = jnp.zeros_like(cacc)
 
+    for copy in indices:
+        copy.wait()
+
     def visit(t, col, row):
         row_pass(tiles_ref, t, col, row, None, racc, jnp.maximum, True)
         col_pass(tiles_ref, t, col, row, None, cacc, jnp.maximum, True)
@@ -168,21 +179,27 @@
     return pl.pallas_call(
         first_stats_kernel,
         out_shape=(*shapes, pltpu.VMEM((NT, TILE, TILE), F32)),
-        in_specs=[pl.BlockSpec(memory_space=pltpu.SMEM)] * 3 + [pl.BlockSpec(memory_space=pl.ANY)] * 3,
+        in_specs=[pl.BlockSpec(memory_space=pltpu.SMEM)] + [pl.BlockSpec(memory_space=pltpu.HBM)] * 5,
         out_specs=(vmem,) * 4,
-        scratch_shapes=[ROWS, COLS, pltpu.SemaphoreType.DMA((STEPS + 2,))],
+        scratch_shapes=[
+            ROWS,
+            COLS,
+            pltpu.SMEM((NT,), jnp.int32),
+            pltpu.SMEM((NT,), jnp.int32),
+            pltpu.SemaphoreType.DMA((STEPS + 4,)),
+        ],
         compiler_params=pltpu.CompilerParams(vmem_limit_bytes=VMEM_LIMIT),
-    )(*ids, source, rhs, dual)
+    )(ids[2], *(pltpu.with_memory_space_constraint(x, pltpu.HBM) for x in (*ids[:2], source, rhs, dual)))
 
 
 def next_stats_kernel(
-    op, first, rows_ref, cols_ref, place, tiles_ref, r0, r1, r2, r3, loc, mine, other, *rest
+    op, first, rows_ref, cols_ref, place, tiles_ref, rowstat, loc, mine, other, *rest
 ):
     if first:
         rowout, colown, colother, rownew, colnew, racc, cacc, rowf, colf = rest
     else:
         rowold, colold, rowout, colown, colother, rownew, colnew, racc, cacc, rowf, colf = rest
-    row = tree(jnp.maximum, r0[0:RT], (r1[0:RT], r2[0:RT], r3[0:RT]))
+    row = rowstat[...]
     if first:
         new = 1.0 / jnp.sqrt(row + EPS)
     else:
@@ -263,7 +280,10 @@
     if index < ITERS - 1:
         rowout, fresh, racc, work = rest
     else:
-        local, link, p0, p1, p2, p3, racc, work = rest
+        dual, rhs, rowf, local, link, dualout, rhsout, rowfout, p0, p1, p2, p3, racc, work = rest
+        own = pl.ds(pl.multiple_of(place[2] * SHARE, SHARE), SHARE)
+        for ref, out in ((dual, dualout), (rhs, rhsout), (rowf, rowfout)):
+            out[...] = ref[own, :]
     for lo, hi, src, first in ((0, CT, loc, 0), (CT, OWN, mine, grad_at), (OWN, CW, other, grad_at)):
         at = slice(lo, hi)
         x, scale = primal[at], colf[at]
@@ -300,6 +320,15 @@
     out[...] = tree(op, own[...], (r1[...], r2[...], r3[...]))
 
 
+def merge_after_kernel(tiles_ref, own, r1, r2, r3, after, out):
+    out[...] = tree(jnp.maximum, own[...], (r1[...], r2[...], r3[...]))
+
+
+def merge_rows_kernel(tiles_ref, own, r1, r2, r3, y0, y1, y2, y3, out, rows):
+    out[...] = tree(jnp.maximum, own[...], (r1[...], r2[...], r3[...]))
+    rows[...] = tree(jnp.maximum, y0[0:RT], (y1[0:RT], y2[0:RT], y3[0:RT]))
+
+
 def core_grad_kernel(place, tiles_ref, colown, got, gradown, gradgot, m0, m1, m2, m3, half):
     link = jnp.maximum(colown[CT:OWN], got[...])
     half[...] = gradown[CT:OWN] + gradgot[...]
@@ -308,15 +337,15 @@
         out[HALF:] = half[pl.ds(pl.multiple_of((place[1] ^ k) * CHUNK, CHUNK), CHUNK), :]
 
 
-def merge_grad_kernel(parts, tiles_ref, own, r1, r2, r3, *outs):
-    link = tree(jnp.maximum, own[0:HALF], (r1[0:HALF], r2[0:HALF], r3[0:HALF]))
-    grad = tree(jnp.add, own[HALF:], (r1[HALF:], r2[HALF:], r3[HALF:]))
-    if parts == 1:
-        outs[0][0:HALF] = link
-        outs[0][HALF:] = grad
-    else:
-        outs[0][...] = link
-        outs[1][...] = grad
+def merge_grad_rows_kernel(tiles_ref, own, r1, r2, r3, y0, y1, y2, y3, both, rows):
+    both[0:HALF] = tree(jnp.maximum, own[0:HALF], (r1[0:HALF], r2[0:HALF], r3[0:HALF]))
+    both[HALF:] = tree(jnp.add, own[HALF:], (r1[HALF:], r2[HALF:], r3[HALF:]))
+    rows[...] = tree(jnp.maximum, y0[...], (y1[...], y2[...], y3[...]))
+
+
+def merge_grad_kernel(tiles_ref, own, r1, r2, r3, link, grad):
+    link[...] = tree(jnp.maximum, own[0:HALF], (r1[0:HALF], r2[0:HALF], r3[0:HALF]))
+    grad[...] = tree(jnp.add, own[HALF:], (r1[HALF:], r2[HALF:], r3[HALF:]))
 
 
 def rows_kernel(
@@ -380,11 +409,10 @@
     cost_square[...] = squares[CT:] + (sums[0] + sums[1])
 
 
-def end_kernel(place, steps, p0, p1, p2, p3, dual, rhs, rowf, out):
-    at = pl.ds(pl.multiple_of(place[2] * SHARE, SHARE), SHARE)
+def end_kernel(steps, p0, p1, p2, p3, dual, rhs, rowf, out):
     total = tree(jnp.add, p0[...], (p1[...], p2[...], p3[...]))
-    scale = rowf[at, :]
-    out[...] = scale * (dual[at, :] + steps[1:2] * (rhs[at, :] - scale * total))
+    scale = rowf[...]
+    out[...] = scale * (dual[...] + steps[1:2] * (rhs[...] - scale * total))
 
 
 def body(
@@ -401,7 +429,10 @@
     start_dual,
 ):
     scen = lax.axis_index("scen")
-    place = jnp.stack([scen % 2, scen // 8, lax.axis_index("col")])
+    core = scen % 2
+    place = jnp.stack(
+        [core, jnp.where(core == 0, scen // 8, (scen // 2) % 4), lax.axis_index("col")]
+    )
     ids = (tile_rows[0, 0], tile_cols[0, 0], place)
 
     def over(swap, x):
@@ -415,17 +446,17 @@
 
     rows = over(swap_y, row_part)
     (link,) = run(functools.partial(core_kernel, jnp.maximum), (), (colown, swap_core(colother)), (HALF,))
+    link, row_stat = run(merge_rows_kernel, (), (*over(swap_first, link), *rows), (HALF, RT))
     gradown, gradother, rhs_rows, dual_rows = run(
         first_backward_kernel, ids, rows, (OWN, HALF, RT, RT), (COLS, ROWS)
     )
     gradgot = swap_core(gradother)
-    (link,) = run(functools.partial(merge_kernel, jnp.maximum), (), over(swap_x, link), (HALF,))
-    (link,) = run(functools.partial(merge_kernel, jnp.maximum), (), over(swap_z, link), (HALF,))
+    (link,) = run(merge_after_kernel, (), (*over(swap_second, link), gradother), (HALF,))
 
     row_part, colown, colother, row_scale, col_scale = run(
         functools.partial(next_stats_kernel, jnp.maximum, True),
         ids,
-        (*rows, colown, link, swap_core(link)),
+        (row_stat, colown, link, swap_core(link)),
         (RT, OWN, HALF, RT, CW),
         (ROWS, COLS, ROWS, COLS),
     )
@@ -437,16 +468,16 @@
         (HALF + CHUNK,) * 4,
         (pltpu.VMEM((HALF, TILE), F32),),
     )
-    got = {k: swap_x(sent[k], k) for k in (2, 1, 3)}
-    (both,) = run(
-        functools.partial(merge_grad_kernel, 1), (), (sent[0], got[1], got[2], got[3]), (HALF + CHUNK,)
-    )
-    link, chunk = run(functools.partial(merge_grad_kernel, 2), (), over(swap_z, both), (HALF, CHUNK))
+    got = {k: swap_first(sent[k], k) for k in (2, 1, 3)}
+    both, row_stat = run(
+        merge_grad_rows_kernel, (), (sent[0], got[1], got[2], got[3], *rows), (HALF + CHUNK, RT)
+    )
+    link, chunk = run(merge_grad_kernel, (), over(swap_second, both), (HALF, CHUNK))
 
     row_part, colown, colother, row_scale, col_scale = run(
         functools.partial(next_stats_kernel, jnp.add, False),
         ids,
-        (*rows, colown, link, swap_core(link), row_scale, col_scale),
+        (row_stat, colown, link, swap_core(link), row_scale, col_scale),
         (RT, OWN, HALF, RT, CW),
         (ROWS, COLS, ROWS, COLS),
     )
@@ -457,8 +488,8 @@
         (*rows, row_scale, rhs_rows, dual_rows, colown, swap_core(colother), col_scale, cost_local[0, 0], chunk),
         (RT, RT, RT, HALF + EIGHT + CHUNK),
     )
-    both, half = run(merge_norm_kernel, (place,), over(swap_x, both), (HALF + EIGHT, HALF))
-    (mine,) = run(merge_all_kernel, (), (*over(swap_z, both), half), (LT + EIGHT,))
+    both, half = run(merge_norm_kernel, (place,), over(swap_first, both), (HALF + EIGHT, HALF))
+    (mine,) = run(merge_all_kernel, (), (*over(swap_second, both), half), (LT + EIGHT,))
     other = swap_core(mine)
     col_scale, cost, upper, primal, rhs_square, cost_square = run(
         setup_kernel,
@@ -482,11 +513,12 @@
     grads, grad_at = (gradown, mine, other), HALF + EIGHT
     for index in range(ITERS):
         given = norms if index == 0 else (steps,)
-        outs = (RT, CW) if index < ITERS - 1 else (CT, LT) + (SHARE,) * 4
+        extra = (dual_scaled, rhs_scaled, row_scale) if index == ITERS - 1 else ()
+        outs = (RT, CW) if index < ITERS - 1 else (CT, LT) + (SHARE,) * 7
         result = run(
             functools.partial(forward_kernel, index, grad_at),
             ids,
-            (*given, *grads, primal, cost, upper, col_scale),
+            (*given, *grads, primal, cost, upper, col_scale, *extra),
             ((CT,) if index == 0 else ()) + outs,
             (ROWS, COLS),
         )
@@ -503,19 +535,19 @@
             (COLS, ROWS),
         )
         (link,) = run(functools.partial(core_kernel, jnp.add), (), (colown, swap_core(colother)), (HALF,))
-        (link,) = run(functools.partial(merge_kernel, jnp.add), (), over(swap_x, link), (HALF,))
-        (link,) = run(functools.partial(merge_kernel, jnp.add), (), over(swap_z, link), (HALF,))
+        (link,) = run(functools.partial(merge_kernel, jnp.add), (), over(swap_first, link), (HALF,))
+        (link,) = run(functools.partial(merge_kernel, jnp.add), (), over(swap_second, link), (HALF,))
         grads, grad_at = (colown, link, swap_core(link)), 0
 
-    local, link, *pieces = result
+    local, link, dual, rhs_own, scale, *pieces = result
     got = {k: swap_y(pieces[k], k) for k in (2, 1, 3)}
     vmem = pl.BlockSpec(memory_space=pltpu.VMEM)
     multipliers = pl.pallas_call(
         end_kernel,
         out_shape=jax.ShapeDtypeStruct((SHARE, TILE), F32),
-        in_specs=[pl.BlockSpec(memory_space=pltpu.SMEM)] + [vmem] * 8,
+        in_specs=[vmem] * 8,
         out_specs=vmem,
-    )(place, steps, pieces[0], got[1], got[2], got[3], dual_scaled, rhs_scaled, row_scale)
+    )(steps, pieces[0], got[1], got[2], got[3], dual, rhs_own, scale)
     return local[None, None], link[None], multipliers[None]
 
 

time: 225 us -> 206 us (0.916)
  waiting for transfers between devices: 97.6 us -> 81 us
    ppermute x30, waiting for transfers between devices: 55.6 us -> 38.8 us  [the longest x15 20.6 us: swap_second(): lax.ppermute(x, 'scen', [(i, i ^ k << (3 if i % 2 else 1)) for i in range...]
  transfers between devices with their start and end apart: 62 -> 62, of which waited for: 42 -> 43; matrix products, arithmetic and copies ran while one was open for 0% -> 0% of each run, Pallas kernels for 4% -> 5%
where the time goes in v4:
time: 206 us
  waiting for transfers between devices  81 us (39%)
  starting transfers between devices  76.4 us (37%)
  Pallas kernels  44.3 us (22%)
  local copies, waits for them, and re-layouts  3.06 us (1%)
    pallas_call x24, Pallas kernels, call(): pl.pallas_call(kernel, out_shape=tuple((jax.ShapeDtypeStruct((n, TILE), F...  35.9 us
    ppermute x21, waiting for transfers between devices, swap_y(): return lax.ppermute(x, 'col', [(i, i ^ k) for i in range(4)])  32.8 us
    ppermute x21, starting transfers between devices, swap_y(): return lax.ppermute(x, 'col', [(i, i ^ k) for i in range(4)])  30.7 us
    ppermute x15, starting transfers between devices, swap_first(): lax.ppermute(x, 'scen', [(i, i ^ k << (1 if i % 2 else 3)) for i in range...  22.4 us
    ppermute x15, starting transfers between devices, swap_second(): lax.ppermute(x, 'scen', [(i, i ^ k << (3 if i % 2 else 1)) for i in range...  21.8 us
    ppermute x15, waiting for transfers between devices, swap_second(): lax.ppermute(x, 'scen', [(i, i ^ k << (3 if i % 2 else 1)) for i in range...  20.6 us
    ppermute x15, waiting for transfers between devices, swap_first(): lax.ppermute(x, 'scen', [(i, i ^ k << (1 if i % 2 else 3)) for i in range...  18.3 us
    ppermute x11, waiting for transfers between devices, swap_core(): return lax.ppermute(x, 'scen', [(i, i ^ 1) for i in range(32)])  9.37 us
  transfers between devices with their start and end apart: 62, of which 43 were waited for; matrix products, arithmetic and copies ran while one was open for 0% of the time, Pallas kernels for 5%

profile of v4, /device:TPU:0, one launch (start us, length us, event | category | flops | bytes accessed | tf_op | source)
XLA Modules:
  0.0 205.8 jit_solution(10448199099903608251)
XLA Ops:
  0.8 6.9 %shard_map.130 = (f32[192,256]{1,0:T(8,128)S(1)}, f32[136,256]{1,0:T(8,128)S(1)}, f32[128,256]{1,0:T(8,128)S(1)}, f32[64,256,256]{2,1,0:T(8,128)S(1)}) custom-call(s32[3]{0:T(128)S(1)} %pad_add_fusion.place, s32[64]{0:T(128)} %bitcast.20, s32[64]{0:T(128)} %bitcast.29, f32[64,256,256]{2,1,0:T(8,128)} %bitcast.42, f32[32,256]{1,0:T(8,128)} %bitcast.43, ...), custom_call_target="tpu_custom_call" | custom-call | tf_op jit(solution)/shard_map/pallas_call | solution.py:179
  7.7 3.2 %collective-permute-start.6 = (f32[192,256]{1,0:T(8,128)S(1)}, f32[192,256]{1,0:T(8,128)S(1)}, u32[]{:S(2)}, u32[]{:S(2)}) collective-permute-start(f32[192,256]{1,0:T(8,128)S(1)} %get-tuple-element.66.y0.r0), channel_id=1, source_target_pairs={{0,3},{1,2},{2,1},{3,0},{4,7},{5,6},{6,5},{7,4},{8,11},{9,10},{10,... | collective-permute-start | bytes 589832 | tf_op jit(solution)/shard_map/ppermute | solution.py:42
  12.2 2.8 %collective-permute-start.3 = (f32[128,256]{1,0:T(8,128)S(1)}, f32[128,256]{1,0:T(8,128)S(1)}, u32[]{:S(2)}, u32[]{:S(2)}) collective-permute-start(f32[128,256]{1,0:T(8,128)S(1)} %shard_map.131.own), channel_id=1, source_target_pairs={{0,96},{4,28},{8,104},{12,20},{16,112},{20,12},{24,120},{28,4},{32... | collective-permute-start | bytes 393224 | tf_op jit(solution)/shard_map/ppermute | solution.py:34
  15.9 4.0 %collective-permute-done.6.y3.r3 = f32[192,256]{1,0:T(8,128)S(1)} collective-permute-done((f32[192,256]{1,0:T(8,128)S(1)}, f32[192,256]{1,0:T(8,128)S(1)}, u32[]{:S(2)}, u32[]{:S(2)}) %collective-permute-start.6) | collective-permute-done | bytes 196640 | tf_op jit(solution)/shard_map/ppermute | solution.py:42
  21.6 3.3 %collective-permute-done.1.r1 = f32[128,256]{1,0:T(8,128)S(1)} collective-permute-done((f32[128,256]{1,0:T(8,128)S(1)}, f32[128,256]{1,0:T(8,128)S(1)}, u32[]{:S(2)}, u32[]{:S(2)}) %collective-permute-start.1) | collective-permute-done | bytes 131104 | tf_op jit(solution)/shard_map/ppermute | solution.py:34
  24.9 4.1 %collective-permute-start.9 = (f32[128,256]{1,0:T(8,128)S(1)}, f32[128,256]{1,0:T(8,128)S(1)}, u32[]{:S(2)}, u32[]{:S(2)}) collective-permute-start(f32[128,256]{1,0:T(8,128)S(1)} %get-tuple-element.68.own), channel_id=1, source_target_pairs={{0,24},{4,100},{8,16},{12,108},{16,8},{20,116},{24,0},{28,124},{32... | collective-permute-start | bytes 393224 | tf_op jit(solution)/shard_map/ppermute | solution.py:38
  29.9 3.4 %shard_map.133 = (f32[136,256]{1,0:T(8,128)S(1)}, f32[128,256]{1,0:T(8,128)S(1)}, f32[128,256]{1,0:T(8,128)S(1)}, f32[128,256]{1,0:T(8,128)S(1)}) custom-call(s32[64]{0:T(128)S(1)} %bitcast.21, s32[64]{0:T(128)S(1)} %bitcast.30, s32[3]{0:T(128)S(1)} %pad_add_fusion.place, f32[64,256,256]{2,1,0:T(8,128)S(1)} %get-tuple-element.63.tiles_ref, ...), custom_call_target="tpu_custom_call" | custom-call | tf_op jit(solution)/shard_map/pallas_call | solution.py:105
  36.9 5.8 %shard_map.135 = (f32[128,256]{1,0:T(8,128)S(1)}, f32[136,256]{1,0:T(8,128)S(1)}, f32[128,256]{1,0:T(8,128)S(1)}, f32[128,256]{1,0:T(8,128)S(1)}, f32[264,256]{1,0:T(8,128)S(1)}) custom-call(s32[64]{0:T(128)S(1)} %bitcast.22, s32[64]{0:T(128)S(1)} %bitcast.31, s32[3]{0:T(128)S(1)} %pad_add_fusion.place, f32[64,256,256]{2,1,0:T(8,128)S(1)} %get-tuple-element.63.tiles_ref, ...), custom_call_target="tpu_custom_call" | custom-call | tf_op jit(solution)/shard_map/pallas_call | solution.py:105
  42.9 3.1 %collective-permute-start.18 = (f32[128,256]{1,0:T(8,128)S(1)}, f32[128,256]{1,0:T(8,128)S(1)}, u32[]{:S(2)}, u32[]{:S(2)}) collective-permute-start(f32[128,256]{1,0:T(8,128)S(1)} %get-tuple-element.77.y0), channel_id=1, source_target_pairs={{0,3},{1,2},{2,1},{3,0},{4,7},{5,6},{6,5},{7,4},{8,11},{9,10},{10,... | collective-permute-start | bytes 393224 | tf_op jit(solution)/shard_map/ppermute | solution.py:42
  48.2 2.7 %collective-permute-start.14 = (f32[160,256]{1,0:T(8,128)S(1)}, f32[160,256]{1,0:T(8,128)S(1)}, u32[]{:S(2)}, u32[]{:S(2)}) collective-permute-start(f32[160,256]{1,0:T(8,128)S(1)} %get-tuple-element.75), channel_id=1, source_target_pairs={{0,64},{4,20},{8,72},{12,28},{16,80},{20,4},{24,88},{28,12},{32,96... | collective-permute-start | bytes 491528 | tf_op jit(solution)/shard_map/ppermute | solution.py:34
  53.5 5.5 %collective-permute-done.17.y2 = f32[128,256]{1,0:T(8,128)S(1)} collective-permute-done((f32[128,256]{1,0:T(8,128)S(1)}, f32[128,256]{1,0:T(8,128)S(1)}, u32[]{:S(2)}, u32[]{:S(2)}) %collective-permute-start.17) | collective-permute-done | bytes 131104 | tf_op jit(solution)/shard_map/ppermute | solution.py:42
  69.8 5.9 %shard_map.139 = (f32[128,256]{1,0:T(8,128)S(1)}, f32[136,256]{1,0:T(8,128)S(1)}, f32[128,256]{1,0:T(8,128)S(1)}, f32[128,256]{1,0:T(8,128)S(1)}, f32[264,256]{1,0:T(8,128)S(1)}) custom-call(s32[64]{0:T(128)S(1)} %bitcast.23, s32[64]{0:T(128)S(1)} %bitcast.32, s32[3]{0:T(128)S(1)} %pad_add_fusion.place, f32[64,256,256]{2,1,0:T(8,128)S(1)} %get-tuple-element.63.tiles_ref, ...), custom_call_target="tpu_custom_call" | custom-call | tf_op jit(solution)/shard_map/pallas_call | solution.py:105
  80.0 5.6 %collective-permute-done.25.r3 = f32[128,256]{1,0:T(8,128)S(1)} collective-permute-done((f32[128,256]{1,0:T(8,128)S(1)}, f32[128,256]{1,0:T(8,128)S(1)}, u32[]{:S(2)}, u32[]{:S(2)}) %collective-permute-start.25) | collective-permute-done | bytes 131104 | tf_op jit(solution)/shard_map/ppermute | solution.py:42
  86.5 2.8 %collective-permute-start.29 = (f32[176,256]{1,0:T(8,128)S(1)}, f32[176,256]{1,0:T(8,128)S(1)}, u32[]{:S(2)}, u32[]{:S(2)}) collective-permute-start(f32[176,256]{1,0:T(8,128)S(1)} %get-tuple-element.91.own), channel_id=1, source_target_pairs={{0,96},{4,28},{8,104},{12,20},{16,112},{20,12},{24,120},{28,4},{32... | collective-permute-start | bytes 540680 | tf_op jit(solution)/shard_map/ppermute | solution.py:34
  90.7 3.6 %collective-permute-done.29.r3 = f32[176,256]{1,0:T(8,128)S(1)} collective-permute-done((f32[176,256]{1,0:T(8,128)S(1)}, f32[176,256]{1,0:T(8,128)S(1)}, u32[]{:S(2)}, u32[]{:S(2)}) %collective-permute-start.29) | collective-permute-done | bytes 180256 | tf_op jit(solution)/shard_map/ppermute | solution.py:34
  115.5 3.7 %shard_map.144 = (f32[8,256]{1,0:T(8,128)S(1)}, f32[128,256]{1,0:T(8,128)S(1)}, f32[264,256]{1,0:T(8,128)S(1)}) custom-call(s32[64]{0:T(128)S(1)} %bitcast.24, s32[64]{0:T(128)S(1)} %bitcast.33, s32[3]{0:T(128)S(1)} %pad_add_fusion.place, f32[64,256,256]{2,1,0:T(8,128)S(1)} %get-tuple-element.63.tiles_ref, f32[8,256]{1,0:T(8,128)S(1)} %get-tuple-element.94.rest_0_, ...), custom_call_target="tpu_custom_call" | custom-call | tf_op jit(solution)/shard_map/pallas_call | solution.py:105
  123.3 2.9 %collective-permute-done.39.r3 = f32[128,256]{1,0:T(8,128)S(1)} collective-permute-done((f32[128,256]{1,0:T(8,128)S(1)}, f32[128,256]{1,0:T(8,128)S(1)}, u32[]{:S(2)}, u32[]{:S(2)}) %collective-permute-start.39) | collective-permute-done | bytes 131104 | tf_op jit(solution)/shard_map/ppermute | solution.py:42
  127.9 3.5 %shard_map.145 = (f32[136,256]{1,0:T(8,128)S(1)}, f32[128,256]{1,0:T(8,128)S(1)}, f32[128,256]{1,0:T(8,128)S(1)}) custom-call(s32[64]{0:T(128)S(1)} %bitcast.25, s32[64]{0:T(128)S(1)} %bitcast.34, s32[3]{0:T(128)S(1)} %pad_add_fusion.place, f32[64,256,256]{2,1,0:T(8,128)S(1)} %get-tuple-element.63.tiles_ref, f32[8,256]{1,0:T(8,128)S(1)} %get-tuple-element.100.steps.rest_0_, ...), custom_call_target="tpu_custom_call" | custom-call | tf_op jit(solution)/shard_map/pallas_call | solution.py:105
  132.9 2.6 %collective-permute-start.43 = (f32[128,256]{1,0:T(8,128)S(1)}, f32[128,256]{1,0:T(8,128)S(1)}, u32[]{:S(2)}, u32[]{:S(2)}) collective-permute-start(f32[128,256]{1,0:T(8,128)S(1)} %shard_map.146.own), channel_id=1, source_target_pairs={{0,96},{4,28},{8,104},{12,20},{16,112},{20,12},{24,120},{28,4},{32... | collective-permute-start | bytes 393224 | tf_op jit(solution)/shard_map/ppermute | solution.py:34
  139.3 2.5 %collective-permute-done.42.r2 = f32[128,256]{1,0:T(8,128)S(1)} collective-permute-done((f32[128,256]{1,0:T(8,128)S(1)}, f32[128,256]{1,0:T(8,128)S(1)}, u32[]{:S(2)}, u32[]{:S(2)}) %collective-permute-start.42) | collective-permute-done | bytes 131104 | tf_op jit(solution)/shard_map/ppermute | solution.py:34
  151.9 3.5 %shard_map.149 = (f32[128,256]{1,0:T(8,128)S(1)}, f32[264,256]{1,0:T(8,128)S(1)}) custom-call(s32[64]{0:T(128)S(1)} %bitcast.26, s32[64]{0:T(128)S(1)} %bitcast.35, s32[3]{0:T(128)S(1)} %pad_add_fusion.place, f32[64,256,256]{2,1,0:T(8,128)S(1)} %get-tuple-element.63.tiles_ref, f32[8,256]{1,0:T(8,128)S(1)} %get-tuple-element.100.steps.rest_0_, ...), custom_call_target="tpu_custom_call" | custom-call | tf_op jit(solution)/shard_map/pallas_call | solution.py:105
  159.6 5.5 %collective-permute-done.50.r3 = f32[128,256]{1,0:T(8,128)S(1)} collective-permute-done((f32[128,256]{1,0:T(8,128)S(1)}, f32[128,256]{1,0:T(8,128)S(1)}, u32[]{:S(2)}, u32[]{:S(2)}) %collective-permute-start.50) | collective-permute-done | bytes 131104 | tf_op jit(solution)/shard_map/ppermute | solution.py:42
  165.7 3.5 %shard_map.150 = (f32[136,256]{1,0:T(8,128)S(1)}, f32[128,256]{1,0:T(8,128)S(1)}, f32[128,256]{1,0:T(8,128)S(1)}) custom-call(s32[64]{0:T(128)S(1)} %bitcast.27, s32[64]{0:T(128)S(1)} %bitcast.36, s32[3]{0:T(128)S(1)} %pad_add_fusion.place, f32[64,256,256]{2,1,0:T(8,128)S(1)} %get-tuple-element.63.tiles_ref, f32[8,256]{1,0:T(8,128)S(1)} %get-tuple-element.100.steps.rest_0_, ...), custom_call_target="tpu_custom_call" | custom-call | tf_op jit(solution)/shard_map/pallas_call | solution.py:105
  189.2 4.2 %shard_map.154 = (f32[8,256]{1,0:T(8,128)}, f32[256,256]{1,0:T(8,128)}, f32[32,256]{1,0:T(8,128)S(1)}, f32[32,256]{1,0:T(8,128)S(1)}, f32[32,256]{1,0:T(8,128)S(...) custom-call(s32[64]{0:T(128)S(1)} %bitcast.28, ...), custom_call_target="tpu_custom_call" | custom-call | tf_op jit(solution)/shard_map/pallas_call | solution.py:105
  (159 shorter events, 110.3 us)
Async XLA Ops:
  7.7 12.1 %collective-permute-start.6 = (f32[192,256]{1,0:T(8,128)S(1)}, f32[192,256]{1,0:T(8,128)S(1)}, u32[]{:S(2)}, u32[]{:S(2)}) collective-permute-start(f32[192,256]{1,0:T(8,128)S(1)} %get-tuple-element.66.y0.r0), channel_id=1, source_target_pairs={{0,3},{1,2},{2,1},{3,0},{4,7},{5,6},{6,5},{7,4},{8,11},{9,10},{10,... | collective-permute-start | bytes 589832 | tf_op jit(solution)/shard_map/ppermute | solution.py:42
  10.9 10.5 %collective-permute-start.5 = (f32[192,256]{1,0:T(8,128)S(1)}, f32[192,256]{1,0:T(8,128)S(1)}, u32[]{:S(2)}, u32[]{:S(2)}) collective-permute-start(f32[192,256]{1,0:T(8,128)S(1)} %get-tuple-element.66.y0.r0), channel_id=1, source_target_pairs={{0,2},{1,3},{2,0},{3,1},{4,6},{5,7},{6,4},{7,5},{8,10},{9,11},{10,... | collective-permute-start | bytes 589832 | tf_op jit(solution)/shard_map/ppermute | solution.py:42
  11.5 9.9 %collective-permute-start.4 = (f32[192,256]{1,0:T(8,128)S(1)}, f32[192,256]{1,0:T(8,128)S(1)}, u32[]{:S(2)}, u32[]{:S(2)}) collective-permute-start(f32[192,256]{1,0:T(8,128)S(1)} %get-tuple-element.66.y0.r0), channel_id=1, source_target_pairs={{0,1},{1,0},{2,3},{3,2},{4,5},{5,4},{6,7},{7,6},{8,9},{9,8},{10,11... | collective-permute-start | bytes 589832 | tf_op jit(solution)/shard_map/ppermute | solution.py:42
  12.2 9.2 %collective-permute-start.3 = (f32[128,256]{1,0:T(8,128)S(1)}, f32[128,256]{1,0:T(8,128)S(1)}, u32[]{:S(2)}, u32[]{:S(2)}) collective-permute-start(f32[128,256]{1,0:T(8,128)S(1)} %shard_map.131.own), channel_id=1, source_target_pairs={{0,96},{4,28},{8,104},{12,20},{16,112},{20,12},{24,120},{28,4},{32... | collective-permute-start | bytes 393224 | tf_op jit(solution)/shard_map/ppermute | solution.py:34
  24.9 8.5 %collective-permute-start.9 = (f32[128,256]{1,0:T(8,128)S(1)}, f32[128,256]{1,0:T(8,128)S(1)}, u32[]{:S(2)}, u32[]{:S(2)}) collective-permute-start(f32[128,256]{1,0:T(8,128)S(1)} %get-tuple-element.68.own), channel_id=1, source_target_pairs={{0,24},{4,100},{8,16},{12,108},{16,8},{20,116},{24,0},{28,124},{32... | collective-permute-start | bytes 393224 | tf_op jit(solution)/shard_map/ppermute | solution.py:38
  35.6 10.5 %collective-permute-start.12 = (f32[128,256]{1,0:T(8,128)S(1)}, f32[128,256]{1,0:T(8,128)S(1)}, u32[]{:S(2)}, u32[]{:S(2)}) collective-permute-start(f32[128,256]{1,0:T(8,128)S(1)} %get-tuple-element.69.after), channel_id=1, source_target_pairs={{0,4},{4,0},{8,12},{12,8},{16,20},{20,16},{24,28},{28,24},{32,36},... | collective-permute-start | bytes 393224 | tf_op jit(solution)/shard_map/ppermute | solution.py:30
  42.9 8.7 %collective-permute-start.18 = (f32[128,256]{1,0:T(8,128)S(1)}, f32[128,256]{1,0:T(8,128)S(1)}, u32[]{:S(2)}, u32[]{:S(2)}) collective-permute-start(f32[128,256]{1,0:T(8,128)S(1)} %get-tuple-element.77.y0), channel_id=1, source_target_pairs={{0,3},{1,2},{2,1},{3,0},{4,7},{5,6},{6,5},{7,4},{8,11},{9,10},{10,... | collective-permute-start | bytes 393224 | tf_op jit(solution)/shard_map/ppermute | solution.py:42
  46.7 12.3 %collective-permute-start.13 = (f32[160,256]{1,0:T(8,128)S(1)}, f32[160,256]{1,0:T(8,128)S(1)}, u32[]{:S(2)}, u32[]{:S(2)}) collective-permute-start(f32[160,256]{1,0:T(8,128)S(1)} %get-tuple-element.74), channel_id=1, source_target_pairs={{0,32},{4,12},{8,40},{12,4},{16,48},{20,28},{24,56},{28,20},{32,0}... | collective-permute-start | bytes 491528 | tf_op jit(solution)/shard_map/ppermute | solution.py:34
  48.2 10.8 %collective-permute-start.14 = (f32[160,256]{1,0:T(8,128)S(1)}, f32[160,256]{1,0:T(8,128)S(1)}, u32[]{:S(2)}, u32[]{:S(2)}) collective-permute-start(f32[160,256]{1,0:T(8,128)S(1)} %get-tuple-element.75), channel_id=1, source_target_pairs={{0,64},{4,20},{8,72},{12,28},{16,80},{20,4},{24,88},{28,12},{32,96... | collective-permute-start | bytes 491528 | tf_op jit(solution)/shard_map/ppermute | solution.py:34
  50.9 8.0 %collective-permute-start.15 = (f32[160,256]{1,0:T(8,128)S(1)}, f32[160,256]{1,0:T(8,128)S(1)}, u32[]{:S(2)}, u32[]{:S(2)}) collective-permute-start(f32[160,256]{1,0:T(8,128)S(1)} %get-tuple-element.76), channel_id=1, source_target_pairs={{0,96},{4,28},{8,104},{12,20},{16,112},{20,12},{24,120},{28,4},{32... | collective-permute-start | bytes 491528 | tf_op jit(solution)/shard_map/ppermute | solution.py:34
  51.4 7.5 %collective-permute-start.17 = (f32[128,256]{1,0:T(8,128)S(1)}, f32[128,256]{1,0:T(8,128)S(1)}, u32[]{:S(2)}, u32[]{:S(2)}) collective-permute-start(f32[128,256]{1,0:T(8,128)S(1)} %get-tuple-element.77.y0), channel_id=1, source_target_pairs={{0,2},{1,3},{2,0},{3,1},{4,6},{5,7},{6,4},{7,5},{8,10},{9,11},{10,... | collective-permute-start | bytes 393224 | tf_op jit(solution)/shard_map/ppermute | solution.py:42
  51.6 7.4 %collective-permute-start.16 = (f32[128,256]{1,0:T(8,128)S(1)}, f32[128,256]{1,0:T(8,128)S(1)}, u32[]{:S(2)}, u32[]{:S(2)}) collective-permute-start(f32[128,256]{1,0:T(8,128)S(1)} %get-tuple-element.77.y0), channel_id=1, source_target_pairs={{0,1},{1,0},{2,3},{3,2},{4,5},{5,4},{6,7},{7,6},{8,9},{9,8},{10,11... | collective-permute-start | bytes 393224 | tf_op jit(solution)/shard_map/ppermute | solution.py:42
  61.1 6.8 %collective-permute-start.20 = (f32[160,256]{1,0:T(8,128)S(1)}, f32[160,256]{1,0:T(8,128)S(1)}, u32[]{:S(2)}, u32[]{:S(2)}) collective-permute-start(f32[160,256]{1,0:T(8,128)S(1)} %get-tuple-element.79.own), channel_id=1, source_target_pairs={{0,16},{4,68},{8,24},{12,76},{16,0},{20,84},{24,8},{28,92},{32,48}... | collective-permute-start | bytes 491528 | tf_op jit(solution)/shard_map/ppermute | solution.py:38
  61.1 7.2 %collective-permute-start.19 = (f32[160,256]{1,0:T(8,128)S(1)}, f32[160,256]{1,0:T(8,128)S(1)}, u32[]{:S(2)}, u32[]{:S(2)}) collective-permute-start(f32[160,256]{1,0:T(8,128)S(1)} %get-tuple-element.79.own), channel_id=1, source_target_pairs={{0,8},{4,36},{8,0},{12,44},{16,24},{20,52},{24,16},{28,60},{32,40}... | collective-permute-start | bytes 491528 | tf_op jit(solution)/shard_map/ppermute | solution.py:38
  75.9 9.7 %collective-permute-start.25 = (f32[128,256]{1,0:T(8,128)S(1)}, f32[128,256]{1,0:T(8,128)S(1)}, u32[]{:S(2)}, u32[]{:S(2)}) collective-permute-start(f32[128,256]{1,0:T(8,128)S(1)} %get-tuple-element.83.r0), channel_id=1, source_target_pairs={{0,3},{1,2},{2,1},{3,0},{4,7},{5,6},{6,5},{7,4},{8,11},{9,10},{10,... | collective-permute-start | bytes 393224 | tf_op jit(solution)/shard_map/ppermute | solution.py:42
  77.9 7.9 %collective-permute-start.24 = (f32[128,256]{1,0:T(8,128)S(1)}, f32[128,256]{1,0:T(8,128)S(1)}, u32[]{:S(2)}, u32[]{:S(2)}) collective-permute-start(f32[128,256]{1,0:T(8,128)S(1)} %get-tuple-element.83.r0), channel_id=1, source_target_pairs={{0,2},{1,3},{2,0},{3,1},{4,6},{5,7},{6,4},{7,5},{8,10},{9,11},{10,... | collective-permute-start | bytes 393224 | tf_op jit(solution)/shard_map/ppermute | solution.py:42
  78.3 8.0 %collective-permute-start.23 = (f32[128,256]{1,0:T(8,128)S(1)}, f32[128,256]{1,0:T(8,128)S(1)}, u32[]{:S(2)}, u32[]{:S(2)}) collective-permute-start(f32[128,256]{1,0:T(8,128)S(1)} %get-tuple-element.83.r0), channel_id=1, source_target_pairs={{0,1},{1,0},{2,3},{3,2},{4,5},{5,4},{6,7},{7,6},{8,9},{9,8},{10,11... | collective-permute-start | bytes 393224 | tf_op jit(solution)/shard_map/ppermute | solution.py:42
  86.5 7.8 %collective-permute-start.29 = (f32[176,256]{1,0:T(8,128)S(1)}, f32[176,256]{1,0:T(8,128)S(1)}, u32[]{:S(2)}, u32[]{:S(2)}) collective-permute-start(f32[176,256]{1,0:T(8,128)S(1)} %get-tuple-element.91.own), channel_id=1, source_target_pairs={{0,96},{4,28},{8,104},{12,20},{16,112},{20,12},{24,120},{28,4},{32... | collective-permute-start | bytes 540680 | tf_op jit(solution)/shard_map/ppermute | solution.py:34
  89.4 7.0 %collective-permute-start.28 = (f32[176,256]{1,0:T(8,128)S(1)}, f32[176,256]{1,0:T(8,128)S(1)}, u32[]{:S(2)}, u32[]{:S(2)}) collective-permute-start(f32[176,256]{1,0:T(8,128)S(1)} %get-tuple-element.91.own), channel_id=1, source_target_pairs={{0,64},{4,20},{8,72},{12,28},{16,80},{20,4},{24,88},{28,12},{32,96... | collective-permute-start | bytes 540680 | tf_op jit(solution)/shard_map/ppermute | solution.py:34
  119.1 7.0 %collective-permute-start.39 = (f32[128,256]{1,0:T(8,128)S(1)}, f32[128,256]{1,0:T(8,128)S(1)}, u32[]{:S(2)}, u32[]{:S(2)}) collective-permute-start(f32[128,256]{1,0:T(8,128)S(1)} %get-tuple-element.101.r0), channel_id=1, source_target_pairs={{0,3},{1,2},{2,1},{3,0},{4,7},{5,6},{6,5},{7,4},{8,11},{9,10},{10,... | collective-permute-start | bytes 393224 | tf_op jit(solution)/shard_map/ppermute | solution.py:42
  120.5 6.8 %collective-permute-start.38 = (f32[128,256]{1,0:T(8,128)S(1)}, f32[128,256]{1,0:T(8,128)S(1)}, u32[]{:S(2)}, u32[]{:S(2)}) collective-permute-start(f32[128,256]{1,0:T(8,128)S(1)} %get-tuple-element.101.r0), channel_id=1, source_target_pairs={{0,2},{1,3},{2,0},{3,1},{4,6},{5,7},{6,4},{7,5},{8,10},{9,11},{10,... | collective-permute-start | bytes 393224 | tf_op jit(solution)/shard_map/ppermute | solution.py:42
  155.5 9.7 %collective-permute-start.50 = (f32[128,256]{1,0:T(8,128)S(1)}, f32[128,256]{1,0:T(8,128)S(1)}, u32[]{:S(2)}, u32[]{:S(2)}) collective-permute-start(f32[128,256]{1,0:T(8,128)S(1)} %get-tuple-element.108.r0), channel_id=1, source_target_pairs={{0,3},{1,2},{2,1},{3,0},{4,7},{5,6},{6,5},{7,4},{8,11},{9,10},{10,... | collective-permute-start | bytes 393224 | tf_op jit(solution)/shard_map/ppermute | solution.py:42
  156.9 8.2 %collective-permute-start.49 = (f32[128,256]{1,0:T(8,128)S(1)}, f32[128,256]{1,0:T(8,128)S(1)}, u32[]{:S(2)}, u32[]{:S(2)}) collective-permute-start(f32[128,256]{1,0:T(8,128)S(1)} %get-tuple-element.108.r0), channel_id=1, source_target_pairs={{0,2},{1,3},{2,0},{3,1},{4,6},{5,7},{6,4},{7,5},{8,10},{9,11},{10,... | collective-permute-start | bytes 393224 | tf_op jit(solution)/shard_map/ppermute | solution.py:42
  158.3 7.5 %collective-permute-start.48 = (f32[128,256]{1,0:T(8,128)S(1)}, f32[128,256]{1,0:T(8,128)S(1)}, u32[]{:S(2)}, u32[]{:S(2)}) collective-permute-start(f32[128,256]{1,0:T(8,128)S(1)} %get-tuple-element.108.r0), channel_id=1, source_target_pairs={{0,1},{1,0},{2,3},{3,2},{4,5},{5,4},{6,7},{7,6},{8,9},{9,8},{10,11... | collective-permute-start | bytes 393224 | tf_op jit(solution)/shard_map/ppermute | solution.py:42
  (54 other events, 432.3 us)

commit v5 on v4

--- a/solution.py
+++ b/solution.py
@@ -192,44 +192,64 @@
     )(ids[2], *(pltpu.with_memory_space_constraint(x, pltpu.HBM) for x in (*ids[:2], source, rhs, dual)))
 
 
-def next_stats_kernel(
-    op, first, rows_ref, cols_ref, place, tiles_ref, rowstat, loc, mine, other, *rest
-):
-    if first:
-        rowout, colown, colother, rownew, colnew, racc, cacc, rowf, colf = rest
-    else:
-        rowold, colold, rowout, colown, colother, rownew, colnew, racc, cacc, rowf, colf = rest
-    row = rowstat[...]
-    if first:
-        new = 1.0 / jnp.sqrt(row + EPS)
-    else:
-        old = rowold[...]
-        new = old / jnp.sqrt(old * row + EPS)
+def second_stats_kernel(
+    rows_ref, cols_ref, place, tiles_ref, r0, r1, r2, r3, loc, mine, other, rowout, colown, colother, rownew,
+    colnew, racc, cacc, rowf, colf,
+):
+    row = tree(jnp.maximum, r0[0:RT], (r1[0:RT], r2[0:RT], r3[0:RT]))
+    new = 1.0 / jnp.sqrt(row + EPS)
     rownew[...] = new
     split_to(rowf, new)
     for lo, hi, src in ((0, CT, loc), (CT, OWN, mine), (OWN, CW, other)):
-        stat = src[0 : hi - lo]
-        if first:
-            new = 1.0 / jnp.sqrt(stat + EPS)
-        else:
-            old = colold[lo:hi]
-            new = old / jnp.sqrt(old * stat + EPS)
+        new = 1.0 / jnp.sqrt(src[0 : hi - lo] + EPS)
         colnew[lo:hi] = new
         split_to(colf, new, lo)
     racc[...] = jnp.zeros_like(racc)
     cacc[...] = jnp.zeros_like(cacc)
 
     def visit(t, col, row):
-        row_pass(tiles_ref, t, col, row, colf, racc, op, True)
-        col_pass(tiles_ref, t, col, row, rowf, cacc, op, True)
+        row_pass(tiles_ref, t, col, row, colf, racc, jnp.maximum, True)
+        col_pass(tiles_ref, t, col, row, rowf, cacc, jnp.maximum, True)
 
     each_tile(rows_ref, cols_ref, place, visit)
     join_from(racc, rowout, 0, RT)
     put_columns(cacc, colown, colother)
 
 
+def third_rows_kernel(
+    rows_ref, cols_ref, place, tiles_ref, r0, r1, r2, r3, loc, mine, other, rowold, colold, rowout, rownew,
+    colnew, racc, colf,
+):
+    row = tree(jnp.maximum, r0[...], (r1[...], r2[...], r3[...]))
+    old = rowold[...]
+    rownew[...] = old / jnp.sqrt(old * row + EPS)
+    for lo, hi, src in ((0, CT, loc), (CT, OWN, mine), (OWN, CW, other)):
+        old = colold[lo:hi]
+        new = old / jnp.sqrt(old * src[0 : hi - lo] + EPS)
+        colnew[lo:hi] = new
+        split_to(colf, new, lo)
+    racc[...] = jnp.zeros_like(racc)
+
+    def visit(t, col, row):
+        row_pass(tiles_ref, t, col, row, colf, racc, jnp.add, True)
+
+    each_tile(rows_ref, cols_ref, place, visit)
+    join_from(racc, rowout, 0, RT)
+
+
+def third_columns_kernel(rows_ref, cols_ref, place, tiles_ref, row_scale, colown, colother, cacc, rowf):
+    split_to(rowf, row_scale[...])
+    cacc[...] = jnp.zeros_like(cacc)
+
+    def visit(t, col, row):
+        col_pass(tiles_ref, t, col, row, rowf, cacc, jnp.add, True)
+
+    each_tile(rows_ref, cols_ref, place, visit)
+    put_columns(cacc, colown, colother)
+
+
 def first_backward_kernel(
-    rows_ref, cols_ref, place, tiles_ref, r0, r1, r2, r3, colown, colother, rhsout, dualout, cacc, work
+    rows_ref, cols_ref, place, tiles_ref, r0, r1, r2, r3, after, colown, colother, rhsout, dualout, cacc, work
 ):
     for k, ref in enumerate((r0, r1, r2, r3)):
         at = pl.ds(pl.multiple_of((place[2] ^ k) * SHARE, SHARE), SHARE)
@@ -320,32 +340,17 @@
     out[...] = tree(op, own[...], (r1[...], r2[...], r3[...]))
 
 
-def merge_after_kernel(tiles_ref, own, r1, r2, r3, after, out):
-    out[...] = tree(jnp.maximum, own[...], (r1[...], r2[...], r3[...]))
-
-
-def merge_rows_kernel(tiles_ref, own, r1, r2, r3, y0, y1, y2, y3, out, rows):
-    out[...] = tree(jnp.maximum, own[...], (r1[...], r2[...], r3[...]))
-    rows[...] = tree(jnp.maximum, y0[0:RT], (y1[0:RT], y2[0:RT], y3[0:RT]))
-
-
-def core_grad_kernel(place, tiles_ref, colown, got, gradown, gradgot, m0, m1, m2, m3, half):
-    link = jnp.maximum(colown[CT:OWN], got[...])
+def merge_grad_kernel(place, tiles_ref, own, r1, r2, r3, gradown, gradgot, m0, m1, m2, m3, half):
+    link = tree(jnp.maximum, own[...], (r1[...], r2[...], r3[...]))
     half[...] = gradown[CT:OWN] + gradgot[...]
     for k, out in enumerate((m0, m1, m2, m3)):
         out[0:HALF] = link
         out[HALF:] = half[pl.ds(pl.multiple_of((place[1] ^ k) * CHUNK, CHUNK), CHUNK), :]
 
 
-def merge_grad_rows_kernel(tiles_ref, own, r1, r2, r3, y0, y1, y2, y3, both, rows):
-    both[0:HALF] = tree(jnp.maximum, own[0:HALF], (r1[0:HALF], r2[0:HALF], r3[0:HALF]))
-    both[HALF:] = tree(jnp.add, own[HALF:], (r1[HALF:], r2[HALF:], r3[HALF:]))
-    rows[...] = tree(jnp.maximum, y0[...], (y1[...], y2[...], y3[...]))
-
-
-def merge_grad_kernel(tiles_ref, own, r1, r2, r3, link, grad):
+def merge_chunk_kernel(tiles_ref, own, r1, r2, r3, link, chunk):
     link[...] = tree(jnp.maximum, own[0:HALF], (r1[0:HALF], r2[0:HALF], r3[0:HALF]))
-    grad[...] = tree(jnp.add, own[HALF:], (r1[HALF:], r2[HALF:], r3[HALF:]))
+    chunk[...] = tree(jnp.add, own[HALF:], (r1[HALF:], r2[HALF:], r3[HALF:]))
 
 
 def rows_kernel(
@@ -367,16 +372,12 @@
     out[OWN + CT :] = chunk[...]
 
 
-def merge_norm_kernel(place, tiles_ref, own, r1, r2, r3, both, half):
+def merge_all_kernel(place, tiles_ref, own, r1, r2, r3, out):
+    at = slice(0, HALF + EIGHT)
+    out[at] = tree(jnp.add, own[at], (r1[at], r2[at], r3[at]))
     for k, ref in enumerate((own, r1, r2, r3)):
-        half[pl.ds(pl.multiple_of((place[1] ^ k) * CHUNK, CHUNK), CHUNK), :] = ref[HALF + EIGHT :]
-    at = slice(0, HALF + EIGHT)
-    both[...] = tree(jnp.add, own[at], (r1[at], r2[at], r3[at]))
-
-
-def merge_all_kernel(tiles_ref, own, r1, r2, r3, half, out):
-    out[0 : HALF + EIGHT] = tree(jnp.add, own[...], (r1[...], r2[...], r3[...]))
-    out[HALF + EIGHT :] = half[...]
+        start = pl.multiple_of((place[1] ^ k) * CHUNK, CHUNK)
+        out[pl.ds(HALF + EIGHT + start, CHUNK), :] = ref[HALF + EIGHT :]
 
 
 def setup_kernel(
@@ -430,9 +431,8 @@
 ):
     scen = lax.axis_index("scen")
     core = scen % 2
-    place = jnp.stack(
-        [core, jnp.where(core == 0, scen // 8, (scen // 2) % 4), lax.axis_index("col")]
-    )
+    x_at, z_at = scen // 8, (scen // 2) % 4
+    place = jnp.stack([core, jnp.where(core == 0, z_at, x_at), lax.axis_index("col")])
     ids = (tile_rows[0, 0], tile_cols[0, 0], place)
 
     def over(swap, x):
@@ -446,50 +446,52 @@
 
     rows = over(swap_y, row_part)
     (link,) = run(functools.partial(core_kernel, jnp.maximum), (), (colown, swap_core(colother)), (HALF,))
-    link, row_stat = run(merge_rows_kernel, (), (*over(swap_first, link), *rows), (HALF, RT))
-    gradown, gradother, rhs_rows, dual_rows = run(
-        first_backward_kernel, ids, rows, (OWN, HALF, RT, RT), (COLS, ROWS)
-    )
-    gradgot = swap_core(gradother)
-    (link,) = run(merge_after_kernel, (), (*over(swap_second, link), gradother), (HALF,))
-
+    (link,) = run(functools.partial(merge_kernel, jnp.maximum), (), over(swap_first, link), (HALF,))
+    (link,) = run(functools.partial(merge_kernel, jnp.maximum), (), over(swap_second, link), (HALF,))
+
+    first_rows = rows
     row_part, colown, colother, row_scale, col_scale = run(
-        functools.partial(next_stats_kernel, jnp.maximum, True),
+        second_stats_kernel,
         ids,
-        (row_stat, colown, link, swap_core(link)),
+        (*rows, colown, link, swap_core(link)),
         (RT, OWN, HALF, RT, CW),
         (ROWS, COLS, ROWS, COLS),
     )
     rows = over(swap_y, row_part)
+    (link,) = run(functools.partial(core_kernel, jnp.maximum), (), (colown, swap_core(colother)), (HALF,))
+    got = over(swap_first, link)
+    gradown, gradother, rhs_rows, dual_rows = run(
+        first_backward_kernel, ids, (*first_rows, got[3]), (OWN, HALF, RT, RT), (COLS, ROWS)
+    )
     sent = run(
-        core_grad_kernel,
+        merge_grad_kernel,
         (place,),
-        (colown, swap_core(colother), gradown, gradgot),
+        (*got, gradown, swap_core(gradother)),
         (HALF + CHUNK,) * 4,
         (pltpu.VMEM((HALF, TILE), F32),),
     )
-    got = {k: swap_first(sent[k], k) for k in (2, 1, 3)}
-    both, row_stat = run(
-        merge_grad_rows_kernel, (), (sent[0], got[1], got[2], got[3], *rows), (HALF + CHUNK, RT)
-    )
-    link, chunk = run(merge_grad_kernel, (), over(swap_second, both), (HALF, CHUNK))
-
-    row_part, colown, colother, row_scale, col_scale = run(
-        functools.partial(next_stats_kernel, jnp.add, False),
+    got = {k: swap_second(sent[k], k) for k in (2, 1, 3)}
+    link, chunk = run(merge_chunk_kernel, (), (sent[0], got[1], got[2], got[3]), (HALF, CHUNK))
+
+    row_part, row_scale, col_scale = run(
+        third_rows_kernel,
         ids,
-        (row_stat, colown, link, swap_core(link), row_scale, col_scale),
-        (RT, OWN, HALF, RT, CW),
-        (ROWS, COLS, ROWS, COLS),
+        (*rows, colown, link, swap_core(link), row_scale, col_scale),
+        (RT, RT, CW),
+        (ROWS, COLS),
     )
     rows = over(swap_y, row_part)
+    colown, colother = run(third_columns_kernel, ids, (row_scale,), (OWN, HALF), (COLS, ROWS))
     row_scale, rhs_scaled, dual_scaled, both = run(
         rows_kernel,
         (),
         (*rows, row_scale, rhs_rows, dual_rows, colown, swap_core(colother), col_scale, cost_local[0, 0], chunk),
         (RT, RT, RT, HALF + EIGHT + CHUNK),
     )
-    both, half = run(merge_norm_kernel, (place,), over(swap_first, both), (HALF + EIGHT, HALF))
-    (mine,) = run(merge_all_kernel, (), (*over(swap_second, both), half), (LT + EIGHT,))
+    (both,) = run(
+        functools.partial(merge_kernel, jnp.add), (), over(swap_first, both), (HALF + EIGHT + CHUNK,)
+    )
+    (mine,) = run(merge_all_kernel, (place,), over(swap_second, both), (LT + EIGHT,))
     other = swap_core(mine)
     col_scale, cost, upper, primal, rhs_square, cost_square = run(
         setup_kernel,
@@ -547,6 +549,7 @@
         out_shape=jax.ShapeDtypeStruct((SHARE, TILE), F32),
         in_specs=[vmem] * 8,
         out_specs=vmem,
+        compiler_params=pltpu.CompilerParams(vmem_limit_bytes=1024 * 1024),
     )(steps, pieces[0], got[1], got[2], got[3], dual, rhs_own, scale)
     return local[None, None], link[None], multipliers[None]
 

time: 206 us -> 200 us (0.971)
  local copies, waits for them, and re-layouts: 3.06 us -> 0.05 us
    ppermute x21, waiting for transfers between devices: 32.8 us -> 28 us  [swap_y(): return lax.ppermute(x, 'col', [(i, i ^ k) for i in range(4)])]
    ppermute x15, waiting for transfers between devices: 18.3 us -> 22.9 us  [swap_first(): lax.ppermute(x, 'scen', [(i, i ^ k << (1 if i % 2 else 3)) for i in range...]
    ppermute x15, waiting for transfers between devices: 20.6 us -> 17.1 us  [swap_second(): lax.ppermute(x, 'scen', [(i, i ^ k << (3 if i % 2 else 1)) for i in range...]
    unnamed x32 -> x16, local copies, waits for them, and re-layouts: 3.06 us -> 0.05 us
    pallas_call x24 -> x25, Pallas kernels: 35.9 us -> 37.3 us  [call(): pl.pallas_call(kernel, out_shape=tuple((jax.ShapeDtypeStruct((n, TILE), F...]
  transfers between devices with their start and end apart: 62 -> 62, of which waited for: 43 -> 41; matrix products, arithmetic and copies ran while one was open for 0% -> 0% of each run, Pallas kernels for 5% -> 4%
where the time goes in v5:
time: 200 us
  waiting for transfers between devices  79.1 us (40%)
  starting transfers between devices  74.9 us (37%)
  Pallas kernels  44.8 us (22%)
    pallas_call x25, Pallas kernels, call(): pl.pallas_call(kernel, out_shape=tuple((jax.ShapeDtypeStruct((n, TILE), F...  37.3 us
    ppermute x21, starting transfers between devices, swap_y(): return lax.ppermute(x, 'col', [(i, i ^ k) for i in range(4)])  30 us
    ppermute x21, waiting for transfers between devices, swap_y(): return lax.ppermute(x, 'col', [(i, i ^ k) for i in range(4)])  28 us
    ppermute x15, waiting for transfers between devices, swap_first(): lax.ppermute(x, 'scen', [(i, i ^ k << (1 if i % 2 else 3)) for i in range...  22.9 us
    ppermute x15, starting transfers between devices, swap_second(): lax.ppermute(x, 'scen', [(i, i ^ k << (3 if i % 2 else 1)) for i in range...  22.4 us
    ppermute x15, starting transfers between devices, swap_first(): lax.ppermute(x, 'scen', [(i, i ^ k << (1 if i % 2 else 3)) for i in range...  20.9 us
    ppermute x15, waiting for transfers between devices, swap_second(): lax.ppermute(x, 'scen', [(i, i ^ k << (3 if i % 2 else 1)) for i in range...  17.1 us
    ppermute x11, waiting for transfers between devices, swap_core(): return lax.ppermute(x, 'scen', [(i, i ^ 1) for i in range(32)])  11 us
  transfers between devices with their start and end apart: 62, of which 41 were waited for; matrix products, arithmetic and copies ran while one was open for 0% of the time, Pallas kernels for 4%

profile of v5, /device:TPU:0, one launch (start us, length us, event | category | flops | bytes accessed | tf_op | source)
XLA Modules:
  0.0 200.0 jit_solution(16569601085782264535)
XLA Ops:
  0.8 6.9 %shard_map.130 = (f32[192,256]{1,0:T(8,128)S(1)}, f32[136,256]{1,0:T(8,128)S(1)}, f32[128,256]{1,0:T(8,128)S(1)}, f32[64,256,256]{2,1,0:T(8,128)S(1)}) custom-call(s32[3]{0:T(128)S(1)} %pad_add_fusion.place, s32[64]{0:T(128)} %bitcast.20, s32[64]{0:T(128)} %bitcast.30, f32[64,256,256]{2,1,0:T(8,128)} %bitcast.44, f32[32,256]{1,0:T(8,128)} %bitcast.45, ...), custom_call_target="tpu_custom_call" | custom-call | tf_op jit(solution)/shard_map/pallas_call | solution.py:179
  9.2 2.9 %collective-permute-start.6 = (f32[128,256]{1,0:T(8,128)S(1)}, f32[128,256]{1,0:T(8,128)S(1)}, u32[]{:S(2)}, u32[]{:S(2)}) collective-permute-start(f32[128,256]{1,0:T(8,128)S(1)} %shard_map.131.own), channel_id=1, source_target_pairs={{0,96},{4,28},{8,104},{12,20},{16,112},{20,12},{24,120},{28,4},{32... | collective-permute-start | bytes 393224 | tf_op jit(solution)/shard_map/ppermute | solution.py:34
  13.3 2.7 %collective-permute-done.6.r3 = f32[128,256]{1,0:T(8,128)S(1)} collective-permute-done((f32[128,256]{1,0:T(8,128)S(1)}, f32[128,256]{1,0:T(8,128)S(1)}, u32[]{:S(2)}, u32[]{:S(2)}) %collective-permute-start.6) | collective-permute-done | bytes 131104 | tf_op jit(solution)/shard_map/ppermute | solution.py:34
  18.6 4.1 %collective-permute-start.9 = (f32[128,256]{1,0:T(8,128)S(1)}, f32[128,256]{1,0:T(8,128)S(1)}, u32[]{:S(2)}, u32[]{:S(2)}) collective-permute-start(f32[128,256]{1,0:T(8,128)S(1)} %shard_map.132.own), channel_id=1, source_target_pairs={{0,24},{4,100},{8,16},{12,108},{16,8},{20,116},{24,0},{28,124},{32... | collective-permute-start | bytes 393224 | tf_op jit(solution)/shard_map/ppermute | solution.py:38
  23.7 3.0 %collective-permute-start.2 = (f32[192,256]{1,0:T(8,128)S(1)}, f32[192,256]{1,0:T(8,128)S(1)}, u32[]{:S(2)}, u32[]{:S(2)}) collective-permute-start(f32[192,256]{1,0:T(8,128)S(1)} %get-tuple-element.58.r0), channel_id=1, source_target_pairs={{0,3},{1,2},{2,1},{3,0},{4,7},{5,6},{6,5},{7,4},{8,11},{9,10},{10,... | collective-permute-start | bytes 589832 | tf_op jit(solution)/shard_map/ppermute | solution.py:42
  29.3 4.3 %collective-permute-done.2.r3 = f32[192,256]{1,0:T(8,128)S(1)} collective-permute-done((f32[192,256]{1,0:T(8,128)S(1)}, f32[192,256]{1,0:T(8,128)S(1)}, u32[]{:S(2)}, u32[]{:S(2)}) %collective-permute-start.2) | collective-permute-done | bytes 196640 | tf_op jit(solution)/shard_map/ppermute | solution.py:42
  35.3 5.8 %shard_map.134 = (f32[128,256]{1,0:T(8,128)S(1)}, f32[136,256]{1,0:T(8,128)S(1)}, f32[128,256]{1,0:T(8,128)S(1)}, f32[128,256]{1,0:T(8,128)S(1)}, f32[264,256]{1,0:T(8,128)S(1)}) custom-call(s32[64]{0:T(128)S(1)} %bitcast.21, s32[64]{0:T(128)S(1)} %bitcast.31, s32[3]{0:T(128)S(1)} %pad_add_fusion.place, f32[64,256,256]{2,1,0:T(8,128)S(1)} %get-tuple-element.57.tiles_ref, ...), custom_call_target="tpu_custom_call" | custom-call | tf_op jit(solution)/shard_map/pallas_call | solution.py:105
  42.5 2.7 %collective-permute-start.17 = (f32[128,256]{1,0:T(8,128)S(1)}, f32[128,256]{1,0:T(8,128)S(1)}, u32[]{:S(2)}, u32[]{:S(2)}) collective-permute-start(f32[128,256]{1,0:T(8,128)S(1)} %shard_map.135.own), channel_id=1, source_target_pairs={{0,96},{4,28},{8,104},{12,20},{16,112},{20,12},{24,120},{28,4},{32... | collective-permute-start | bytes 393224 | tf_op jit(solution)/shard_map/ppermute | solution.py:34
  49.2 3.4 %shard_map.136 = (f32[136,256]{1,0:T(8,128)S(1)}, f32[128,256]{1,0:T(8,128)S(1)}, f32[128,256]{1,0:T(8,128)S(1)}, f32[128,256]{1,0:T(8,128)S(1)}) custom-call(s32[64]{0:T(128)S(1)} %bitcast.22, s32[64]{0:T(128)S(1)} %bitcast.32, s32[3]{0:T(128)S(1)} %pad_add_fusion.place, f32[64,256,256]{2,1,0:T(8,128)S(1)} %get-tuple-element.57.tiles_ref, ...), custom_call_target="tpu_custom_call" | custom-call | tf_op jit(solution)/shard_map/pallas_call | solution.py:105
  55.2 3.3 %collective-permute-start.20 = (f32[160,256]{1,0:T(8,128)S(1)}, f32[160,256]{1,0:T(8,128)S(1)}, u32[]{:S(2)}, u32[]{:S(2)}) collective-permute-start(f32[160,256]{1,0:T(8,128)S(1)} %get-tuple-element.68), channel_id=1, source_target_pairs={{0,16},{4,68},{8,24},{12,76},{16,0},{20,84},{24,8},{28,92},{32,48}... | collective-permute-start | bytes 491528 | tf_op jit(solution)/shard_map/ppermute | solution.py:38
  59.4 2.7 %collective-permute-start.13 = (f32[128,256]{1,0:T(8,128)S(1)}, f32[128,256]{1,0:T(8,128)S(1)}, u32[]{:S(2)}, u32[]{:S(2)}) collective-permute-start(f32[128,256]{1,0:T(8,128)S(1)} %get-tuple-element.61.r0), channel_id=1, source_target_pairs={{0,3},{1,2},{2,1},{3,0},{4,7},{5,6},{6,5},{7,4},{8,11},{9,10},{10,... | collective-permute-start | bytes 393224 | tf_op jit(solution)/shard_map/ppermute | solution.py:42
  70.0 3.6 %shard_map.139 = (f32[128,256]{1,0:T(8,128)S(1)}, f32[128,256]{1,0:T(8,128)S(1)}, f32[264,256]{1,0:T(8,128)S(1)}) custom-call(s32[64]{0:T(128)S(1)} %bitcast.23, s32[64]{0:T(128)S(1)} %bitcast.33, s32[3]{0:T(128)S(1)} %pad_add_fusion.place, f32[64,256,256]{2,1,0:T(8,128)S(1)} %get-tuple-element.57.tiles_ref, f32[128,256]{1,0:T(8,128)S(1)} %get-tuple-element.61.r0, ...), custom_call_target="tpu_custom_call" | custom-call | tf_op jit(solution)/shard_map/pallas_call | solution.py:105
  77.7 3.7 %shard_map.140 = (f32[136,256]{1,0:T(8,128)S(1)}, f32[128,256]{1,0:T(8,128)S(1)}) custom-call(s32[64]{0:T(128)S(1)} %bitcast.24, s32[64]{0:T(128)S(1)} %bitcast.34, s32[3]{0:T(128)S(1)} %pad_add_fusion.place, f32[64,256,256]{2,1,0:T(8,128)S(1)} %get-tuple-element.57.tiles_ref, f32[128,256]{1,0:T(8,128)S(1)} %get-tuple-element.74.row_scale.rowold), custom_call_target="tpu_custom_call" | custom-call | tf_op jit(solution)/shard_map/pallas_call | solution.py:105
  83.1 3.2 %collective-permute-start.29 = (f32[176,256]{1,0:T(8,128)S(1)}, f32[176,256]{1,0:T(8,128)S(1)}, u32[]{:S(2)}, u32[]{:S(2)}) collective-permute-start(f32[176,256]{1,0:T(8,128)S(1)} %get-tuple-element.81.own), channel_id=1, source_target_pairs={{0,96},{4,28},{8,104},{12,20},{16,112},{20,12},{24,120},{28,4},{32... | collective-permute-start | bytes 540680 | tf_op jit(solution)/shard_map/ppermute | solution.py:34
  87.3 4.0 %collective-permute-done.29.r3 = f32[176,256]{1,0:T(8,128)S(1)} collective-permute-done((f32[176,256]{1,0:T(8,128)S(1)}, f32[176,256]{1,0:T(8,128)S(1)}, u32[]{:S(2)}, u32[]{:S(2)}) %collective-permute-start.29) | collective-permute-done | bytes 180256 | tf_op jit(solution)/shard_map/ppermute | solution.py:34
  97.6 3.2 %collective-permute-done.32.r3 = f32[176,256]{1,0:T(8,128)S(1)} collective-permute-done((f32[176,256]{1,0:T(8,128)S(1)}, f32[176,256]{1,0:T(8,128)S(1)}, u32[]{:S(2)}, u32[]{:S(2)}) %collective-permute-start.32) | collective-permute-done | bytes 180256 | tf_op jit(solution)/shard_map/ppermute | solution.py:38
  113.2 3.7 %shard_map.145 = (f32[8,256]{1,0:T(8,128)S(1)}, f32[128,256]{1,0:T(8,128)S(1)}, f32[264,256]{1,0:T(8,128)S(1)}) custom-call(s32[64]{0:T(128)S(1)} %bitcast.25, s32[64]{0:T(128)S(1)} %bitcast.35, s32[3]{0:T(128)S(1)} %pad_add_fusion.place, f32[64,256,256]{2,1,0:T(8,128)S(1)} %get-tuple-element.57.tiles_ref, f32[8,256]{1,0:T(8,128)S(1)} %get-tuple-element.82.rest_0_, ...), custom_call_target="tpu_custom_call" | custom-call | tf_op jit(solution)/shard_map/pallas_call | solution.py:105
  121.1 2.8 %collective-permute-done.39.r3 = f32[128,256]{1,0:T(8,128)S(1)} collective-permute-done((f32[128,256]{1,0:T(8,128)S(1)}, f32[128,256]{1,0:T(8,128)S(1)}, u32[]{:S(2)}, u32[]{:S(2)}) %collective-permute-start.39) | collective-permute-done | bytes 131104 | tf_op jit(solution)/shard_map/ppermute | solution.py:42
  125.7 3.4 %shard_map.146 = (f32[136,256]{1,0:T(8,128)S(1)}, f32[128,256]{1,0:T(8,128)S(1)}, f32[128,256]{1,0:T(8,128)S(1)}) custom-call(s32[64]{0:T(128)S(1)} %bitcast.26, s32[64]{0:T(128)S(1)} %bitcast.36, s32[3]{0:T(128)S(1)} %pad_add_fusion.place, f32[64,256,256]{2,1,0:T(8,128)S(1)} %get-tuple-element.57.tiles_ref, f32[8,256]{1,0:T(8,128)S(1)} %get-tuple-element.88.steps.rest_0_, ...), custom_call_target="tpu_custom_call" | custom-call | tf_op jit(solution)/shard_map/pallas_call | solution.py:105
  130.6 2.6 %collective-permute-start.43 = (f32[128,256]{1,0:T(8,128)S(1)}, f32[128,256]{1,0:T(8,128)S(1)}, u32[]{:S(2)}, u32[]{:S(2)}) collective-permute-start(f32[128,256]{1,0:T(8,128)S(1)} %shard_map.147.own), channel_id=1, source_target_pairs={{0,96},{4,28},{8,104},{12,20},{16,112},{20,12},{24,120},{28,4},{32... | collective-permute-start | bytes 393224 | tf_op jit(solution)/shard_map/ppermute | solution.py:34
  149.9 3.5 %shard_map.150 = (f32[128,256]{1,0:T(8,128)S(1)}, f32[264,256]{1,0:T(8,128)S(1)}) custom-call(s32[64]{0:T(128)S(1)} %bitcast.27, s32[64]{0:T(128)S(1)} %bitcast.37, s32[3]{0:T(128)S(1)} %pad_add_fusion.place, f32[64,256,256]{2,1,0:T(8,128)S(1)} %get-tuple-element.57.tiles_ref, f32[8,256]{1,0:T(8,128)S(1)} %get-tuple-element.88.steps.rest_0_, ...), custom_call_target="tpu_custom_call" | custom-call | tf_op jit(solution)/shard_map/pallas_call | solution.py:105
  157.6 5.5 %collective-permute-done.50.r3 = f32[128,256]{1,0:T(8,128)S(1)} collective-permute-done((f32[128,256]{1,0:T(8,128)S(1)}, f32[128,256]{1,0:T(8,128)S(1)}, u32[]{:S(2)}, u32[]{:S(2)}) %collective-permute-start.50) | collective-permute-done | bytes 131104 | tf_op jit(solution)/shard_map/ppermute | solution.py:42
  163.7 3.5 %shard_map.151 = (f32[136,256]{1,0:T(8,128)S(1)}, f32[128,256]{1,0:T(8,128)S(1)}, f32[128,256]{1,0:T(8,128)S(1)}) custom-call(s32[64]{0:T(128)S(1)} %bitcast.28, s32[64]{0:T(128)S(1)} %bitcast.38, s32[3]{0:T(128)S(1)} %pad_add_fusion.place, f32[64,256,256]{2,1,0:T(8,128)S(1)} %get-tuple-element.57.tiles_ref, f32[8,256]{1,0:T(8,128)S(1)} %get-tuple-element.88.steps.rest_0_, ...), custom_call_target="tpu_custom_call" | custom-call | tf_op jit(solution)/shard_map/pallas_call | solution.py:105
  187.2 4.2 %shard_map.155 = (f32[8,256]{1,0:T(8,128)}, f32[256,256]{1,0:T(8,128)}, f32[32,256]{1,0:T(8,128)S(1)}, f32[32,256]{1,0:T(8,128)S(1)}, f32[32,256]{1,0:T(8,128)S(...) custom-call(s32[64]{0:T(128)S(1)} %bitcast.29, ...), custom_call_target="tpu_custom_call" | custom-call | tf_op jit(solution)/shard_map/pallas_call | solution.py:105
  (144 shorter events, 110.3 us)
Async XLA Ops:
  9.2 6.8 %collective-permute-start.6 = (f32[128,256]{1,0:T(8,128)S(1)}, f32[128,256]{1,0:T(8,128)S(1)}, u32[]{:S(2)}, u32[]{:S(2)}) collective-permute-start(f32[128,256]{1,0:T(8,128)S(1)} %shard_map.131.own), channel_id=1, source_target_pairs={{0,96},{4,28},{8,104},{12,20},{16,112},{20,12},{24,120},{28,4},{32... | collective-permute-start | bytes 393224 | tf_op jit(solution)/shard_map/ppermute | solution.py:34
  18.6 8.7 %collective-permute-start.9 = (f32[128,256]{1,0:T(8,128)S(1)}, f32[128,256]{1,0:T(8,128)S(1)}, u32[]{:S(2)}, u32[]{:S(2)}) collective-permute-start(f32[128,256]{1,0:T(8,128)S(1)} %shard_map.132.own), channel_id=1, source_target_pairs={{0,24},{4,100},{8,16},{12,108},{16,8},{20,116},{24,0},{28,124},{32... | collective-permute-start | bytes 393224 | tf_op jit(solution)/shard_map/ppermute | solution.py:38
  23.7 9.9 %collective-permute-start.2 = (f32[192,256]{1,0:T(8,128)S(1)}, f32[192,256]{1,0:T(8,128)S(1)}, u32[]{:S(2)}, u32[]{:S(2)}) collective-permute-start(f32[192,256]{1,0:T(8,128)S(1)} %get-tuple-element.58.r0), channel_id=1, source_target_pairs={{0,3},{1,2},{2,1},{3,0},{4,7},{5,6},{6,5},{7,4},{8,11},{9,10},{10,... | collective-permute-start | bytes 589832 | tf_op jit(solution)/shard_map/ppermute | solution.py:42
  26.7 8.6 %collective-permute-start.1 = (f32[192,256]{1,0:T(8,128)S(1)}, f32[192,256]{1,0:T(8,128)S(1)}, u32[]{:S(2)}, u32[]{:S(2)}) collective-permute-start(f32[192,256]{1,0:T(8,128)S(1)} %get-tuple-element.58.r0), channel_id=1, source_target_pairs={{0,2},{1,3},{2,0},{3,1},{4,6},{5,7},{6,4},{7,5},{8,10},{9,11},{10,... | collective-permute-start | bytes 589832 | tf_op jit(solution)/shard_map/ppermute | solution.py:42
  27.3 7.9 %collective-permute-start = (f32[192,256]{1,0:T(8,128)S(1)}, f32[192,256]{1,0:T(8,128)S(1)}, u32[]{:S(2)}, u32[]{:S(2)}) collective-permute-start(f32[192,256]{1,0:T(8,128)S(1)} %get-tuple-element.58.r0), channel_id=1, source_target_pairs={{0,1},{1,0},{2,3},{3,2},{4,5},{5,4},{6,7},{7,6},{8,9},{9,8},{10,11... | collective-permute-start | bytes 589832 | tf_op jit(solution)/shard_map/ppermute | solution.py:42
  45.2 7.4 %collective-permute-start.16 = (f32[128,256]{1,0:T(8,128)S(1)}, f32[128,256]{1,0:T(8,128)S(1)}, u32[]{:S(2)}, u32[]{:S(2)}) collective-permute-start(f32[128,256]{1,0:T(8,128)S(1)} %shard_map.135.own), channel_id=1, source_target_pairs={{0,64},{4,20},{8,72},{12,28},{16,80},{20,4},{24,88},{28,12},{32,96... | collective-permute-start | bytes 393224 | tf_op jit(solution)/shard_map/ppermute | solution.py:34
  54.6 8.1 %collective-permute-start.19 = (f32[160,256]{1,0:T(8,128)S(1)}, f32[160,256]{1,0:T(8,128)S(1)}, u32[]{:S(2)}, u32[]{:S(2)}) collective-permute-start(f32[160,256]{1,0:T(8,128)S(1)} %get-tuple-element.67), channel_id=1, source_target_pairs={{0,8},{4,36},{8,0},{12,44},{16,24},{20,52},{24,16},{28,60},{32,40}... | collective-permute-start | bytes 491528 | tf_op jit(solution)/shard_map/ppermute | solution.py:38
  55.2 8.3 %collective-permute-start.20 = (f32[160,256]{1,0:T(8,128)S(1)}, f32[160,256]{1,0:T(8,128)S(1)}, u32[]{:S(2)}, u32[]{:S(2)}) collective-permute-start(f32[160,256]{1,0:T(8,128)S(1)} %get-tuple-element.68), channel_id=1, source_target_pairs={{0,16},{4,68},{8,24},{12,76},{16,0},{20,84},{24,8},{28,92},{32,48}... | collective-permute-start | bytes 491528 | tf_op jit(solution)/shard_map/ppermute | solution.py:38
  58.4 6.8 %collective-permute-start.21 = (f32[160,256]{1,0:T(8,128)S(1)}, f32[160,256]{1,0:T(8,128)S(1)}, u32[]{:S(2)}, u32[]{:S(2)}) collective-permute-start(f32[160,256]{1,0:T(8,128)S(1)} %get-tuple-element.69), channel_id=1, source_target_pairs={{0,24},{4,100},{8,16},{12,108},{16,8},{20,116},{24,0},{28,124},{32... | collective-permute-start | bytes 491528 | tf_op jit(solution)/shard_map/ppermute | solution.py:38
  59.4 8.4 %collective-permute-start.13 = (f32[128,256]{1,0:T(8,128)S(1)}, f32[128,256]{1,0:T(8,128)S(1)}, u32[]{:S(2)}, u32[]{:S(2)}) collective-permute-start(f32[128,256]{1,0:T(8,128)S(1)} %get-tuple-element.61.r0), channel_id=1, source_target_pairs={{0,3},{1,2},{2,1},{3,0},{4,7},{5,6},{6,5},{7,4},{8,11},{9,10},{10,... | collective-permute-start | bytes 393224 | tf_op jit(solution)/shard_map/ppermute | solution.py:42
  62.1 7.9 %collective-permute-start.12 = (f32[128,256]{1,0:T(8,128)S(1)}, f32[128,256]{1,0:T(8,128)S(1)}, u32[]{:S(2)}, u32[]{:S(2)}) collective-permute-start(f32[128,256]{1,0:T(8,128)S(1)} %get-tuple-element.61.r0), channel_id=1, source_target_pairs={{0,2},{1,3},{2,0},{3,1},{4,6},{5,7},{6,4},{7,5},{8,10},{9,11},{10,... | collective-permute-start | bytes 393224 | tf_op jit(solution)/shard_map/ppermute | solution.py:42
  62.7 7.3 %collective-permute-start.11 = (f32[128,256]{1,0:T(8,128)S(1)}, f32[128,256]{1,0:T(8,128)S(1)}, u32[]{:S(2)}, u32[]{:S(2)}) collective-permute-start(f32[128,256]{1,0:T(8,128)S(1)} %get-tuple-element.61.r0), channel_id=1, source_target_pairs={{0,1},{1,0},{2,3},{3,2},{4,5},{5,4},{6,7},{7,6},{8,9},{9,8},{10,11... | collective-permute-start | bytes 393224 | tf_op jit(solution)/shard_map/ppermute | solution.py:42
  73.6 8.0 %collective-permute-start.25 = (f32[128,256]{1,0:T(8,128)S(1)}, f32[128,256]{1,0:T(8,128)S(1)}, u32[]{:S(2)}, u32[]{:S(2)}) collective-permute-start(f32[128,256]{1,0:T(8,128)S(1)} %get-tuple-element.73.r0), channel_id=1, source_target_pairs={{0,3},{1,2},{2,1},{3,0},{4,7},{5,6},{6,5},{7,4},{8,11},{9,10},{10,... | collective-permute-start | bytes 393224 | tf_op jit(solution)/shard_map/ppermute | solution.py:42
  75.8 7.0 %collective-permute-start.24 = (f32[128,256]{1,0:T(8,128)S(1)}, f32[128,256]{1,0:T(8,128)S(1)}, u32[]{:S(2)}, u32[]{:S(2)}) collective-permute-start(f32[128,256]{1,0:T(8,128)S(1)} %get-tuple-element.73.r0), channel_id=1, source_target_pairs={{0,2},{1,3},{2,0},{3,1},{4,6},{5,7},{6,4},{7,5},{8,10},{9,11},{10,... | collective-permute-start | bytes 393224 | tf_op jit(solution)/shard_map/ppermute | solution.py:42
  83.1 8.2 %collective-permute-start.29 = (f32[176,256]{1,0:T(8,128)S(1)}, f32[176,256]{1,0:T(8,128)S(1)}, u32[]{:S(2)}, u32[]{:S(2)}) collective-permute-start(f32[176,256]{1,0:T(8,128)S(1)} %get-tuple-element.81.own), channel_id=1, source_target_pairs={{0,96},{4,28},{8,104},{12,20},{16,112},{20,12},{24,120},{28,4},{32... | collective-permute-start | bytes 540680 | tf_op jit(solution)/shard_map/ppermute | solution.py:34
  86.3 7.0 %collective-permute-start.28 = (f32[176,256]{1,0:T(8,128)S(1)}, f32[176,256]{1,0:T(8,128)S(1)}, u32[]{:S(2)}, u32[]{:S(2)}) collective-permute-start(f32[176,256]{1,0:T(8,128)S(1)} %get-tuple-element.81.own), channel_id=1, source_target_pairs={{0,64},{4,20},{8,72},{12,28},{16,80},{20,4},{24,88},{28,12},{32,96... | collective-permute-start | bytes 540680 | tf_op jit(solution)/shard_map/ppermute | solution.py:34
  86.4 7.0 %collective-permute-start.27 = (f32[176,256]{1,0:T(8,128)S(1)}, f32[176,256]{1,0:T(8,128)S(1)}, u32[]{:S(2)}, u32[]{:S(2)}) collective-permute-start(f32[176,256]{1,0:T(8,128)S(1)} %get-tuple-element.81.own), channel_id=1, source_target_pairs={{0,32},{4,12},{8,40},{12,4},{16,48},{20,28},{24,56},{28,20},{32,0}... | collective-permute-start | bytes 540680 | tf_op jit(solution)/shard_map/ppermute | solution.py:34
  93.4 7.3 %collective-permute-start.32 = (f32[176,256]{1,0:T(8,128)S(1)}, f32[176,256]{1,0:T(8,128)S(1)}, u32[]{:S(2)}, u32[]{:S(2)}) collective-permute-start(f32[176,256]{1,0:T(8,128)S(1)} %shard_map.142.own), channel_id=1, source_target_pairs={{0,24},{4,100},{8,16},{12,108},{16,8},{20,116},{24,0},{28,124},{32... | collective-permute-start | bytes 540680 | tf_op jit(solution)/shard_map/ppermute | solution.py:38
  95.7 7.0 %collective-permute-start.31 = (f32[176,256]{1,0:T(8,128)S(1)}, f32[176,256]{1,0:T(8,128)S(1)}, u32[]{:S(2)}, u32[]{:S(2)}) collective-permute-start(f32[176,256]{1,0:T(8,128)S(1)} %shard_map.142.own), channel_id=1, source_target_pairs={{0,16},{4,68},{8,24},{12,76},{16,0},{20,84},{24,8},{28,92},{32,48}... | collective-permute-start | bytes 540680 | tf_op jit(solution)/shard_map/ppermute | solution.py:38
  116.9 7.0 %collective-permute-start.39 = (f32[128,256]{1,0:T(8,128)S(1)}, f32[128,256]{1,0:T(8,128)S(1)}, u32[]{:S(2)}, u32[]{:S(2)}) collective-permute-start(f32[128,256]{1,0:T(8,128)S(1)} %get-tuple-element.89.r0), channel_id=1, source_target_pairs={{0,3},{1,2},{2,1},{3,0},{4,7},{5,6},{6,5},{7,4},{8,11},{9,10},{10,... | collective-permute-start | bytes 393224 | tf_op jit(solution)/shard_map/ppermute | solution.py:42
  118.3 6.8 %collective-permute-start.38 = (f32[128,256]{1,0:T(8,128)S(1)}, f32[128,256]{1,0:T(8,128)S(1)}, u32[]{:S(2)}, u32[]{:S(2)}) collective-permute-start(f32[128,256]{1,0:T(8,128)S(1)} %get-tuple-element.89.r0), channel_id=1, source_target_pairs={{0,2},{1,3},{2,0},{3,1},{4,6},{5,7},{6,4},{7,5},{8,10},{9,11},{10,... | collective-permute-start | bytes 393224 | tf_op jit(solution)/shard_map/ppermute | solution.py:42
  153.4 9.7 %collective-permute-start.50 = (f32[128,256]{1,0:T(8,128)S(1)}, f32[128,256]{1,0:T(8,128)S(1)}, u32[]{:S(2)}, u32[]{:S(2)}) collective-permute-start(f32[128,256]{1,0:T(8,128)S(1)} %get-tuple-element.96.r0), channel_id=1, source_target_pairs={{0,3},{1,2},{2,1},{3,0},{4,7},{5,6},{6,5},{7,4},{8,11},{9,10},{10,... | collective-permute-start | bytes 393224 | tf_op jit(solution)/shard_map/ppermute | solution.py:42
  154.9 8.2 %collective-permute-start.49 = (f32[128,256]{1,0:T(8,128)S(1)}, f32[128,256]{1,0:T(8,128)S(1)}, u32[]{:S(2)}, u32[]{:S(2)}) collective-permute-start(f32[128,256]{1,0:T(8,128)S(1)} %get-tuple-element.96.r0), channel_id=1, source_target_pairs={{0,2},{1,3},{2,0},{3,1},{4,6},{5,7},{6,4},{7,5},{8,10},{9,11},{10,... | collective-permute-start | bytes 393224 | tf_op jit(solution)/shard_map/ppermute | solution.py:42
  156.0 7.8 %collective-permute-start.48 = (f32[128,256]{1,0:T(8,128)S(1)}, f32[128,256]{1,0:T(8,128)S(1)}, u32[]{:S(2)}, u32[]{:S(2)}) collective-permute-start(f32[128,256]{1,0:T(8,128)S(1)} %get-tuple-element.96.r0), channel_id=1, source_target_pairs={{0,1},{1,0},{2,3},{3,2},{4,5},{5,4},{6,7},{7,6},{8,9},{9,8},{10,11... | collective-permute-start | bytes 393224 | tf_op jit(solution)/shard_map/ppermute | solution.py:42
  (46 other events, 363.1 us)

commit v6 on v5

--- a/solution.py
+++ b/solution.py
@@ -193,7 +193,7 @@
 
 
 def second_stats_kernel(
-    rows_ref, cols_ref, place, tiles_ref, r0, r1, r2, r3, loc, mine, other, rowout, colown, colother, rownew,
+    rows_ref, cols_ref, place, tiles_ref, r0, r1, r3, r2, loc, mine, other, rowout, colown, colother, rownew,
     colnew, racc, cacc, rowf, colf,
 ):
     row = tree(jnp.maximum, r0[0:RT], (r1[0:RT], r2[0:RT], r3[0:RT]))
@@ -217,7 +217,7 @@
 
 
 def third_rows_kernel(
-    rows_ref, cols_ref, place, tiles_ref, r0, r1, r2, r3, loc, mine, other, rowold, colold, rowout, rownew,
+    rows_ref, cols_ref, place, tiles_ref, r0, r1, r3, r2, loc, mine, other, rowold, colold, rowout, rownew,
     colnew, racc, colf,
 ):
     row = tree(jnp.maximum, r0[...], (r1[...], r2[...], r3[...]))
@@ -249,7 +249,7 @@
 
 
 def first_backward_kernel(
-    rows_ref, cols_ref, place, tiles_ref, r0, r1, r2, r3, after, colown, colother, rhsout, dualout, cacc, work
+    rows_ref, cols_ref, place, tiles_ref, r0, r1, r3, r2, after, colown, colother, rhsout, dualout, cacc, work
 ):
     for k, ref in enumerate((r0, r1, r2, r3)):
         at = pl.ds(pl.multiple_of((place[2] ^ k) * SHARE, SHARE), SHARE)
@@ -266,7 +266,7 @@
 
 
 def backward_kernel(
-    rows_ref, cols_ref, place, tiles_ref, steps, r0, r1, r2, r3, dual, rhs, rowf, colown, colother, dualnew,
+    rows_ref, cols_ref, place, tiles_ref, steps, r0, r1, r3, r2, dual, rhs, rowf, colown, colother, dualnew,
     cacc, work,
 ):
     total = tree(jnp.add, r0[...], (r1[...], r2[...], r3[...]))
@@ -284,7 +284,7 @@
 
 def forward_kernel(index, grad_at, rows_ref, cols_ref, place, tiles_ref, *rest):
     if index == 0:
-        c0, c1, c2, c3, rhs_square, *rest = rest
+        c0, c1, c3, c2, rhs_square, *rest = rest
     else:
         steps, *rest = rest
     loc, mine, other, primal, cost, upper, colf, *rest = rest
@@ -336,11 +336,11 @@
     out[...] = op(colown[CT:OWN], got[...])
 
 
-def merge_kernel(op, tiles_ref, own, r1, r2, r3, out):
+def merge_kernel(op, tiles_ref, own, r1, r3, r2, out):
     out[...] = tree(op, own[...], (r1[...], r2[...], r3[...]))
 
 
-def merge_grad_kernel(place, tiles_ref, own, r1, r2, r3, gradown, gradgot, m0, m1, m2, m3, half):
+def merge_grad_kernel(place, tiles_ref, own, r1, r3, r2, gradown, gradgot, m0, m1, m2, m3, half):
     link = tree(jnp.maximum, own[...], (r1[...], r2[...], r3[...]))
     half[...] = gradown[CT:OWN] + gradgot[...]
     for k, out in enumerate((m0, m1, m2, m3)):
@@ -348,13 +348,13 @@
         out[HALF:] = half[pl.ds(pl.multiple_of((place[1] ^ k) * CHUNK, CHUNK), CHUNK), :]
 
 
-def merge_chunk_kernel(tiles_ref, own, r1, r2, r3, link, chunk):
+def merge_chunk_kernel(tiles_ref, own, r2, r1, r3, link, chunk):
     link[...] = tree(jnp.maximum, own[0:HALF], (r1[0:HALF], r2[0:HALF], r3[0:HALF]))
     chunk[...] = tree(jnp.add, own[HALF:], (r1[HALF:], r2[HALF:], r3[HALF:]))
 
 
 def rows_kernel(
-    tiles_ref, r0, r1, r2, r3, rowold, rhs, dual, colown, got, colold, cost, chunk, rownew, rhs_scaled,
+    tiles_ref, r0, r1, r3, r2, rowold, rhs, dual, colown, got, colold, cost, chunk, rownew, rhs_scaled,
     dual_scaled, out,
 ):
     total = tree(jnp.add, r0[...], (r1[...], r2[...], r3[...]))
@@ -372,7 +372,7 @@
     out[OWN + CT :] = chunk[...]
 
 
-def merge_all_kernel(place, tiles_ref, own, r1, r2, r3, out):
+def merge_all_kernel(place, tiles_ref, own, r1, r3, r2, out):
     at = slice(0, HALF + EIGHT)
     out[at] = tree(jnp.add, own[at], (r1[at], r2[at], r3[at]))
     for k, ref in enumerate((own, r1, r2, r3)):
@@ -410,7 +410,7 @@
     cost_square[...] = squares[CT:] + (sums[0] + sums[1])
 
 
-def end_kernel(steps, p0, p1, p2, p3, dual, rhs, rowf, out):
+def end_kernel(steps, p0, p2, p1, p3, dual, rhs, rowf, out):
     total = tree(jnp.add, p0[...], (p1[...], p2[...], p3[...]))
     scale = rowf[...]
     out[...] = scale * (dual[...] + steps[1:2] * (rhs[...] - scale * total))
@@ -437,7 +437,7 @@
 
     def over(swap, x):
         got = {k: swap(x, k) for k in (2, 1, 3)}
-        return x, got[1], got[2], got[3]
+        return x, got[1], got[3], got[2]
 
     row_part, colown, colother, tiles = first_stats(ids, tile_values[0, 0], rhs[0], start_dual[0])
 
@@ -461,7 +461,7 @@
     (link,) = run(functools.partial(core_kernel, jnp.maximum), (), (colown, swap_core(colother)), (HALF,))
     got = over(swap_first, link)
     gradown, gradother, rhs_rows, dual_rows = run(
-        first_backward_kernel, ids, (*first_rows, got[3]), (OWN, HALF, RT, RT), (COLS, ROWS)
+        first_backward_kernel, ids, (*first_rows, got[2]), (OWN, HALF, RT, RT), (COLS, ROWS)
     )
     sent = run(
         merge_grad_kernel,
@@ -471,7 +471,7 @@
         (pltpu.VMEM((HALF, TILE), F32),),
     )
     got = {k: swap_second(sent[k], k) for k in (2, 1, 3)}
-    link, chunk = run(merge_chunk_kernel, (), (sent[0], got[1], got[2], got[3]), (HALF, CHUNK))
+    link, chunk = run(merge_chunk_kernel, (), (sent[0], got[2], got[1], got[3]), (HALF, CHUNK))
 
     row_part, row_scale, col_scale = run(
         third_rows_kernel,
@@ -550,7 +550,7 @@
         in_specs=[vmem] * 8,
         out_specs=vmem,
         compiler_params=pltpu.CompilerParams(vmem_limit_bytes=1024 * 1024),
-    )(steps, pieces[0], got[1], got[2], got[3], dual, rhs_own, scale)
+    )(steps, pieces[0], got[2], got[1], got[3], dual, rhs_own, scale)
     return local[None, None], link[None], multipliers[None]
 
 

time: 200 us -> 194 us (0.970)
  starting transfers between devices: 74.9 us -> 68.7 us
    ppermute x21, starting transfers between devices: 30 us -> 27.7 us  [swap_y(): return lax.ppermute(x, 'col', [(i, i ^ k) for i in range(4)])]
  transfers between devices with their start and end apart: 62 -> 62, of which waited for: 41 -> 43; matrix products, arithmetic and copies ran while one was open for 0% -> 0% of each run, Pallas kernels for 4% -> 4%
where the time goes in v6:
time: 194 us
  waiting for transfers between devices  79.6 us (41%)
  starting transfers between devices  68.7 us (35%)
  Pallas kernels  44.9 us (23%)
    pallas_call x25, Pallas kernels, call(): pl.pallas_call(kernel, out_shape=tuple((jax.ShapeDtypeStruct((n, TILE), F...  37.3 us
    ppermute x21, waiting for transfers between devices, swap_y(): return lax.ppermute(x, 'col', [(i, i ^ k) for i in range(4)])  29.2 us
    ppermute x21, starting transfers between devices, swap_y(): return lax.ppermute(x, 'col', [(i, i ^ k) for i in range(4)])  27.7 us
    ppermute x15, waiting for transfers between devices, swap_first(): lax.ppermute(x, 'scen', [(i, i ^ k << (1 if i % 2 else 3)) for i in range...  21.9 us
    ppermute x15, starting transfers between devices, swap_second(): lax.ppermute(x, 'scen', [(i, i ^ k << (3 if i % 2 else 1)) for i in range...  20.8 us
    ppermute x15, starting transfers between devices, swap_first(): lax.ppermute(x, 'scen', [(i, i ^ k << (1 if i % 2 else 3)) for i in range...  19.2 us
    ppermute x15, waiting for transfers between devices, swap_second(): lax.ppermute(x, 'scen', [(i, i ^ k << (3 if i % 2 else 1)) for i in range...  17.6 us
    ppermute x11, waiting for transfers between devices, swap_core(): return lax.ppermute(x, 'scen', [(i, i ^ 1) for i in range(32)])  10.9 us
  transfers between devices with their start and end apart: 62, of which 43 were waited for; matrix products, arithmetic and copies ran while one was open for 0% of the time, Pallas kernels for 4%

profile of v6, /device:TPU:0, one launch (start us, length us, event | category | flops | bytes accessed | tf_op | source)
XLA Modules:
  0.0 194.3 jit_solution(18115506903374452377)
XLA Ops:
  0.8 6.9 %shard_map.130 = (f32[192,256]{1,0:T(8,128)S(1)}, f32[136,256]{1,0:T(8,128)S(1)}, f32[128,256]{1,0:T(8,128)S(1)}, f32[64,256,256]{2,1,0:T(8,128)S(1)}) custom-call(s32[3]{0:T(128)S(1)} %pad_add_fusion.place, s32[64]{0:T(128)} %bitcast.20, s32[64]{0:T(128)} %bitcast.30, f32[64,256,256]{2,1,0:T(8,128)} %bitcast.44, f32[32,256]{1,0:T(8,128)} %bitcast.45, ...), custom_call_target="tpu_custom_call" | custom-call | tf_op jit(solution)/shard_map/pallas_call | solution.py:179
  9.2 3.2 %collective-permute-start.6 = (f32[128,256]{1,0:T(8,128)S(1)}, f32[128,256]{1,0:T(8,128)S(1)}, u32[]{:S(2)}, u32[]{:S(2)}) collective-permute-start(f32[128,256]{1,0:T(8,128)S(1)} %shard_map.131.own), channel_id=1, source_target_pairs={{0,64},{4,20},{8,72},{12,28},{16,80},{20,4},{24,88},{28,12},{32,96... | collective-permute-start | bytes 393224 | tf_op jit(solution)/shard_map/ppermute | solution.py:34
  18.6 4.0 %collective-permute-start.9 = (f32[128,256]{1,0:T(8,128)S(1)}, f32[128,256]{1,0:T(8,128)S(1)}, u32[]{:S(2)}, u32[]{:S(2)}) collective-permute-start(f32[128,256]{1,0:T(8,128)S(1)} %shard_map.132.own), channel_id=1, source_target_pairs={{0,16},{4,68},{8,24},{12,76},{16,0},{20,84},{24,8},{28,92},{32,48}... | collective-permute-start | bytes 393224 | tf_op jit(solution)/shard_map/ppermute | solution.py:38
  23.5 3.2 %collective-permute-start.2 = (f32[192,256]{1,0:T(8,128)S(1)}, f32[192,256]{1,0:T(8,128)S(1)}, u32[]{:S(2)}, u32[]{:S(2)}) collective-permute-start(f32[192,256]{1,0:T(8,128)S(1)} %get-tuple-element.58.r0), channel_id=1, source_target_pairs={{0,2},{1,3},{2,0},{3,1},{4,6},{5,7},{6,4},{7,5},{8,10},{9,11},{10,... | collective-permute-start | bytes 589832 | tf_op jit(solution)/shard_map/ppermute | solution.py:42
  28.8 2.9 %collective-permute-done.2.r2 = f32[192,256]{1,0:T(8,128)S(1)} collective-permute-done((f32[192,256]{1,0:T(8,128)S(1)}, f32[192,256]{1,0:T(8,128)S(1)}, u32[]{:S(2)}, u32[]{:S(2)}) %collective-permute-start.2) | collective-permute-done | bytes 196640 | tf_op jit(solution)/shard_map/ppermute | solution.py:42
  31.8 3.1 %collective-permute-done.1.r3 = f32[192,256]{1,0:T(8,128)S(1)} collective-permute-done((f32[192,256]{1,0:T(8,128)S(1)}, f32[192,256]{1,0:T(8,128)S(1)}, u32[]{:S(2)}, u32[]{:S(2)}) %collective-permute-start.1) | collective-permute-done | bytes 196640 | tf_op jit(solution)/shard_map/ppermute | solution.py:42
  34.9 5.8 %shard_map.134 = (f32[128,256]{1,0:T(8,128)S(1)}, f32[136,256]{1,0:T(8,128)S(1)}, f32[128,256]{1,0:T(8,128)S(1)}, f32[128,256]{1,0:T(8,128)S(1)}, f32[264,256]{1,0:T(8,128)S(1)}) custom-call(s32[64]{0:T(128)S(1)} %bitcast.21, s32[64]{0:T(128)S(1)} %bitcast.31, s32[3]{0:T(128)S(1)} %pad_add_fusion.place, f32[64,256,256]{2,1,0:T(8,128)S(1)} %get-tuple-element.57.tiles_ref, ...), custom_call_target="tpu_custom_call" | custom-call | tf_op jit(solution)/shard_map/pallas_call | solution.py:105
  48.4 3.4 %shard_map.136 = (f32[136,256]{1,0:T(8,128)S(1)}, f32[128,256]{1,0:T(8,128)S(1)}, f32[128,256]{1,0:T(8,128)S(1)}, f32[128,256]{1,0:T(8,128)S(1)}) custom-call(s32[64]{0:T(128)S(1)} %bitcast.22, s32[64]{0:T(128)S(1)} %bitcast.32, s32[3]{0:T(128)S(1)} %pad_add_fusion.place, f32[64,256,256]{2,1,0:T(8,128)S(1)} %get-tuple-element.57.tiles_ref, ...), custom_call_target="tpu_custom_call" | custom-call | tf_op jit(solution)/shard_map/pallas_call | solution.py:105
  53.9 3.1 %collective-permute-start.19 = (f32[160,256]{1,0:T(8,128)S(1)}, f32[160,256]{1,0:T(8,128)S(1)}, u32[]{:S(2)}, u32[]{:S(2)}) collective-permute-start(f32[160,256]{1,0:T(8,128)S(1)} %get-tuple-element.67), channel_id=1, source_target_pairs={{0,16},{4,68},{8,24},{12,76},{16,0},{20,84},{24,8},{28,92},{32,48}... | collective-permute-start | bytes 491528 | tf_op jit(solution)/shard_map/ppermute | solution.py:38
  67.2 3.6 %shard_map.139 = (f32[128,256]{1,0:T(8,128)S(1)}, f32[128,256]{1,0:T(8,128)S(1)}, f32[264,256]{1,0:T(8,128)S(1)}) custom-call(s32[64]{0:T(128)S(1)} %bitcast.23, s32[64]{0:T(128)S(1)} %bitcast.33, s32[3]{0:T(128)S(1)} %pad_add_fusion.place, f32[64,256,256]{2,1,0:T(8,128)S(1)} %get-tuple-element.57.tiles_ref, f32[128,256]{1,0:T(8,128)S(1)} %get-tuple-element.61.r0, ...), custom_call_target="tpu_custom_call" | custom-call | tf_op jit(solution)/shard_map/pallas_call | solution.py:105
  74.6 3.7 %shard_map.140 = (f32[136,256]{1,0:T(8,128)S(1)}, f32[128,256]{1,0:T(8,128)S(1)}) custom-call(s32[64]{0:T(128)S(1)} %bitcast.24, s32[64]{0:T(128)S(1)} %bitcast.34, s32[3]{0:T(128)S(1)} %pad_add_fusion.place, f32[64,256,256]{2,1,0:T(8,128)S(1)} %get-tuple-element.57.tiles_ref, f32[128,256]{1,0:T(8,128)S(1)} %get-tuple-element.74.row_scale.rowold), custom_call_target="tpu_custom_call" | custom-call | tf_op jit(solution)/shard_map/pallas_call | solution.py:105
  83.9 3.5 %collective-permute-done.29.r2 = f32[176,256]{1,0:T(8,128)S(1)} collective-permute-done((f32[176,256]{1,0:T(8,128)S(1)}, f32[176,256]{1,0:T(8,128)S(1)}, u32[]{:S(2)}, u32[]{:S(2)}) %collective-permute-start.29) | collective-permute-done | bytes 180256 | tf_op jit(solution)/shard_map/ppermute | solution.py:34
  89.4 3.1 %collective-permute-start.32 = (f32[176,256]{1,0:T(8,128)S(1)}, f32[176,256]{1,0:T(8,128)S(1)}, u32[]{:S(2)}, u32[]{:S(2)}) collective-permute-start(f32[176,256]{1,0:T(8,128)S(1)} %shard_map.142.own), channel_id=1, source_target_pairs={{0,16},{4,68},{8,24},{12,76},{16,0},{20,84},{24,8},{28,92},{32,48}... | collective-permute-start | bytes 540680 | tf_op jit(solution)/shard_map/ppermute | solution.py:38
  110.5 3.7 %shard_map.145 = (f32[8,256]{1,0:T(8,128)S(1)}, f32[128,256]{1,0:T(8,128)S(1)}, f32[264,256]{1,0:T(8,128)S(1)}) custom-call(s32[64]{0:T(128)S(1)} %bitcast.25, s32[64]{0:T(128)S(1)} %bitcast.35, s32[3]{0:T(128)S(1)} %pad_add_fusion.place, f32[64,256,256]{2,1,0:T(8,128)S(1)} %get-tuple-element.57.tiles_ref, f32[8,256]{1,0:T(8,128)S(1)} %get-tuple-element.82.rest_0_, ...), custom_call_target="tpu_custom_call" | custom-call | tf_op jit(solution)/shard_map/pallas_call | solution.py:105
  117.7 3.7 %collective-permute-done.39.r2 = f32[128,256]{1,0:T(8,128)S(1)} collective-permute-done((f32[128,256]{1,0:T(8,128)S(1)}, f32[128,256]{1,0:T(8,128)S(1)}, u32[]{:S(2)}, u32[]{:S(2)}) %collective-permute-start.39) | collective-permute-done | bytes 131104 | tf_op jit(solution)/shard_map/ppermute | solution.py:42
  122.5 3.4 %shard_map.146 = (f32[136,256]{1,0:T(8,128)S(1)}, f32[128,256]{1,0:T(8,128)S(1)}, f32[128,256]{1,0:T(8,128)S(1)}) custom-call(s32[64]{0:T(128)S(1)} %bitcast.26, s32[64]{0:T(128)S(1)} %bitcast.36, s32[3]{0:T(128)S(1)} %pad_add_fusion.place, f32[64,256,256]{2,1,0:T(8,128)S(1)} %get-tuple-element.57.tiles_ref, f32[8,256]{1,0:T(8,128)S(1)} %get-tuple-element.88.steps.rest_0_, ...), custom_call_target="tpu_custom_call" | custom-call | tf_op jit(solution)/shard_map/pallas_call | solution.py:105
  130.9 3.0 %collective-permute-done.43.r2 = f32[128,256]{1,0:T(8,128)S(1)} collective-permute-done((f32[128,256]{1,0:T(8,128)S(1)}, f32[128,256]{1,0:T(8,128)S(1)}, u32[]{:S(2)}, u32[]{:S(2)}) %collective-permute-start.43) | collective-permute-done | bytes 131104 | tf_op jit(solution)/shard_map/ppermute | solution.py:34
  139.4 3.0 %collective-permute-done.46.r2 = f32[128,256]{1,0:T(8,128)S(1)} collective-permute-done((f32[128,256]{1,0:T(8,128)S(1)}, f32[128,256]{1,0:T(8,128)S(1)}, u32[]{:S(2)}, u32[]{:S(2)}) %collective-permute-start.46) | collective-permute-done | bytes 131104 | tf_op jit(solution)/shard_map/ppermute | solution.py:38
  145.7 3.5 %shard_map.150 = (f32[128,256]{1,0:T(8,128)S(1)}, f32[264,256]{1,0:T(8,128)S(1)}) custom-call(s32[64]{0:T(128)S(1)} %bitcast.27, s32[64]{0:T(128)S(1)} %bitcast.37, s32[3]{0:T(128)S(1)} %pad_add_fusion.place, f32[64,256,256]{2,1,0:T(8,128)S(1)} %get-tuple-element.57.tiles_ref, f32[8,256]{1,0:T(8,128)S(1)} %get-tuple-element.88.steps.rest_0_, ...), custom_call_target="tpu_custom_call" | custom-call | tf_op jit(solution)/shard_map/pallas_call | solution.py:105
  152.8 4.4 %collective-permute-done.50.r2 = f32[128,256]{1,0:T(8,128)S(1)} collective-permute-done((f32[128,256]{1,0:T(8,128)S(1)}, f32[128,256]{1,0:T(8,128)S(1)}, u32[]{:S(2)}, u32[]{:S(2)}) %collective-permute-start.50) | collective-permute-done | bytes 131104 | tf_op jit(solution)/shard_map/ppermute | solution.py:42
  159.2 3.5 %shard_map.151 = (f32[136,256]{1,0:T(8,128)S(1)}, f32[128,256]{1,0:T(8,128)S(1)}, f32[128,256]{1,0:T(8,128)S(1)}) custom-call(s32[64]{0:T(128)S(1)} %bitcast.28, s32[64]{0:T(128)S(1)} %bitcast.38, s32[3]{0:T(128)S(1)} %pad_add_fusion.place, f32[64,256,256]{2,1,0:T(8,128)S(1)} %get-tuple-element.57.tiles_ref, f32[8,256]{1,0:T(8,128)S(1)} %get-tuple-element.88.steps.rest_0_, ...), custom_call_target="tpu_custom_call" | custom-call | tf_op jit(solution)/shard_map/pallas_call | solution.py:105
  167.7 3.0 %collective-permute-done.54.r2 = f32[128,256]{1,0:T(8,128)S(1)} collective-permute-done((f32[128,256]{1,0:T(8,128)S(1)}, f32[128,256]{1,0:T(8,128)S(1)}, u32[]{:S(2)}, u32[]{:S(2)}) %collective-permute-start.54) | collective-permute-done | bytes 131104 | tf_op jit(solution)/shard_map/ppermute | solution.py:34
  175.7 3.0 %collective-permute-done.57.r2 = f32[128,256]{1,0:T(8,128)S(1)} collective-permute-done((f32[128,256]{1,0:T(8,128)S(1)}, f32[128,256]{1,0:T(8,128)S(1)}, u32[]{:S(2)}, u32[]{:S(2)}) %collective-permute-start.57) | collective-permute-done | bytes 131104 | tf_op jit(solution)/shard_map/ppermute | solution.py:38
  182.0 4.2 %shard_map.155 = (f32[8,256]{1,0:T(8,128)}, f32[256,256]{1,0:T(8,128)}, f32[32,256]{1,0:T(8,128)S(1)}, f32[32,256]{1,0:T(8,128)S(1)}, f32[32,256]{1,0:T(8,128)S(...) custom-call(s32[64]{0:T(128)S(1)} %bitcast.29, ...), custom_call_target="tpu_custom_call" | custom-call | tf_op jit(solution)/shard_map/pallas_call | solution.py:105
  (144 shorter events, 105.4 us)
Async XLA Ops:
  9.2 6.6 %collective-permute-start.6 = (f32[128,256]{1,0:T(8,128)S(1)}, f32[128,256]{1,0:T(8,128)S(1)}, u32[]{:S(2)}, u32[]{:S(2)}) collective-permute-start(f32[128,256]{1,0:T(8,128)S(1)} %shard_map.131.own), channel_id=1, source_target_pairs={{0,64},{4,20},{8,72},{12,28},{16,80},{20,4},{24,88},{28,12},{32,96... | collective-permute-start | bytes 393224 | tf_op jit(solution)/shard_map/ppermute | solution.py:34
  18.6 9.2 %collective-permute-start.9 = (f32[128,256]{1,0:T(8,128)S(1)}, f32[128,256]{1,0:T(8,128)S(1)}, u32[]{:S(2)}, u32[]{:S(2)}) collective-permute-start(f32[128,256]{1,0:T(8,128)S(1)} %shard_map.132.own), channel_id=1, source_target_pairs={{0,16},{4,68},{8,24},{12,76},{16,0},{20,84},{24,8},{28,92},{32,48}... | collective-permute-start | bytes 393224 | tf_op jit(solution)/shard_map/ppermute | solution.py:38
  23.5 8.2 %collective-permute-start.2 = (f32[192,256]{1,0:T(8,128)S(1)}, f32[192,256]{1,0:T(8,128)S(1)}, u32[]{:S(2)}, u32[]{:S(2)}) collective-permute-start(f32[192,256]{1,0:T(8,128)S(1)} %get-tuple-element.58.r0), channel_id=1, source_target_pairs={{0,2},{1,3},{2,0},{3,1},{4,6},{5,7},{6,4},{7,5},{8,10},{9,11},{10,... | collective-permute-start | bytes 589832 | tf_op jit(solution)/shard_map/ppermute | solution.py:42
  26.7 8.1 %collective-permute-start.1 = (f32[192,256]{1,0:T(8,128)S(1)}, f32[192,256]{1,0:T(8,128)S(1)}, u32[]{:S(2)}, u32[]{:S(2)}) collective-permute-start(f32[192,256]{1,0:T(8,128)S(1)} %get-tuple-element.58.r0), channel_id=1, source_target_pairs={{0,3},{1,2},{2,1},{3,0},{4,7},{5,6},{6,5},{7,4},{8,11},{9,10},{10,... | collective-permute-start | bytes 589832 | tf_op jit(solution)/shard_map/ppermute | solution.py:42
  27.8 7.1 %collective-permute-start = (f32[192,256]{1,0:T(8,128)S(1)}, f32[192,256]{1,0:T(8,128)S(1)}, u32[]{:S(2)}, u32[]{:S(2)}) collective-permute-start(f32[192,256]{1,0:T(8,128)S(1)} %get-tuple-element.58.r0), channel_id=1, source_target_pairs={{0,1},{1,0},{2,3},{3,2},{4,5},{5,4},{6,7},{7,6},{8,9},{9,8},{10,11... | collective-permute-start | bytes 589832 | tf_op jit(solution)/shard_map/ppermute | solution.py:42
  44.3 7.6 %collective-permute-start.17 = (f32[128,256]{1,0:T(8,128)S(1)}, f32[128,256]{1,0:T(8,128)S(1)}, u32[]{:S(2)}, u32[]{:S(2)}) collective-permute-start(f32[128,256]{1,0:T(8,128)S(1)} %shard_map.135.own), channel_id=1, source_target_pairs={{0,64},{4,20},{8,72},{12,28},{16,80},{20,4},{24,88},{28,12},{32,96... | collective-permute-start | bytes 393224 | tf_op jit(solution)/shard_map/ppermute | solution.py:34
  53.9 8.1 %collective-permute-start.19 = (f32[160,256]{1,0:T(8,128)S(1)}, f32[160,256]{1,0:T(8,128)S(1)}, u32[]{:S(2)}, u32[]{:S(2)}) collective-permute-start(f32[160,256]{1,0:T(8,128)S(1)} %get-tuple-element.67), channel_id=1, source_target_pairs={{0,16},{4,68},{8,24},{12,76},{16,0},{20,84},{24,8},{28,92},{32,48}... | collective-permute-start | bytes 491528 | tf_op jit(solution)/shard_map/ppermute | solution.py:38
  57.0 6.5 %collective-permute-start.21 = (f32[160,256]{1,0:T(8,128)S(1)}, f32[160,256]{1,0:T(8,128)S(1)}, u32[]{:S(2)}, u32[]{:S(2)}) collective-permute-start(f32[160,256]{1,0:T(8,128)S(1)} %get-tuple-element.69), channel_id=1, source_target_pairs={{0,24},{4,100},{8,16},{12,108},{16,8},{20,116},{24,0},{28,124},{32... | collective-permute-start | bytes 491528 | tf_op jit(solution)/shard_map/ppermute | solution.py:38
  59.9 7.1 %collective-permute-start.12 = (f32[128,256]{1,0:T(8,128)S(1)}, f32[128,256]{1,0:T(8,128)S(1)}, u32[]{:S(2)}, u32[]{:S(2)}) collective-permute-start(f32[128,256]{1,0:T(8,128)S(1)} %get-tuple-element.61.r0), channel_id=1, source_target_pairs={{0,3},{1,2},{2,1},{3,0},{4,7},{5,6},{6,5},{7,4},{8,11},{9,10},{10,... | collective-permute-start | bytes 393224 | tf_op jit(solution)/shard_map/ppermute | solution.py:42
  70.7 7.7 %collective-permute-start.25 = (f32[128,256]{1,0:T(8,128)S(1)}, f32[128,256]{1,0:T(8,128)S(1)}, u32[]{:S(2)}, u32[]{:S(2)}) collective-permute-start(f32[128,256]{1,0:T(8,128)S(1)} %get-tuple-element.73.r0), channel_id=1, source_target_pairs={{0,2},{1,3},{2,0},{3,1},{4,6},{5,7},{6,4},{7,5},{8,10},{9,11},{10,... | collective-permute-start | bytes 393224 | tf_op jit(solution)/shard_map/ppermute | solution.py:42
  72.8 7.3 %collective-permute-start.24 = (f32[128,256]{1,0:T(8,128)S(1)}, f32[128,256]{1,0:T(8,128)S(1)}, u32[]{:S(2)}, u32[]{:S(2)}) collective-permute-start(f32[128,256]{1,0:T(8,128)S(1)} %get-tuple-element.73.r0), channel_id=1, source_target_pairs={{0,3},{1,2},{2,1},{3,0},{4,7},{5,6},{6,5},{7,4},{8,11},{9,10},{10,... | collective-permute-start | bytes 393224 | tf_op jit(solution)/shard_map/ppermute | solution.py:42
  80.3 7.1 %collective-permute-start.29 = (f32[176,256]{1,0:T(8,128)S(1)}, f32[176,256]{1,0:T(8,128)S(1)}, u32[]{:S(2)}, u32[]{:S(2)}) collective-permute-start(f32[176,256]{1,0:T(8,128)S(1)} %get-tuple-element.81.own), channel_id=1, source_target_pairs={{0,64},{4,20},{8,72},{12,28},{16,80},{20,4},{24,88},{28,12},{32,96... | collective-permute-start | bytes 540680 | tf_op jit(solution)/shard_map/ppermute | solution.py:34
  82.4 6.9 %collective-permute-start.28 = (f32[176,256]{1,0:T(8,128)S(1)}, f32[176,256]{1,0:T(8,128)S(1)}, u32[]{:S(2)}, u32[]{:S(2)}) collective-permute-start(f32[176,256]{1,0:T(8,128)S(1)} %get-tuple-element.81.own), channel_id=1, source_target_pairs={{0,96},{4,28},{8,104},{12,20},{16,112},{20,12},{24,120},{28,4},{32... | collective-permute-start | bytes 540680 | tf_op jit(solution)/shard_map/ppermute | solution.py:34
  89.4 7.1 %collective-permute-start.32 = (f32[176,256]{1,0:T(8,128)S(1)}, f32[176,256]{1,0:T(8,128)S(1)}, u32[]{:S(2)}, u32[]{:S(2)}) collective-permute-start(f32[176,256]{1,0:T(8,128)S(1)} %shard_map.142.own), channel_id=1, source_target_pairs={{0,16},{4,68},{8,24},{12,76},{16,0},{20,84},{24,8},{28,92},{32,48}... | collective-permute-start | bytes 540680 | tf_op jit(solution)/shard_map/ppermute | solution.py:38
  92.5 6.7 %collective-permute-start.31 = (f32[176,256]{1,0:T(8,128)S(1)}, f32[176,256]{1,0:T(8,128)S(1)}, u32[]{:S(2)}, u32[]{:S(2)}) collective-permute-start(f32[176,256]{1,0:T(8,128)S(1)} %shard_map.142.own), channel_id=1, source_target_pairs={{0,24},{4,100},{8,16},{12,108},{16,8},{20,116},{24,0},{28,124},{32... | collective-permute-start | bytes 540680 | tf_op jit(solution)/shard_map/ppermute | solution.py:38
  114.1 7.3 %collective-permute-start.39 = (f32[128,256]{1,0:T(8,128)S(1)}, f32[128,256]{1,0:T(8,128)S(1)}, u32[]{:S(2)}, u32[]{:S(2)}) collective-permute-start(f32[128,256]{1,0:T(8,128)S(1)} %get-tuple-element.89.r0), channel_id=1, source_target_pairs={{0,2},{1,3},{2,0},{3,1},{4,6},{5,7},{6,4},{7,5},{8,10},{9,11},{10,... | collective-permute-start | bytes 393224 | tf_op jit(solution)/shard_map/ppermute | solution.py:42
  115.3 7.2 %collective-permute-start.38 = (f32[128,256]{1,0:T(8,128)S(1)}, f32[128,256]{1,0:T(8,128)S(1)}, u32[]{:S(2)}, u32[]{:S(2)}) collective-permute-start(f32[128,256]{1,0:T(8,128)S(1)} %get-tuple-element.89.r0), channel_id=1, source_target_pairs={{0,3},{1,2},{2,1},{3,0},{4,7},{5,6},{6,5},{7,4},{8,11},{9,10},{10,... | collective-permute-start | bytes 393224 | tf_op jit(solution)/shard_map/ppermute | solution.py:42
  127.4 6.5 %collective-permute-start.43 = (f32[128,256]{1,0:T(8,128)S(1)}, f32[128,256]{1,0:T(8,128)S(1)}, u32[]{:S(2)}, u32[]{:S(2)}) collective-permute-start(f32[128,256]{1,0:T(8,128)S(1)} %shard_map.147.own), channel_id=1, source_target_pairs={{0,64},{4,20},{8,72},{12,28},{16,80},{20,4},{24,88},{28,12},{32,96... | collective-permute-start | bytes 393224 | tf_op jit(solution)/shard_map/ppermute | solution.py:34
  135.9 6.6 %collective-permute-start.46 = (f32[128,256]{1,0:T(8,128)S(1)}, f32[128,256]{1,0:T(8,128)S(1)}, u32[]{:S(2)}, u32[]{:S(2)}) collective-permute-start(f32[128,256]{1,0:T(8,128)S(1)} %shard_map.148.own), channel_id=1, source_target_pairs={{0,16},{4,68},{8,24},{12,76},{16,0},{20,84},{24,8},{28,92},{32,48}... | collective-permute-start | bytes 393224 | tf_op jit(solution)/shard_map/ppermute | solution.py:38
  149.3 7.9 %collective-permute-start.50 = (f32[128,256]{1,0:T(8,128)S(1)}, f32[128,256]{1,0:T(8,128)S(1)}, u32[]{:S(2)}, u32[]{:S(2)}) collective-permute-start(f32[128,256]{1,0:T(8,128)S(1)} %get-tuple-element.96.r0), channel_id=1, source_target_pairs={{0,2},{1,3},{2,0},{3,1},{4,6},{5,7},{6,4},{7,5},{8,10},{9,11},{10,... | collective-permute-start | bytes 393224 | tf_op jit(solution)/shard_map/ppermute | solution.py:42
  150.5 8.7 %collective-permute-start.49 = (f32[128,256]{1,0:T(8,128)S(1)}, f32[128,256]{1,0:T(8,128)S(1)}, u32[]{:S(2)}, u32[]{:S(2)}) collective-permute-start(f32[128,256]{1,0:T(8,128)S(1)} %get-tuple-element.96.r0), channel_id=1, source_target_pairs={{0,3},{1,2},{2,1},{3,0},{4,7},{5,6},{6,5},{7,4},{8,11},{9,10},{10,... | collective-permute-start | bytes 393224 | tf_op jit(solution)/shard_map/ppermute | solution.py:42
  152.4 6.8 %collective-permute-start.48 = (f32[128,256]{1,0:T(8,128)S(1)}, f32[128,256]{1,0:T(8,128)S(1)}, u32[]{:S(2)}, u32[]{:S(2)}) collective-permute-start(f32[128,256]{1,0:T(8,128)S(1)} %get-tuple-element.96.r0), channel_id=1, source_target_pairs={{0,1},{1,0},{2,3},{3,2},{4,5},{5,4},{6,7},{7,6},{8,9},{9,8},{10,11... | collective-permute-start | bytes 393224 | tf_op jit(solution)/shard_map/ppermute | solution.py:42
  164.1 6.6 %collective-permute-start.54 = (f32[128,256]{1,0:T(8,128)S(1)}, f32[128,256]{1,0:T(8,128)S(1)}, u32[]{:S(2)}, u32[]{:S(2)}) collective-permute-start(f32[128,256]{1,0:T(8,128)S(1)} %shard_map.152.own), channel_id=1, source_target_pairs={{0,64},{4,20},{8,72},{12,28},{16,80},{20,4},{24,88},{28,12},{32,96... | collective-permute-start | bytes 393224 | tf_op jit(solution)/shard_map/ppermute | solution.py:34
  172.1 6.6 %collective-permute-start.57 = (f32[128,256]{1,0:T(8,128)S(1)}, f32[128,256]{1,0:T(8,128)S(1)}, u32[]{:S(2)}, u32[]{:S(2)}) collective-permute-start(f32[128,256]{1,0:T(8,128)S(1)} %shard_map.153.own), channel_id=1, source_target_pairs={{0,16},{4,68},{8,24},{12,76},{16,0},{20,84},{24,8},{28,92},{32,48}... | collective-permute-start | bytes 393224 | tf_op jit(solution)/shard_map/ppermute | solution.py:38
  (46 other events, 344.1 us)

commit v7 on v6

--- a/solution.py
+++ b/solution.py
@@ -340,7 +340,11 @@
     out[...] = tree(op, own[...], (r1[...], r2[...], r3[...]))
 
 
-def merge_grad_kernel(place, tiles_ref, own, r1, r3, r2, gradown, gradgot, m0, m1, m2, m3, half):
+def merge_after_kernel(tiles_ref, own, r1, r3, r2, after, out):
+    out[...] = tree(jnp.maximum, own[...], (r1[...], r2[...], r3[...]))
+
+
+def merge_grad_kernel(place, tiles_ref, own, r1, r3, r2, gradown, gradgot, after, m0, m1, m2, m3, half):
     link = tree(jnp.maximum, own[...], (r1[...], r2[...], r3[...]))
     half[...] = gradown[CT:OWN] + gradgot[...]
     for k, out in enumerate((m0, m1, m2, m3)):
@@ -446,7 +450,7 @@
 
     rows = over(swap_y, row_part)
     (link,) = run(functools.partial(core_kernel, jnp.maximum), (), (colown, swap_core(colother)), (HALF,))
-    (link,) = run(functools.partial(merge_kernel, jnp.maximum), (), over(swap_first, link), (HALF,))
+    (link,) = run(merge_after_kernel, (), (*over(swap_first, link), rows[3]), (HALF,))
     (link,) = run(functools.partial(merge_kernel, jnp.maximum), (), over(swap_second, link), (HALF,))
 
     first_rows = rows
@@ -466,7 +470,7 @@
     sent = run(
         merge_grad_kernel,
         (place,),
-        (*got, gradown, swap_core(gradother)),
+        (*got, gradown, swap_core(gradother), rows[3]),
         (HALF + CHUNK,) * 4,
         (pltpu.VMEM((HALF, TILE), F32),),
     )

time: 194 us -> 189 us (0.974)
  waiting for transfers between devices: 79.6 us -> 75.9 us
  starting transfers between devices: 68.7 us -> 66.7 us
    ppermute x15, waiting for transfers between devices: 17.6 us -> 22.4 us  [swap_second(): lax.ppermute(x, 'scen', [(i, i ^ k << (3 if i % 2 else 1)) for i in range...]
    ppermute x21, waiting for transfers between devices: 29.2 us -> 24.7 us  [swap_y(): return lax.ppermute(x, 'col', [(i, i ^ k) for i in range(4)])]
    ppermute x15, waiting for transfers between devices: 21.9 us -> 19.3 us  [swap_first(): lax.ppermute(x, 'scen', [(i, i ^ k << (1 if i % 2 else 3)) for i in range...]
  transfers between devices with their start and end apart: 62 -> 62, of which waited for: 43 -> 47; matrix products, arithmetic and copies ran while one was open for 0% -> 0% of each run, Pallas kernels for 4% -> 4%
where the time goes in v7:
time: 189 us
  waiting for transfers between devices  75.9 us (40%)
  starting transfers between devices  66.7 us (35%)
  Pallas kernels  44.8 us (24%)
    pallas_call x25, Pallas kernels, call(): pl.pallas_call(kernel, out_shape=tuple((jax.ShapeDtypeStruct((n, TILE), F...  37.3 us
    ppermute x21, starting transfers between devices, swap_y(): return lax.ppermute(x, 'col', [(i, i ^ k) for i in range(4)])  26.5 us
    ppermute x21, waiting for transfers between devices, swap_y(): return lax.ppermute(x, 'col', [(i, i ^ k) for i in range(4)])  24.7 us
    ppermute x15, waiting for transfers between devices, swap_second(): lax.ppermute(x, 'scen', [(i, i ^ k << (3 if i % 2 else 1)) for i in range...  22.4 us
    ppermute x15, starting transfers between devices, swap_second(): lax.ppermute(x, 'scen', [(i, i ^ k << (3 if i % 2 else 1)) for i in range...  20.2 us
    ppermute x15, waiting for transfers between devices, swap_first(): lax.ppermute(x, 'scen', [(i, i ^ k << (1 if i % 2 else 3)) for i in range...  19.3 us
    ppermute x15, starting transfers between devices, swap_first(): lax.ppermute(x, 'scen', [(i, i ^ k << (1 if i % 2 else 3)) for i in range...  19.1 us
    ppermute x11, waiting for transfers between devices, swap_core(): return lax.ppermute(x, 'scen', [(i, i ^ 1) for i in range(32)])  9.53 us
  transfers between devices with their start and end apart: 62, of which 47 were waited for; matrix products, arithmetic and copies ran while one was open for 0% of the time, Pallas kernels for 4%

profile of v7, /device:TPU:0, one launch (start us, length us, event | category | flops | bytes accessed | tf_op | source)
XLA Modules:
  0.0 188.6 jit_solution(6405301208412284764)
XLA Ops:
  0.8 6.9 %shard_map.130 = (f32[192,256]{1,0:T(8,128)S(1)}, f32[136,256]{1,0:T(8,128)S(1)}, f32[128,256]{1,0:T(8,128)S(1)}, f32[64,256,256]{2,1,0:T(8,128)S(1)}) custom-call(s32[3]{0:T(128)S(1)} %pad_add_fusion.place, s32[64]{0:T(128)} %bitcast.20, s32[64]{0:T(128)} %bitcast.30, f32[64,256,256]{2,1,0:T(8,128)} %bitcast.44, f32[32,256]{1,0:T(8,128)} %bitcast.45, ...), custom_call_target="tpu_custom_call" | custom-call | tf_op jit(solution)/shard_map/pallas_call | solution.py:179
  7.8 3.4 %collective-permute-start.2 = (f32[192,256]{1,0:T(8,128)S(1)}, f32[192,256]{1,0:T(8,128)S(1)}, u32[]{:S(2)}, u32[]{:S(2)}) collective-permute-start(f32[192,256]{1,0:T(8,128)S(1)} %get-tuple-element.58.r0), channel_id=1, source_target_pairs={{0,2},{1,3},{2,0},{3,1},{4,6},{5,7},{6,4},{7,5},{8,10},{9,11},{10,... | collective-permute-start | bytes 589832 | tf_op jit(solution)/shard_map/ppermute | solution.py:42
  11.2 3.1 %collective-permute-start.6 = (f32[128,256]{1,0:T(8,128)S(1)}, f32[128,256]{1,0:T(8,128)S(1)}, u32[]{:S(2)}, u32[]{:S(2)}) collective-permute-start(f32[128,256]{1,0:T(8,128)S(1)} %shard_map.131.own), channel_id=1, source_target_pairs={{0,64},{4,20},{8,72},{12,28},{16,80},{20,4},{24,88},{28,12},{32,96... | collective-permute-start | bytes 393224 | tf_op jit(solution)/shard_map/ppermute | solution.py:34
  17.7 2.7 %collective-permute-done.5.r3 = f32[128,256]{1,0:T(8,128)S(1)} collective-permute-done((f32[128,256]{1,0:T(8,128)S(1)}, f32[128,256]{1,0:T(8,128)S(1)}, u32[]{:S(2)}, u32[]{:S(2)}) %collective-permute-start.5) | collective-permute-done | bytes 131104 | tf_op jit(solution)/shard_map/ppermute | solution.py:34
  20.5 4.0 %collective-permute-start.9 = (f32[128,256]{1,0:T(8,128)S(1)}, f32[128,256]{1,0:T(8,128)S(1)}, u32[]{:S(2)}, u32[]{:S(2)}) collective-permute-start(f32[128,256]{1,0:T(8,128)S(1)} %shard_map.132.own), channel_id=1, source_target_pairs={{0,16},{4,68},{8,24},{12,76},{16,0},{20,84},{24,8},{28,92},{32,48}... | collective-permute-start | bytes 393224 | tf_op jit(solution)/shard_map/ppermute | solution.py:38
  27.4 3.2 %collective-permute-done.8.r3 = f32[128,256]{1,0:T(8,128)S(1)} collective-permute-done((f32[128,256]{1,0:T(8,128)S(1)}, f32[128,256]{1,0:T(8,128)S(1)}, u32[]{:S(2)}, u32[]{:S(2)}) %collective-permute-start.8) | collective-permute-done | bytes 131104 | tf_op jit(solution)/shard_map/ppermute | solution.py:38
  32.4 5.8 %shard_map.134 = (f32[128,256]{1,0:T(8,128)S(1)}, f32[136,256]{1,0:T(8,128)S(1)}, f32[128,256]{1,0:T(8,128)S(1)}, f32[128,256]{1,0:T(8,128)S(1)}, f32[264,256]{1,0:T(8,128)S(1)}) custom-call(s32[64]{0:T(128)S(1)} %bitcast.21, s32[64]{0:T(128)S(1)} %bitcast.31, s32[3]{0:T(128)S(1)} %pad_add_fusion.place, f32[64,256,256]{2,1,0:T(8,128)S(1)} %get-tuple-element.57.tiles_ref, ...), custom_call_target="tpu_custom_call" | custom-call | tf_op jit(solution)/shard_map/pallas_call | solution.py:105
  45.9 3.4 %shard_map.136 = (f32[136,256]{1,0:T(8,128)S(1)}, f32[128,256]{1,0:T(8,128)S(1)}, f32[128,256]{1,0:T(8,128)S(1)}, f32[128,256]{1,0:T(8,128)S(1)}) custom-call(s32[64]{0:T(128)S(1)} %bitcast.22, s32[64]{0:T(128)S(1)} %bitcast.32, s32[3]{0:T(128)S(1)} %pad_add_fusion.place, f32[64,256,256]{2,1,0:T(8,128)S(1)} %get-tuple-element.57.tiles_ref, ...), custom_call_target="tpu_custom_call" | custom-call | tf_op jit(solution)/shard_map/pallas_call | solution.py:105
  51.4 3.8 %collective-permute-start.19 = (f32[160,256]{1,0:T(8,128)S(1)}, f32[160,256]{1,0:T(8,128)S(1)}, u32[]{:S(2)}, u32[]{:S(2)}) collective-permute-start(f32[160,256]{1,0:T(8,128)S(1)} %get-tuple-element.67), channel_id=1, source_target_pairs={{0,16},{4,68},{8,24},{12,76},{16,0},{20,84},{24,8},{28,92},{32,48}... | collective-permute-start | bytes 491528 | tf_op jit(solution)/shard_map/ppermute | solution.py:38
  63.1 3.6 %shard_map.139 = (f32[128,256]{1,0:T(8,128)S(1)}, f32[128,256]{1,0:T(8,128)S(1)}, f32[264,256]{1,0:T(8,128)S(1)}) custom-call(s32[64]{0:T(128)S(1)} %bitcast.23, s32[64]{0:T(128)S(1)} %bitcast.33, s32[3]{0:T(128)S(1)} %pad_add_fusion.place, f32[64,256,256]{2,1,0:T(8,128)S(1)} %get-tuple-element.57.tiles_ref, f32[128,256]{1,0:T(8,128)S(1)} %get-tuple-element.61.r0, ...), custom_call_target="tpu_custom_call" | custom-call | tf_op jit(solution)/shard_map/pallas_call | solution.py:105
  70.3 3.7 %shard_map.140 = (f32[136,256]{1,0:T(8,128)S(1)}, f32[128,256]{1,0:T(8,128)S(1)}) custom-call(s32[64]{0:T(128)S(1)} %bitcast.24, s32[64]{0:T(128)S(1)} %bitcast.34, s32[3]{0:T(128)S(1)} %pad_add_fusion.place, f32[64,256,256]{2,1,0:T(8,128)S(1)} %get-tuple-element.57.tiles_ref, f32[128,256]{1,0:T(8,128)S(1)} %get-tuple-element.74.row_scale.rowold), custom_call_target="tpu_custom_call" | custom-call | tf_op jit(solution)/shard_map/pallas_call | solution.py:105
  80.4 3.6 %collective-permute-done.29.r2 = f32[176,256]{1,0:T(8,128)S(1)} collective-permute-done((f32[176,256]{1,0:T(8,128)S(1)}, f32[176,256]{1,0:T(8,128)S(1)}, u32[]{:S(2)}, u32[]{:S(2)}) %collective-permute-start.29) | collective-permute-done | bytes 180256 | tf_op jit(solution)/shard_map/ppermute | solution.py:34
  89.5 3.5 %collective-permute-done.32.r2 = f32[176,256]{1,0:T(8,128)S(1)} collective-permute-done((f32[176,256]{1,0:T(8,128)S(1)}, f32[176,256]{1,0:T(8,128)S(1)}, u32[]{:S(2)}, u32[]{:S(2)}) %collective-permute-start.32) | collective-permute-done | bytes 180256 | tf_op jit(solution)/shard_map/ppermute | solution.py:38
  105.2 3.7 %shard_map.145 = (f32[8,256]{1,0:T(8,128)S(1)}, f32[128,256]{1,0:T(8,128)S(1)}, f32[264,256]{1,0:T(8,128)S(1)}) custom-call(s32[64]{0:T(128)S(1)} %bitcast.25, s32[64]{0:T(128)S(1)} %bitcast.35, s32[3]{0:T(128)S(1)} %pad_add_fusion.place, f32[64,256,256]{2,1,0:T(8,128)S(1)} %get-tuple-element.57.tiles_ref, f32[8,256]{1,0:T(8,128)S(1)} %get-tuple-element.82.rest_0_, ...), custom_call_target="tpu_custom_call" | custom-call | tf_op jit(solution)/shard_map/pallas_call | solution.py:105
  112.5 4.2 %collective-permute-done.39.r2 = f32[128,256]{1,0:T(8,128)S(1)} collective-permute-done((f32[128,256]{1,0:T(8,128)S(1)}, f32[128,256]{1,0:T(8,128)S(1)}, u32[]{:S(2)}, u32[]{:S(2)}) %collective-permute-start.39) | collective-permute-done | bytes 131104 | tf_op jit(solution)/shard_map/ppermute | solution.py:42
  117.4 3.4 %shard_map.146 = (f32[136,256]{1,0:T(8,128)S(1)}, f32[128,256]{1,0:T(8,128)S(1)}, f32[128,256]{1,0:T(8,128)S(1)}) custom-call(s32[64]{0:T(128)S(1)} %bitcast.26, s32[64]{0:T(128)S(1)} %bitcast.36, s32[3]{0:T(128)S(1)} %pad_add_fusion.place, f32[64,256,256]{2,1,0:T(8,128)S(1)} %get-tuple-element.57.tiles_ref, f32[8,256]{1,0:T(8,128)S(1)} %get-tuple-element.88.steps.rest_0_, ...), custom_call_target="tpu_custom_call" | custom-call | tf_op jit(solution)/shard_map/pallas_call | solution.py:105
  125.9 3.0 %collective-permute-done.43.r2 = f32[128,256]{1,0:T(8,128)S(1)} collective-permute-done((f32[128,256]{1,0:T(8,128)S(1)}, f32[128,256]{1,0:T(8,128)S(1)}, u32[]{:S(2)}, u32[]{:S(2)}) %collective-permute-start.43) | collective-permute-done | bytes 131104 | tf_op jit(solution)/shard_map/ppermute | solution.py:34
  133.9 3.0 %collective-permute-done.46.r2 = f32[128,256]{1,0:T(8,128)S(1)} collective-permute-done((f32[128,256]{1,0:T(8,128)S(1)}, f32[128,256]{1,0:T(8,128)S(1)}, u32[]{:S(2)}, u32[]{:S(2)}) %collective-permute-start.46) | collective-permute-done | bytes 131104 | tf_op jit(solution)/shard_map/ppermute | solution.py:38
  140.1 3.5 %shard_map.150 = (f32[128,256]{1,0:T(8,128)S(1)}, f32[264,256]{1,0:T(8,128)S(1)}) custom-call(s32[64]{0:T(128)S(1)} %bitcast.27, s32[64]{0:T(128)S(1)} %bitcast.37, s32[3]{0:T(128)S(1)} %pad_add_fusion.place, f32[64,256,256]{2,1,0:T(8,128)S(1)} %get-tuple-element.57.tiles_ref, f32[8,256]{1,0:T(8,128)S(1)} %get-tuple-element.88.steps.rest_0_, ...), custom_call_target="tpu_custom_call" | custom-call | tf_op jit(solution)/shard_map/pallas_call | solution.py:105
  147.2 4.4 %collective-permute-done.50.r2 = f32[128,256]{1,0:T(8,128)S(1)} collective-permute-done((f32[128,256]{1,0:T(8,128)S(1)}, f32[128,256]{1,0:T(8,128)S(1)}, u32[]{:S(2)}, u32[]{:S(2)}) %collective-permute-start.50) | collective-permute-done | bytes 131104 | tf_op jit(solution)/shard_map/ppermute | solution.py:42
  153.6 3.5 %shard_map.151 = (f32[136,256]{1,0:T(8,128)S(1)}, f32[128,256]{1,0:T(8,128)S(1)}, f32[128,256]{1,0:T(8,128)S(1)}) custom-call(s32[64]{0:T(128)S(1)} %bitcast.28, s32[64]{0:T(128)S(1)} %bitcast.38, s32[3]{0:T(128)S(1)} %pad_add_fusion.place, f32[64,256,256]{2,1,0:T(8,128)S(1)} %get-tuple-element.57.tiles_ref, f32[8,256]{1,0:T(8,128)S(1)} %get-tuple-element.88.steps.rest_0_, ...), custom_call_target="tpu_custom_call" | custom-call | tf_op jit(solution)/shard_map/pallas_call | solution.py:105
  162.1 3.0 %collective-permute-done.54.r2 = f32[128,256]{1,0:T(8,128)S(1)} collective-permute-done((f32[128,256]{1,0:T(8,128)S(1)}, f32[128,256]{1,0:T(8,128)S(1)}, u32[]{:S(2)}, u32[]{:S(2)}) %collective-permute-start.54) | collective-permute-done | bytes 131104 | tf_op jit(solution)/shard_map/ppermute | solution.py:34
  170.4 3.0 %collective-permute-done.57.r2 = f32[128,256]{1,0:T(8,128)S(1)} collective-permute-done((f32[128,256]{1,0:T(8,128)S(1)}, f32[128,256]{1,0:T(8,128)S(1)}, u32[]{:S(2)}, u32[]{:S(2)}) %collective-permute-start.57) | collective-permute-done | bytes 131104 | tf_op jit(solution)/shard_map/ppermute | solution.py:38
  176.3 4.2 %shard_map.155 = (f32[8,256]{1,0:T(8,128)}, f32[256,256]{1,0:T(8,128)}, f32[32,256]{1,0:T(8,128)S(1)}, f32[32,256]{1,0:T(8,128)S(1)}, f32[32,256]{1,0:T(8,128)S(...) custom-call(s32[64]{0:T(128)S(1)} %bitcast.29, ...), custom_call_target="tpu_custom_call" | custom-call | tf_op jit(solution)/shard_map/pallas_call | solution.py:105
  (144 shorter events, 98.0 us)
Async XLA Ops:
  7.8 8.8 %collective-permute-start.2 = (f32[192,256]{1,0:T(8,128)S(1)}, f32[192,256]{1,0:T(8,128)S(1)}, u32[]{:S(2)}, u32[]{:S(2)}) collective-permute-start(f32[192,256]{1,0:T(8,128)S(1)} %get-tuple-element.58.r0), channel_id=1, source_target_pairs={{0,2},{1,3},{2,0},{3,1},{4,6},{5,7},{6,4},{7,5},{8,10},{9,11},{10,... | collective-permute-start | bytes 589832 | tf_op jit(solution)/shard_map/ppermute | solution.py:42
  11.2 6.6 %collective-permute-start.6 = (f32[128,256]{1,0:T(8,128)S(1)}, f32[128,256]{1,0:T(8,128)S(1)}, u32[]{:S(2)}, u32[]{:S(2)}) collective-permute-start(f32[128,256]{1,0:T(8,128)S(1)} %shard_map.131.own), channel_id=1, source_target_pairs={{0,64},{4,20},{8,72},{12,28},{16,80},{20,4},{24,88},{28,12},{32,96... | collective-permute-start | bytes 393224 | tf_op jit(solution)/shard_map/ppermute | solution.py:34
  20.5 6.9 %collective-permute-start.9 = (f32[128,256]{1,0:T(8,128)S(1)}, f32[128,256]{1,0:T(8,128)S(1)}, u32[]{:S(2)}, u32[]{:S(2)}) collective-permute-start(f32[128,256]{1,0:T(8,128)S(1)} %shard_map.132.own), channel_id=1, source_target_pairs={{0,16},{4,68},{8,24},{12,76},{16,0},{20,84},{24,8},{28,92},{32,48}... | collective-permute-start | bytes 393224 | tf_op jit(solution)/shard_map/ppermute | solution.py:38
  25.5 6.9 %collective-permute-start.1 = (f32[192,256]{1,0:T(8,128)S(1)}, f32[192,256]{1,0:T(8,128)S(1)}, u32[]{:S(2)}, u32[]{:S(2)}) collective-permute-start(f32[192,256]{1,0:T(8,128)S(1)} %get-tuple-element.58.r0), channel_id=1, source_target_pairs={{0,3},{1,2},{2,1},{3,0},{4,7},{5,6},{6,5},{7,4},{8,11},{9,10},{10,... | collective-permute-start | bytes 589832 | tf_op jit(solution)/shard_map/ppermute | solution.py:42
  41.7 7.7 %collective-permute-start.13 = (f32[128,256]{1,0:T(8,128)S(1)}, f32[128,256]{1,0:T(8,128)S(1)}, u32[]{:S(2)}, u32[]{:S(2)}) collective-permute-start(f32[128,256]{1,0:T(8,128)S(1)} %get-tuple-element.61.r0), channel_id=1, source_target_pairs={{0,2},{1,3},{2,0},{3,1},{4,6},{5,7},{6,4},{7,5},{8,10},{9,11},{10,... | collective-permute-start | bytes 393224 | tf_op jit(solution)/shard_map/ppermute | solution.py:42
  43.3 6.5 %collective-permute-start.17 = (f32[128,256]{1,0:T(8,128)S(1)}, f32[128,256]{1,0:T(8,128)S(1)}, u32[]{:S(2)}, u32[]{:S(2)}) collective-permute-start(f32[128,256]{1,0:T(8,128)S(1)} %shard_map.135.own), channel_id=1, source_target_pairs={{0,64},{4,20},{8,72},{12,28},{16,80},{20,4},{24,88},{28,12},{32,96... | collective-permute-start | bytes 393224 | tf_op jit(solution)/shard_map/ppermute | solution.py:34
  51.4 7.1 %collective-permute-start.19 = (f32[160,256]{1,0:T(8,128)S(1)}, f32[160,256]{1,0:T(8,128)S(1)}, u32[]{:S(2)}, u32[]{:S(2)}) collective-permute-start(f32[160,256]{1,0:T(8,128)S(1)} %get-tuple-element.67), channel_id=1, source_target_pairs={{0,16},{4,68},{8,24},{12,76},{16,0},{20,84},{24,8},{28,92},{32,48}... | collective-permute-start | bytes 491528 | tf_op jit(solution)/shard_map/ppermute | solution.py:38
  55.1 6.5 %collective-permute-start.21 = (f32[160,256]{1,0:T(8,128)S(1)}, f32[160,256]{1,0:T(8,128)S(1)}, u32[]{:S(2)}, u32[]{:S(2)}) collective-permute-start(f32[160,256]{1,0:T(8,128)S(1)} %get-tuple-element.69), channel_id=1, source_target_pairs={{0,24},{4,100},{8,16},{12,108},{16,8},{20,116},{24,0},{28,124},{32... | collective-permute-start | bytes 491528 | tf_op jit(solution)/shard_map/ppermute | solution.py:38
  66.7 7.8 %collective-permute-start.25 = (f32[128,256]{1,0:T(8,128)S(1)}, f32[128,256]{1,0:T(8,128)S(1)}, u32[]{:S(2)}, u32[]{:S(2)}) collective-permute-start(f32[128,256]{1,0:T(8,128)S(1)} %get-tuple-element.73.r0), channel_id=1, source_target_pairs={{0,2},{1,3},{2,0},{3,1},{4,6},{5,7},{6,4},{7,5},{8,10},{9,11},{10,... | collective-permute-start | bytes 393224 | tf_op jit(solution)/shard_map/ppermute | solution.py:42
  68.3 8.3 %collective-permute-start.24 = (f32[128,256]{1,0:T(8,128)S(1)}, f32[128,256]{1,0:T(8,128)S(1)}, u32[]{:S(2)}, u32[]{:S(2)}) collective-permute-start(f32[128,256]{1,0:T(8,128)S(1)} %get-tuple-element.73.r0), channel_id=1, source_target_pairs={{0,3},{1,2},{2,1},{3,0},{4,7},{5,6},{6,5},{7,4},{8,11},{9,10},{10,... | collective-permute-start | bytes 393224 | tf_op jit(solution)/shard_map/ppermute | solution.py:42
  76.9 7.2 %collective-permute-start.29 = (f32[176,256]{1,0:T(8,128)S(1)}, f32[176,256]{1,0:T(8,128)S(1)}, u32[]{:S(2)}, u32[]{:S(2)}) collective-permute-start(f32[176,256]{1,0:T(8,128)S(1)} %get-tuple-element.81.own), channel_id=1, source_target_pairs={{0,64},{4,20},{8,72},{12,28},{16,80},{20,4},{24,88},{28,12},{32,96... | collective-permute-start | bytes 540680 | tf_op jit(solution)/shard_map/ppermute | solution.py:34
  78.3 7.6 %collective-permute-start.28 = (f32[176,256]{1,0:T(8,128)S(1)}, f32[176,256]{1,0:T(8,128)S(1)}, u32[]{:S(2)}, u32[]{:S(2)}) collective-permute-start(f32[176,256]{1,0:T(8,128)S(1)} %get-tuple-element.81.own), channel_id=1, source_target_pairs={{0,96},{4,28},{8,104},{12,20},{16,112},{20,12},{24,120},{28,4},{32... | collective-permute-start | bytes 540680 | tf_op jit(solution)/shard_map/ppermute | solution.py:34
  79.5 6.4 %collective-permute-start.27 = (f32[176,256]{1,0:T(8,128)S(1)}, f32[176,256]{1,0:T(8,128)S(1)}, u32[]{:S(2)}, u32[]{:S(2)}) collective-permute-start(f32[176,256]{1,0:T(8,128)S(1)} %get-tuple-element.81.own), channel_id=1, source_target_pairs={{0,32},{4,12},{8,40},{12,4},{16,48},{20,28},{24,56},{28,20},{32,0}... | collective-permute-start | bytes 540680 | tf_op jit(solution)/shard_map/ppermute | solution.py:34
  85.9 7.1 %collective-permute-start.32 = (f32[176,256]{1,0:T(8,128)S(1)}, f32[176,256]{1,0:T(8,128)S(1)}, u32[]{:S(2)}, u32[]{:S(2)}) collective-permute-start(f32[176,256]{1,0:T(8,128)S(1)} %shard_map.142.own), channel_id=1, source_target_pairs={{0,16},{4,68},{8,24},{12,76},{16,0},{20,84},{24,8},{28,92},{32,48}... | collective-permute-start | bytes 540680 | tf_op jit(solution)/shard_map/ppermute | solution.py:38
  88.1 6.9 %collective-permute-start.31 = (f32[176,256]{1,0:T(8,128)S(1)}, f32[176,256]{1,0:T(8,128)S(1)}, u32[]{:S(2)}, u32[]{:S(2)}) collective-permute-start(f32[176,256]{1,0:T(8,128)S(1)} %shard_map.142.own), channel_id=1, source_target_pairs={{0,24},{4,100},{8,16},{12,108},{16,8},{20,116},{24,0},{28,124},{32... | collective-permute-start | bytes 540680 | tf_op jit(solution)/shard_map/ppermute | solution.py:38
  108.9 7.8 %collective-permute-start.39 = (f32[128,256]{1,0:T(8,128)S(1)}, f32[128,256]{1,0:T(8,128)S(1)}, u32[]{:S(2)}, u32[]{:S(2)}) collective-permute-start(f32[128,256]{1,0:T(8,128)S(1)} %get-tuple-element.89.r0), channel_id=1, source_target_pairs={{0,2},{1,3},{2,0},{3,1},{4,6},{5,7},{6,4},{7,5},{8,10},{9,11},{10,... | collective-permute-start | bytes 393224 | tf_op jit(solution)/shard_map/ppermute | solution.py:42
  110.4 7.0 %collective-permute-start.38 = (f32[128,256]{1,0:T(8,128)S(1)}, f32[128,256]{1,0:T(8,128)S(1)}, u32[]{:S(2)}, u32[]{:S(2)}) collective-permute-start(f32[128,256]{1,0:T(8,128)S(1)} %get-tuple-element.89.r0), channel_id=1, source_target_pairs={{0,3},{1,2},{2,1},{3,0},{4,7},{5,6},{6,5},{7,4},{8,11},{9,10},{10,... | collective-permute-start | bytes 393224 | tf_op jit(solution)/shard_map/ppermute | solution.py:42
  122.3 6.6 %collective-permute-start.43 = (f32[128,256]{1,0:T(8,128)S(1)}, f32[128,256]{1,0:T(8,128)S(1)}, u32[]{:S(2)}, u32[]{:S(2)}) collective-permute-start(f32[128,256]{1,0:T(8,128)S(1)} %shard_map.147.own), channel_id=1, source_target_pairs={{0,64},{4,20},{8,72},{12,28},{16,80},{20,4},{24,88},{28,12},{32,96... | collective-permute-start | bytes 393224 | tf_op jit(solution)/shard_map/ppermute | solution.py:34
  130.3 6.6 %collective-permute-start.46 = (f32[128,256]{1,0:T(8,128)S(1)}, f32[128,256]{1,0:T(8,128)S(1)}, u32[]{:S(2)}, u32[]{:S(2)}) collective-permute-start(f32[128,256]{1,0:T(8,128)S(1)} %shard_map.148.own), channel_id=1, source_target_pairs={{0,16},{4,68},{8,24},{12,76},{16,0},{20,84},{24,8},{28,92},{32,48}... | collective-permute-start | bytes 393224 | tf_op jit(solution)/shard_map/ppermute | solution.py:38
  143.7 7.9 %collective-permute-start.50 = (f32[128,256]{1,0:T(8,128)S(1)}, f32[128,256]{1,0:T(8,128)S(1)}, u32[]{:S(2)}, u32[]{:S(2)}) collective-permute-start(f32[128,256]{1,0:T(8,128)S(1)} %get-tuple-element.96.r0), channel_id=1, source_target_pairs={{0,2},{1,3},{2,0},{3,1},{4,6},{5,7},{6,4},{7,5},{8,10},{9,11},{10,... | collective-permute-start | bytes 393224 | tf_op jit(solution)/shard_map/ppermute | solution.py:42
  145.1 8.5 %collective-permute-start.49 = (f32[128,256]{1,0:T(8,128)S(1)}, f32[128,256]{1,0:T(8,128)S(1)}, u32[]{:S(2)}, u32[]{:S(2)}) collective-permute-start(f32[128,256]{1,0:T(8,128)S(1)} %get-tuple-element.96.r0), channel_id=1, source_target_pairs={{0,3},{1,2},{2,1},{3,0},{4,7},{5,6},{6,5},{7,4},{8,11},{9,10},{10,... | collective-permute-start | bytes 393224 | tf_op jit(solution)/shard_map/ppermute | solution.py:42
  146.8 6.8 %collective-permute-start.48 = (f32[128,256]{1,0:T(8,128)S(1)}, f32[128,256]{1,0:T(8,128)S(1)}, u32[]{:S(2)}, u32[]{:S(2)}) collective-permute-start(f32[128,256]{1,0:T(8,128)S(1)} %get-tuple-element.96.r0), channel_id=1, source_target_pairs={{0,1},{1,0},{2,3},{3,2},{4,5},{5,4},{6,7},{7,6},{8,9},{9,8},{10,11... | collective-permute-start | bytes 393224 | tf_op jit(solution)/shard_map/ppermute | solution.py:42
  158.5 6.5 %collective-permute-start.54 = (f32[128,256]{1,0:T(8,128)S(1)}, f32[128,256]{1,0:T(8,128)S(1)}, u32[]{:S(2)}, u32[]{:S(2)}) collective-permute-start(f32[128,256]{1,0:T(8,128)S(1)} %shard_map.152.own), channel_id=1, source_target_pairs={{0,64},{4,20},{8,72},{12,28},{16,80},{20,4},{24,88},{28,12},{32,96... | collective-permute-start | bytes 393224 | tf_op jit(solution)/shard_map/ppermute | solution.py:34
  166.8 6.6 %collective-permute-start.57 = (f32[128,256]{1,0:T(8,128)S(1)}, f32[128,256]{1,0:T(8,128)S(1)}, u32[]{:S(2)}, u32[]{:S(2)}) collective-permute-start(f32[128,256]{1,0:T(8,128)S(1)} %shard_map.153.own), channel_id=1, source_target_pairs={{0,16},{4,68},{8,24},{12,76},{16,0},{20,84},{24,8},{28,92},{32,48}... | collective-permute-start | bytes 393224 | tf_op jit(solution)/shard_map/ppermute | solution.py:38
  (46 other events, 325.5 us)

commit v8 on v7

--- a/solution.py
+++ b/solution.py
@@ -95,12 +95,14 @@
 ROWS = pltpu.VMEM((2, RT, LANES), F32)
 COLS = pltpu.VMEM((2, CW, LANES), F32)
 OWN = CT + HALF
+PLACE = 2 * NT
 EIGHT = 2 * CT
 CHUNK = HALF // 4
 
 
 def call(kernel, smem, tiles, operands, outs, scratch=()):
     operands = [pltpu.with_memory_space_constraint(tiles, pltpu.VMEM)] + list(operands)
+    smem = [pltpu.with_memory_space_constraint(x, pltpu.SMEM) for x in smem]
     vmem = pl.BlockSpec(memory_space=pltpu.VMEM)
     return pl.pallas_call(
         kernel,
@@ -112,17 +114,13 @@
     )(*smem, *operands)
 
 
-def each_tile(rows_ref, cols_ref, place_ref, visit, ready=None):
-    turn = place_ref[0] * HALF
-
+def each_tile(index_ref, visit, ready=None):
     def group(step, carry):
         if ready is not None:
             ready(step)
         for i in range(GROUP):
             t = step * GROUP + i
-            col = cols_ref[t]
-            col = jnp.where(col < CT, col, CT + ((col - CT) ^ turn))
-            visit(t, col, rows_ref[t])
+            visit(t, index_ref[NT + t], index_ref[t])
         return carry
 
     lax.fori_loop(0, STEPS, group, 0)
@@ -134,7 +132,7 @@
 
 
 def first_stats_kernel(
-    place, rows_hbm, cols_hbm, source, rhs, dual, rowout, colown, colother, tiles_ref, racc, cacc,
+    place, rows_hbm, cols_hbm, source, rhs, dual, rowout, colown, colother, tiles_ref, index_ref, racc, cacc,
     rows_ref, cols_ref, sems,
 ):
     indices = [
@@ -143,6 +141,8 @@
     ]
     for copy in indices:
         copy.start()
+    for i in range(3):
+        index_ref[PLACE + i] = place[i]
 
     def load(step):
         part = pl.ds(step * GROUP, GROUP)
@@ -161,12 +161,21 @@
 
     for copy in indices:
         copy.wait()
+    turn = place[0] * HALF
+
+    def enter(t, carry):
+        col = cols_ref[t]
+        index_ref[t] = rows_ref[t]
+        index_ref[NT + t] = jnp.where(col < CT, col, CT + ((col - CT) ^ turn))
+        return carry
+
+    lax.fori_loop(0, NT, enter, 0)
 
     def visit(t, col, row):
         row_pass(tiles_ref, t, col, row, None, racc, jnp.maximum, True)
         col_pass(tiles_ref, t, col, row, None, cacc, jnp.maximum, True)
 
-    each_tile(rows_ref, cols_ref, place, visit, lambda step: load(step).wait())
+    each_tile(index_ref, visit, lambda step: load(step).wait())
     join_from(racc, rowout, 0, RT)
     put_columns(cacc, colown, colother)
     for copy in extra:
@@ -178,9 +187,9 @@
     shapes = [jax.ShapeDtypeStruct((n, TILE), F32) for n in (RT + 2 * SHARE, OWN, HALF)]
     return pl.pallas_call(
         first_stats_kernel,
-        out_shape=(*shapes, pltpu.VMEM((NT, TILE, TILE), F32)),
+        out_shape=(*shapes, pltpu.VMEM((NT, TILE, TILE), F32), pltpu.SMEM((PLACE + 8,), jnp.int32)),
         in_specs=[pl.BlockSpec(memory_space=pltpu.SMEM)] + [pl.BlockSpec(memory_space=pltpu.HBM)] * 5,
-        out_specs=(vmem,) * 4,
+        out_specs=(vmem,) * 4 + (pl.BlockSpec(memory_space=pltpu.SMEM),),
         scratch_shapes=[
             ROWS,
             COLS,
@@ -193,7 +202,7 @@
 
 
 def second_stats_kernel(
-    rows_ref, cols_ref, place, tiles_ref, r0, r1, r3, r2, loc, mine, other, rowout, colown, colother, rownew,
+    index_ref, tiles_ref, r0, r1, r3, r2, loc, mine, other, rowout, colown, colother, rownew,
     colnew, racc, cacc, rowf, colf,
 ):
     row = tree(jnp.maximum, r0[0:RT], (r1[0:RT], r2[0:RT], r3[0:RT]))
@@ -211,13 +220,13 @@
         row_pass(tiles_ref, t, col, row, colf, racc, jnp.maximum, True)
         col_pass(tiles_ref, t, col, row, rowf, cacc, jnp.maximum, True)
 
-    each_tile(rows_ref, cols_ref, place, visit)
+    each_tile(index_ref, visit)
     join_from(racc, rowout, 0, RT)
     put_columns(cacc, colown, colother)
 
 
 def third_rows_kernel(
-    rows_ref, cols_ref, place, tiles_ref, r0, r1, r3, r2, loc, mine, other, rowold, colold, rowout, rownew,
+    index_ref, tiles_ref, r0, r1, r3, r2, loc, mine, other, rowold, colold, rowout, rownew,
     colnew, racc, colf,
 ):
     row = tree(jnp.maximum, r0[...], (r1[...], r2[...], r3[...]))
@@ -233,26 +242,26 @@
     def visit(t, col, row):
         row_pass(tiles_ref, t, col, row, colf, racc, jnp.add, True)
 
-    each_tile(rows_ref, cols_ref, place, visit)
+    each_tile(index_ref, visit)
     join_from(racc, rowout, 0, RT)
 
 
-def third_columns_kernel(rows_ref, cols_ref, place, tiles_ref, row_scale, colown, colother, cacc, rowf):
+def third_columns_kernel(index_ref, tiles_ref, row_scale, colown, colother, cacc, rowf):
     split_to(rowf, row_scale[...])
     cacc[...] = jnp.zeros_like(cacc)
 
     def visit(t, col, row):
         col_pass(tiles_ref, t, col, row, rowf, cacc, jnp.add, True)
 
-    each_tile(rows_ref, cols_ref, place, visit)
+    each_tile(index_ref, visit)
     put_columns(cacc, colown, colother)
 
 
 def first_backward_kernel(
-    rows_ref, cols_ref, place, tiles_ref, r0, r1, r3, r2, after, colown, colother, rhsout, dualout, cacc, work
+    index_ref, tiles_ref, r0, r1, r3, r2, after, colown, colother, rhsout, dualout, cacc, work
 ):
     for k, ref in enumerate((r0, r1, r2, r3)):
-        at = pl.ds(pl.multiple_of((place[2] ^ k) * SHARE, SHARE), SHARE)
+        at = pl.ds(pl.multiple_of((index_ref[PLACE + 2] ^ k) * SHARE, SHARE), SHARE)
         rhsout[at, :] = ref[RT : RT + SHARE]
         dualout[at, :] = ref[RT + SHARE :]
     split_to(work, dualout[...])
@@ -261,12 +270,12 @@
     def visit(t, col, row):
         col_pass(tiles_ref, t, col, row, work, cacc, jnp.add, False)
 
-    each_tile(rows_ref, cols_ref, place, visit)
+    each_tile(index_ref, visit)
     put_columns(cacc, colown, colother)
 
 
 def backward_kernel(
-    rows_ref, cols_ref, place, tiles_ref, steps, r0, r1, r3, r2, dual, rhs, rowf, colown, colother, dualnew,
+    index_ref, tiles_ref, steps, r0, r1, r3, r2, dual, rhs, rowf, colown, colother, dualnew,
     cacc, work,
 ):
     total = tree(jnp.add, r0[...], (r1[...], r2[...], r3[...]))
@@ -278,11 +287,11 @@
     def visit(t, col, row):
         col_pass(tiles_ref, t, col, row, work, cacc, jnp.add, False)
 
-    each_tile(rows_ref, cols_ref, place, visit)
+    each_tile(index_ref, visit)
     put_columns(cacc, colown, colother)
 
 
-def forward_kernel(index, grad_at, rows_ref, cols_ref, place, tiles_ref, *rest):
+def forward_kernel(index, grad_at, index_ref, tiles_ref, *rest):
     if index == 0:
         c0, c1, c3, c2, rhs_square, *rest = rest
     else:
@@ -301,7 +310,7 @@
         rowout, fresh, racc, work = rest
     else:
         dual, rhs, rowf, local, link, dualout, rhsout, rowfout, p0, p1, p2, p3, racc, work = rest
-        own = pl.ds(pl.multiple_of(place[2] * SHARE, SHARE), SHARE)
+        own = pl.ds(pl.multiple_of(index_ref[PLACE + 2] * SHARE, SHARE), SHARE)
         for ref, out in ((dual, dualout), (rhs, rhsout), (rowf, rowfout)):
             out[...] = ref[own, :]
     for lo, hi, src, first in ((0, CT, loc, 0), (CT, OWN, mine, grad_at), (OWN, CW, other, grad_at)):
@@ -314,7 +323,7 @@
         elif lo == 0:
             local[...] = scale * new
         else:
-            half = place[0] if lo == CT else 1 - place[0]
+            half = index_ref[PLACE + 0] if lo == CT else 1 - index_ref[PLACE + 0]
             link[pl.ds(pl.multiple_of(half * HALF, HALF), HALF), :] = scale * new
         split_to(work, scale * (2.0 * new - x), lo)
     racc[...] = jnp.zeros_like(racc)
@@ -322,12 +331,12 @@
     def visit(t, col, row):
         row_pass(tiles_ref, t, col, row, work, racc, jnp.add, False)
 
-    each_tile(rows_ref, cols_ref, place, visit)
+    each_tile(index_ref, visit)
     if index < ITERS - 1:
         join_from(racc, rowout, 0, RT)
     else:
         for k, out in enumerate((p0, p1, p2, p3)):
-            at = pl.ds(pl.multiple_of((place[2] ^ k) * SHARE, SHARE), SHARE)
+            at = pl.ds(pl.multiple_of((index_ref[PLACE + 2] ^ k) * SHARE, SHARE), SHARE)
             for w in range(2):
                 out[:, w * LANES : (w + 1) * LANES] = racc[w, at, :]
 
@@ -344,12 +353,12 @@
     out[...] = tree(jnp.maximum, own[...], (r1[...], r2[...], r3[...]))
 
 
-def merge_grad_kernel(place, tiles_ref, own, r1, r3, r2, gradown, gradgot, after, m0, m1, m2, m3, half):
+def merge_grad_kernel(index_ref, tiles_ref, own, r1, r3, r2, gradown, gradgot, after, m0, m1, m2, m3, half):
     link = tree(jnp.maximum, own[...], (r1[...], r2[...], r3[...]))
     half[...] = gradown[CT:OWN] + gradgot[...]
     for k, out in enumerate((m0, m1, m2, m3)):
         out[0:HALF] = link
-        out[HALF:] = half[pl.ds(pl.multiple_of((place[1] ^ k) * CHUNK, CHUNK), CHUNK), :]
+        out[HALF:] = half[pl.ds(pl.multiple_of((index_ref[PLACE + 1] ^ k) * CHUNK, CHUNK), CHUNK), :]
 
 
 def merge_chunk_kernel(tiles_ref, own, r2, r1, r3, link, chunk):
@@ -376,16 +385,16 @@
     out[OWN + CT :] = chunk[...]
 
 
-def merge_all_kernel(place, tiles_ref, own, r1, r3, r2, out):
+def merge_all_kernel(index_ref, tiles_ref, own, r1, r3, r2, out):
     at = slice(0, HALF + EIGHT)
     out[at] = tree(jnp.add, own[at], (r1[at], r2[at], r3[at]))
     for k, ref in enumerate((own, r1, r2, r3)):
-        start = pl.multiple_of((place[1] ^ k) * CHUNK, CHUNK)
+        start = pl.multiple_of((index_ref[PLACE + 1] ^ k) * CHUNK, CHUNK)
         out[pl.ds(HALF + EIGHT + start, CHUNK), :] = ref[HALF + EIGHT :]
 
 
 def setup_kernel(
-    place, tiles_ref, own, back, colown, colold, cost_loc, cost_lnk, bound_loc, bound_lnk, start_loc, start_lnk,
+    index_ref, tiles_ref, own, back, colown, colold, cost_loc, cost_lnk, bound_loc, bound_lnk, start_loc, start_lnk,
     colnew, cost, upper, primal, rhs_square, cost_square,
 ):
     squares = own[HALF : HALF + EIGHT] + back[HALF : HALF + EIGHT]
@@ -393,8 +402,8 @@
     sums = []
     for lo, hi, stat, half in (
         (0, CT, colown, None),
-        (CT, OWN, own, place[0]),
-        (OWN, CW, back, 1 - place[0]),
+        (CT, OWN, own, index_ref[PLACE + 0]),
+        (OWN, CW, back, 1 - index_ref[PLACE + 0]),
     ):
         at = slice(lo, hi)
         if half is None:
@@ -443,7 +452,7 @@
         got = {k: swap(x, k) for k in (2, 1, 3)}
         return x, got[1], got[3], got[2]
 
-    row_part, colown, colother, tiles = first_stats(ids, tile_values[0, 0], rhs[0], start_dual[0])
+    row_part, colown, colother, tiles, index = first_stats(ids, tile_values[0, 0], rhs[0], start_dual[0])
 
     def run(kernel, smem, operands, outs, scratch=()):
         return call(kernel, smem, tiles, operands, outs, scratch)
@@ -456,7 +465,7 @@
     first_rows = rows
     row_part, colown, colother, row_scale, col_scale = run(
         second_stats_kernel,
-        ids,
+        (index,),
         (*rows, colown, link, swap_core(link)),
         (RT, OWN, HALF, RT, CW),
         (ROWS, COLS, ROWS, COLS),
@@ -465,11 +474,11 @@
     (link,) = run(functools.partial(core_kernel, jnp.maximum), (), (colown, swap_core(colother)), (HALF,))
     got = over(swap_first, link)
     gradown, gradother, rhs_rows, dual_rows = run(
-        first_backward_kernel, ids, (*first_rows, got[2]), (OWN, HALF, RT, RT), (COLS, ROWS)
+        first_backward_kernel, (index,), (*first_rows, got[2]), (OWN, HALF, RT, RT), (COLS, ROWS)
     )
     sent = run(
         merge_grad_kernel,
-        (place,),
+        (index,),
         (*got, gradown, swap_core(gradother), rows[3]),
         (HALF + CHUNK,) * 4,
         (pltpu.VMEM((HALF, TILE), F32),),
@@ -479,13 +488,13 @@
 
     row_part, row_scale, col_scale = run(
         third_rows_kernel,
-        ids,
+        (index,),
         (*rows, colown, link, swap_core(link), row_scale, col_scale),
         (RT, RT, CW),
         (ROWS, COLS),
     )
     rows = over(swap_y, row_part)
-    colown, colother = run(third_columns_kernel, ids, (row_scale,), (OWN, HALF), (COLS, ROWS))
+    colown, colother = run(third_columns_kernel, (index,), (row_scale,), (OWN, HALF), (COLS, ROWS))
     row_scale, rhs_scaled, dual_scaled, both = run(
         rows_kernel,
         (),
@@ -495,11 +504,11 @@
     (both,) = run(
         functools.partial(merge_kernel, jnp.add), (), over(swap_first, both), (HALF + EIGHT + CHUNK,)
     )
-    (mine,) = run(merge_all_kernel, (place,), over(swap_second, both), (LT + EIGHT,))
+    (mine,) = run(merge_all_kernel, (index,), over(swap_second, both), (LT + EIGHT,))
     other = swap_core(mine)
     col_scale, cost, upper, primal, rhs_square, cost_square = run(
         setup_kernel,
-        (place,),
+        (index,),
         (
             mine,
             other,
@@ -517,25 +526,25 @@
     norms = (*over(swap_y, cost_square), rhs_square)
 
     grads, grad_at = (gradown, mine, other), HALF + EIGHT
-    for index in range(ITERS):
-        given = norms if index == 0 else (steps,)
-        extra = (dual_scaled, rhs_scaled, row_scale) if index == ITERS - 1 else ()
-        outs = (RT, CW) if index < ITERS - 1 else (CT, LT) + (SHARE,) * 7
+    for step in range(ITERS):
+        given = norms if step == 0 else (steps,)
+        extra = (dual_scaled, rhs_scaled, row_scale) if step == ITERS - 1 else ()
+        outs = (RT, CW) if step < ITERS - 1 else (CT, LT) + (SHARE,) * 7
         result = run(
-            functools.partial(forward_kernel, index, grad_at),
-            ids,
+            functools.partial(forward_kernel, step, grad_at),
+            (index,),
             (*given, *grads, primal, cost, upper, col_scale, *extra),
-            ((CT,) if index == 0 else ()) + outs,
+            ((CT,) if step == 0 else ()) + outs,
             (ROWS, COLS),
         )
-        if index == 0:
+        if step == 0:
             steps, *result = result
-        if index == ITERS - 1:
+        if step == ITERS - 1:
             break
         row_part, primal = result
         colown, colother, dual_scaled = run(
             backward_kernel,
-            ids,
+            (index,),
             (steps, *over(swap_y, row_part), dual_scaled, rhs_scaled, row_scale),
             (OWN, HALF, RT),
             (COLS, ROWS),

time: 189 us -> 182 us (0.963)
  Pallas kernels: 44.8 us -> 38.2 us
    pallas_call x25, Pallas kernels: 37.3 us -> 30.6 us  [call(): pl.pallas_call(kernel, out_shape=tuple((jax.ShapeDtypeStruct((n, TILE), F...]
  transfers between devices with their start and end apart: 62 -> 62, of which waited for: 47 -> 47; matrix products, arithmetic and copies ran while one was open for 0% -> 0% of each run, Pallas kernels for 4% -> 3%
where the time goes in v8:
time: 182 us
  waiting for transfers between devices  76.2 us (42%)
  starting transfers between devices  66.9 us (37%)
  Pallas kernels  38.2 us (21%)
    pallas_call x25, Pallas kernels, call(): pl.pallas_call(kernel, out_shape=tuple((jax.ShapeDtypeStruct((n, TILE), F...  30.6 us
    ppermute x21, starting transfers between devices, swap_y(): return lax.ppermute(x, 'col', [(i, i ^ k) for i in range(4)])  26.7 us
    ppermute x21, waiting for transfers between devices, swap_y(): return lax.ppermute(x, 'col', [(i, i ^ k) for i in range(4)])  25.3 us
    ppermute x15, waiting for transfers between devices, swap_second(): lax.ppermute(x, 'scen', [(i, i ^ k << (3 if i % 2 else 1)) for i in range...  22.3 us
    ppermute x15, starting transfers between devices, swap_second(): lax.ppermute(x, 'scen', [(i, i ^ k << (3 if i % 2 else 1)) for i in range...  20.1 us
    ppermute x15, waiting for transfers between devices, swap_first(): lax.ppermute(x, 'scen', [(i, i ^ k << (1 if i % 2 else 3)) for i in range...  19.6 us
    ppermute x15, starting transfers between devices, swap_first(): lax.ppermute(x, 'scen', [(i, i ^ k << (1 if i % 2 else 3)) for i in range...  19.1 us
    ppermute x11, waiting for transfers between devices, swap_core(): return lax.ppermute(x, 'scen', [(i, i ^ 1) for i in range(32)])  8.96 us
  transfers between devices with their start and end apart: 62, of which 47 were waited for; matrix products, arithmetic and copies ran while one was open for 0% of the time, Pallas kernels for 3%

profile of v8, /device:TPU:0, one launch (start us, length us, event | category | flops | bytes accessed | tf_op | source)
XLA Modules:
  0.0 182.3 jit_solution(2587703424011918093)
XLA Ops:
  0.8 6.9 %shard_map.130 = (f32[192,256]{1,0:T(8,128)S(1)}, f32[136,256]{1,0:T(8,128)S(1)}, f32[128,256]{1,0:T(8,128)S(1)}, f32[64,256,256]{2,1,0:T(8,128)S(1)}, s32[136]{0:T(256)S(4)}) custom-call(s32[3]{0:T(128)S(1)} %pad_add_fusion.place, s32[64]{0:T(128)} %bitcast.28, s32[64]{0:T(128)} %bitcast.29, f32[64,256,256]{2,1,0:T(8,128)} %bitcast.24, f32[32,256]{1,0:T(8,128)} %bitcast.25, ...), custom_call_target="tpu_custom_call" | custom-call | tf_op jit(solution)/shard_map/pallas_call | solution.py:188
  7.8 3.4 %collective-permute-start.2 = (f32[192,256]{1,0:T(8,128)S(1)}, f32[192,256]{1,0:T(8,128)S(1)}, u32[]{:S(2)}, u32[]{:S(2)}) collective-permute-start(f32[192,256]{1,0:T(8,128)S(1)} %get-tuple-element.60.r0), channel_id=1, source_target_pairs={{0,2},{1,3},{2,0},{3,1},{4,6},{5,7},{6,4},{7,5},{8,10},{9,11},{10,... | collective-permute-start | bytes 589832 | tf_op jit(solution)/shard_map/ppermute | solution.py:42
  11.2 3.1 %collective-permute-start.6 = (f32[128,256]{1,0:T(8,128)S(1)}, f32[128,256]{1,0:T(8,128)S(1)}, u32[]{:S(2)}, u32[]{:S(2)}) collective-permute-start(f32[128,256]{1,0:T(8,128)S(1)} %shard_map.131.own), channel_id=1, source_target_pairs={{0,64},{4,20},{8,72},{12,28},{16,80},{20,4},{24,88},{28,12},{32,96... | collective-permute-start | bytes 393224 | tf_op jit(solution)/shard_map/ppermute | solution.py:34
  17.7 2.7 %collective-permute-done.5.r3 = f32[128,256]{1,0:T(8,128)S(1)} collective-permute-done((f32[128,256]{1,0:T(8,128)S(1)}, f32[128,256]{1,0:T(8,128)S(1)}, u32[]{:S(2)}, u32[]{:S(2)}) %collective-permute-start.5) | collective-permute-done | bytes 131104 | tf_op jit(solution)/shard_map/ppermute | solution.py:34
  20.5 4.0 %collective-permute-start.9 = (f32[128,256]{1,0:T(8,128)S(1)}, f32[128,256]{1,0:T(8,128)S(1)}, u32[]{:S(2)}, u32[]{:S(2)}) collective-permute-start(f32[128,256]{1,0:T(8,128)S(1)} %shard_map.132.own), channel_id=1, source_target_pairs={{0,16},{4,68},{8,24},{12,76},{16,0},{20,84},{24,8},{28,92},{32,48}... | collective-permute-start | bytes 393224 | tf_op jit(solution)/shard_map/ppermute | solution.py:38
  27.4 3.2 %collective-permute-done.8.r3 = f32[128,256]{1,0:T(8,128)S(1)} collective-permute-done((f32[128,256]{1,0:T(8,128)S(1)}, f32[128,256]{1,0:T(8,128)S(1)}, u32[]{:S(2)}, u32[]{:S(2)}) %collective-permute-start.8) | collective-permute-done | bytes 131104 | tf_op jit(solution)/shard_map/ppermute | solution.py:38
  32.3 5.2 %shard_map.134 = (f32[128,256]{1,0:T(8,128)S(1)}, f32[136,256]{1,0:T(8,128)S(1)}, f32[128,256]{1,0:T(8,128)S(1)}, f32[128,256]{1,0:T(8,128)S(1)}, f32[264,256]{1,0:T(8,128)S(1)}) custom-call(s32[136]{0:T(256)S(4)} %get-tuple-element.58.index_ref, f32[64,256,256]{2,1,0:T(8,128)S(1)} %get-tuple-element.59.tiles_ref, f32[192,256]{1,0:T(8,128)S(1)} %get-tuple-element.60.r0, ...), custom_call_target="tpu_custom_call" | custom-call | tf_op jit(solution)/shard_map/pallas_call | solution.py:107
  45.3 2.9 %shard_map.136 = (f32[136,256]{1,0:T(8,128)S(1)}, f32[128,256]{1,0:T(8,128)S(1)}, f32[128,256]{1,0:T(8,128)S(1)}, f32[128,256]{1,0:T(8,128)S(1)}) custom-call(s32[136]{0:T(256)S(4)} %get-tuple-element.58.index_ref, f32[64,256,256]{2,1,0:T(8,128)S(1)} %get-tuple-element.59.tiles_ref, f32[192,256]{1,0:T(8,128)S(1)} %get-tuple-element.60.r0, ...), custom_call_target="tpu_custom_call" | custom-call | tf_op jit(solution)/shard_map/pallas_call | solution.py:107
  49.7 3.8 %collective-permute-start.19 = (f32[160,256]{1,0:T(8,128)S(1)}, f32[160,256]{1,0:T(8,128)S(1)}, u32[]{:S(2)}, u32[]{:S(2)}) collective-permute-start(f32[160,256]{1,0:T(8,128)S(1)} %get-tuple-element.69), channel_id=1, source_target_pairs={{0,16},{4,68},{8,24},{12,76},{16,0},{20,84},{24,8},{28,92},{32,48}... | collective-permute-start | bytes 491528 | tf_op jit(solution)/shard_map/ppermute | solution.py:38
  61.4 3.0 %shard_map.139 = (f32[128,256]{1,0:T(8,128)S(1)}, f32[128,256]{1,0:T(8,128)S(1)}, f32[264,256]{1,0:T(8,128)S(1)}) custom-call(s32[136]{0:T(256)S(4)} %get-tuple-element.58.index_ref, f32[64,256,256]{2,1,0:T(8,128)S(1)} %get-tuple-element.59.tiles_ref, f32[128,256]{1,0:T(8,128)S(1)} %get-tuple-element.63.r0, f32[128,256]{1,0:T(8,128)S(1)} %collective-permute-done.11.r1, ...), custom_call_target="tpu_custom_call" | custom-call | tf_op jit(solution)/shard_map/pallas_call | solution.py:107
  68.1 3.2 %shard_map.140 = (f32[136,256]{1,0:T(8,128)S(1)}, f32[128,256]{1,0:T(8,128)S(1)}) custom-call(s32[136]{0:T(256)S(4)} %get-tuple-element.58.index_ref, f32[64,256,256]{2,1,0:T(8,128)S(1)} %get-tuple-element.59.tiles_ref, f32[128,256]{1,0:T(8,128)S(1)} %get-tuple-element.76.row_scale.rowold), custom_call_target="tpu_custom_call" | custom-call | tf_op jit(solution)/shard_map/pallas_call | solution.py:107
  78.2 3.6 %collective-permute-done.29.r2 = f32[176,256]{1,0:T(8,128)S(1)} collective-permute-done((f32[176,256]{1,0:T(8,128)S(1)}, f32[176,256]{1,0:T(8,128)S(1)}, u32[]{:S(2)}, u32[]{:S(2)}) %collective-permute-start.29) | collective-permute-done | bytes 180256 | tf_op jit(solution)/shard_map/ppermute | solution.py:34
  87.2 3.5 %collective-permute-done.32.r2 = f32[176,256]{1,0:T(8,128)S(1)} collective-permute-done((f32[176,256]{1,0:T(8,128)S(1)}, f32[176,256]{1,0:T(8,128)S(1)}, u32[]{:S(2)}, u32[]{:S(2)}) %collective-permute-start.32) | collective-permute-done | bytes 180256 | tf_op jit(solution)/shard_map/ppermute | solution.py:38
  101.9 3.1 %shard_map.145 = (f32[8,256]{1,0:T(8,128)S(1)}, f32[128,256]{1,0:T(8,128)S(1)}, f32[264,256]{1,0:T(8,128)S(1)}) custom-call(s32[136]{0:T(256)S(4)} %get-tuple-element.58.index_ref, f32[64,256,256]{2,1,0:T(8,128)S(1)} %get-tuple-element.59.tiles_ref, f32[8,256]{1,0:T(8,128)S(1)} %get-tuple-element.84.rest_0_, f32[8,256]{1,0:T(8,128)S(1)} %collective-permute-done.34.rest_1_, ...), custom_call_target="tpu_custom_call" | custom-call | tf_op jit(solution)/shard_map/pallas_call | solution.py:107
  108.6 4.1 %collective-permute-done.39.r2 = f32[128,256]{1,0:T(8,128)S(1)} collective-permute-done((f32[128,256]{1,0:T(8,128)S(1)}, f32[128,256]{1,0:T(8,128)S(1)}, u32[]{:S(2)}, u32[]{:S(2)}) %collective-permute-start.39) | collective-permute-done | bytes 131104 | tf_op jit(solution)/shard_map/ppermute | solution.py:42
  113.6 2.9 %shard_map.146 = (f32[136,256]{1,0:T(8,128)S(1)}, f32[128,256]{1,0:T(8,128)S(1)}, f32[128,256]{1,0:T(8,128)S(1)}) custom-call(s32[136]{0:T(256)S(4)} %get-tuple-element.58.index_ref, f32[64,256,256]{2,1,0:T(8,128)S(1)} %get-tuple-element.59.tiles_ref, f32[8,256]{1,0:T(8,128)S(1)} %get-tuple-element.90.steps.rest_0_, f32[128,256]{1,0:T(8,128)S(1)} %get-tuple-element.91.r0, ...), custom_call_target="tpu_custom_call" | custom-call | tf_op jit(solution)/shard_map/pallas_call | solution.py:107
  121.5 3.0 %collective-permute-done.43.r2 = f32[128,256]{1,0:T(8,128)S(1)} collective-permute-done((f32[128,256]{1,0:T(8,128)S(1)}, f32[128,256]{1,0:T(8,128)S(1)}, u32[]{:S(2)}, u32[]{:S(2)}) %collective-permute-start.43) | collective-permute-done | bytes 131104 | tf_op jit(solution)/shard_map/ppermute | solution.py:34
  129.5 3.0 %collective-permute-done.46.r2 = f32[128,256]{1,0:T(8,128)S(1)} collective-permute-done((f32[128,256]{1,0:T(8,128)S(1)}, f32[128,256]{1,0:T(8,128)S(1)}, u32[]{:S(2)}, u32[]{:S(2)}) %collective-permute-start.46) | collective-permute-done | bytes 131104 | tf_op jit(solution)/shard_map/ppermute | solution.py:38
  135.6 3.0 %shard_map.150 = (f32[128,256]{1,0:T(8,128)S(1)}, f32[264,256]{1,0:T(8,128)S(1)}) custom-call(s32[136]{0:T(256)S(4)} %get-tuple-element.58.index_ref, f32[64,256,256]{2,1,0:T(8,128)S(1)} %get-tuple-element.59.tiles_ref, f32[8,256]{1,0:T(8,128)S(1)} %get-tuple-element.90.steps.rest_0_, f32[136,256]{1,0:T(8,128)S(1)} %get-tuple-element.95.colown.rest_1_, ...), custom_call_target="tpu_custom_call" | custom-call | tf_op jit(solution)/shard_map/pallas_call | solution.py:107
  142.2 4.4 %collective-permute-done.50.r2 = f32[128,256]{1,0:T(8,128)S(1)} collective-permute-done((f32[128,256]{1,0:T(8,128)S(1)}, f32[128,256]{1,0:T(8,128)S(1)}, u32[]{:S(2)}, u32[]{:S(2)}) %collective-permute-start.50) | collective-permute-done | bytes 131104 | tf_op jit(solution)/shard_map/ppermute | solution.py:42
  148.5 2.9 %shard_map.151 = (f32[136,256]{1,0:T(8,128)S(1)}, f32[128,256]{1,0:T(8,128)S(1)}, f32[128,256]{1,0:T(8,128)S(1)}) custom-call(s32[136]{0:T(256)S(4)} %get-tuple-element.58.index_ref, f32[64,256,256]{2,1,0:T(8,128)S(1)} %get-tuple-element.59.tiles_ref, f32[8,256]{1,0:T(8,128)S(1)} %get-tuple-element.90.steps.rest_0_, f32[128,256]{1,0:T(8,128)S(1)} %get-tuple-element.98.r0, ...), custom_call_target="tpu_custom_call" | custom-call | tf_op jit(solution)/shard_map/pallas_call | solution.py:107
  156.5 3.0 %collective-permute-done.54.r2 = f32[128,256]{1,0:T(8,128)S(1)} collective-permute-done((f32[128,256]{1,0:T(8,128)S(1)}, f32[128,256]{1,0:T(8,128)S(1)}, u32[]{:S(2)}, u32[]{:S(2)}) %collective-permute-start.54) | collective-permute-done | bytes 131104 | tf_op jit(solution)/shard_map/ppermute | solution.py:34
  164.8 3.0 %collective-permute-done.57.r2 = f32[128,256]{1,0:T(8,128)S(1)} collective-permute-done((f32[128,256]{1,0:T(8,128)S(1)}, f32[128,256]{1,0:T(8,128)S(1)}, u32[]{:S(2)}, u32[]{:S(2)}) %collective-permute-start.57) | collective-permute-done | bytes 131104 | tf_op jit(solution)/shard_map/ppermute | solution.py:38
  170.7 3.7 %shard_map.155 = (f32[8,256]{1,0:T(8,128)}, f32[256,256]{1,0:T(8,128)}, f32[32,256]{1,0:T(8,128)S(1)}, f32[32,256]{1,0:T(8,128)S(1)}, f32[32,256]{1,0:T(8,128)S(...) custom-call(s32[136]{0:T(256)S(4)} %get-tuple-element.58.index_ref, ...), custom_call_target="tpu_custom_call" | custom-call | tf_op jit(solution)/shard_map/pallas_call | solution.py:107
  (140 shorter events, 97.0 us)
Async XLA Ops:
  7.8 8.8 %collective-permute-start.2 = (f32[192,256]{1,0:T(8,128)S(1)}, f32[192,256]{1,0:T(8,128)S(1)}, u32[]{:S(2)}, u32[]{:S(2)}) collective-permute-start(f32[192,256]{1,0:T(8,128)S(1)} %get-tuple-element.60.r0), channel_id=1, source_target_pairs={{0,2},{1,3},{2,0},{3,1},{4,6},{5,7},{6,4},{7,5},{8,10},{9,11},{10,... | collective-permute-start | bytes 589832 | tf_op jit(solution)/shard_map/ppermute | solution.py:42
  11.2 6.6 %collective-permute-start.6 = (f32[128,256]{1,0:T(8,128)S(1)}, f32[128,256]{1,0:T(8,128)S(1)}, u32[]{:S(2)}, u32[]{:S(2)}) collective-permute-start(f32[128,256]{1,0:T(8,128)S(1)} %shard_map.131.own), channel_id=1, source_target_pairs={{0,64},{4,20},{8,72},{12,28},{16,80},{20,4},{24,88},{28,12},{32,96... | collective-permute-start | bytes 393224 | tf_op jit(solution)/shard_map/ppermute | solution.py:34
  20.5 6.9 %collective-permute-start.9 = (f32[128,256]{1,0:T(8,128)S(1)}, f32[128,256]{1,0:T(8,128)S(1)}, u32[]{:S(2)}, u32[]{:S(2)}) collective-permute-start(f32[128,256]{1,0:T(8,128)S(1)} %shard_map.132.own), channel_id=1, source_target_pairs={{0,16},{4,68},{8,24},{12,76},{16,0},{20,84},{24,8},{28,92},{32,48}... | collective-permute-start | bytes 393224 | tf_op jit(solution)/shard_map/ppermute | solution.py:38
  25.5 6.9 %collective-permute-start.1 = (f32[192,256]{1,0:T(8,128)S(1)}, f32[192,256]{1,0:T(8,128)S(1)}, u32[]{:S(2)}, u32[]{:S(2)}) collective-permute-start(f32[192,256]{1,0:T(8,128)S(1)} %get-tuple-element.60.r0), channel_id=1, source_target_pairs={{0,3},{1,2},{2,1},{3,0},{4,7},{5,6},{6,5},{7,4},{8,11},{9,10},{10,... | collective-permute-start | bytes 589832 | tf_op jit(solution)/shard_map/ppermute | solution.py:42
  41.1 7.4 %collective-permute-start.13 = (f32[128,256]{1,0:T(8,128)S(1)}, f32[128,256]{1,0:T(8,128)S(1)}, u32[]{:S(2)}, u32[]{:S(2)}) collective-permute-start(f32[128,256]{1,0:T(8,128)S(1)} %get-tuple-element.63.r0), channel_id=1, source_target_pairs={{0,2},{1,3},{2,0},{3,1},{4,6},{5,7},{6,4},{7,5},{8,10},{9,11},{10,... | collective-permute-start | bytes 393224 | tf_op jit(solution)/shard_map/ppermute | solution.py:42
  42.7 6.5 %collective-permute-start.17 = (f32[128,256]{1,0:T(8,128)S(1)}, f32[128,256]{1,0:T(8,128)S(1)}, u32[]{:S(2)}, u32[]{:S(2)}) collective-permute-start(f32[128,256]{1,0:T(8,128)S(1)} %shard_map.135.own), channel_id=1, source_target_pairs={{0,64},{4,20},{8,72},{12,28},{16,80},{20,4},{24,88},{28,12},{32,96... | collective-permute-start | bytes 393224 | tf_op jit(solution)/shard_map/ppermute | solution.py:34
  49.7 7.1 %collective-permute-start.19 = (f32[160,256]{1,0:T(8,128)S(1)}, f32[160,256]{1,0:T(8,128)S(1)}, u32[]{:S(2)}, u32[]{:S(2)}) collective-permute-start(f32[160,256]{1,0:T(8,128)S(1)} %get-tuple-element.69), channel_id=1, source_target_pairs={{0,16},{4,68},{8,24},{12,76},{16,0},{20,84},{24,8},{28,92},{32,48}... | collective-permute-start | bytes 491528 | tf_op jit(solution)/shard_map/ppermute | solution.py:38
  53.4 6.5 %collective-permute-start.21 = (f32[160,256]{1,0:T(8,128)S(1)}, f32[160,256]{1,0:T(8,128)S(1)}, u32[]{:S(2)}, u32[]{:S(2)}) collective-permute-start(f32[160,256]{1,0:T(8,128)S(1)} %get-tuple-element.71), channel_id=1, source_target_pairs={{0,24},{4,100},{8,16},{12,108},{16,8},{20,116},{24,0},{28,124},{32... | collective-permute-start | bytes 491528 | tf_op jit(solution)/shard_map/ppermute | solution.py:38
  64.4 7.7 %collective-permute-start.25 = (f32[128,256]{1,0:T(8,128)S(1)}, f32[128,256]{1,0:T(8,128)S(1)}, u32[]{:S(2)}, u32[]{:S(2)}) collective-permute-start(f32[128,256]{1,0:T(8,128)S(1)} %get-tuple-element.75.r0), channel_id=1, source_target_pairs={{0,2},{1,3},{2,0},{3,1},{4,6},{5,7},{6,4},{7,5},{8,10},{9,11},{10,... | collective-permute-start | bytes 393224 | tf_op jit(solution)/shard_map/ppermute | solution.py:42
  66.1 8.3 %collective-permute-start.24 = (f32[128,256]{1,0:T(8,128)S(1)}, f32[128,256]{1,0:T(8,128)S(1)}, u32[]{:S(2)}, u32[]{:S(2)}) collective-permute-start(f32[128,256]{1,0:T(8,128)S(1)} %get-tuple-element.75.r0), channel_id=1, source_target_pairs={{0,3},{1,2},{2,1},{3,0},{4,7},{5,6},{6,5},{7,4},{8,11},{9,10},{10,... | collective-permute-start | bytes 393224 | tf_op jit(solution)/shard_map/ppermute | solution.py:42
  74.6 7.1 %collective-permute-start.29 = (f32[176,256]{1,0:T(8,128)S(1)}, f32[176,256]{1,0:T(8,128)S(1)}, u32[]{:S(2)}, u32[]{:S(2)}) collective-permute-start(f32[176,256]{1,0:T(8,128)S(1)} %get-tuple-element.83.own), channel_id=1, source_target_pairs={{0,64},{4,20},{8,72},{12,28},{16,80},{20,4},{24,88},{28,12},{32,96... | collective-permute-start | bytes 540680 | tf_op jit(solution)/shard_map/ppermute | solution.py:34
  76.3 7.3 %collective-permute-start.28 = (f32[176,256]{1,0:T(8,128)S(1)}, f32[176,256]{1,0:T(8,128)S(1)}, u32[]{:S(2)}, u32[]{:S(2)}) collective-permute-start(f32[176,256]{1,0:T(8,128)S(1)} %get-tuple-element.83.own), channel_id=1, source_target_pairs={{0,96},{4,28},{8,104},{12,20},{16,112},{20,12},{24,120},{28,4},{32... | collective-permute-start | bytes 540680 | tf_op jit(solution)/shard_map/ppermute | solution.py:34
  83.6 7.1 %collective-permute-start.32 = (f32[176,256]{1,0:T(8,128)S(1)}, f32[176,256]{1,0:T(8,128)S(1)}, u32[]{:S(2)}, u32[]{:S(2)}) collective-permute-start(f32[176,256]{1,0:T(8,128)S(1)} %shard_map.142.own), channel_id=1, source_target_pairs={{0,16},{4,68},{8,24},{12,76},{16,0},{20,84},{24,8},{28,92},{32,48}... | collective-permute-start | bytes 540680 | tf_op jit(solution)/shard_map/ppermute | solution.py:38
  85.8 6.9 %collective-permute-start.31 = (f32[176,256]{1,0:T(8,128)S(1)}, f32[176,256]{1,0:T(8,128)S(1)}, u32[]{:S(2)}, u32[]{:S(2)}) collective-permute-start(f32[176,256]{1,0:T(8,128)S(1)} %shard_map.142.own), channel_id=1, source_target_pairs={{0,24},{4,100},{8,16},{12,108},{16,8},{20,116},{24,0},{28,124},{32... | collective-permute-start | bytes 540680 | tf_op jit(solution)/shard_map/ppermute | solution.py:38
  105.1 7.7 %collective-permute-start.39 = (f32[128,256]{1,0:T(8,128)S(1)}, f32[128,256]{1,0:T(8,128)S(1)}, u32[]{:S(2)}, u32[]{:S(2)}) collective-permute-start(f32[128,256]{1,0:T(8,128)S(1)} %get-tuple-element.91.r0), channel_id=1, source_target_pairs={{0,2},{1,3},{2,0},{3,1},{4,6},{5,7},{6,4},{7,5},{8,10},{9,11},{10,... | collective-permute-start | bytes 393224 | tf_op jit(solution)/shard_map/ppermute | solution.py:42
  106.5 7.1 %collective-permute-start.38 = (f32[128,256]{1,0:T(8,128)S(1)}, f32[128,256]{1,0:T(8,128)S(1)}, u32[]{:S(2)}, u32[]{:S(2)}) collective-permute-start(f32[128,256]{1,0:T(8,128)S(1)} %get-tuple-element.91.r0), channel_id=1, source_target_pairs={{0,3},{1,2},{2,1},{3,0},{4,7},{5,6},{6,5},{7,4},{8,11},{9,10},{10,... | collective-permute-start | bytes 393224 | tf_op jit(solution)/shard_map/ppermute | solution.py:42
  117.9 6.6 %collective-permute-start.43 = (f32[128,256]{1,0:T(8,128)S(1)}, f32[128,256]{1,0:T(8,128)S(1)}, u32[]{:S(2)}, u32[]{:S(2)}) collective-permute-start(f32[128,256]{1,0:T(8,128)S(1)} %shard_map.147.own), channel_id=1, source_target_pairs={{0,64},{4,20},{8,72},{12,28},{16,80},{20,4},{24,88},{28,12},{32,96... | collective-permute-start | bytes 393224 | tf_op jit(solution)/shard_map/ppermute | solution.py:34
  119.4 6.4 %collective-permute-start.42 = (f32[128,256]{1,0:T(8,128)S(1)}, f32[128,256]{1,0:T(8,128)S(1)}, u32[]{:S(2)}, u32[]{:S(2)}) collective-permute-start(f32[128,256]{1,0:T(8,128)S(1)} %shard_map.147.own), channel_id=1, source_target_pairs={{0,96},{4,28},{8,104},{12,20},{16,112},{20,12},{24,120},{28,4},{32... | collective-permute-start | bytes 393224 | tf_op jit(solution)/shard_map/ppermute | solution.py:34
  125.9 6.6 %collective-permute-start.46 = (f32[128,256]{1,0:T(8,128)S(1)}, f32[128,256]{1,0:T(8,128)S(1)}, u32[]{:S(2)}, u32[]{:S(2)}) collective-permute-start(f32[128,256]{1,0:T(8,128)S(1)} %shard_map.148.own), channel_id=1, source_target_pairs={{0,16},{4,68},{8,24},{12,76},{16,0},{20,84},{24,8},{28,92},{32,48}... | collective-permute-start | bytes 393224 | tf_op jit(solution)/shard_map/ppermute | solution.py:38
  138.6 7.9 %collective-permute-start.50 = (f32[128,256]{1,0:T(8,128)S(1)}, f32[128,256]{1,0:T(8,128)S(1)}, u32[]{:S(2)}, u32[]{:S(2)}) collective-permute-start(f32[128,256]{1,0:T(8,128)S(1)} %get-tuple-element.98.r0), channel_id=1, source_target_pairs={{0,2},{1,3},{2,0},{3,1},{4,6},{5,7},{6,4},{7,5},{8,10},{9,11},{10,... | collective-permute-start | bytes 393224 | tf_op jit(solution)/shard_map/ppermute | solution.py:42
  140.0 8.5 %collective-permute-start.49 = (f32[128,256]{1,0:T(8,128)S(1)}, f32[128,256]{1,0:T(8,128)S(1)}, u32[]{:S(2)}, u32[]{:S(2)}) collective-permute-start(f32[128,256]{1,0:T(8,128)S(1)} %get-tuple-element.98.r0), channel_id=1, source_target_pairs={{0,3},{1,2},{2,1},{3,0},{4,7},{5,6},{6,5},{7,4},{8,11},{9,10},{10,... | collective-permute-start | bytes 393224 | tf_op jit(solution)/shard_map/ppermute | solution.py:42
  141.6 6.9 %collective-permute-start.48 = (f32[128,256]{1,0:T(8,128)S(1)}, f32[128,256]{1,0:T(8,128)S(1)}, u32[]{:S(2)}, u32[]{:S(2)}) collective-permute-start(f32[128,256]{1,0:T(8,128)S(1)} %get-tuple-element.98.r0), channel_id=1, source_target_pairs={{0,1},{1,0},{2,3},{3,2},{4,5},{5,4},{6,7},{7,6},{8,9},{9,8},{10,11... | collective-permute-start | bytes 393224 | tf_op jit(solution)/shard_map/ppermute | solution.py:42
  152.9 6.5 %collective-permute-start.54 = (f32[128,256]{1,0:T(8,128)S(1)}, f32[128,256]{1,0:T(8,128)S(1)}, u32[]{:S(2)}, u32[]{:S(2)}) collective-permute-start(f32[128,256]{1,0:T(8,128)S(1)} %shard_map.152.own), channel_id=1, source_target_pairs={{0,64},{4,20},{8,72},{12,28},{16,80},{20,4},{24,88},{28,12},{32,96... | collective-permute-start | bytes 393224 | tf_op jit(solution)/shard_map/ppermute | solution.py:34
  161.2 6.6 %collective-permute-start.57 = (f32[128,256]{1,0:T(8,128)S(1)}, f32[128,256]{1,0:T(8,128)S(1)}, u32[]{:S(2)}, u32[]{:S(2)}) collective-permute-start(f32[128,256]{1,0:T(8,128)S(1)} %shard_map.153.own), channel_id=1, source_target_pairs={{0,16},{4,68},{8,24},{12,76},{16,0},{20,84},{24,8},{28,92},{32,48}... | collective-permute-start | bytes 393224 | tf_op jit(solution)/shard_map/ppermute | solution.py:38
  (44 other events, 279.6 us)

commit v9 on v8

--- a/solution.py
+++ b/solution.py
@@ -18,6 +18,8 @@
 CW = CT + LT
 GROUP = 8
 STEPS = NT // GROUP
+PIECE = GROUP // 2
+LOADS = NT // PIECE
 
 EPS = 1e-06
 STEP = 0.9
@@ -82,6 +84,25 @@
         colout_ref[at] = op(colout_ref[at], s)
 
 
+def both_pass(tiles_ref, t, col, row, rowf_ref, colf_ref, rowout_ref, colout_ref):
+    parts = [None, None]
+    for h in range(2):
+        at = slice(h * LANES, (h + 1) * LANES)
+        blocks = [jnp.abs(tiles_ref[t, at, w * LANES : (w + 1) * LANES]) for w in range(2)]
+        factor = None if rowf_ref is None else jnp.broadcast_to(rowf_ref[h, pl.ds(row, 1), :], (LANES, LANES)).T
+        scaled = blocks if colf_ref is None else [a * colf_ref[w, pl.ds(col, 1), :] for w, a in enumerate(blocks)]
+        s = jnp.max(jnp.maximum(scaled[0], scaled[1]).T, axis=0, keepdims=True)
+        at = (h, pl.ds(row, 1), slice(None))
+        rowout_ref[at] = jnp.maximum(rowout_ref[at], s)
+        for w, a in enumerate(blocks):
+            a = a if factor is None else a * factor
+            s = jnp.max(a.reshape(16, 8, LANES), axis=0)
+            parts[w] = s if parts[w] is None else jnp.maximum(parts[w], s)
+    for w in range(2):
+        at = (w, pl.ds(col, 1), slice(None))
+        colout_ref[at] = jnp.maximum(colout_ref[at], jnp.max(parts[w], axis=0, keepdims=True))
+
+
 def split_to(ref, value, lo=0):
     for w in range(2):
         ref[w, lo : lo + value.shape[0], :] = value[:, w * LANES : (w + 1) * LANES]
@@ -100,7 +121,7 @@
 CHUNK = HALF // 4
 
 
-def call(kernel, smem, tiles, operands, outs, scratch=()):
+def call(kernel, smem, tiles, operands, outs, scratch=(), to_hbm=0):
     operands = [pltpu.with_memory_space_constraint(tiles, pltpu.VMEM)] + list(operands)
     smem = [pltpu.with_memory_space_constraint(x, pltpu.SMEM) for x in smem]
     vmem = pl.BlockSpec(memory_space=pltpu.VMEM)
@@ -108,7 +129,7 @@
         kernel,
         out_shape=tuple(jax.ShapeDtypeStruct((n, TILE), F32) for n in outs),
         in_specs=[pl.BlockSpec(memory_space=pltpu.SMEM) for _ in smem] + [vmem for _ in operands],
-        out_specs=tuple(vmem for _ in outs),
+        out_specs=tuple(pl.BlockSpec(memory_space=pltpu.HBM) if i < to_hbm else vmem for i in range(len(outs))),
         scratch_shapes=list(scratch),
         compiler_params=pltpu.CompilerParams(vmem_limit_bytes=VMEM_LIMIT),
     )(*smem, *operands)
@@ -116,9 +137,9 @@
 
 def each_tile(index_ref, visit, ready=None):
     def group(step, carry):
-        if ready is not None:
-            ready(step)
         for i in range(GROUP):
+            if ready is not None and i % PIECE == 0:
+                ready(step * (GROUP // PIECE) + i // PIECE)
             t = step * GROUP + i
             visit(t, index_ref[NT + t], index_ref[t])
         return carry
@@ -136,7 +157,7 @@
     rows_ref, cols_ref, sems,
 ):
     indices = [
-        pltpu.make_async_copy(src, dst, sems.at[STEPS + 2 + i])
+        pltpu.make_async_copy(src, dst, sems.at[LOADS + 2 + i])
         for i, (src, dst) in enumerate(((rows_hbm, rows_ref), (cols_hbm, cols_ref)))
     ]
     for copy in indices:
@@ -145,13 +166,13 @@
         index_ref[PLACE + i] = place[i]
 
     def load(step):
-        part = pl.ds(step * GROUP, GROUP)
+        part = pl.ds(step * PIECE, PIECE)
         return pltpu.make_async_copy(source.at[part], tiles_ref.at[part], sems.at[step])
 
-    for step in range(STEPS):
+    for step in range(LOADS):
         load(step).start()
     extra = [
-        pltpu.make_async_copy(src, rowout.at[pl.ds(RT + i * SHARE, SHARE)], sems.at[STEPS + i])
+        pltpu.make_async_copy(src, rowout.at[pl.ds(RT + i * SHARE, SHARE)], sems.at[LOADS + i])
         for i, src in enumerate((rhs, dual))
     ]
     for copy in extra:
@@ -172,8 +193,7 @@
     lax.fori_loop(0, NT, enter, 0)
 
     def visit(t, col, row):
-        row_pass(tiles_ref, t, col, row, None, racc, jnp.maximum, True)
-        col_pass(tiles_ref, t, col, row, None, cacc, jnp.maximum, True)
+        both_pass(tiles_ref, t, col, row, None, None, racc, cacc)
 
     each_tile(index_ref, visit, lambda step: load(step).wait())
     join_from(racc, rowout, 0, RT)
@@ -195,7 +215,7 @@
             COLS,
             pltpu.SMEM((NT,), jnp.int32),
             pltpu.SMEM((NT,), jnp.int32),
-            pltpu.SemaphoreType.DMA((STEPS + 4,)),
+            pltpu.SemaphoreType.DMA((LOADS + 4,)),
         ],
         compiler_params=pltpu.CompilerParams(vmem_limit_bytes=VMEM_LIMIT),
     )(ids[2], *(pltpu.with_memory_space_constraint(x, pltpu.HBM) for x in (*ids[:2], source, rhs, dual)))
@@ -217,8 +237,7 @@
     cacc[...] = jnp.zeros_like(cacc)
 
     def visit(t, col, row):
-        row_pass(tiles_ref, t, col, row, colf, racc, jnp.maximum, True)
-        col_pass(tiles_ref, t, col, row, rowf, cacc, jnp.maximum, True)
+        both_pass(tiles_ref, t, col, row, rowf, colf, racc, cacc)
 
     each_tile(index_ref, visit)
     join_from(racc, rowout, 0, RT)
@@ -309,7 +328,8 @@
     if index < ITERS - 1:
         rowout, fresh, racc, work = rest
     else:
-        dual, rhs, rowf, local, link, dualout, rhsout, rowfout, p0, p1, p2, p3, racc, work = rest
+        dual, rhs, rowf, local_hbm, link_hbm, dualout, rhsout, rowfout, p0, p1, p2, p3, *rest = rest
+        racc, work, local, link, sems = rest
         own = pl.ds(pl.multiple_of(index_ref[PLACE + 2] * SHARE, SHARE), SHARE)
         for ref, out in ((dual, dualout), (rhs, rhsout), (rowf, rowfout)):
             out[...] = ref[own, :]
@@ -326,6 +346,14 @@
             half = index_ref[PLACE + 0] if lo == CT else 1 - index_ref[PLACE + 0]
             link[pl.ds(pl.multiple_of(half * HALF, HALF), HALF), :] = scale * new
         split_to(work, scale * (2.0 * new - x), lo)
+    leaving = []
+    if index == ITERS - 1:
+        leaving = [
+            pltpu.make_async_copy(src, dst, sems.at[i])
+            for i, (src, dst) in enumerate(((local, local_hbm), (link, link_hbm)))
+        ]
+    for copy in leaving:
+        copy.start()
     racc[...] = jnp.zeros_like(racc)
 
     def visit(t, col, row):
@@ -339,6 +367,8 @@
             at = pl.ds(pl.multiple_of((index_ref[PLACE + 2] ^ k) * SHARE, SHARE), SHARE)
             for w in range(2):
                 out[:, w * LANES : (w + 1) * LANES] = racc[w, at, :]
+    for copy in leaving:
+        copy.wait()
 
 
 def core_kernel(op, tiles_ref, colown, got, out):
@@ -454,8 +484,8 @@
 
     row_part, colown, colother, tiles, index = first_stats(ids, tile_values[0, 0], rhs[0], start_dual[0])
 
-    def run(kernel, smem, operands, outs, scratch=()):
-        return call(kernel, smem, tiles, operands, outs, scratch)
+    def run(kernel, smem, operands, outs, scratch=(), to_hbm=0):
+        return call(kernel, smem, tiles, operands, outs, scratch, to_hbm)
 
     rows = over(swap_y, row_part)
     (link,) = run(functools.partial(core_kernel, jnp.maximum), (), (colown, swap_core(colother)), (HALF,))
@@ -526,6 +556,7 @@
     norms = (*over(swap_y, cost_square), rhs_square)
 
     grads, grad_at = (gradown, mine, other), HALF + EIGHT
+    leaving = (pltpu.VMEM((CT, TILE), F32), pltpu.VMEM((LT, TILE), F32), pltpu.SemaphoreType.DMA((2,)))
     for step in range(ITERS):
         given = norms if step == 0 else (steps,)
         extra = (dual_scaled, rhs_scaled, row_scale) if step == ITERS - 1 else ()
@@ -535,7 +566,8 @@
             (index,),
             (*given, *grads, primal, cost, upper, col_scale, *extra),
             ((CT,) if step == 0 else ()) + outs,
-            (ROWS, COLS),
+            (ROWS, COLS) + (leaving if step == ITERS - 1 else ()),
+            2 if step == ITERS - 1 else 0,
         )
         if step == 0:
             steps, *result = result

time: 182 us -> 182 us (level)
  no operation moved by 1% of the time
where the time goes in v9:
time: 182 us
  waiting for transfers between devices  76.2 us (42%)
  starting transfers between devices  67 us (37%)
  Pallas kernels  37.6 us (21%)
    pallas_call x25, Pallas kernels, call(): pl.pallas_call(kernel, out_shape=tuple((jax.ShapeDtypeStruct((n, TILE), F...  30.2 us
    ppermute x21, starting transfers between devices, swap_y(): return lax.ppermute(x, 'col', [(i, i ^ k) for i in range(4)])  26.8 us
    ppermute x21, waiting for transfers between devices, swap_y(): return lax.ppermute(x, 'col', [(i, i ^ k) for i in range(4)])  25.3 us
    ppermute x15, waiting for transfers between devices, swap_second(): lax.ppermute(x, 'scen', [(i, i ^ k << (3 if i % 2 else 1)) for i in range...  22.4 us
    ppermute x15, starting transfers between devices, swap_second(): lax.ppermute(x, 'scen', [(i, i ^ k << (3 if i % 2 else 1)) for i in range...  20.2 us
    ppermute x15, waiting for transfers between devices, swap_first(): lax.ppermute(x, 'scen', [(i, i ^ k << (1 if i % 2 else 3)) for i in range...  19.6 us
    ppermute x15, starting transfers between devices, swap_first(): lax.ppermute(x, 'scen', [(i, i ^ k << (1 if i % 2 else 3)) for i in range...  19.1 us
    ppermute x11, waiting for transfers between devices, swap_core(): return lax.ppermute(x, 'scen', [(i, i ^ 1) for i in range(32)])  8.96 us
  transfers between devices with their start and end apart: 62, of which 47 were waited for; matrix products, arithmetic and copies ran while one was open for 0% of the time, Pallas kernels for 3%

profile of v9, /device:TPU:0, one launch (start us, length us, event | category | flops | bytes accessed | tf_op | source)
XLA Modules:
  0.0 181.8 jit_solution(1404250591878165576)
XLA Ops:
  0.8 6.8 %shard_map.130 = (f32[192,256]{1,0:T(8,128)S(1)}, f32[136,256]{1,0:T(8,128)S(1)}, f32[128,256]{1,0:T(8,128)S(1)}, f32[64,256,256]{2,1,0:T(8,128)S(1)}, s32[136]{0:T(256)S(4)}) custom-call(s32[3]{0:T(128)S(1)} %pad_add_fusion.place, s32[64]{0:T(128)} %bitcast.28, s32[64]{0:T(128)} %bitcast.29, f32[64,256,256]{2,1,0:T(8,128)} %bitcast.24, f32[32,256]{1,0:T(8,128)} %bitcast.25, ...), custom_call_target="tpu_custom_call" | custom-call | tf_op jit(solution)/shard_map/pallas_call | solution.py:208
  7.6 3.4 %collective-permute-start.2 = (f32[192,256]{1,0:T(8,128)S(1)}, f32[192,256]{1,0:T(8,128)S(1)}, u32[]{:S(2)}, u32[]{:S(2)}) collective-permute-start(f32[192,256]{1,0:T(8,128)S(1)} %get-tuple-element.60.r0), channel_id=1, source_target_pairs={{0,2},{1,3},{2,0},{3,1},{4,6},{5,7},{6,4},{7,5},{8,10},{9,11},{10,... | collective-permute-start | bytes 589832 | tf_op jit(solution)/shard_map/ppermute | solution.py:44
  11.0 3.1 %collective-permute-start.6 = (f32[128,256]{1,0:T(8,128)S(1)}, f32[128,256]{1,0:T(8,128)S(1)}, u32[]{:S(2)}, u32[]{:S(2)}) collective-permute-start(f32[128,256]{1,0:T(8,128)S(1)} %shard_map.131.own), channel_id=1, source_target_pairs={{0,64},{4,20},{8,72},{12,28},{16,80},{20,4},{24,88},{28,12},{32,96... | collective-permute-start | bytes 393224 | tf_op jit(solution)/shard_map/ppermute | solution.py:36
  17.5 2.7 %collective-permute-done.5.r3 = f32[128,256]{1,0:T(8,128)S(1)} collective-permute-done((f32[128,256]{1,0:T(8,128)S(1)}, f32[128,256]{1,0:T(8,128)S(1)}, u32[]{:S(2)}, u32[]{:S(2)}) %collective-permute-start.5) | collective-permute-done | bytes 131104 | tf_op jit(solution)/shard_map/ppermute | solution.py:36
  20.3 4.0 %collective-permute-start.9 = (f32[128,256]{1,0:T(8,128)S(1)}, f32[128,256]{1,0:T(8,128)S(1)}, u32[]{:S(2)}, u32[]{:S(2)}) collective-permute-start(f32[128,256]{1,0:T(8,128)S(1)} %shard_map.132.own), channel_id=1, source_target_pairs={{0,16},{4,68},{8,24},{12,76},{16,0},{20,84},{24,8},{28,92},{32,48}... | collective-permute-start | bytes 393224 | tf_op jit(solution)/shard_map/ppermute | solution.py:40
  27.2 3.2 %collective-permute-done.8.r3 = f32[128,256]{1,0:T(8,128)S(1)} collective-permute-done((f32[128,256]{1,0:T(8,128)S(1)}, f32[128,256]{1,0:T(8,128)S(1)}, u32[]{:S(2)}, u32[]{:S(2)}) %collective-permute-start.8) | collective-permute-done | bytes 131104 | tf_op jit(solution)/shard_map/ppermute | solution.py:40
  32.2 5.5 %shard_map.134 = (f32[128,256]{1,0:T(8,128)S(1)}, f32[136,256]{1,0:T(8,128)S(1)}, f32[128,256]{1,0:T(8,128)S(1)}, f32[128,256]{1,0:T(8,128)S(1)}, f32[264,256]{1,0:T(8,128)S(1)}) custom-call(s32[136]{0:T(256)S(4)} %get-tuple-element.58.index_ref, f32[64,256,256]{2,1,0:T(8,128)S(1)} %get-tuple-element.59.tiles_ref, f32[192,256]{1,0:T(8,128)S(1)} %get-tuple-element.60.r0, ...), custom_call_target="tpu_custom_call" | custom-call | tf_op jit(solution)/shard_map/pallas_call | solution.py:128
  45.4 2.8 %shard_map.136 = (f32[136,256]{1,0:T(8,128)S(1)}, f32[128,256]{1,0:T(8,128)S(1)}, f32[128,256]{1,0:T(8,128)S(1)}, f32[128,256]{1,0:T(8,128)S(1)}) custom-call(s32[136]{0:T(256)S(4)} %get-tuple-element.58.index_ref, f32[64,256,256]{2,1,0:T(8,128)S(1)} %get-tuple-element.59.tiles_ref, f32[192,256]{1,0:T(8,128)S(1)} %get-tuple-element.60.r0, ...), custom_call_target="tpu_custom_call" | custom-call | tf_op jit(solution)/shard_map/pallas_call | solution.py:128
  49.7 3.8 %collective-permute-start.19 = (f32[160,256]{1,0:T(8,128)S(1)}, f32[160,256]{1,0:T(8,128)S(1)}, u32[]{:S(2)}, u32[]{:S(2)}) collective-permute-start(f32[160,256]{1,0:T(8,128)S(1)} %get-tuple-element.69), channel_id=1, source_target_pairs={{0,16},{4,68},{8,24},{12,76},{16,0},{20,84},{24,8},{28,92},{32,48}... | collective-permute-start | bytes 491528 | tf_op jit(solution)/shard_map/ppermute | solution.py:40
  61.5 3.0 %shard_map.139 = (f32[128,256]{1,0:T(8,128)S(1)}, f32[128,256]{1,0:T(8,128)S(1)}, f32[264,256]{1,0:T(8,128)S(1)}) custom-call(s32[136]{0:T(256)S(4)} %get-tuple-element.58.index_ref, f32[64,256,256]{2,1,0:T(8,128)S(1)} %get-tuple-element.59.tiles_ref, f32[128,256]{1,0:T(8,128)S(1)} %get-tuple-element.63.r0, f32[128,256]{1,0:T(8,128)S(1)} %collective-permute-done.11.r1, ...), custom_call_target="tpu_custom_call" | custom-call | tf_op jit(solution)/shard_map/pallas_call | solution.py:128
  68.2 3.2 %shard_map.140 = (f32[136,256]{1,0:T(8,128)S(1)}, f32[128,256]{1,0:T(8,128)S(1)}) custom-call(s32[136]{0:T(256)S(4)} %get-tuple-element.58.index_ref, f32[64,256,256]{2,1,0:T(8,128)S(1)} %get-tuple-element.59.tiles_ref, f32[128,256]{1,0:T(8,128)S(1)} %get-tuple-element.76.row_scale.rowold), custom_call_target="tpu_custom_call" | custom-call | tf_op jit(solution)/shard_map/pallas_call | solution.py:128
  78.2 3.6 %collective-permute-done.29.r2 = f32[176,256]{1,0:T(8,128)S(1)} collective-permute-done((f32[176,256]{1,0:T(8,128)S(1)}, f32[176,256]{1,0:T(8,128)S(1)}, u32[]{:S(2)}, u32[]{:S(2)}) %collective-permute-start.29) | collective-permute-done | bytes 180256 | tf_op jit(solution)/shard_map/ppermute | solution.py:36
  87.3 3.5 %collective-permute-done.32.r2 = f32[176,256]{1,0:T(8,128)S(1)} collective-permute-done((f32[176,256]{1,0:T(8,128)S(1)}, f32[176,256]{1,0:T(8,128)S(1)}, u32[]{:S(2)}, u32[]{:S(2)}) %collective-permute-start.32) | collective-permute-done | bytes 180256 | tf_op jit(solution)/shard_map/ppermute | solution.py:40
  102.0 3.1 %shard_map.145 = (f32[8,256]{1,0:T(8,128)S(1)}, f32[128,256]{1,0:T(8,128)S(1)}, f32[264,256]{1,0:T(8,128)S(1)}) custom-call(s32[136]{0:T(256)S(4)} %get-tuple-element.58.index_ref, f32[64,256,256]{2,1,0:T(8,128)S(1)} %get-tuple-element.59.tiles_ref, f32[8,256]{1,0:T(8,128)S(1)} %get-tuple-element.84.rest_0_, f32[8,256]{1,0:T(8,128)S(1)} %collective-permute-done.34.rest_1_, ...), custom_call_target="tpu_custom_call" | custom-call | tf_op jit(solution)/shard_map/pallas_call | solution.py:128
  108.7 4.1 %collective-permute-done.39.r2 = f32[128,256]{1,0:T(8,128)S(1)} collective-permute-done((f32[128,256]{1,0:T(8,128)S(1)}, f32[128,256]{1,0:T(8,128)S(1)}, u32[]{:S(2)}, u32[]{:S(2)}) %collective-permute-start.39) | collective-permute-done | bytes 131104 | tf_op jit(solution)/shard_map/ppermute | solution.py:44
  113.6 2.9 %shard_map.146 = (f32[136,256]{1,0:T(8,128)S(1)}, f32[128,256]{1,0:T(8,128)S(1)}, f32[128,256]{1,0:T(8,128)S(1)}) custom-call(s32[136]{0:T(256)S(4)} %get-tuple-element.58.index_ref, f32[64,256,256]{2,1,0:T(8,128)S(1)} %get-tuple-element.59.tiles_ref, f32[8,256]{1,0:T(8,128)S(1)} %get-tuple-element.90.steps.rest_0_, f32[128,256]{1,0:T(8,128)S(1)} %get-tuple-element.91.r0, ...), custom_call_target="tpu_custom_call" | custom-call | tf_op jit(solution)/shard_map/pallas_call | solution.py:128
  121.5 3.0 %collective-permute-done.43.r2 = f32[128,256]{1,0:T(8,128)S(1)} collective-permute-done((f32[128,256]{1,0:T(8,128)S(1)}, f32[128,256]{1,0:T(8,128)S(1)}, u32[]{:S(2)}, u32[]{:S(2)}) %collective-permute-start.43) | collective-permute-done | bytes 131104 | tf_op jit(solution)/shard_map/ppermute | solution.py:36
  129.5 3.0 %collective-permute-done.46.r2 = f32[128,256]{1,0:T(8,128)S(1)} collective-permute-done((f32[128,256]{1,0:T(8,128)S(1)}, f32[128,256]{1,0:T(8,128)S(1)}, u32[]{:S(2)}, u32[]{:S(2)}) %collective-permute-start.46) | collective-permute-done | bytes 131104 | tf_op jit(solution)/shard_map/ppermute | solution.py:40
  135.7 3.0 %shard_map.150 = (f32[128,256]{1,0:T(8,128)S(1)}, f32[264,256]{1,0:T(8,128)S(1)}) custom-call(s32[136]{0:T(256)S(4)} %get-tuple-element.58.index_ref, f32[64,256,256]{2,1,0:T(8,128)S(1)} %get-tuple-element.59.tiles_ref, f32[8,256]{1,0:T(8,128)S(1)} %get-tuple-element.90.steps.rest_0_, f32[136,256]{1,0:T(8,128)S(1)} %get-tuple-element.95.colown.rest_1_, ...), custom_call_target="tpu_custom_call" | custom-call | tf_op jit(solution)/shard_map/pallas_call | solution.py:128
  142.2 4.4 %collective-permute-done.50.r2 = f32[128,256]{1,0:T(8,128)S(1)} collective-permute-done((f32[128,256]{1,0:T(8,128)S(1)}, f32[128,256]{1,0:T(8,128)S(1)}, u32[]{:S(2)}, u32[]{:S(2)}) %collective-permute-start.50) | collective-permute-done | bytes 131104 | tf_op jit(solution)/shard_map/ppermute | solution.py:44
  148.6 2.9 %shard_map.151 = (f32[136,256]{1,0:T(8,128)S(1)}, f32[128,256]{1,0:T(8,128)S(1)}, f32[128,256]{1,0:T(8,128)S(1)}) custom-call(s32[136]{0:T(256)S(4)} %get-tuple-element.58.index_ref, f32[64,256,256]{2,1,0:T(8,128)S(1)} %get-tuple-element.59.tiles_ref, f32[8,256]{1,0:T(8,128)S(1)} %get-tuple-element.90.steps.rest_0_, f32[128,256]{1,0:T(8,128)S(1)} %get-tuple-element.98.r0, ...), custom_call_target="tpu_custom_call" | custom-call | tf_op jit(solution)/shard_map/pallas_call | solution.py:128
  156.5 3.0 %collective-permute-done.54.r2 = f32[128,256]{1,0:T(8,128)S(1)} collective-permute-done((f32[128,256]{1,0:T(8,128)S(1)}, f32[128,256]{1,0:T(8,128)S(1)}, u32[]{:S(2)}, u32[]{:S(2)}) %collective-permute-start.54) | collective-permute-done | bytes 131104 | tf_op jit(solution)/shard_map/ppermute | solution.py:36
  164.9 3.0 %collective-permute-done.57.r2 = f32[128,256]{1,0:T(8,128)S(1)} collective-permute-done((f32[128,256]{1,0:T(8,128)S(1)}, f32[128,256]{1,0:T(8,128)S(1)}, u32[]{:S(2)}, u32[]{:S(2)}) %collective-permute-start.57) | collective-permute-done | bytes 131104 | tf_op jit(solution)/shard_map/ppermute | solution.py:40
  170.8 3.0 %shard_map.155 = (f32[8,256]{1,0:T(8,128)}, f32[256,256]{1,0:T(8,128)}, f32[32,256]{1,0:T(8,128)S(1)}, f32[32,256]{1,0:T(8,128)S(1)}, f32[32,256]{1,0:T(8,128)S(...) custom-call(s32[136]{0:T(256)S(4)} %get-tuple-element.58.index_ref, ...), custom_call_target="tpu_custom_call" | custom-call | tf_op jit(solution)/shard_map/pallas_call | solution.py:128
  (140 shorter events, 97.1 us)
Async XLA Ops:
  7.6 8.8 %collective-permute-start.2 = (f32[192,256]{1,0:T(8,128)S(1)}, f32[192,256]{1,0:T(8,128)S(1)}, u32[]{:S(2)}, u32[]{:S(2)}) collective-permute-start(f32[192,256]{1,0:T(8,128)S(1)} %get-tuple-element.60.r0), channel_id=1, source_target_pairs={{0,2},{1,3},{2,0},{3,1},{4,6},{5,7},{6,4},{7,5},{8,10},{9,11},{10,... | collective-permute-start | bytes 589832 | tf_op jit(solution)/shard_map/ppermute | solution.py:44
  11.0 6.6 %collective-permute-start.6 = (f32[128,256]{1,0:T(8,128)S(1)}, f32[128,256]{1,0:T(8,128)S(1)}, u32[]{:S(2)}, u32[]{:S(2)}) collective-permute-start(f32[128,256]{1,0:T(8,128)S(1)} %shard_map.131.own), channel_id=1, source_target_pairs={{0,64},{4,20},{8,72},{12,28},{16,80},{20,4},{24,88},{28,12},{32,96... | collective-permute-start | bytes 393224 | tf_op jit(solution)/shard_map/ppermute | solution.py:36
  20.3 6.9 %collective-permute-start.9 = (f32[128,256]{1,0:T(8,128)S(1)}, f32[128,256]{1,0:T(8,128)S(1)}, u32[]{:S(2)}, u32[]{:S(2)}) collective-permute-start(f32[128,256]{1,0:T(8,128)S(1)} %shard_map.132.own), channel_id=1, source_target_pairs={{0,16},{4,68},{8,24},{12,76},{16,0},{20,84},{24,8},{28,92},{32,48}... | collective-permute-start | bytes 393224 | tf_op jit(solution)/shard_map/ppermute | solution.py:40
  25.3 6.9 %collective-permute-start.1 = (f32[192,256]{1,0:T(8,128)S(1)}, f32[192,256]{1,0:T(8,128)S(1)}, u32[]{:S(2)}, u32[]{:S(2)}) collective-permute-start(f32[192,256]{1,0:T(8,128)S(1)} %get-tuple-element.60.r0), channel_id=1, source_target_pairs={{0,3},{1,2},{2,1},{3,0},{4,7},{5,6},{6,5},{7,4},{8,11},{9,10},{10,... | collective-permute-start | bytes 589832 | tf_op jit(solution)/shard_map/ppermute | solution.py:44
  41.2 7.4 %collective-permute-start.13 = (f32[128,256]{1,0:T(8,128)S(1)}, f32[128,256]{1,0:T(8,128)S(1)}, u32[]{:S(2)}, u32[]{:S(2)}) collective-permute-start(f32[128,256]{1,0:T(8,128)S(1)} %get-tuple-element.63.r0), channel_id=1, source_target_pairs={{0,2},{1,3},{2,0},{3,1},{4,6},{5,7},{6,4},{7,5},{8,10},{9,11},{10,... | collective-permute-start | bytes 393224 | tf_op jit(solution)/shard_map/ppermute | solution.py:44
  42.7 6.5 %collective-permute-start.17 = (f32[128,256]{1,0:T(8,128)S(1)}, f32[128,256]{1,0:T(8,128)S(1)}, u32[]{:S(2)}, u32[]{:S(2)}) collective-permute-start(f32[128,256]{1,0:T(8,128)S(1)} %shard_map.135.own), channel_id=1, source_target_pairs={{0,64},{4,20},{8,72},{12,28},{16,80},{20,4},{24,88},{28,12},{32,96... | collective-permute-start | bytes 393224 | tf_op jit(solution)/shard_map/ppermute | solution.py:36
  49.7 7.1 %collective-permute-start.19 = (f32[160,256]{1,0:T(8,128)S(1)}, f32[160,256]{1,0:T(8,128)S(1)}, u32[]{:S(2)}, u32[]{:S(2)}) collective-permute-start(f32[160,256]{1,0:T(8,128)S(1)} %get-tuple-element.69), channel_id=1, source_target_pairs={{0,16},{4,68},{8,24},{12,76},{16,0},{20,84},{24,8},{28,92},{32,48}... | collective-permute-start | bytes 491528 | tf_op jit(solution)/shard_map/ppermute | solution.py:40
  53.5 6.5 %collective-permute-start.21 = (f32[160,256]{1,0:T(8,128)S(1)}, f32[160,256]{1,0:T(8,128)S(1)}, u32[]{:S(2)}, u32[]{:S(2)}) collective-permute-start(f32[160,256]{1,0:T(8,128)S(1)} %get-tuple-element.71), channel_id=1, source_target_pairs={{0,24},{4,100},{8,16},{12,108},{16,8},{20,116},{24,0},{28,124},{32... | collective-permute-start | bytes 491528 | tf_op jit(solution)/shard_map/ppermute | solution.py:40
  64.5 7.7 %collective-permute-start.25 = (f32[128,256]{1,0:T(8,128)S(1)}, f32[128,256]{1,0:T(8,128)S(1)}, u32[]{:S(2)}, u32[]{:S(2)}) collective-permute-start(f32[128,256]{1,0:T(8,128)S(1)} %get-tuple-element.75.r0), channel_id=1, source_target_pairs={{0,2},{1,3},{2,0},{3,1},{4,6},{5,7},{6,4},{7,5},{8,10},{9,11},{10,... | collective-permute-start | bytes 393224 | tf_op jit(solution)/shard_map/ppermute | solution.py:44
  66.2 8.3 %collective-permute-start.24 = (f32[128,256]{1,0:T(8,128)S(1)}, f32[128,256]{1,0:T(8,128)S(1)}, u32[]{:S(2)}, u32[]{:S(2)}) collective-permute-start(f32[128,256]{1,0:T(8,128)S(1)} %get-tuple-element.75.r0), channel_id=1, source_target_pairs={{0,3},{1,2},{2,1},{3,0},{4,7},{5,6},{6,5},{7,4},{8,11},{9,10},{10,... | collective-permute-start | bytes 393224 | tf_op jit(solution)/shard_map/ppermute | solution.py:44
  74.7 7.1 %collective-permute-start.29 = (f32[176,256]{1,0:T(8,128)S(1)}, f32[176,256]{1,0:T(8,128)S(1)}, u32[]{:S(2)}, u32[]{:S(2)}) collective-permute-start(f32[176,256]{1,0:T(8,128)S(1)} %get-tuple-element.83.own), channel_id=1, source_target_pairs={{0,64},{4,20},{8,72},{12,28},{16,80},{20,4},{24,88},{28,12},{32,96... | collective-permute-start | bytes 540680 | tf_op jit(solution)/shard_map/ppermute | solution.py:36
  76.3 7.3 %collective-permute-start.28 = (f32[176,256]{1,0:T(8,128)S(1)}, f32[176,256]{1,0:T(8,128)S(1)}, u32[]{:S(2)}, u32[]{:S(2)}) collective-permute-start(f32[176,256]{1,0:T(8,128)S(1)} %get-tuple-element.83.own), channel_id=1, source_target_pairs={{0,96},{4,28},{8,104},{12,20},{16,112},{20,12},{24,120},{28,4},{32... | collective-permute-start | bytes 540680 | tf_op jit(solution)/shard_map/ppermute | solution.py:36
  83.7 7.1 %collective-permute-start.32 = (f32[176,256]{1,0:T(8,128)S(1)}, f32[176,256]{1,0:T(8,128)S(1)}, u32[]{:S(2)}, u32[]{:S(2)}) collective-permute-start(f32[176,256]{1,0:T(8,128)S(1)} %shard_map.142.own), channel_id=1, source_target_pairs={{0,16},{4,68},{8,24},{12,76},{16,0},{20,84},{24,8},{28,92},{32,48}... | collective-permute-start | bytes 540680 | tf_op jit(solution)/shard_map/ppermute | solution.py:40
  85.9 6.9 %collective-permute-start.31 = (f32[176,256]{1,0:T(8,128)S(1)}, f32[176,256]{1,0:T(8,128)S(1)}, u32[]{:S(2)}, u32[]{:S(2)}) collective-permute-start(f32[176,256]{1,0:T(8,128)S(1)} %shard_map.142.own), channel_id=1, source_target_pairs={{0,24},{4,100},{8,16},{12,108},{16,8},{20,116},{24,0},{28,124},{32... | collective-permute-start | bytes 540680 | tf_op jit(solution)/shard_map/ppermute | solution.py:40
  105.1 7.7 %collective-permute-start.39 = (f32[128,256]{1,0:T(8,128)S(1)}, f32[128,256]{1,0:T(8,128)S(1)}, u32[]{:S(2)}, u32[]{:S(2)}) collective-permute-start(f32[128,256]{1,0:T(8,128)S(1)} %get-tuple-element.91.r0), channel_id=1, source_target_pairs={{0,2},{1,3},{2,0},{3,1},{4,6},{5,7},{6,4},{7,5},{8,10},{9,11},{10,... | collective-permute-start | bytes 393224 | tf_op jit(solution)/shard_map/ppermute | solution.py:44
  106.6 7.1 %collective-permute-start.38 = (f32[128,256]{1,0:T(8,128)S(1)}, f32[128,256]{1,0:T(8,128)S(1)}, u32[]{:S(2)}, u32[]{:S(2)}) collective-permute-start(f32[128,256]{1,0:T(8,128)S(1)} %get-tuple-element.91.r0), channel_id=1, source_target_pairs={{0,3},{1,2},{2,1},{3,0},{4,7},{5,6},{6,5},{7,4},{8,11},{9,10},{10,... | collective-permute-start | bytes 393224 | tf_op jit(solution)/shard_map/ppermute | solution.py:44
  118.0 6.6 %collective-permute-start.43 = (f32[128,256]{1,0:T(8,128)S(1)}, f32[128,256]{1,0:T(8,128)S(1)}, u32[]{:S(2)}, u32[]{:S(2)}) collective-permute-start(f32[128,256]{1,0:T(8,128)S(1)} %shard_map.147.own), channel_id=1, source_target_pairs={{0,64},{4,20},{8,72},{12,28},{16,80},{20,4},{24,88},{28,12},{32,96... | collective-permute-start | bytes 393224 | tf_op jit(solution)/shard_map/ppermute | solution.py:36
  119.5 6.4 %collective-permute-start.42 = (f32[128,256]{1,0:T(8,128)S(1)}, f32[128,256]{1,0:T(8,128)S(1)}, u32[]{:S(2)}, u32[]{:S(2)}) collective-permute-start(f32[128,256]{1,0:T(8,128)S(1)} %shard_map.147.own), channel_id=1, source_target_pairs={{0,96},{4,28},{8,104},{12,20},{16,112},{20,12},{24,120},{28,4},{32... | collective-permute-start | bytes 393224 | tf_op jit(solution)/shard_map/ppermute | solution.py:36
  126.0 6.6 %collective-permute-start.46 = (f32[128,256]{1,0:T(8,128)S(1)}, f32[128,256]{1,0:T(8,128)S(1)}, u32[]{:S(2)}, u32[]{:S(2)}) collective-permute-start(f32[128,256]{1,0:T(8,128)S(1)} %shard_map.148.own), channel_id=1, source_target_pairs={{0,16},{4,68},{8,24},{12,76},{16,0},{20,84},{24,8},{28,92},{32,48}... | collective-permute-start | bytes 393224 | tf_op jit(solution)/shard_map/ppermute | solution.py:40
  138.7 7.9 %collective-permute-start.50 = (f32[128,256]{1,0:T(8,128)S(1)}, f32[128,256]{1,0:T(8,128)S(1)}, u32[]{:S(2)}, u32[]{:S(2)}) collective-permute-start(f32[128,256]{1,0:T(8,128)S(1)} %get-tuple-element.98.r0), channel_id=1, source_target_pairs={{0,2},{1,3},{2,0},{3,1},{4,6},{5,7},{6,4},{7,5},{8,10},{9,11},{10,... | collective-permute-start | bytes 393224 | tf_op jit(solution)/shard_map/ppermute | solution.py:44
  140.1 8.5 %collective-permute-start.49 = (f32[128,256]{1,0:T(8,128)S(1)}, f32[128,256]{1,0:T(8,128)S(1)}, u32[]{:S(2)}, u32[]{:S(2)}) collective-permute-start(f32[128,256]{1,0:T(8,128)S(1)} %get-tuple-element.98.r0), channel_id=1, source_target_pairs={{0,3},{1,2},{2,1},{3,0},{4,7},{5,6},{6,5},{7,4},{8,11},{9,10},{10,... | collective-permute-start | bytes 393224 | tf_op jit(solution)/shard_map/ppermute | solution.py:44
  141.7 7.0 %collective-permute-start.48 = (f32[128,256]{1,0:T(8,128)S(1)}, f32[128,256]{1,0:T(8,128)S(1)}, u32[]{:S(2)}, u32[]{:S(2)}) collective-permute-start(f32[128,256]{1,0:T(8,128)S(1)} %get-tuple-element.98.r0), channel_id=1, source_target_pairs={{0,1},{1,0},{2,3},{3,2},{4,5},{5,4},{6,7},{7,6},{8,9},{9,8},{10,11... | collective-permute-start | bytes 393224 | tf_op jit(solution)/shard_map/ppermute | solution.py:44
  153.0 6.5 %collective-permute-start.54 = (f32[128,256]{1,0:T(8,128)S(1)}, f32[128,256]{1,0:T(8,128)S(1)}, u32[]{:S(2)}, u32[]{:S(2)}) collective-permute-start(f32[128,256]{1,0:T(8,128)S(1)} %shard_map.152.own), channel_id=1, source_target_pairs={{0,64},{4,20},{8,72},{12,28},{16,80},{20,4},{24,88},{28,12},{32,96... | collective-permute-start | bytes 393224 | tf_op jit(solution)/shard_map/ppermute | solution.py:36
  161.3 6.6 %collective-permute-start.57 = (f32[128,256]{1,0:T(8,128)S(1)}, f32[128,256]{1,0:T(8,128)S(1)}, u32[]{:S(2)}, u32[]{:S(2)}) collective-permute-start(f32[128,256]{1,0:T(8,128)S(1)} %shard_map.153.own), channel_id=1, source_target_pairs={{0,16},{4,68},{8,24},{12,76},{16,0},{20,84},{24,8},{28,92},{32,48}... | collective-permute-start | bytes 393224 | tf_op jit(solution)/shard_map/ppermute | solution.py:40
  (44 other events, 279.7 us)

commit v10 on v9

--- a/solution.py
+++ b/solution.py
@@ -222,10 +222,10 @@
 
 
 def second_stats_kernel(
-    index_ref, tiles_ref, r0, r1, r3, r2, loc, mine, other, rowout, colown, colother, rownew,
+    index_ref, tiles_ref, near, far, loc, mine, other, rowout, colown, colother, rownew,
     colnew, racc, cacc, rowf, colf,
 ):
-    row = tree(jnp.maximum, r0[0:RT], (r1[0:RT], r2[0:RT], r3[0:RT]))
+    row = jnp.maximum(near[0:RT], far[0:RT])
     new = 1.0 / jnp.sqrt(row + EPS)
     rownew[...] = new
     split_to(rowf, new)
@@ -245,10 +245,10 @@
 
 
 def third_rows_kernel(
-    index_ref, tiles_ref, r0, r1, r3, r2, loc, mine, other, rowold, colold, rowout, rownew,
+    index_ref, tiles_ref, near, far, loc, mine, other, rowold, colold, rowout, rownew,
     colnew, racc, colf,
 ):
-    row = tree(jnp.maximum, r0[...], (r1[...], r2[...], r3[...]))
+    row = jnp.maximum(near[...], far[...])
     old = rowold[...]
     rownew[...] = old / jnp.sqrt(old * row + EPS)
     for lo, hi, src in ((0, CT, loc), (CT, OWN, mine), (OWN, CW, other)):
@@ -277,12 +277,12 @@
 
 
 def first_backward_kernel(
-    index_ref, tiles_ref, r0, r1, r3, r2, after, colown, colother, rhsout, dualout, cacc, work
-):
-    for k, ref in enumerate((r0, r1, r2, r3)):
+    index_ref, tiles_ref, near, far, after, colown, colother, rhsout, dualout, cacc, work
+):
+    for k, ref, start in ((0, near, RT), (1, near, RT + 2 * SHARE), (3, far, RT), (2, far, RT + 2 * SHARE)):
         at = pl.ds(pl.multiple_of((index_ref[PLACE + 2] ^ k) * SHARE, SHARE), SHARE)
-        rhsout[at, :] = ref[RT : RT + SHARE]
-        dualout[at, :] = ref[RT + SHARE :]
+        rhsout[at, :] = ref[start : start + SHARE]
+        dualout[at, :] = ref[start + SHARE : start + 2 * SHARE]
     split_to(work, dualout[...])
     cacc[...] = jnp.zeros_like(cacc)
 
@@ -379,11 +379,17 @@
     out[...] = tree(op, own[...], (r1[...], r2[...], r3[...]))
 
 
-def merge_after_kernel(tiles_ref, own, r1, r3, r2, after, out):
+def merge_rows_kernel(tiles_ref, own, r1, r3, r2, mine, got, out, near):
     out[...] = tree(jnp.maximum, own[...], (r1[...], r2[...], r3[...]))
-
-
-def merge_grad_kernel(index_ref, tiles_ref, own, r1, r3, r2, gradown, gradgot, after, m0, m1, m2, m3, half):
+    near[0:RT] = jnp.maximum(mine[0:RT], got[0:RT])
+    near[RT : RT + 2 * SHARE] = mine[RT:]
+    near[RT + 2 * SHARE :] = got[RT:]
+
+
+def merge_grad_kernel(
+    index_ref, tiles_ref, own, r1, r3, r2, gradown, gradgot, mine, got, m0, m1, m2, m3, near, half
+):
+    near[...] = jnp.maximum(mine[...], got[...])
     link = tree(jnp.maximum, own[...], (r1[...], r2[...], r3[...]))
     half[...] = gradown[CT:OWN] + gradgot[...]
     for k, out in enumerate((m0, m1, m2, m3)):
@@ -487,39 +493,41 @@
     def run(kernel, smem, operands, outs, scratch=(), to_hbm=0):
         return call(kernel, smem, tiles, operands, outs, scratch, to_hbm)
 
-    rows = over(swap_y, row_part)
     (link,) = run(functools.partial(core_kernel, jnp.maximum), (), (colown, swap_core(colother)), (HALF,))
-    (link,) = run(merge_after_kernel, (), (*over(swap_first, link), rows[3]), (HALF,))
+    link, near = run(
+        merge_rows_kernel, (), (*over(swap_first, link), row_part, swap_y(row_part, 1)), (HALF, RT + 4 * SHARE)
+    )
+    far = swap_y(near, 3)
     (link,) = run(functools.partial(merge_kernel, jnp.maximum), (), over(swap_second, link), (HALF,))
 
-    first_rows = rows
+    gathered = (near, far)
     row_part, colown, colother, row_scale, col_scale = run(
         second_stats_kernel,
         (index,),
-        (*rows, colown, link, swap_core(link)),
+        (near, far, colown, link, swap_core(link)),
         (RT, OWN, HALF, RT, CW),
         (ROWS, COLS, ROWS, COLS),
     )
-    rows = over(swap_y, row_part)
     (link,) = run(functools.partial(core_kernel, jnp.maximum), (), (colown, swap_core(colother)), (HALF,))
     got = over(swap_first, link)
     gradown, gradother, rhs_rows, dual_rows = run(
-        first_backward_kernel, (index,), (*first_rows, got[2]), (OWN, HALF, RT, RT), (COLS, ROWS)
-    )
-    sent = run(
+        first_backward_kernel, (index,), (*gathered, got[2]), (OWN, HALF, RT, RT), (COLS, ROWS)
+    )
+    *sent, near = run(
         merge_grad_kernel,
         (index,),
-        (*got, gradown, swap_core(gradother), rows[3]),
-        (HALF + CHUNK,) * 4,
+        (*got, gradown, swap_core(gradother), row_part, swap_y(row_part, 1)),
+        (HALF + CHUNK,) * 4 + (RT,),
         (pltpu.VMEM((HALF, TILE), F32),),
     )
+    far = swap_y(near, 3)
     got = {k: swap_second(sent[k], k) for k in (2, 1, 3)}
     link, chunk = run(merge_chunk_kernel, (), (sent[0], got[2], got[1], got[3]), (HALF, CHUNK))
 
     row_part, row_scale, col_scale = run(
         third_rows_kernel,
         (index,),
-        (*rows, colown, link, swap_core(link), row_scale, col_scale),
+        (near, far, colown, link, swap_core(link), row_scale, col_scale),
         (RT, RT, CW),
         (ROWS, COLS),
     )

time: 182 us -> 182 us (level)
    ppermute x11, waiting for transfers between devices: 8.96 us -> 12 us  [swap_core(): return lax.ppermute(x, 'scen', [(i, i ^ 1) for i in range(32)])]
    ppermute x15, waiting for transfers between devices: 22.4 us -> 20.2 us  [swap_second(): lax.ppermute(x, 'scen', [(i, i ^ k << (3 if i % 2 else 1)) for i in range...]
    ppermute x21 -> x19, waiting for transfers between devices: 25.3 us -> 24.2 us  [swap_y(): return lax.ppermute(x, 'col', [(i, i ^ k) for i in range(4)])]
    ppermute x21 -> x19, starting transfers between devices: 26.8 us -> 25.7 us  [swap_y(): return lax.ppermute(x, 'col', [(i, i ^ k) for i in range(4)])]
  transfers between devices with their start and end apart: 62 -> 60, of which waited for: 47 -> 43; matrix products, arithmetic and copies ran while one was open for 0% -> 0% of each run, Pallas kernels for 3% -> 3%
where the time goes in v10:
time: 182 us
  waiting for transfers between devices  76.9 us (42%)
  starting transfers between devices  66.4 us (36%)
  Pallas kernels  37.6 us (21%)
    pallas_call x25, Pallas kernels, call(): pl.pallas_call(kernel, out_shape=tuple((jax.ShapeDtypeStruct((n, TILE), F...  30.2 us
    ppermute x19, starting transfers between devices, swap_y(): return lax.ppermute(x, 'col', [(i, i ^ k) for i in range(4)])  25.7 us
    ppermute x19, waiting for transfers between devices, swap_y(): return lax.ppermute(x, 'col', [(i, i ^ k) for i in range(4)])  24.2 us
    ppermute x15, waiting for transfers between devices, swap_first(): lax.ppermute(x, 'scen', [(i, i ^ k << (1 if i % 2 else 3)) for i in range...  20.5 us
    ppermute x15, waiting for transfers between devices, swap_second(): lax.ppermute(x, 'scen', [(i, i ^ k << (3 if i % 2 else 1)) for i in range...  20.2 us
    ppermute x15, starting transfers between devices, swap_second(): lax.ppermute(x, 'scen', [(i, i ^ k << (3 if i % 2 else 1)) for i in range...  20 us
    ppermute x15, starting transfers between devices, swap_first(): lax.ppermute(x, 'scen', [(i, i ^ k << (1 if i % 2 else 3)) for i in range...  19.7 us
    ppermute x11, waiting for transfers between devices, swap_core(): return lax.ppermute(x, 'scen', [(i, i ^ 1) for i in range(32)])  12 us
  transfers between devices with their start and end apart: 60, of which 43 were waited for; matrix products, arithmetic and copies ran while one was open for 0% of the time, Pallas kernels for 3%

profile of v10, /device:TPU:0, one launch (start us, length us, event | category | flops | bytes accessed | tf_op | source)
XLA Modules:
  0.0 182.0 jit_solution(14705444960050576964)
XLA Ops:
  0.8 6.8 %shard_map.130 = (f32[192,256]{1,0:T(8,128)S(1)}, f32[136,256]{1,0:T(8,128)S(1)}, f32[128,256]{1,0:T(8,128)S(1)}, f32[64,256,256]{2,1,0:T(8,128)S(1)}, s32[136]{0:T(256)S(4)}) custom-call(s32[3]{0:T(128)S(1)} %pad_add_fusion.place, s32[64]{0:T(128)} %bitcast.28, s32[64]{0:T(128)} %bitcast.29, f32[64,256,256]{2,1,0:T(8,128)} %bitcast.24, f32[32,256]{1,0:T(8,128)} %bitcast.25, ...), custom_call_target="tpu_custom_call" | custom-call | tf_op jit(solution)/shard_map/pallas_call | solution.py:208
  9.4 3.1 %collective-permute-start.3 = (f32[128,256]{1,0:T(8,128)S(1)}, f32[128,256]{1,0:T(8,128)S(1)}, u32[]{:S(2)}, u32[]{:S(2)}) collective-permute-start(f32[128,256]{1,0:T(8,128)S(1)} %shard_map.131.own), channel_id=1, source_target_pairs={{0,64},{4,20},{8,72},{12,28},{16,80},{20,4},{24,88},{28,12},{32,96... | collective-permute-start | bytes 393224 | tf_op jit(solution)/shard_map/ppermute | solution.py:36
  15.9 2.7 %collective-permute-done.2.r3 = f32[128,256]{1,0:T(8,128)S(1)} collective-permute-done((f32[128,256]{1,0:T(8,128)S(1)}, f32[128,256]{1,0:T(8,128)S(1)}, u32[]{:S(2)}, u32[]{:S(2)}) %collective-permute-start.2) | collective-permute-done | bytes 131104 | tf_op jit(solution)/shard_map/ppermute | solution.py:36
  18.7 4.0 %collective-permute-start.8 = (f32[128,256]{1,0:T(8,128)S(1)}, f32[128,256]{1,0:T(8,128)S(1)}, u32[]{:S(2)}, u32[]{:S(2)}) collective-permute-start(f32[128,256]{1,0:T(8,128)S(1)} %get-tuple-element.67.own), channel_id=1, source_target_pairs={{0,16},{4,68},{8,24},{12,76},{16,0},{20,84},{24,8},{28,92},{32,48}... | collective-permute-start | bytes 393224 | tf_op jit(solution)/shard_map/ppermute | solution.py:40
  31.4 5.4 %shard_map.134 = (f32[128,256]{1,0:T(8,128)S(1)}, f32[136,256]{1,0:T(8,128)S(1)}, f32[128,256]{1,0:T(8,128)S(1)}, f32[128,256]{1,0:T(8,128)S(1)}, f32[264,256]{1,0:T(8,128)S(1)}) custom-call(s32[136]{0:T(256)S(4)} %get-tuple-element.61.index_ref, f32[64,256,256]{2,1,0:T(8,128)S(1)} %get-tuple-element.62.tiles_ref, f32[256,256]{1,0:T(8,128)S(1)} %get-tuple-element.66.near, ...), custom_call_target="tpu_custom_call" | custom-call | tf_op jit(solution)/shard_map/pallas_call | solution.py:128
  44.6 2.9 %shard_map.136 = (f32[136,256]{1,0:T(8,128)S(1)}, f32[128,256]{1,0:T(8,128)S(1)}, f32[128,256]{1,0:T(8,128)S(1)}, f32[128,256]{1,0:T(8,128)S(1)}) custom-call(s32[136]{0:T(256)S(4)} %get-tuple-element.61.index_ref, f32[64,256,256]{2,1,0:T(8,128)S(1)} %get-tuple-element.62.tiles_ref, f32[256,256]{1,0:T(8,128)S(1)} %get-tuple-element.66.near, ...), custom_call_target="tpu_custom_call" | custom-call | tf_op jit(solution)/shard_map/pallas_call | solution.py:128
  49.0 3.6 %collective-permute-start.17 = (f32[160,256]{1,0:T(8,128)S(1)}, f32[160,256]{1,0:T(8,128)S(1)}, u32[]{:S(2)}, u32[]{:S(2)}) collective-permute-start(f32[160,256]{1,0:T(8,128)S(1)} %get-tuple-element.75), channel_id=1, source_target_pairs={{0,16},{4,68},{8,24},{12,76},{16,0},{20,84},{24,8},{28,92},{32,48}... | collective-permute-start | bytes 491528 | tf_op jit(solution)/shard_map/ppermute | solution.py:40
  60.6 3.0 %shard_map.139 = (f32[128,256]{1,0:T(8,128)S(1)}, f32[128,256]{1,0:T(8,128)S(1)}, f32[264,256]{1,0:T(8,128)S(1)}) custom-call(s32[136]{0:T(256)S(4)} %get-tuple-element.61.index_ref, f32[64,256,256]{2,1,0:T(8,128)S(1)} %get-tuple-element.62.tiles_ref, f32[128,256]{1,0:T(8,128)S(1)} %get-tuple-element.73.near, f32[128,256]{1,0:T(8,128)S(1)} %collective-permute-done.16.far, ...), custom_call_target="tpu_custom_call" | custom-call | tf_op jit(solution)/shard_map/pallas_call | solution.py:128
  67.2 3.2 %shard_map.140 = (f32[136,256]{1,0:T(8,128)S(1)}, f32[128,256]{1,0:T(8,128)S(1)}) custom-call(s32[136]{0:T(256)S(4)} %get-tuple-element.61.index_ref, f32[64,256,256]{2,1,0:T(8,128)S(1)} %get-tuple-element.62.tiles_ref, f32[128,256]{1,0:T(8,128)S(1)} %get-tuple-element.82.row_scale.rowold), custom_call_target="tpu_custom_call" | custom-call | tf_op jit(solution)/shard_map/pallas_call | solution.py:128
  70.8 2.7 %collective-permute-done.22.r3 = f32[128,256]{1,0:T(8,128)S(1)} collective-permute-done((f32[128,256]{1,0:T(8,128)S(1)}, f32[128,256]{1,0:T(8,128)S(1)}, u32[]{:S(2)}, u32[]{:S(2)}) %collective-permute-start.22) | collective-permute-done | bytes 131104 | tf_op jit(solution)/shard_map/ppermute | solution.py:44
  73.8 2.9 %collective-permute-start.27 = (f32[176,256]{1,0:T(8,128)S(1)}, f32[176,256]{1,0:T(8,128)S(1)}, u32[]{:S(2)}, u32[]{:S(2)}) collective-permute-start(f32[176,256]{1,0:T(8,128)S(1)} %get-tuple-element.89.own), channel_id=1, source_target_pairs={{0,64},{4,20},{8,72},{12,28},{16,80},{20,4},{24,88},{28,12},{32,96... | collective-permute-start | bytes 540680 | tf_op jit(solution)/shard_map/ppermute | solution.py:36
  77.9 3.0 %collective-permute-done.27.r2 = f32[176,256]{1,0:T(8,128)S(1)} collective-permute-done((f32[176,256]{1,0:T(8,128)S(1)}, f32[176,256]{1,0:T(8,128)S(1)}, u32[]{:S(2)}, u32[]{:S(2)}) %collective-permute-start.27) | collective-permute-done | bytes 180256 | tf_op jit(solution)/shard_map/ppermute | solution.py:36
  87.1 3.6 %collective-permute-done.30.r2 = f32[176,256]{1,0:T(8,128)S(1)} collective-permute-done((f32[176,256]{1,0:T(8,128)S(1)}, f32[176,256]{1,0:T(8,128)S(1)}, u32[]{:S(2)}, u32[]{:S(2)}) %collective-permute-start.30) | collective-permute-done | bytes 180256 | tf_op jit(solution)/shard_map/ppermute | solution.py:40
  101.3 3.1 %shard_map.145 = (f32[8,256]{1,0:T(8,128)S(1)}, f32[128,256]{1,0:T(8,128)S(1)}, f32[264,256]{1,0:T(8,128)S(1)}) custom-call(s32[136]{0:T(256)S(4)} %get-tuple-element.61.index_ref, f32[64,256,256]{2,1,0:T(8,128)S(1)} %get-tuple-element.62.tiles_ref, f32[8,256]{1,0:T(8,128)S(1)} %get-tuple-element.90.rest_0_, f32[8,256]{1,0:T(8,128)S(1)} %collective-permute-done.32.rest_1_, ...), custom_call_target="tpu_custom_call" | custom-call | tf_op jit(solution)/shard_map/pallas_call | solution.py:128
  108.0 4.1 %collective-permute-done.37.r2 = f32[128,256]{1,0:T(8,128)S(1)} collective-permute-done((f32[128,256]{1,0:T(8,128)S(1)}, f32[128,256]{1,0:T(8,128)S(1)}, u32[]{:S(2)}, u32[]{:S(2)}) %collective-permute-start.37) | collective-permute-done | bytes 131104 | tf_op jit(solution)/shard_map/ppermute | solution.py:44
  113.2 2.9 %shard_map.146 = (f32[136,256]{1,0:T(8,128)S(1)}, f32[128,256]{1,0:T(8,128)S(1)}, f32[128,256]{1,0:T(8,128)S(1)}) custom-call(s32[136]{0:T(256)S(4)} %get-tuple-element.61.index_ref, f32[64,256,256]{2,1,0:T(8,128)S(1)} %get-tuple-element.62.tiles_ref, f32[8,256]{1,0:T(8,128)S(1)} %get-tuple-element.96.steps.rest_0_, f32[128,256]{1,0:T(8,128)S(1)} %get-tuple-element.97.r0, ...), custom_call_target="tpu_custom_call" | custom-call | tf_op jit(solution)/shard_map/pallas_call | solution.py:128
  121.1 3.0 %collective-permute-done.41.r2 = f32[128,256]{1,0:T(8,128)S(1)} collective-permute-done((f32[128,256]{1,0:T(8,128)S(1)}, f32[128,256]{1,0:T(8,128)S(1)}, u32[]{:S(2)}, u32[]{:S(2)}) %collective-permute-start.41) | collective-permute-done | bytes 131104 | tf_op jit(solution)/shard_map/ppermute | solution.py:36
  129.6 3.0 %collective-permute-done.44.r2 = f32[128,256]{1,0:T(8,128)S(1)} collective-permute-done((f32[128,256]{1,0:T(8,128)S(1)}, f32[128,256]{1,0:T(8,128)S(1)}, u32[]{:S(2)}, u32[]{:S(2)}) %collective-permute-start.44) | collective-permute-done | bytes 131104 | tf_op jit(solution)/shard_map/ppermute | solution.py:40
  135.5 3.0 %shard_map.150 = (f32[128,256]{1,0:T(8,128)S(1)}, f32[264,256]{1,0:T(8,128)S(1)}) custom-call(s32[136]{0:T(256)S(4)} %get-tuple-element.61.index_ref, f32[64,256,256]{2,1,0:T(8,128)S(1)} %get-tuple-element.62.tiles_ref, f32[8,256]{1,0:T(8,128)S(1)} %get-tuple-element.96.steps.rest_0_, f32[136,256]{1,0:T(8,128)S(1)} %get-tuple-element.101.colown.rest_1_, ...), custom_call_target="tpu_custom_call" | custom-call | tf_op jit(solution)/shard_map/pallas_call | solution.py:128
  142.0 4.3 %collective-permute-done.48.r2 = f32[128,256]{1,0:T(8,128)S(1)} collective-permute-done((f32[128,256]{1,0:T(8,128)S(1)}, f32[128,256]{1,0:T(8,128)S(1)}, u32[]{:S(2)}, u32[]{:S(2)}) %collective-permute-start.48) | collective-permute-done | bytes 131104 | tf_op jit(solution)/shard_map/ppermute | solution.py:44
  148.4 2.9 %shard_map.151 = (f32[136,256]{1,0:T(8,128)S(1)}, f32[128,256]{1,0:T(8,128)S(1)}, f32[128,256]{1,0:T(8,128)S(1)}) custom-call(s32[136]{0:T(256)S(4)} %get-tuple-element.61.index_ref, f32[64,256,256]{2,1,0:T(8,128)S(1)} %get-tuple-element.62.tiles_ref, f32[8,256]{1,0:T(8,128)S(1)} %get-tuple-element.96.steps.rest_0_, f32[128,256]{1,0:T(8,128)S(1)} %get-tuple-element.104.r0, ...), custom_call_target="tpu_custom_call" | custom-call | tf_op jit(solution)/shard_map/pallas_call | solution.py:128
  156.3 3.0 %collective-permute-done.52.r2 = f32[128,256]{1,0:T(8,128)S(1)} collective-permute-done((f32[128,256]{1,0:T(8,128)S(1)}, f32[128,256]{1,0:T(8,128)S(1)}, u32[]{:S(2)}, u32[]{:S(2)}) %collective-permute-start.52) | collective-permute-done | bytes 131104 | tf_op jit(solution)/shard_map/ppermute | solution.py:36
  164.3 3.0 %collective-permute-done.55.r2 = f32[128,256]{1,0:T(8,128)S(1)} collective-permute-done((f32[128,256]{1,0:T(8,128)S(1)}, f32[128,256]{1,0:T(8,128)S(1)}, u32[]{:S(2)}, u32[]{:S(2)}) %collective-permute-start.55) | collective-permute-done | bytes 131104 | tf_op jit(solution)/shard_map/ppermute | solution.py:40
  170.5 3.0 %shard_map.155 = (f32[8,256]{1,0:T(8,128)}, f32[256,256]{1,0:T(8,128)}, f32[32,256]{1,0:T(8,128)S(1)}, f32[32,256]{1,0:T(8,128)S(1)}, f32[32,256]{1,0:T(8,128)S(...) custom-call(s32[136]{0:T(256)S(4)} %get-tuple-element.61.index_ref, ...), custom_call_target="tpu_custom_call" | custom-call | tf_op jit(solution)/shard_map/pallas_call | solution.py:128
  (136 shorter events, 98.8 us)
Async XLA Ops:
  7.6 7.3 %collective-permute-start.4 = (f32[192,256]{1,0:T(8,128)S(1)}, f32[192,256]{1,0:T(8,128)S(1)}, u32[]{:S(2)}, u32[]{:S(2)}) collective-permute-start(f32[192,256]{1,0:T(8,128)S(1)} %get-tuple-element.65.mine), channel_id=1, source_target_pairs={{0,1},{1,0},{2,3},{3,2},{4,5},{5,4},{6,7},{7,6},{8,9},{9,8},{10,11... | collective-permute-start | bytes 589832 | tf_op jit(solution)/shard_map/ppermute | solution.py:44
  9.4 6.6 %collective-permute-start.3 = (f32[128,256]{1,0:T(8,128)S(1)}, f32[128,256]{1,0:T(8,128)S(1)}, u32[]{:S(2)}, u32[]{:S(2)}) collective-permute-start(f32[128,256]{1,0:T(8,128)S(1)} %shard_map.131.own), channel_id=1, source_target_pairs={{0,64},{4,20},{8,72},{12,28},{16,80},{20,4},{24,88},{28,12},{32,96... | collective-permute-start | bytes 393224 | tf_op jit(solution)/shard_map/ppermute | solution.py:36
  18.7 7.7 %collective-permute-start.8 = (f32[128,256]{1,0:T(8,128)S(1)}, f32[128,256]{1,0:T(8,128)S(1)}, u32[]{:S(2)}, u32[]{:S(2)}) collective-permute-start(f32[128,256]{1,0:T(8,128)S(1)} %get-tuple-element.67.own), channel_id=1, source_target_pairs={{0,16},{4,68},{8,24},{12,76},{16,0},{20,84},{24,8},{28,92},{32,48}... | collective-permute-start | bytes 393224 | tf_op jit(solution)/shard_map/ppermute | solution.py:40
  23.7 7.7 %collective-permute-start.5 = (f32[256,256]{1,0:T(8,128)S(1)}, f32[256,256]{1,0:T(8,128)S(1)}, u32[]{:S(2)}, u32[]{:S(2)}) collective-permute-start(f32[256,256]{1,0:T(8,128)S(1)} %get-tuple-element.66.near), channel_id=1, source_target_pairs={{0,3},{1,2},{2,1},{3,0},{4,7},{5,6},{6,5},{7,4},{8,11},{9,10},{10,... | collective-permute-start | bytes 786440 | tf_op jit(solution)/shard_map/ppermute | solution.py:44
  40.5 7.0 %collective-permute-start.15 = (f32[128,256]{1,0:T(8,128)S(1)}, f32[128,256]{1,0:T(8,128)S(1)}, u32[]{:S(2)}, u32[]{:S(2)}) collective-permute-start(f32[128,256]{1,0:T(8,128)S(1)} %get-tuple-element.72.mine), channel_id=1, source_target_pairs={{0,1},{1,0},{2,3},{3,2},{4,5},{5,4},{6,7},{7,6},{8,9},{9,8},{10,11... | collective-permute-start | bytes 393224 | tf_op jit(solution)/shard_map/ppermute | solution.py:44
  40.6 7.0 %collective-permute-start.13 = (f32[128,256]{1,0:T(8,128)S(1)}, f32[128,256]{1,0:T(8,128)S(1)}, u32[]{:S(2)}, u32[]{:S(2)}) collective-permute-start(f32[128,256]{1,0:T(8,128)S(1)} %shard_map.135.own), channel_id=1, source_target_pairs={{0,64},{4,20},{8,72},{12,28},{16,80},{20,4},{24,88},{28,12},{32,96... | collective-permute-start | bytes 393224 | tf_op jit(solution)/shard_map/ppermute | solution.py:36
  49.0 7.0 %collective-permute-start.17 = (f32[160,256]{1,0:T(8,128)S(1)}, f32[160,256]{1,0:T(8,128)S(1)}, u32[]{:S(2)}, u32[]{:S(2)}) collective-permute-start(f32[160,256]{1,0:T(8,128)S(1)} %get-tuple-element.75), channel_id=1, source_target_pairs={{0,16},{4,68},{8,24},{12,76},{16,0},{20,84},{24,8},{28,92},{32,48}... | collective-permute-start | bytes 491528 | tf_op jit(solution)/shard_map/ppermute | solution.py:40
  52.6 6.5 %collective-permute-start.19 = (f32[160,256]{1,0:T(8,128)S(1)}, f32[160,256]{1,0:T(8,128)S(1)}, u32[]{:S(2)}, u32[]{:S(2)}) collective-permute-start(f32[160,256]{1,0:T(8,128)S(1)} %get-tuple-element.77), channel_id=1, source_target_pairs={{0,24},{4,100},{8,16},{12,108},{16,8},{20,116},{24,0},{28,124},{32... | collective-permute-start | bytes 491528 | tf_op jit(solution)/shard_map/ppermute | solution.py:40
  63.6 7.2 %collective-permute-start.23 = (f32[128,256]{1,0:T(8,128)S(1)}, f32[128,256]{1,0:T(8,128)S(1)}, u32[]{:S(2)}, u32[]{:S(2)}) collective-permute-start(f32[128,256]{1,0:T(8,128)S(1)} %get-tuple-element.81.r0), channel_id=1, source_target_pairs={{0,2},{1,3},{2,0},{3,1},{4,6},{5,7},{6,4},{7,5},{8,10},{9,11},{10,... | collective-permute-start | bytes 393224 | tf_op jit(solution)/shard_map/ppermute | solution.py:44
  65.9 7.7 %collective-permute-start.22 = (f32[128,256]{1,0:T(8,128)S(1)}, f32[128,256]{1,0:T(8,128)S(1)}, u32[]{:S(2)}, u32[]{:S(2)}) collective-permute-start(f32[128,256]{1,0:T(8,128)S(1)} %get-tuple-element.81.r0), channel_id=1, source_target_pairs={{0,3},{1,2},{2,1},{3,0},{4,7},{5,6},{6,5},{7,4},{8,11},{9,10},{10,... | collective-permute-start | bytes 393224 | tf_op jit(solution)/shard_map/ppermute | solution.py:44
  66.5 7.1 %collective-permute-start.21 = (f32[128,256]{1,0:T(8,128)S(1)}, f32[128,256]{1,0:T(8,128)S(1)}, u32[]{:S(2)}, u32[]{:S(2)}) collective-permute-start(f32[128,256]{1,0:T(8,128)S(1)} %get-tuple-element.81.r0), channel_id=1, source_target_pairs={{0,1},{1,0},{2,3},{3,2},{4,5},{5,4},{6,7},{7,6},{8,9},{9,8},{10,11... | collective-permute-start | bytes 393224 | tf_op jit(solution)/shard_map/ppermute | solution.py:44
  73.8 7.1 %collective-permute-start.27 = (f32[176,256]{1,0:T(8,128)S(1)}, f32[176,256]{1,0:T(8,128)S(1)}, u32[]{:S(2)}, u32[]{:S(2)}) collective-permute-start(f32[176,256]{1,0:T(8,128)S(1)} %get-tuple-element.89.own), channel_id=1, source_target_pairs={{0,64},{4,20},{8,72},{12,28},{16,80},{20,4},{24,88},{28,12},{32,96... | collective-permute-start | bytes 540680 | tf_op jit(solution)/shard_map/ppermute | solution.py:36
  76.8 6.7 %collective-permute-start.26 = (f32[176,256]{1,0:T(8,128)S(1)}, f32[176,256]{1,0:T(8,128)S(1)}, u32[]{:S(2)}, u32[]{:S(2)}) collective-permute-start(f32[176,256]{1,0:T(8,128)S(1)} %get-tuple-element.89.own), channel_id=1, source_target_pairs={{0,96},{4,28},{8,104},{12,20},{16,112},{20,12},{24,120},{28,4},{32... | collective-permute-start | bytes 540680 | tf_op jit(solution)/shard_map/ppermute | solution.py:36
  83.5 7.2 %collective-permute-start.30 = (f32[176,256]{1,0:T(8,128)S(1)}, f32[176,256]{1,0:T(8,128)S(1)}, u32[]{:S(2)}, u32[]{:S(2)}) collective-permute-start(f32[176,256]{1,0:T(8,128)S(1)} %shard_map.142.own), channel_id=1, source_target_pairs={{0,16},{4,68},{8,24},{12,76},{16,0},{20,84},{24,8},{28,92},{32,48}... | collective-permute-start | bytes 540680 | tf_op jit(solution)/shard_map/ppermute | solution.py:40
  85.0 7.5 %collective-permute-start.29 = (f32[176,256]{1,0:T(8,128)S(1)}, f32[176,256]{1,0:T(8,128)S(1)}, u32[]{:S(2)}, u32[]{:S(2)}) collective-permute-start(f32[176,256]{1,0:T(8,128)S(1)} %shard_map.142.own), channel_id=1, source_target_pairs={{0,24},{4,100},{8,16},{12,108},{16,8},{20,116},{24,0},{28,124},{32... | collective-permute-start | bytes 540680 | tf_op jit(solution)/shard_map/ppermute | solution.py:40
  104.4 7.7 %collective-permute-start.37 = (f32[128,256]{1,0:T(8,128)S(1)}, f32[128,256]{1,0:T(8,128)S(1)}, u32[]{:S(2)}, u32[]{:S(2)}) collective-permute-start(f32[128,256]{1,0:T(8,128)S(1)} %get-tuple-element.97.r0), channel_id=1, source_target_pairs={{0,2},{1,3},{2,0},{3,1},{4,6},{5,7},{6,4},{7,5},{8,10},{9,11},{10,... | collective-permute-start | bytes 393224 | tf_op jit(solution)/shard_map/ppermute | solution.py:44
  117.5 6.5 %collective-permute-start.41 = (f32[128,256]{1,0:T(8,128)S(1)}, f32[128,256]{1,0:T(8,128)S(1)}, u32[]{:S(2)}, u32[]{:S(2)}) collective-permute-start(f32[128,256]{1,0:T(8,128)S(1)} %shard_map.147.own), channel_id=1, source_target_pairs={{0,64},{4,20},{8,72},{12,28},{16,80},{20,4},{24,88},{28,12},{32,96... | collective-permute-start | bytes 393224 | tf_op jit(solution)/shard_map/ppermute | solution.py:36
  126.0 6.6 %collective-permute-start.44 = (f32[128,256]{1,0:T(8,128)S(1)}, f32[128,256]{1,0:T(8,128)S(1)}, u32[]{:S(2)}, u32[]{:S(2)}) collective-permute-start(f32[128,256]{1,0:T(8,128)S(1)} %shard_map.148.own), channel_id=1, source_target_pairs={{0,16},{4,68},{8,24},{12,76},{16,0},{20,84},{24,8},{28,92},{32,48}... | collective-permute-start | bytes 393224 | tf_op jit(solution)/shard_map/ppermute | solution.py:40
  127.3 6.7 %collective-permute-start.43 = (f32[128,256]{1,0:T(8,128)S(1)}, f32[128,256]{1,0:T(8,128)S(1)}, u32[]{:S(2)}, u32[]{:S(2)}) collective-permute-start(f32[128,256]{1,0:T(8,128)S(1)} %shard_map.148.own), channel_id=1, source_target_pairs={{0,24},{4,100},{8,16},{12,108},{16,8},{20,116},{24,0},{28,124},{32... | collective-permute-start | bytes 393224 | tf_op jit(solution)/shard_map/ppermute | solution.py:40
  138.5 7.8 %collective-permute-start.48 = (f32[128,256]{1,0:T(8,128)S(1)}, f32[128,256]{1,0:T(8,128)S(1)}, u32[]{:S(2)}, u32[]{:S(2)}) collective-permute-start(f32[128,256]{1,0:T(8,128)S(1)} %get-tuple-element.104.r0), channel_id=1, source_target_pairs={{0,2},{1,3},{2,0},{3,1},{4,6},{5,7},{6,4},{7,5},{8,10},{9,11},{10,... | collective-permute-start | bytes 393224 | tf_op jit(solution)/shard_map/ppermute | solution.py:44
  140.0 8.4 %collective-permute-start.47 = (f32[128,256]{1,0:T(8,128)S(1)}, f32[128,256]{1,0:T(8,128)S(1)}, u32[]{:S(2)}, u32[]{:S(2)}) collective-permute-start(f32[128,256]{1,0:T(8,128)S(1)} %get-tuple-element.104.r0), channel_id=1, source_target_pairs={{0,3},{1,2},{2,1},{3,0},{4,7},{5,6},{6,5},{7,4},{8,11},{9,10},{10,... | collective-permute-start | bytes 393224 | tf_op jit(solution)/shard_map/ppermute | solution.py:44
  141.5 6.9 %collective-permute-start.46 = (f32[128,256]{1,0:T(8,128)S(1)}, f32[128,256]{1,0:T(8,128)S(1)}, u32[]{:S(2)}, u32[]{:S(2)}) collective-permute-start(f32[128,256]{1,0:T(8,128)S(1)} %get-tuple-element.104.r0), channel_id=1, source_target_pairs={{0,1},{1,0},{2,3},{3,2},{4,5},{5,4},{6,7},{7,6},{8,9},{9,8},{10,11... | collective-permute-start | bytes 393224 | tf_op jit(solution)/shard_map/ppermute | solution.py:44
  152.7 6.6 %collective-permute-start.52 = (f32[128,256]{1,0:T(8,128)S(1)}, f32[128,256]{1,0:T(8,128)S(1)}, u32[]{:S(2)}, u32[]{:S(2)}) collective-permute-start(f32[128,256]{1,0:T(8,128)S(1)} %shard_map.152.own), channel_id=1, source_target_pairs={{0,64},{4,20},{8,72},{12,28},{16,80},{20,4},{24,88},{28,12},{32,96... | collective-permute-start | bytes 393224 | tf_op jit(solution)/shard_map/ppermute | solution.py:36
  160.7 6.6 %collective-permute-start.55 = (f32[128,256]{1,0:T(8,128)S(1)}, f32[128,256]{1,0:T(8,128)S(1)}, u32[]{:S(2)}, u32[]{:S(2)}) collective-permute-start(f32[128,256]{1,0:T(8,128)S(1)} %shard_map.153.own), channel_id=1, source_target_pairs={{0,16},{4,68},{8,24},{12,76},{16,0},{20,84},{24,8},{28,92},{32,48}... | collective-permute-start | bytes 393224 | tf_op jit(solution)/shard_map/ppermute | solution.py:40
  (42 other events, 270.4 us)

commit v11 on v10

--- a/solution.py
+++ b/solution.py
@@ -221,27 +221,33 @@
     )(ids[2], *(pltpu.with_memory_space_constraint(x, pltpu.HBM) for x in (*ids[:2], source, rhs, dual)))
 
 
-def second_stats_kernel(
-    index_ref, tiles_ref, near, far, loc, mine, other, rowout, colown, colother, rownew,
-    colnew, racc, cacc, rowf, colf,
+def second_columns_kernel(
+    index_ref, tiles_ref, near, far, loc, mine, other, colown, colother, rownew, colnew, cacc, rowf
 ):
     row = jnp.maximum(near[0:RT], far[0:RT])
     new = 1.0 / jnp.sqrt(row + EPS)
     rownew[...] = new
     split_to(rowf, new)
     for lo, hi, src in ((0, CT, loc), (CT, OWN, mine), (OWN, CW, other)):
-        new = 1.0 / jnp.sqrt(src[0 : hi - lo] + EPS)
-        colnew[lo:hi] = new
-        split_to(colf, new, lo)
+        colnew[lo:hi] = 1.0 / jnp.sqrt(src[0 : hi - lo] + EPS)
+    cacc[...] = jnp.zeros_like(cacc)
+
+    def visit(t, col, row):
+        col_pass(tiles_ref, t, col, row, rowf, cacc, jnp.maximum, True)
+
+    each_tile(index_ref, visit)
+    put_columns(cacc, colown, colother)
+
+
+def second_rows_kernel(index_ref, tiles_ref, col_scale, rowout, racc, colf):
+    split_to(colf, col_scale[...])
     racc[...] = jnp.zeros_like(racc)
-    cacc[...] = jnp.zeros_like(cacc)
-
-    def visit(t, col, row):
-        both_pass(tiles_ref, t, col, row, rowf, colf, racc, cacc)
+
+    def visit(t, col, row):
+        row_pass(tiles_ref, t, col, row, colf, racc, jnp.maximum, True)
 
     each_tile(index_ref, visit)
     join_from(racc, rowout, 0, RT)
-    put_columns(cacc, colown, colother)
 
 
 def third_rows_kernel(
@@ -375,6 +381,10 @@
     out[...] = op(colown[CT:OWN], got[...])
 
 
+def core_after_kernel(tiles_ref, colown, got, after, out):
+    out[...] = jnp.maximum(colown[CT:OWN], got[...])
+
+
 def merge_kernel(op, tiles_ref, own, r1, r3, r2, out):
     out[...] = tree(op, own[...], (r1[...], r2[...], r3[...]))
 
@@ -501,14 +511,16 @@
     (link,) = run(functools.partial(merge_kernel, jnp.maximum), (), over(swap_second, link), (HALF,))
 
     gathered = (near, far)
-    row_part, colown, colother, row_scale, col_scale = run(
-        second_stats_kernel,
+    colown, colother, row_scale, col_scale = run(
+        second_columns_kernel,
         (index,),
         (near, far, colown, link, swap_core(link)),
-        (RT, OWN, HALF, RT, CW),
-        (ROWS, COLS, ROWS, COLS),
-    )
-    (link,) = run(functools.partial(core_kernel, jnp.maximum), (), (colown, swap_core(colother)), (HALF,))
+        (OWN, HALF, RT, CW),
+        (COLS, ROWS),
+    )
+    colgot = swap_core(colother)
+    (row_part,) = run(second_rows_kernel, (index,), (col_scale,), (RT,), (ROWS, COLS))
+    (link,) = run(core_after_kernel, (), (colown, colgot, row_part), (HALF,))
     got = over(swap_first, link)
     gradown, gradother, rhs_rows, dual_rows = run(
         first_backward_kernel, (index,), (*gathered, got[2]), (OWN, HALF, RT, RT), (COLS, ROWS)

time: 182 us -> 182 us (level)
    pallas_call x25 -> x26, Pallas kernels: 30.2 us -> 30.6 us  [call(): pl.pallas_call(kernel, out_shape=tuple((jax.ShapeDtypeStruct((n, TILE), F...]
  transfers between devices with their start and end apart: 60 -> 60, of which waited for: 43 -> 41; matrix products, arithmetic and copies ran while one was open for 0% -> 0% of each run, Pallas kernels for 3% -> 5%
where the time goes in v11:
time: 182 us; the launch traced here: 181 us
  waiting for transfers between devices  75.6 us (42%)
  starting transfers between devices  66.7 us (37%)
  Pallas kernels  38 us (21%)
    pallas_call x26, Pallas kernels, call(): pl.pallas_call(kernel, out_shape=tuple((jax.ShapeDtypeStruct((n, TILE), F...  30.6 us
    ppermute x19, starting transfers between devices, swap_y(): return lax.ppermute(x, 'col', [(i, i ^ k) for i in range(4)])  26.2 us
    ppermute x19, waiting for transfers between devices, swap_y(): return lax.ppermute(x, 'col', [(i, i ^ k) for i in range(4)])  24 us
    ppermute x15, waiting for transfers between devices, swap_first(): lax.ppermute(x, 'scen', [(i, i ^ k << (1 if i % 2 else 3)) for i in range...  20.4 us
    ppermute x15, waiting for transfers between devices, swap_second(): lax.ppermute(x, 'scen', [(i, i ^ k << (3 if i % 2 else 1)) for i in range...  20.3 us
    ppermute x15, starting transfers between devices, swap_second(): lax.ppermute(x, 'scen', [(i, i ^ k << (3 if i % 2 else 1)) for i in range...  20 us
    ppermute x15, starting transfers between devices, swap_first(): lax.ppermute(x, 'scen', [(i, i ^ k << (1 if i % 2 else 3)) for i in range...  19.6 us
    ppermute x11, waiting for transfers between devices, swap_core(): return lax.ppermute(x, 'scen', [(i, i ^ 1) for i in range(32)])  10.8 us
  transfers between devices with their start and end apart: 60, of which 41 were waited for; matrix products, arithmetic and copies ran while one was open for 0% of the time, Pallas kernels for 5%

profile of v11, /device:TPU:0, one launch (start us, length us, event | category | flops | bytes accessed | tf_op | source)
XLA Modules:
  0.0 181.4 jit_solution(322368258801803870)
XLA Ops:
  0.8 6.8 %shard_map.130 = (f32[192,256]{1,0:T(8,128)S(1)}, f32[136,256]{1,0:T(8,128)S(1)}, f32[128,256]{1,0:T(8,128)S(1)}, f32[64,256,256]{2,1,0:T(8,128)S(1)}, s32[136]{0:T(256)S(4)}) custom-call(s32[3]{0:T(128)S(1)} %pad_add_fusion.place, s32[64]{0:T(128)} %bitcast.28, s32[64]{0:T(128)} %bitcast.29, f32[64,256,256]{2,1,0:T(8,128)} %bitcast.24, f32[32,256]{1,0:T(8,128)} %bitcast.25, ...), custom_call_target="tpu_custom_call" | custom-call | tf_op jit(solution)/shard_map/pallas_call | solution.py:208
  9.4 3.1 %collective-permute-start.3 = (f32[128,256]{1,0:T(8,128)S(1)}, f32[128,256]{1,0:T(8,128)S(1)}, u32[]{:S(2)}, u32[]{:S(2)}) collective-permute-start(f32[128,256]{1,0:T(8,128)S(1)} %shard_map.131.own), channel_id=1, source_target_pairs={{0,64},{4,20},{8,72},{12,28},{16,80},{20,4},{24,88},{28,12},{32,96... | collective-permute-start | bytes 393224 | tf_op jit(solution)/shard_map/ppermute | solution.py:36
  15.9 2.7 %collective-permute-done.2.r3 = f32[128,256]{1,0:T(8,128)S(1)} collective-permute-done((f32[128,256]{1,0:T(8,128)S(1)}, f32[128,256]{1,0:T(8,128)S(1)}, u32[]{:S(2)}, u32[]{:S(2)}) %collective-permute-start.2) | collective-permute-done | bytes 131104 | tf_op jit(solution)/shard_map/ppermute | solution.py:36
  18.7 4.0 %collective-permute-start.8 = (f32[128,256]{1,0:T(8,128)S(1)}, f32[128,256]{1,0:T(8,128)S(1)}, u32[]{:S(2)}, u32[]{:S(2)}) collective-permute-start(f32[128,256]{1,0:T(8,128)S(1)} %get-tuple-element.66.own), channel_id=1, source_target_pairs={{0,16},{4,68},{8,24},{12,76},{16,0},{20,84},{24,8},{28,92},{32,48}... | collective-permute-start | bytes 393224 | tf_op jit(solution)/shard_map/ppermute | solution.py:40
  31.4 3.0 %shard_map.134 = (f32[136,256]{1,0:T(8,128)S(1)}, f32[128,256]{1,0:T(8,128)S(1)}, f32[128,256]{1,0:T(8,128)S(1)}, f32[264,256]{1,0:T(8,128)S(1)}) custom-call(s32[136]{0:T(256)S(4)} %get-tuple-element.60.index_ref, f32[64,256,256]{2,1,0:T(8,128)S(1)} %get-tuple-element.61.tiles_ref, f32[256,256]{1,0:T(8,128)S(1)} %get-tuple-element.65.near, ...), custom_call_target="tpu_custom_call" | custom-call | tf_op jit(solution)/shard_map/pallas_call | solution.py:128
  34.5 2.9 %shard_map.135.after.mine = f32[128,256]{1,0:T(8,128)S(1)} custom-call(s32[136]{0:T(256)S(4)} %get-tuple-element.60.index_ref, f32[64,256,256]{2,1,0:T(8,128)S(1)} %get-tuple-element.61.tiles_ref, f32[264,256]{1,0:T(8,128)S(1)} %get-tuple-element.69.col_scale.colold), custom_call_target="tpu_custom_call" | custom-call | tf_op jit(solution)/shard_map/pallas_call | solution.py:128
  43.7 2.9 %shard_map.137 = (f32[136,256]{1,0:T(8,128)S(1)}, f32[128,256]{1,0:T(8,128)S(1)}, f32[128,256]{1,0:T(8,128)S(1)}, f32[128,256]{1,0:T(8,128)S(1)}) custom-call(s32[136]{0:T(256)S(4)} %get-tuple-element.60.index_ref, f32[64,256,256]{2,1,0:T(8,128)S(1)} %get-tuple-element.61.tiles_ref, f32[256,256]{1,0:T(8,128)S(1)} %get-tuple-element.65.near, ...), custom_call_target="tpu_custom_call" | custom-call | tf_op jit(solution)/shard_map/pallas_call | solution.py:128
  48.1 3.6 %collective-permute-start.17 = (f32[160,256]{1,0:T(8,128)S(1)}, f32[160,256]{1,0:T(8,128)S(1)}, u32[]{:S(2)}, u32[]{:S(2)}) collective-permute-start(f32[160,256]{1,0:T(8,128)S(1)} %get-tuple-element.74), channel_id=1, source_target_pairs={{0,16},{4,68},{8,24},{12,76},{16,0},{20,84},{24,8},{28,92},{32,48}... | collective-permute-start | bytes 491528 | tf_op jit(solution)/shard_map/ppermute | solution.py:40
  59.9 3.0 %shard_map.140 = (f32[128,256]{1,0:T(8,128)S(1)}, f32[128,256]{1,0:T(8,128)S(1)}, f32[264,256]{1,0:T(8,128)S(1)}) custom-call(s32[136]{0:T(256)S(4)} %get-tuple-element.60.index_ref, f32[64,256,256]{2,1,0:T(8,128)S(1)} %get-tuple-element.61.tiles_ref, f32[128,256]{1,0:T(8,128)S(1)} %get-tuple-element.72.near, f32[128,256]{1,0:T(8,128)S(1)} %collective-permute-done.16.far, ...), custom_call_target="tpu_custom_call" | custom-call | tf_op jit(solution)/shard_map/pallas_call | solution.py:128
  66.8 3.2 %shard_map.141 = (f32[136,256]{1,0:T(8,128)S(1)}, f32[128,256]{1,0:T(8,128)S(1)}) custom-call(s32[136]{0:T(256)S(4)} %get-tuple-element.60.index_ref, f32[64,256,256]{2,1,0:T(8,128)S(1)} %get-tuple-element.61.tiles_ref, f32[128,256]{1,0:T(8,128)S(1)} %get-tuple-element.80.row_scale.rowold), custom_call_target="tpu_custom_call" | custom-call | tf_op jit(solution)/shard_map/pallas_call | solution.py:128
  73.4 2.8 %collective-permute-start.27 = (f32[176,256]{1,0:T(8,128)S(1)}, f32[176,256]{1,0:T(8,128)S(1)}, u32[]{:S(2)}, u32[]{:S(2)}) collective-permute-start(f32[176,256]{1,0:T(8,128)S(1)} %get-tuple-element.87.own), channel_id=1, source_target_pairs={{0,64},{4,20},{8,72},{12,28},{16,80},{20,4},{24,88},{28,12},{32,96... | collective-permute-start | bytes 540680 | tf_op jit(solution)/shard_map/ppermute | solution.py:36
  77.3 3.1 %collective-permute-done.27.r2 = f32[176,256]{1,0:T(8,128)S(1)} collective-permute-done((f32[176,256]{1,0:T(8,128)S(1)}, f32[176,256]{1,0:T(8,128)S(1)}, u32[]{:S(2)}, u32[]{:S(2)}) %collective-permute-start.27) | collective-permute-done | bytes 180256 | tf_op jit(solution)/shard_map/ppermute | solution.py:36
  86.5 3.6 %collective-permute-done.30.r2 = f32[176,256]{1,0:T(8,128)S(1)} collective-permute-done((f32[176,256]{1,0:T(8,128)S(1)}, f32[176,256]{1,0:T(8,128)S(1)}, u32[]{:S(2)}, u32[]{:S(2)}) %collective-permute-start.30) | collective-permute-done | bytes 180256 | tf_op jit(solution)/shard_map/ppermute | solution.py:40
  100.5 3.1 %shard_map.146 = (f32[8,256]{1,0:T(8,128)S(1)}, f32[128,256]{1,0:T(8,128)S(1)}, f32[264,256]{1,0:T(8,128)S(1)}) custom-call(s32[136]{0:T(256)S(4)} %get-tuple-element.60.index_ref, f32[64,256,256]{2,1,0:T(8,128)S(1)} %get-tuple-element.61.tiles_ref, f32[8,256]{1,0:T(8,128)S(1)} %get-tuple-element.88.rest_0_, f32[8,256]{1,0:T(8,128)S(1)} %collective-permute-done.32.rest_1_, ...), custom_call_target="tpu_custom_call" | custom-call | tf_op jit(solution)/shard_map/pallas_call | solution.py:128
  107.2 4.0 %collective-permute-done.37.r2 = f32[128,256]{1,0:T(8,128)S(1)} collective-permute-done((f32[128,256]{1,0:T(8,128)S(1)}, f32[128,256]{1,0:T(8,128)S(1)}, u32[]{:S(2)}, u32[]{:S(2)}) %collective-permute-start.37) | collective-permute-done | bytes 131104 | tf_op jit(solution)/shard_map/ppermute | solution.py:44
  112.5 2.9 %shard_map.147 = (f32[136,256]{1,0:T(8,128)S(1)}, f32[128,256]{1,0:T(8,128)S(1)}, f32[128,256]{1,0:T(8,128)S(1)}) custom-call(s32[136]{0:T(256)S(4)} %get-tuple-element.60.index_ref, f32[64,256,256]{2,1,0:T(8,128)S(1)} %get-tuple-element.61.tiles_ref, f32[8,256]{1,0:T(8,128)S(1)} %get-tuple-element.94.steps.rest_0_, f32[128,256]{1,0:T(8,128)S(1)} %get-tuple-element.95.r0, ...), custom_call_target="tpu_custom_call" | custom-call | tf_op jit(solution)/shard_map/pallas_call | solution.py:128
  120.4 3.0 %collective-permute-done.41.r2 = f32[128,256]{1,0:T(8,128)S(1)} collective-permute-done((f32[128,256]{1,0:T(8,128)S(1)}, f32[128,256]{1,0:T(8,128)S(1)}, u32[]{:S(2)}, u32[]{:S(2)}) %collective-permute-start.41) | collective-permute-done | bytes 131104 | tf_op jit(solution)/shard_map/ppermute | solution.py:36
  128.9 3.0 %collective-permute-done.44.r2 = f32[128,256]{1,0:T(8,128)S(1)} collective-permute-done((f32[128,256]{1,0:T(8,128)S(1)}, f32[128,256]{1,0:T(8,128)S(1)}, u32[]{:S(2)}, u32[]{:S(2)}) %collective-permute-start.44) | collective-permute-done | bytes 131104 | tf_op jit(solution)/shard_map/ppermute | solution.py:40
  134.7 3.0 %shard_map.151 = (f32[128,256]{1,0:T(8,128)S(1)}, f32[264,256]{1,0:T(8,128)S(1)}) custom-call(s32[136]{0:T(256)S(4)} %get-tuple-element.60.index_ref, f32[64,256,256]{2,1,0:T(8,128)S(1)} %get-tuple-element.61.tiles_ref, f32[8,256]{1,0:T(8,128)S(1)} %get-tuple-element.94.steps.rest_0_, f32[136,256]{1,0:T(8,128)S(1)} %get-tuple-element.99.colown.rest_1_, ...), custom_call_target="tpu_custom_call" | custom-call | tf_op jit(solution)/shard_map/pallas_call | solution.py:128
  141.3 4.3 %collective-permute-done.48.r2 = f32[128,256]{1,0:T(8,128)S(1)} collective-permute-done((f32[128,256]{1,0:T(8,128)S(1)}, f32[128,256]{1,0:T(8,128)S(1)}, u32[]{:S(2)}, u32[]{:S(2)}) %collective-permute-start.48) | collective-permute-done | bytes 131104 | tf_op jit(solution)/shard_map/ppermute | solution.py:44
  147.7 2.9 %shard_map.152 = (f32[136,256]{1,0:T(8,128)S(1)}, f32[128,256]{1,0:T(8,128)S(1)}, f32[128,256]{1,0:T(8,128)S(1)}) custom-call(s32[136]{0:T(256)S(4)} %get-tuple-element.60.index_ref, f32[64,256,256]{2,1,0:T(8,128)S(1)} %get-tuple-element.61.tiles_ref, f32[8,256]{1,0:T(8,128)S(1)} %get-tuple-element.94.steps.rest_0_, f32[128,256]{1,0:T(8,128)S(1)} %get-tuple-element.102.r0, ...), custom_call_target="tpu_custom_call" | custom-call | tf_op jit(solution)/shard_map/pallas_call | solution.py:128
  155.6 3.0 %collective-permute-done.52.r2 = f32[128,256]{1,0:T(8,128)S(1)} collective-permute-done((f32[128,256]{1,0:T(8,128)S(1)}, f32[128,256]{1,0:T(8,128)S(1)}, u32[]{:S(2)}, u32[]{:S(2)}) %collective-permute-start.52) | collective-permute-done | bytes 131104 | tf_op jit(solution)/shard_map/ppermute | solution.py:36
  163.6 3.0 %collective-permute-done.55.r2 = f32[128,256]{1,0:T(8,128)S(1)} collective-permute-done((f32[128,256]{1,0:T(8,128)S(1)}, f32[128,256]{1,0:T(8,128)S(1)}, u32[]{:S(2)}, u32[]{:S(2)}) %collective-permute-start.55) | collective-permute-done | bytes 131104 | tf_op jit(solution)/shard_map/ppermute | solution.py:40
  169.8 3.0 %shard_map.156 = (f32[8,256]{1,0:T(8,128)}, f32[256,256]{1,0:T(8,128)}, f32[32,256]{1,0:T(8,128)S(1)}, f32[32,256]{1,0:T(8,128)S(1)}, f32[32,256]{1,0:T(8,128)S(...) custom-call(s32[136]{0:T(256)S(4)} %get-tuple-element.60.index_ref, ...), custom_call_target="tpu_custom_call" | custom-call | tf_op jit(solution)/shard_map/pallas_call | solution.py:128
  (137 shorter events, 100.6 us)
Async XLA Ops:
  7.6 7.3 %collective-permute-start.4 = (f32[192,256]{1,0:T(8,128)S(1)}, f32[192,256]{1,0:T(8,128)S(1)}, u32[]{:S(2)}, u32[]{:S(2)}) collective-permute-start(f32[192,256]{1,0:T(8,128)S(1)} %get-tuple-element.64.mine), channel_id=1, source_target_pairs={{0,1},{1,0},{2,3},{3,2},{4,5},{5,4},{6,7},{7,6},{8,9},{9,8},{10,11... | collective-permute-start | bytes 589832 | tf_op jit(solution)/shard_map/ppermute | solution.py:44
  9.4 6.5 %collective-permute-start.3 = (f32[128,256]{1,0:T(8,128)S(1)}, f32[128,256]{1,0:T(8,128)S(1)}, u32[]{:S(2)}, u32[]{:S(2)}) collective-permute-start(f32[128,256]{1,0:T(8,128)S(1)} %shard_map.131.own), channel_id=1, source_target_pairs={{0,64},{4,20},{8,72},{12,28},{16,80},{20,4},{24,88},{28,12},{32,96... | collective-permute-start | bytes 393224 | tf_op jit(solution)/shard_map/ppermute | solution.py:36
  18.7 7.7 %collective-permute-start.8 = (f32[128,256]{1,0:T(8,128)S(1)}, f32[128,256]{1,0:T(8,128)S(1)}, u32[]{:S(2)}, u32[]{:S(2)}) collective-permute-start(f32[128,256]{1,0:T(8,128)S(1)} %get-tuple-element.66.own), channel_id=1, source_target_pairs={{0,16},{4,68},{8,24},{12,76},{16,0},{20,84},{24,8},{28,92},{32,48}... | collective-permute-start | bytes 393224 | tf_op jit(solution)/shard_map/ppermute | solution.py:40
  23.7 7.7 %collective-permute-start.5 = (f32[256,256]{1,0:T(8,128)S(1)}, f32[256,256]{1,0:T(8,128)S(1)}, u32[]{:S(2)}, u32[]{:S(2)}) collective-permute-start(f32[256,256]{1,0:T(8,128)S(1)} %get-tuple-element.65.near), channel_id=1, source_target_pairs={{0,3},{1,2},{2,1},{3,0},{4,7},{5,6},{6,5},{7,4},{8,11},{9,10},{10,... | collective-permute-start | bytes 786440 | tf_op jit(solution)/shard_map/ppermute | solution.py:44
  39.6 7.0 %collective-permute-start.15 = (f32[128,256]{1,0:T(8,128)S(1)}, f32[128,256]{1,0:T(8,128)S(1)}, u32[]{:S(2)}, u32[]{:S(2)}) collective-permute-start(f32[128,256]{1,0:T(8,128)S(1)} %shard_map.135.after.mine), channel_id=1, source_target_pairs={{0,1},{1,0},{2,3},{3,2},{4,5},{5,4},{6,7},{7,6},{8,9},{9,8},{10,11... | collective-permute-start | bytes 393224 | tf_op jit(solution)/shard_map/ppermute | solution.py:44
  39.8 6.8 %collective-permute-start.13 = (f32[128,256]{1,0:T(8,128)S(1)}, f32[128,256]{1,0:T(8,128)S(1)}, u32[]{:S(2)}, u32[]{:S(2)}) collective-permute-start(f32[128,256]{1,0:T(8,128)S(1)} %shard_map.136.own), channel_id=1, source_target_pairs={{0,64},{4,20},{8,72},{12,28},{16,80},{20,4},{24,88},{28,12},{32,96... | collective-permute-start | bytes 393224 | tf_op jit(solution)/shard_map/ppermute | solution.py:36
  48.1 7.0 %collective-permute-start.17 = (f32[160,256]{1,0:T(8,128)S(1)}, f32[160,256]{1,0:T(8,128)S(1)}, u32[]{:S(2)}, u32[]{:S(2)}) collective-permute-start(f32[160,256]{1,0:T(8,128)S(1)} %get-tuple-element.74), channel_id=1, source_target_pairs={{0,16},{4,68},{8,24},{12,76},{16,0},{20,84},{24,8},{28,92},{32,48}... | collective-permute-start | bytes 491528 | tf_op jit(solution)/shard_map/ppermute | solution.py:40
  62.9 7.2 %collective-permute-start.23 = (f32[128,256]{1,0:T(8,128)S(1)}, f32[128,256]{1,0:T(8,128)S(1)}, u32[]{:S(2)}, u32[]{:S(2)}) collective-permute-start(f32[128,256]{1,0:T(8,128)S(1)} %get-tuple-element.79.r0), channel_id=1, source_target_pairs={{0,2},{1,3},{2,0},{3,1},{4,6},{5,7},{6,4},{7,5},{8,10},{9,11},{10,... | collective-permute-start | bytes 393224 | tf_op jit(solution)/shard_map/ppermute | solution.py:44
  65.0 7.8 %collective-permute-start.22 = (f32[128,256]{1,0:T(8,128)S(1)}, f32[128,256]{1,0:T(8,128)S(1)}, u32[]{:S(2)}, u32[]{:S(2)}) collective-permute-start(f32[128,256]{1,0:T(8,128)S(1)} %get-tuple-element.79.r0), channel_id=1, source_target_pairs={{0,3},{1,2},{2,1},{3,0},{4,7},{5,6},{6,5},{7,4},{8,11},{9,10},{10,... | collective-permute-start | bytes 393224 | tf_op jit(solution)/shard_map/ppermute | solution.py:44
  66.1 7.1 %collective-permute-start.21 = (f32[128,256]{1,0:T(8,128)S(1)}, f32[128,256]{1,0:T(8,128)S(1)}, u32[]{:S(2)}, u32[]{:S(2)}) collective-permute-start(f32[128,256]{1,0:T(8,128)S(1)} %get-tuple-element.79.r0), channel_id=1, source_target_pairs={{0,1},{1,0},{2,3},{3,2},{4,5},{5,4},{6,7},{7,6},{8,9},{9,8},{10,11... | collective-permute-start | bytes 393224 | tf_op jit(solution)/shard_map/ppermute | solution.py:44
  73.4 7.1 %collective-permute-start.27 = (f32[176,256]{1,0:T(8,128)S(1)}, f32[176,256]{1,0:T(8,128)S(1)}, u32[]{:S(2)}, u32[]{:S(2)}) collective-permute-start(f32[176,256]{1,0:T(8,128)S(1)} %get-tuple-element.87.own), channel_id=1, source_target_pairs={{0,64},{4,20},{8,72},{12,28},{16,80},{20,4},{24,88},{28,12},{32,96... | collective-permute-start | bytes 540680 | tf_op jit(solution)/shard_map/ppermute | solution.py:36
  76.2 6.7 %collective-permute-start.26 = (f32[176,256]{1,0:T(8,128)S(1)}, f32[176,256]{1,0:T(8,128)S(1)}, u32[]{:S(2)}, u32[]{:S(2)}) collective-permute-start(f32[176,256]{1,0:T(8,128)S(1)} %get-tuple-element.87.own), channel_id=1, source_target_pairs={{0,96},{4,28},{8,104},{12,20},{16,112},{20,12},{24,120},{28,4},{32... | collective-permute-start | bytes 540680 | tf_op jit(solution)/shard_map/ppermute | solution.py:36
  83.0 7.2 %collective-permute-start.30 = (f32[176,256]{1,0:T(8,128)S(1)}, f32[176,256]{1,0:T(8,128)S(1)}, u32[]{:S(2)}, u32[]{:S(2)}) collective-permute-start(f32[176,256]{1,0:T(8,128)S(1)} %shard_map.143.own), channel_id=1, source_target_pairs={{0,16},{4,68},{8,24},{12,76},{16,0},{20,84},{24,8},{28,92},{32,48}... | collective-permute-start | bytes 540680 | tf_op jit(solution)/shard_map/ppermute | solution.py:40
  84.1 7.9 %collective-permute-start.29 = (f32[176,256]{1,0:T(8,128)S(1)}, f32[176,256]{1,0:T(8,128)S(1)}, u32[]{:S(2)}, u32[]{:S(2)}) collective-permute-start(f32[176,256]{1,0:T(8,128)S(1)} %shard_map.143.own), channel_id=1, source_target_pairs={{0,24},{4,100},{8,16},{12,108},{16,8},{20,116},{24,0},{28,124},{32... | collective-permute-start | bytes 540680 | tf_op jit(solution)/shard_map/ppermute | solution.py:40
  103.6 7.5 %collective-permute-start.37 = (f32[128,256]{1,0:T(8,128)S(1)}, f32[128,256]{1,0:T(8,128)S(1)}, u32[]{:S(2)}, u32[]{:S(2)}) collective-permute-start(f32[128,256]{1,0:T(8,128)S(1)} %get-tuple-element.95.r0), channel_id=1, source_target_pairs={{0,2},{1,3},{2,0},{3,1},{4,6},{5,7},{6,4},{7,5},{8,10},{9,11},{10,... | collective-permute-start | bytes 393224 | tf_op jit(solution)/shard_map/ppermute | solution.py:44
  116.8 6.6 %collective-permute-start.41 = (f32[128,256]{1,0:T(8,128)S(1)}, f32[128,256]{1,0:T(8,128)S(1)}, u32[]{:S(2)}, u32[]{:S(2)}) collective-permute-start(f32[128,256]{1,0:T(8,128)S(1)} %shard_map.148.own), channel_id=1, source_target_pairs={{0,64},{4,20},{8,72},{12,28},{16,80},{20,4},{24,88},{28,12},{32,96... | collective-permute-start | bytes 393224 | tf_op jit(solution)/shard_map/ppermute | solution.py:36
  125.3 6.6 %collective-permute-start.44 = (f32[128,256]{1,0:T(8,128)S(1)}, f32[128,256]{1,0:T(8,128)S(1)}, u32[]{:S(2)}, u32[]{:S(2)}) collective-permute-start(f32[128,256]{1,0:T(8,128)S(1)} %shard_map.149.own), channel_id=1, source_target_pairs={{0,16},{4,68},{8,24},{12,76},{16,0},{20,84},{24,8},{28,92},{32,48}... | collective-permute-start | bytes 393224 | tf_op jit(solution)/shard_map/ppermute | solution.py:40
  126.6 6.7 %collective-permute-start.43 = (f32[128,256]{1,0:T(8,128)S(1)}, f32[128,256]{1,0:T(8,128)S(1)}, u32[]{:S(2)}, u32[]{:S(2)}) collective-permute-start(f32[128,256]{1,0:T(8,128)S(1)} %shard_map.149.own), channel_id=1, source_target_pairs={{0,24},{4,100},{8,16},{12,108},{16,8},{20,116},{24,0},{28,124},{32... | collective-permute-start | bytes 393224 | tf_op jit(solution)/shard_map/ppermute | solution.py:40
  137.7 7.9 %collective-permute-start.48 = (f32[128,256]{1,0:T(8,128)S(1)}, f32[128,256]{1,0:T(8,128)S(1)}, u32[]{:S(2)}, u32[]{:S(2)}) collective-permute-start(f32[128,256]{1,0:T(8,128)S(1)} %get-tuple-element.102.r0), channel_id=1, source_target_pairs={{0,2},{1,3},{2,0},{3,1},{4,6},{5,7},{6,4},{7,5},{8,10},{9,11},{10,... | collective-permute-start | bytes 393224 | tf_op jit(solution)/shard_map/ppermute | solution.py:44
  139.2 8.4 %collective-permute-start.47 = (f32[128,256]{1,0:T(8,128)S(1)}, f32[128,256]{1,0:T(8,128)S(1)}, u32[]{:S(2)}, u32[]{:S(2)}) collective-permute-start(f32[128,256]{1,0:T(8,128)S(1)} %get-tuple-element.102.r0), channel_id=1, source_target_pairs={{0,3},{1,2},{2,1},{3,0},{4,7},{5,6},{6,5},{7,4},{8,11},{9,10},{10,... | collective-permute-start | bytes 393224 | tf_op jit(solution)/shard_map/ppermute | solution.py:44
  140.9 6.8 %collective-permute-start.46 = (f32[128,256]{1,0:T(8,128)S(1)}, f32[128,256]{1,0:T(8,128)S(1)}, u32[]{:S(2)}, u32[]{:S(2)}) collective-permute-start(f32[128,256]{1,0:T(8,128)S(1)} %get-tuple-element.102.r0), channel_id=1, source_target_pairs={{0,1},{1,0},{2,3},{3,2},{4,5},{5,4},{6,7},{7,6},{8,9},{9,8},{10,11... | collective-permute-start | bytes 393224 | tf_op jit(solution)/shard_map/ppermute | solution.py:44
  152.0 6.6 %collective-permute-start.52 = (f32[128,256]{1,0:T(8,128)S(1)}, f32[128,256]{1,0:T(8,128)S(1)}, u32[]{:S(2)}, u32[]{:S(2)}) collective-permute-start(f32[128,256]{1,0:T(8,128)S(1)} %shard_map.153.own), channel_id=1, source_target_pairs={{0,64},{4,20},{8,72},{12,28},{16,80},{20,4},{24,88},{28,12},{32,96... | collective-permute-start | bytes 393224 | tf_op jit(solution)/shard_map/ppermute | solution.py:36
  160.0 6.6 %collective-permute-start.55 = (f32[128,256]{1,0:T(8,128)S(1)}, f32[128,256]{1,0:T(8,128)S(1)}, u32[]{:S(2)}, u32[]{:S(2)}) collective-permute-start(f32[128,256]{1,0:T(8,128)S(1)} %shard_map.154.own), channel_id=1, source_target_pairs={{0,16},{4,68},{8,24},{12,76},{16,0},{20,84},{24,8},{28,92},{32,48}... | collective-permute-start | bytes 393224 | tf_op jit(solution)/shard_map/ppermute | solution.py:40
  161.3 6.6 %collective-permute-start.54 = (f32[128,256]{1,0:T(8,128)S(1)}, f32[128,256]{1,0:T(8,128)S(1)}, u32[]{:S(2)}, u32[]{:S(2)}) collective-permute-start(f32[128,256]{1,0:T(8,128)S(1)} %shard_map.154.own), channel_id=1, source_target_pairs={{0,24},{4,100},{8,16},{12,108},{16,8},{20,116},{24,0},{28,124},{32... | collective-permute-start | bytes 393224 | tf_op jit(solution)/shard_map/ppermute | solution.py:40
  (42 other events, 272.4 us)

commit v12 on v11

--- a/solution.py
+++ b/solution.py
@@ -153,7 +153,7 @@
 
 
 def first_stats_kernel(
-    place, rows_hbm, cols_hbm, source, rhs, dual, rowout, colown, colother, tiles_ref, index_ref, racc, cacc,
+    place, rows_hbm, cols_hbm, source, dual, rowout, colown, colother, tiles_ref, index_ref, racc, cacc,
     rows_ref, cols_ref, sems,
 ):
     indices = [
@@ -173,7 +173,7 @@
         load(step).start()
     extra = [
         pltpu.make_async_copy(src, rowout.at[pl.ds(RT + i * SHARE, SHARE)], sems.at[LOADS + i])
-        for i, src in enumerate((rhs, dual))
+        for i, src in enumerate((dual,))
     ]
     for copy in extra:
         copy.start()
@@ -202,13 +202,13 @@
         copy.wait()
 
 
-def first_stats(ids, source, rhs, dual):
+def first_stats(ids, source, dual):
     vmem = pl.BlockSpec(memory_space=pltpu.VMEM)
-    shapes = [jax.ShapeDtypeStruct((n, TILE), F32) for n in (RT + 2 * SHARE, OWN, HALF)]
+    shapes = [jax.ShapeDtypeStruct((n, TILE), F32) for n in (RT + SHARE, OWN, HALF)]
     return pl.pallas_call(
         first_stats_kernel,
         out_shape=(*shapes, pltpu.VMEM((NT, TILE, TILE), F32), pltpu.SMEM((PLACE + 8,), jnp.int32)),
-        in_specs=[pl.BlockSpec(memory_space=pltpu.SMEM)] + [pl.BlockSpec(memory_space=pltpu.HBM)] * 5,
+        in_specs=[pl.BlockSpec(memory_space=pltpu.SMEM)] + [pl.BlockSpec(memory_space=pltpu.HBM)] * 4,
         out_specs=(vmem,) * 4 + (pl.BlockSpec(memory_space=pltpu.SMEM),),
         scratch_shapes=[
             ROWS,
@@ -218,7 +218,19 @@
             pltpu.SemaphoreType.DMA((LOADS + 4,)),
         ],
         compiler_params=pltpu.CompilerParams(vmem_limit_bytes=VMEM_LIMIT),
-    )(ids[2], *(pltpu.with_memory_space_constraint(x, pltpu.HBM) for x in (*ids[:2], source, rhs, dual)))
+    )(ids[2], *(pltpu.with_memory_space_constraint(x, pltpu.HBM) for x in (*ids[:2], source, dual)))
+
+
+def gather_rows(index_ref, near, far, out):
+    for k, ref, start in ((0, near, RT), (1, near, RT + SHARE), (3, far, RT), (2, far, RT + SHARE)):
+        at = pl.ds(pl.multiple_of((index_ref[PLACE + 2] ^ k) * SHARE, SHARE), SHARE)
+        out[at, :] = ref[start : start + SHARE]
+
+
+def merge_near(mine, got, near):
+    near[0:RT] = jnp.maximum(mine[0:RT], got[0:RT])
+    near[RT : RT + SHARE] = mine[RT:]
+    near[RT + SHARE :] = got[RT:]
 
 
 def second_columns_kernel(
@@ -239,7 +251,8 @@
     put_columns(cacc, colown, colother)
 
 
-def second_rows_kernel(index_ref, tiles_ref, col_scale, rowout, racc, colf):
+def second_rows_kernel(index_ref, tiles_ref, col_scale, rhs, rowout, racc, colf):
+    rowout[RT:] = rhs[...]
     split_to(colf, col_scale[...])
     racc[...] = jnp.zeros_like(racc)
 
@@ -252,9 +265,10 @@
 
 def third_rows_kernel(
     index_ref, tiles_ref, near, far, loc, mine, other, rowold, colold, rowout, rownew,
-    colnew, racc, colf,
-):
-    row = jnp.maximum(near[...], far[...])
+    colnew, rhsout, racc, colf,
+):
+    gather_rows(index_ref, near, far, rhsout)
+    row = jnp.maximum(near[0:RT], far[0:RT])
     old = rowold[...]
     rownew[...] = old / jnp.sqrt(old * row + EPS)
     for lo, hi, src in ((0, CT, loc), (CT, OWN, mine), (OWN, CW, other)):
@@ -283,12 +297,9 @@
 
 
 def first_backward_kernel(
-    index_ref, tiles_ref, near, far, after, colown, colother, rhsout, dualout, cacc, work
-):
-    for k, ref, start in ((0, near, RT), (1, near, RT + 2 * SHARE), (3, far, RT), (2, far, RT + 2 * SHARE)):
-        at = pl.ds(pl.multiple_of((index_ref[PLACE + 2] ^ k) * SHARE, SHARE), SHARE)
-        rhsout[at, :] = ref[start : start + SHARE]
-        dualout[at, :] = ref[start + SHARE : start + 2 * SHARE]
+    index_ref, tiles_ref, near, far, after, colown, colother, dualout, cacc, work
+):
+    gather_rows(index_ref, near, far, dualout)
     split_to(work, dualout[...])
     cacc[...] = jnp.zeros_like(cacc)
 
@@ -391,15 +402,13 @@
 
 def merge_rows_kernel(tiles_ref, own, r1, r3, r2, mine, got, out, near):
     out[...] = tree(jnp.maximum, own[...], (r1[...], r2[...], r3[...]))
-    near[0:RT] = jnp.maximum(mine[0:RT], got[0:RT])
-    near[RT : RT + 2 * SHARE] = mine[RT:]
-    near[RT + 2 * SHARE :] = got[RT:]
+    merge_near(mine, got, near)
 
 
 def merge_grad_kernel(
     index_ref, tiles_ref, own, r1, r3, r2, gradown, gradgot, mine, got, m0, m1, m2, m3, near, half
 ):
-    near[...] = jnp.maximum(mine[...], got[...])
+    merge_near(mine, got, near)
     link = tree(jnp.maximum, own[...], (r1[...], r2[...], r3[...]))
     half[...] = gradown[CT:OWN] + gradgot[...]
     for k, out in enumerate((m0, m1, m2, m3)):
@@ -498,14 +507,14 @@
         got = {k: swap(x, k) for k in (2, 1, 3)}
         return x, got[1], got[3], got[2]
 
-    row_part, colown, colother, tiles, index = first_stats(ids, tile_values[0, 0], rhs[0], start_dual[0])
+    row_part, colown, colother, tiles, index = first_stats(ids, tile_values[0, 0], start_dual[0])
 
     def run(kernel, smem, operands, outs, scratch=(), to_hbm=0):
         return call(kernel, smem, tiles, operands, outs, scratch, to_hbm)
 
     (link,) = run(functools.partial(core_kernel, jnp.maximum), (), (colown, swap_core(colother)), (HALF,))
     link, near = run(
-        merge_rows_kernel, (), (*over(swap_first, link), row_part, swap_y(row_part, 1)), (HALF, RT + 4 * SHARE)
+        merge_rows_kernel, (), (*over(swap_first, link), row_part, swap_y(row_part, 1)), (HALF, RT + 2 * SHARE)
     )
     far = swap_y(near, 3)
     (link,) = run(functools.partial(merge_kernel, jnp.maximum), (), over(swap_second, link), (HALF,))
@@ -519,28 +528,28 @@
         (COLS, ROWS),
     )
     colgot = swap_core(colother)
-    (row_part,) = run(second_rows_kernel, (index,), (col_scale,), (RT,), (ROWS, COLS))
+    (row_part,) = run(second_rows_kernel, (index,), (col_scale, rhs[0]), (RT + SHARE,), (ROWS, COLS))
     (link,) = run(core_after_kernel, (), (colown, colgot, row_part), (HALF,))
     got = over(swap_first, link)
-    gradown, gradother, rhs_rows, dual_rows = run(
-        first_backward_kernel, (index,), (*gathered, got[2]), (OWN, HALF, RT, RT), (COLS, ROWS)
+    gradown, gradother, dual_rows = run(
+        first_backward_kernel, (index,), (*gathered, got[2]), (OWN, HALF, RT), (COLS, ROWS)
     )
     *sent, near = run(
         merge_grad_kernel,
         (index,),
         (*got, gradown, swap_core(gradother), row_part, swap_y(row_part, 1)),
-        (HALF + CHUNK,) * 4 + (RT,),
+        (HALF + CHUNK,) * 4 + (RT + 2 * SHARE,),
         (pltpu.VMEM((HALF, TILE), F32),),
     )
     far = swap_y(near, 3)
     got = {k: swap_second(sent[k], k) for k in (2, 1, 3)}
     link, chunk = run(merge_chunk_kernel, (), (sent[0], got[2], got[1], got[3]), (HALF, CHUNK))
 
-    row_part, row_scale, col_scale = run(
+    row_part, row_scale, col_scale, rhs_rows = run(
         third_rows_kernel,
         (index,),
         (near, far, colown, link, swap_core(link), row_scale, col_scale),
-        (RT, RT, CW),
+        (RT, RT, CW, RT),
         (ROWS, COLS),
     )
     rows = over(swap_y, row_part)

time: 182 us -> 180 us (0.989)
    ppermute x11, waiting for transfers between devices: 10.8 us -> 7.99 us  [swap_core(): return lax.ppermute(x, 'scen', [(i, i ^ 1) for i in range(32)])]
  transfers between devices with their start and end apart: 60 -> 60, of which waited for: 41 -> 43; matrix products, arithmetic and copies ran while one was open for 0% -> 0% of each run, Pallas kernels for 5% -> 5%
where the time goes in v12:
time: 180 us
  waiting for transfers between devices  73.8 us (41%)
  starting transfers between devices  67.1 us (37%)
  Pallas kernels  38 us (21%)
    pallas_call x26, Pallas kernels, call(): pl.pallas_call(kernel, out_shape=tuple((jax.ShapeDtypeStruct((n, TILE), F...  30.6 us
    ppermute x19, starting transfers between devices, swap_y(): return lax.ppermute(x, 'col', [(i, i ^ k) for i in range(4)])  26.9 us
    ppermute x19, waiting for transfers between devices, swap_y(): return lax.ppermute(x, 'col', [(i, i ^ k) for i in range(4)])  24.9 us
    ppermute x15, waiting for transfers between devices, swap_first(): lax.ppermute(x, 'scen', [(i, i ^ k << (1 if i % 2 else 3)) for i in range...  20.7 us
    ppermute x15, waiting for transfers between devices, swap_second(): lax.ppermute(x, 'scen', [(i, i ^ k << (3 if i % 2 else 1)) for i in range...  20.2 us
    ppermute x15, starting transfers between devices, swap_second(): lax.ppermute(x, 'scen', [(i, i ^ k << (3 if i % 2 else 1)) for i in range...  20.2 us
    ppermute x15, starting transfers between devices, swap_first(): lax.ppermute(x, 'scen', [(i, i ^ k << (1 if i % 2 else 3)) for i in range...  19.1 us
    ppermute x11, waiting for transfers between devices, swap_core(): return lax.ppermute(x, 'scen', [(i, i ^ 1) for i in range(32)])  7.99 us
  transfers between devices with their start and end apart: 60, of which 43 were waited for; matrix products, arithmetic and copies ran while one was open for 0% of the time, Pallas kernels for 5%

profile of v12, /device:TPU:0, one launch (start us, length us, event | category | flops | bytes accessed | tf_op | source)
XLA Modules:
  0.0 180.0 jit_solution(4955665457624994135)
XLA Ops:
  0.8 6.8 %shard_map.130 = (f32[160,256]{1,0:T(8,128)S(1)}, f32[136,256]{1,0:T(8,128)S(1)}, f32[128,256]{1,0:T(8,128)S(1)}, f32[64,256,256]{2,1,0:T(8,128)S(1)}, s32[136]{0:T(256)S(4)}) custom-call(s32[3]{0:T(128)S(1)} %pad_add_fusion.place, s32[64]{0:T(128)} %bitcast.28, s32[64]{0:T(128)} %bitcast.29, f32[64,256,256]{2,1,0:T(8,128)} %bitcast.25, f32[32,256]{1,0:T(8,128)} %bitcast.26), custom_call_target="tpu_custom_call" | custom-call | tf_op jit(solution)/shard_map/pallas_call | solution.py:208
  9.4 3.1 %collective-permute-start.3 = (f32[128,256]{1,0:T(8,128)S(1)}, f32[128,256]{1,0:T(8,128)S(1)}, u32[]{:S(2)}, u32[]{:S(2)}) collective-permute-start(f32[128,256]{1,0:T(8,128)S(1)} %shard_map.131.own), channel_id=1, source_target_pairs={{0,64},{4,20},{8,72},{12,28},{16,80},{20,4},{24,88},{28,12},{32,96... | collective-permute-start | bytes 393224 | tf_op jit(solution)/shard_map/ppermute | solution.py:36
  15.9 2.7 %collective-permute-done.2.r3 = f32[128,256]{1,0:T(8,128)S(1)} collective-permute-done((f32[128,256]{1,0:T(8,128)S(1)}, f32[128,256]{1,0:T(8,128)S(1)}, u32[]{:S(2)}, u32[]{:S(2)}) %collective-permute-start.2) | collective-permute-done | bytes 131104 | tf_op jit(solution)/shard_map/ppermute | solution.py:36
  18.7 4.0 %collective-permute-start.8 = (f32[128,256]{1,0:T(8,128)S(1)}, f32[128,256]{1,0:T(8,128)S(1)}, u32[]{:S(2)}, u32[]{:S(2)}) collective-permute-start(f32[128,256]{1,0:T(8,128)S(1)} %get-tuple-element.66.own), channel_id=1, source_target_pairs={{0,16},{4,68},{8,24},{12,76},{16,0},{20,84},{24,8},{28,92},{32,48}... | collective-permute-start | bytes 393224 | tf_op jit(solution)/shard_map/ppermute | solution.py:40
  30.6 3.0 %shard_map.134 = (f32[136,256]{1,0:T(8,128)S(1)}, f32[128,256]{1,0:T(8,128)S(1)}, f32[128,256]{1,0:T(8,128)S(1)}, f32[264,256]{1,0:T(8,128)S(1)}) custom-call(s32[136]{0:T(256)S(4)} %get-tuple-element.60.index_ref, f32[64,256,256]{2,1,0:T(8,128)S(1)} %get-tuple-element.61.tiles_ref, f32[192,256]{1,0:T(8,128)S(1)} %get-tuple-element.65.near, ...), custom_call_target="tpu_custom_call" | custom-call | tf_op jit(solution)/shard_map/pallas_call | solution.py:128
  33.7 2.9 %shard_map.135.after.mine = f32[160,256]{1,0:T(8,128)S(1)} custom-call(s32[136]{0:T(256)S(4)} %get-tuple-element.60.index_ref, f32[64,256,256]{2,1,0:T(8,128)S(1)} %get-tuple-element.61.tiles_ref, f32[264,256]{1,0:T(8,128)S(1)} %get-tuple-element.69.col_scale.colold, f32[32,256]{1,0:T(8,128)S(1)} %bitcast.22), custom_call_target="tpu_custom_call" | custom-call | tf_op jit(solution)/shard_map/pallas_call | solution.py:128
  42.9 2.8 %shard_map.137 = (f32[136,256]{1,0:T(8,128)S(1)}, f32[128,256]{1,0:T(8,128)S(1)}, f32[128,256]{1,0:T(8,128)S(1)}) custom-call(s32[136]{0:T(256)S(4)} %get-tuple-element.60.index_ref, f32[64,256,256]{2,1,0:T(8,128)S(1)} %get-tuple-element.61.tiles_ref, f32[192,256]{1,0:T(8,128)S(1)} %get-tuple-element.65.near, f32[192,256]{1,0:T(8,128)S(1)} %collective-permute-done.5.far, ...), custom_call_target="tpu_custom_call" | custom-call | tf_op jit(solution)/shard_map/pallas_call | solution.py:128
  47.2 3.8 %collective-permute-start.17 = (f32[160,256]{1,0:T(8,128)S(1)}, f32[160,256]{1,0:T(8,128)S(1)}, u32[]{:S(2)}, u32[]{:S(2)}) collective-permute-start(f32[160,256]{1,0:T(8,128)S(1)} %get-tuple-element.74), channel_id=1, source_target_pairs={{0,16},{4,68},{8,24},{12,76},{16,0},{20,84},{24,8},{28,92},{32,48}... | collective-permute-start | bytes 491528 | tf_op jit(solution)/shard_map/ppermute | solution.py:40
  59.0 3.0 %shard_map.140 = (f32[128,256]{1,0:T(8,128)S(1)}, f32[128,256]{1,0:T(8,128)S(1)}, f32[264,256]{1,0:T(8,128)S(1)}, f32[128,256]{1,0:T(8,128)S(1)}) custom-call(s32[136]{0:T(256)S(4)} %get-tuple-element.60.index_ref, f32[64,256,256]{2,1,0:T(8,128)S(1)} %get-tuple-element.61.tiles_ref, f32[192,256]{1,0:T(8,128)S(1)} %get-tuple-element.72.near, ...), custom_call_target="tpu_custom_call" | custom-call | tf_op jit(solution)/shard_map/pallas_call | solution.py:128
  65.8 3.2 %shard_map.141 = (f32[136,256]{1,0:T(8,128)S(1)}, f32[128,256]{1,0:T(8,128)S(1)}) custom-call(s32[136]{0:T(256)S(4)} %get-tuple-element.60.index_ref, f32[64,256,256]{2,1,0:T(8,128)S(1)} %get-tuple-element.61.tiles_ref, f32[128,256]{1,0:T(8,128)S(1)} %get-tuple-element.80.row_scale.rowold), custom_call_target="tpu_custom_call" | custom-call | tf_op jit(solution)/shard_map/pallas_call | solution.py:128
  69.2 2.7 %collective-permute-done.22.r3 = f32[128,256]{1,0:T(8,128)S(1)} collective-permute-done((f32[128,256]{1,0:T(8,128)S(1)}, f32[128,256]{1,0:T(8,128)S(1)}, u32[]{:S(2)}, u32[]{:S(2)}) %collective-permute-start.22) | collective-permute-done | bytes 131104 | tf_op jit(solution)/shard_map/ppermute | solution.py:44
  76.0 3.5 %collective-permute-done.27.r2 = f32[176,256]{1,0:T(8,128)S(1)} collective-permute-done((f32[176,256]{1,0:T(8,128)S(1)}, f32[176,256]{1,0:T(8,128)S(1)}, u32[]{:S(2)}, u32[]{:S(2)}) %collective-permute-start.27) | collective-permute-done | bytes 180256 | tf_op jit(solution)/shard_map/ppermute | solution.py:36
  85.1 3.5 %collective-permute-done.30.r2 = f32[176,256]{1,0:T(8,128)S(1)} collective-permute-done((f32[176,256]{1,0:T(8,128)S(1)}, f32[176,256]{1,0:T(8,128)S(1)}, u32[]{:S(2)}, u32[]{:S(2)}) %collective-permute-start.30) | collective-permute-done | bytes 180256 | tf_op jit(solution)/shard_map/ppermute | solution.py:40
  99.3 3.1 %shard_map.146 = (f32[8,256]{1,0:T(8,128)S(1)}, f32[128,256]{1,0:T(8,128)S(1)}, f32[264,256]{1,0:T(8,128)S(1)}) custom-call(s32[136]{0:T(256)S(4)} %get-tuple-element.60.index_ref, f32[64,256,256]{2,1,0:T(8,128)S(1)} %get-tuple-element.61.tiles_ref, f32[8,256]{1,0:T(8,128)S(1)} %get-tuple-element.88.rest_0_, f32[8,256]{1,0:T(8,128)S(1)} %collective-permute-done.32.rest_1_, ...), custom_call_target="tpu_custom_call" | custom-call | tf_op jit(solution)/shard_map/pallas_call | solution.py:128
  106.0 4.1 %collective-permute-done.37.r2 = f32[128,256]{1,0:T(8,128)S(1)} collective-permute-done((f32[128,256]{1,0:T(8,128)S(1)}, f32[128,256]{1,0:T(8,128)S(1)}, u32[]{:S(2)}, u32[]{:S(2)}) %collective-permute-start.37) | collective-permute-done | bytes 131104 | tf_op jit(solution)/shard_map/ppermute | solution.py:44
  111.2 2.9 %shard_map.147 = (f32[136,256]{1,0:T(8,128)S(1)}, f32[128,256]{1,0:T(8,128)S(1)}, f32[128,256]{1,0:T(8,128)S(1)}) custom-call(s32[136]{0:T(256)S(4)} %get-tuple-element.60.index_ref, f32[64,256,256]{2,1,0:T(8,128)S(1)} %get-tuple-element.61.tiles_ref, f32[8,256]{1,0:T(8,128)S(1)} %get-tuple-element.94.steps.rest_0_, f32[128,256]{1,0:T(8,128)S(1)} %get-tuple-element.95.r0, ...), custom_call_target="tpu_custom_call" | custom-call | tf_op jit(solution)/shard_map/pallas_call | solution.py:128
  119.1 3.0 %collective-permute-done.41.r2 = f32[128,256]{1,0:T(8,128)S(1)} collective-permute-done((f32[128,256]{1,0:T(8,128)S(1)}, f32[128,256]{1,0:T(8,128)S(1)}, u32[]{:S(2)}, u32[]{:S(2)}) %collective-permute-start.41) | collective-permute-done | bytes 131104 | tf_op jit(solution)/shard_map/ppermute | solution.py:36
  127.5 3.0 %collective-permute-done.44.r2 = f32[128,256]{1,0:T(8,128)S(1)} collective-permute-done((f32[128,256]{1,0:T(8,128)S(1)}, f32[128,256]{1,0:T(8,128)S(1)}, u32[]{:S(2)}, u32[]{:S(2)}) %collective-permute-start.44) | collective-permute-done | bytes 131104 | tf_op jit(solution)/shard_map/ppermute | solution.py:40
  133.7 3.0 %shard_map.151 = (f32[128,256]{1,0:T(8,128)S(1)}, f32[264,256]{1,0:T(8,128)S(1)}) custom-call(s32[136]{0:T(256)S(4)} %get-tuple-element.60.index_ref, f32[64,256,256]{2,1,0:T(8,128)S(1)} %get-tuple-element.61.tiles_ref, f32[8,256]{1,0:T(8,128)S(1)} %get-tuple-element.94.steps.rest_0_, f32[136,256]{1,0:T(8,128)S(1)} %get-tuple-element.99.colown.rest_1_, ...), custom_call_target="tpu_custom_call" | custom-call | tf_op jit(solution)/shard_map/pallas_call | solution.py:128
  140.3 4.4 %collective-permute-done.48.r2 = f32[128,256]{1,0:T(8,128)S(1)} collective-permute-done((f32[128,256]{1,0:T(8,128)S(1)}, f32[128,256]{1,0:T(8,128)S(1)}, u32[]{:S(2)}, u32[]{:S(2)}) %collective-permute-start.48) | collective-permute-done | bytes 131104 | tf_op jit(solution)/shard_map/ppermute | solution.py:44
  146.6 2.9 %shard_map.152 = (f32[136,256]{1,0:T(8,128)S(1)}, f32[128,256]{1,0:T(8,128)S(1)}, f32[128,256]{1,0:T(8,128)S(1)}) custom-call(s32[136]{0:T(256)S(4)} %get-tuple-element.60.index_ref, f32[64,256,256]{2,1,0:T(8,128)S(1)} %get-tuple-element.61.tiles_ref, f32[8,256]{1,0:T(8,128)S(1)} %get-tuple-element.94.steps.rest_0_, f32[128,256]{1,0:T(8,128)S(1)} %get-tuple-element.102.r0, ...), custom_call_target="tpu_custom_call" | custom-call | tf_op jit(solution)/shard_map/pallas_call | solution.py:128
  154.5 3.0 %collective-permute-done.52.r2 = f32[128,256]{1,0:T(8,128)S(1)} collective-permute-done((f32[128,256]{1,0:T(8,128)S(1)}, f32[128,256]{1,0:T(8,128)S(1)}, u32[]{:S(2)}, u32[]{:S(2)}) %collective-permute-start.52) | collective-permute-done | bytes 131104 | tf_op jit(solution)/shard_map/ppermute | solution.py:36
  162.7 3.0 %collective-permute-done.55.r2 = f32[128,256]{1,0:T(8,128)S(1)} collective-permute-done((f32[128,256]{1,0:T(8,128)S(1)}, f32[128,256]{1,0:T(8,128)S(1)}, u32[]{:S(2)}, u32[]{:S(2)}) %collective-permute-start.55) | collective-permute-done | bytes 131104 | tf_op jit(solution)/shard_map/ppermute | solution.py:40
  168.5 3.0 %shard_map.156 = (f32[8,256]{1,0:T(8,128)}, f32[256,256]{1,0:T(8,128)}, f32[32,256]{1,0:T(8,128)S(1)}, f32[32,256]{1,0:T(8,128)S(1)}, f32[32,256]{1,0:T(8,128)S(...) custom-call(s32[136]{0:T(256)S(4)} %get-tuple-element.60.index_ref, ...), custom_call_target="tpu_custom_call" | custom-call | tf_op jit(solution)/shard_map/pallas_call | solution.py:128
  (139 shorter events, 98.8 us)
Async XLA Ops:
  7.6 6.6 %collective-permute-start.4 = (f32[160,256]{1,0:T(8,128)S(1)}, f32[160,256]{1,0:T(8,128)S(1)}, u32[]{:S(2)}, u32[]{:S(2)}) collective-permute-start(f32[160,256]{1,0:T(8,128)S(1)} %get-tuple-element.64.mine), channel_id=1, source_target_pairs={{0,1},{1,0},{2,3},{3,2},{4,5},{5,4},{6,7},{7,6},{8,9},{9,8},{10,11... | collective-permute-start | bytes 491528 | tf_op jit(solution)/shard_map/ppermute | solution.py:44
  9.4 6.5 %collective-permute-start.3 = (f32[128,256]{1,0:T(8,128)S(1)}, f32[128,256]{1,0:T(8,128)S(1)}, u32[]{:S(2)}, u32[]{:S(2)}) collective-permute-start(f32[128,256]{1,0:T(8,128)S(1)} %shard_map.131.own), channel_id=1, source_target_pairs={{0,64},{4,20},{8,72},{12,28},{16,80},{20,4},{24,88},{28,12},{32,96... | collective-permute-start | bytes 393224 | tf_op jit(solution)/shard_map/ppermute | solution.py:36
  18.7 7.7 %collective-permute-start.8 = (f32[128,256]{1,0:T(8,128)S(1)}, f32[128,256]{1,0:T(8,128)S(1)}, u32[]{:S(2)}, u32[]{:S(2)}) collective-permute-start(f32[128,256]{1,0:T(8,128)S(1)} %get-tuple-element.66.own), channel_id=1, source_target_pairs={{0,16},{4,68},{8,24},{12,76},{16,0},{20,84},{24,8},{28,92},{32,48}... | collective-permute-start | bytes 393224 | tf_op jit(solution)/shard_map/ppermute | solution.py:40
  23.7 6.9 %collective-permute-start.5 = (f32[192,256]{1,0:T(8,128)S(1)}, f32[192,256]{1,0:T(8,128)S(1)}, u32[]{:S(2)}, u32[]{:S(2)}) collective-permute-start(f32[192,256]{1,0:T(8,128)S(1)} %get-tuple-element.65.near), channel_id=1, source_target_pairs={{0,3},{1,2},{2,1},{3,0},{4,7},{5,6},{6,5},{7,4},{8,11},{9,10},{10,... | collective-permute-start | bytes 589832 | tf_op jit(solution)/shard_map/ppermute | solution.py:44
  38.7 7.1 %collective-permute-start.15 = (f32[160,256]{1,0:T(8,128)S(1)}, f32[160,256]{1,0:T(8,128)S(1)}, u32[]{:S(2)}, u32[]{:S(2)}) collective-permute-start(f32[160,256]{1,0:T(8,128)S(1)} %shard_map.135.after.mine), channel_id=1, source_target_pairs={{0,1},{1,0},{2,3},{3,2},{4,5},{5,4},{6,7},{7,6},{8,9},{9,8},{10,11... | collective-permute-start | bytes 491528 | tf_op jit(solution)/shard_map/ppermute | solution.py:44
  39.8 6.5 %collective-permute-start.13 = (f32[128,256]{1,0:T(8,128)S(1)}, f32[128,256]{1,0:T(8,128)S(1)}, u32[]{:S(2)}, u32[]{:S(2)}) collective-permute-start(f32[128,256]{1,0:T(8,128)S(1)} %shard_map.136.own), channel_id=1, source_target_pairs={{0,64},{4,20},{8,72},{12,28},{16,80},{20,4},{24,88},{28,12},{32,96... | collective-permute-start | bytes 393224 | tf_op jit(solution)/shard_map/ppermute | solution.py:36
  47.2 7.2 %collective-permute-start.17 = (f32[160,256]{1,0:T(8,128)S(1)}, f32[160,256]{1,0:T(8,128)S(1)}, u32[]{:S(2)}, u32[]{:S(2)}) collective-permute-start(f32[160,256]{1,0:T(8,128)S(1)} %get-tuple-element.74), channel_id=1, source_target_pairs={{0,16},{4,68},{8,24},{12,76},{16,0},{20,84},{24,8},{28,92},{32,48}... | collective-permute-start | bytes 491528 | tf_op jit(solution)/shard_map/ppermute | solution.py:40
  51.0 6.5 %collective-permute-start.19 = (f32[160,256]{1,0:T(8,128)S(1)}, f32[160,256]{1,0:T(8,128)S(1)}, u32[]{:S(2)}, u32[]{:S(2)}) collective-permute-start(f32[160,256]{1,0:T(8,128)S(1)} %get-tuple-element.76), channel_id=1, source_target_pairs={{0,24},{4,100},{8,16},{12,108},{16,8},{20,116},{24,0},{28,124},{32... | collective-permute-start | bytes 491528 | tf_op jit(solution)/shard_map/ppermute | solution.py:40
  51.7 7.0 %collective-permute-start.16 = (f32[192,256]{1,0:T(8,128)S(1)}, f32[192,256]{1,0:T(8,128)S(1)}, u32[]{:S(2)}, u32[]{:S(2)}) collective-permute-start(f32[192,256]{1,0:T(8,128)S(1)} %get-tuple-element.72.near), channel_id=1, source_target_pairs={{0,3},{1,2},{2,1},{3,0},{4,7},{5,6},{6,5},{7,4},{8,11},{9,10},{10,... | collective-permute-start | bytes 589832 | tf_op jit(solution)/shard_map/ppermute | solution.py:44
  62.0 7.2 %collective-permute-start.23 = (f32[128,256]{1,0:T(8,128)S(1)}, f32[128,256]{1,0:T(8,128)S(1)}, u32[]{:S(2)}, u32[]{:S(2)}) collective-permute-start(f32[128,256]{1,0:T(8,128)S(1)} %get-tuple-element.79.r0), channel_id=1, source_target_pairs={{0,2},{1,3},{2,0},{3,1},{4,6},{5,7},{6,4},{7,5},{8,10},{9,11},{10,... | collective-permute-start | bytes 393224 | tf_op jit(solution)/shard_map/ppermute | solution.py:44
  64.3 7.7 %collective-permute-start.22 = (f32[128,256]{1,0:T(8,128)S(1)}, f32[128,256]{1,0:T(8,128)S(1)}, u32[]{:S(2)}, u32[]{:S(2)}) collective-permute-start(f32[128,256]{1,0:T(8,128)S(1)} %get-tuple-element.79.r0), channel_id=1, source_target_pairs={{0,3},{1,2},{2,1},{3,0},{4,7},{5,6},{6,5},{7,4},{8,11},{9,10},{10,... | collective-permute-start | bytes 393224 | tf_op jit(solution)/shard_map/ppermute | solution.py:44
  65.1 7.1 %collective-permute-start.21 = (f32[128,256]{1,0:T(8,128)S(1)}, f32[128,256]{1,0:T(8,128)S(1)}, u32[]{:S(2)}, u32[]{:S(2)}) collective-permute-start(f32[128,256]{1,0:T(8,128)S(1)} %get-tuple-element.79.r0), channel_id=1, source_target_pairs={{0,1},{1,0},{2,3},{3,2},{4,5},{5,4},{6,7},{7,6},{8,9},{9,8},{10,11... | collective-permute-start | bytes 393224 | tf_op jit(solution)/shard_map/ppermute | solution.py:44
  72.4 7.1 %collective-permute-start.27 = (f32[176,256]{1,0:T(8,128)S(1)}, f32[176,256]{1,0:T(8,128)S(1)}, u32[]{:S(2)}, u32[]{:S(2)}) collective-permute-start(f32[176,256]{1,0:T(8,128)S(1)} %get-tuple-element.87.own), channel_id=1, source_target_pairs={{0,64},{4,20},{8,72},{12,28},{16,80},{20,4},{24,88},{28,12},{32,96... | collective-permute-start | bytes 540680 | tf_op jit(solution)/shard_map/ppermute | solution.py:36
  74.8 6.7 %collective-permute-start.26 = (f32[176,256]{1,0:T(8,128)S(1)}, f32[176,256]{1,0:T(8,128)S(1)}, u32[]{:S(2)}, u32[]{:S(2)}) collective-permute-start(f32[176,256]{1,0:T(8,128)S(1)} %get-tuple-element.87.own), channel_id=1, source_target_pairs={{0,96},{4,28},{8,104},{12,20},{16,112},{20,12},{24,120},{28,4},{32... | collective-permute-start | bytes 540680 | tf_op jit(solution)/shard_map/ppermute | solution.py:36
  81.6 7.1 %collective-permute-start.30 = (f32[176,256]{1,0:T(8,128)S(1)}, f32[176,256]{1,0:T(8,128)S(1)}, u32[]{:S(2)}, u32[]{:S(2)}) collective-permute-start(f32[176,256]{1,0:T(8,128)S(1)} %shard_map.143.own), channel_id=1, source_target_pairs={{0,16},{4,68},{8,24},{12,76},{16,0},{20,84},{24,8},{28,92},{32,48}... | collective-permute-start | bytes 540680 | tf_op jit(solution)/shard_map/ppermute | solution.py:40
  83.6 7.0 %collective-permute-start.29 = (f32[176,256]{1,0:T(8,128)S(1)}, f32[176,256]{1,0:T(8,128)S(1)}, u32[]{:S(2)}, u32[]{:S(2)}) collective-permute-start(f32[176,256]{1,0:T(8,128)S(1)} %shard_map.143.own), channel_id=1, source_target_pairs={{0,24},{4,100},{8,16},{12,108},{16,8},{20,116},{24,0},{28,124},{32... | collective-permute-start | bytes 540680 | tf_op jit(solution)/shard_map/ppermute | solution.py:40
  102.4 7.6 %collective-permute-start.37 = (f32[128,256]{1,0:T(8,128)S(1)}, f32[128,256]{1,0:T(8,128)S(1)}, u32[]{:S(2)}, u32[]{:S(2)}) collective-permute-start(f32[128,256]{1,0:T(8,128)S(1)} %get-tuple-element.95.r0), channel_id=1, source_target_pairs={{0,2},{1,3},{2,0},{3,1},{4,6},{5,7},{6,4},{7,5},{8,10},{9,11},{10,... | collective-permute-start | bytes 393224 | tf_op jit(solution)/shard_map/ppermute | solution.py:44
  115.6 6.5 %collective-permute-start.41 = (f32[128,256]{1,0:T(8,128)S(1)}, f32[128,256]{1,0:T(8,128)S(1)}, u32[]{:S(2)}, u32[]{:S(2)}) collective-permute-start(f32[128,256]{1,0:T(8,128)S(1)} %shard_map.148.own), channel_id=1, source_target_pairs={{0,64},{4,20},{8,72},{12,28},{16,80},{20,4},{24,88},{28,12},{32,96... | collective-permute-start | bytes 393224 | tf_op jit(solution)/shard_map/ppermute | solution.py:36
  123.9 6.6 %collective-permute-start.44 = (f32[128,256]{1,0:T(8,128)S(1)}, f32[128,256]{1,0:T(8,128)S(1)}, u32[]{:S(2)}, u32[]{:S(2)}) collective-permute-start(f32[128,256]{1,0:T(8,128)S(1)} %shard_map.149.own), channel_id=1, source_target_pairs={{0,16},{4,68},{8,24},{12,76},{16,0},{20,84},{24,8},{28,92},{32,48}... | collective-permute-start | bytes 393224 | tf_op jit(solution)/shard_map/ppermute | solution.py:40
  136.7 7.9 %collective-permute-start.48 = (f32[128,256]{1,0:T(8,128)S(1)}, f32[128,256]{1,0:T(8,128)S(1)}, u32[]{:S(2)}, u32[]{:S(2)}) collective-permute-start(f32[128,256]{1,0:T(8,128)S(1)} %get-tuple-element.102.r0), channel_id=1, source_target_pairs={{0,2},{1,3},{2,0},{3,1},{4,6},{5,7},{6,4},{7,5},{8,10},{9,11},{10,... | collective-permute-start | bytes 393224 | tf_op jit(solution)/shard_map/ppermute | solution.py:44
  138.0 8.6 %collective-permute-start.47 = (f32[128,256]{1,0:T(8,128)S(1)}, f32[128,256]{1,0:T(8,128)S(1)}, u32[]{:S(2)}, u32[]{:S(2)}) collective-permute-start(f32[128,256]{1,0:T(8,128)S(1)} %get-tuple-element.102.r0), channel_id=1, source_target_pairs={{0,3},{1,2},{2,1},{3,0},{4,7},{5,6},{6,5},{7,4},{8,11},{9,10},{10,... | collective-permute-start | bytes 393224 | tf_op jit(solution)/shard_map/ppermute | solution.py:44
  139.5 7.1 %collective-permute-start.46 = (f32[128,256]{1,0:T(8,128)S(1)}, f32[128,256]{1,0:T(8,128)S(1)}, u32[]{:S(2)}, u32[]{:S(2)}) collective-permute-start(f32[128,256]{1,0:T(8,128)S(1)} %get-tuple-element.102.r0), channel_id=1, source_target_pairs={{0,1},{1,0},{2,3},{3,2},{4,5},{5,4},{6,7},{7,6},{8,9},{9,8},{10,11... | collective-permute-start | bytes 393224 | tf_op jit(solution)/shard_map/ppermute | solution.py:44
  151.0 6.5 %collective-permute-start.52 = (f32[128,256]{1,0:T(8,128)S(1)}, f32[128,256]{1,0:T(8,128)S(1)}, u32[]{:S(2)}, u32[]{:S(2)}) collective-permute-start(f32[128,256]{1,0:T(8,128)S(1)} %shard_map.153.own), channel_id=1, source_target_pairs={{0,64},{4,20},{8,72},{12,28},{16,80},{20,4},{24,88},{28,12},{32,96... | collective-permute-start | bytes 393224 | tf_op jit(solution)/shard_map/ppermute | solution.py:36
  159.1 6.6 %collective-permute-start.55 = (f32[128,256]{1,0:T(8,128)S(1)}, f32[128,256]{1,0:T(8,128)S(1)}, u32[]{:S(2)}, u32[]{:S(2)}) collective-permute-start(f32[128,256]{1,0:T(8,128)S(1)} %shard_map.154.own), channel_id=1, source_target_pairs={{0,16},{4,68},{8,24},{12,76},{16,0},{20,84},{24,8},{28,92},{32,48}... | collective-permute-start | bytes 393224 | tf_op jit(solution)/shard_map/ppermute | solution.py:40
  (43 other events, 280.1 us)
